TPU v7x, 32 devices: a whole 2x2x4 slice. The times are simulated.
32 devices in a mesh: dp: 8 (over y, x, core), tensor: 4 (over z).
Axes of the slice: x: 2, y: 2, z: 4, core: 2. Of those that a mesh axis runs over, the one named last changes fastest.
Arguments:
- frames_in: bfloat16 [8, 1024, 1536], P('dp', 'tensor'), may hold values from -6 to 6
- text_states: bfloat16 [8, 64, 1536], P('dp'), may hold values from -6 to 6
- ln_gain: bfloat16 [2, 3, 1536], P(None, None, 'dp'), may hold values from 0.5 to 1.5
- ln_bias: bfloat16 [2, 3, 1536], P(None, None, 'dp'), may hold values from -2 to 2
- w_self: bfloat16 [2, 1536, 3, 1536], P(None, 'dp', None, 'tensor'), may hold values from -0.15625 to 0.15625
- w_self_out: bfloat16 [2, 1536, 1536], P(None, 'tensor', 'dp'), may hold values from -0.625 to 0.625
- w_cross_q: bfloat16 [2, 1536, 1536], P(None, 'dp', 'tensor'), may hold values from -0.15625 to 0.15625
- w_cross_kv: bfloat16 [2, 1536, 2, 1536], P(None, 'dp', None, 'tensor'), may hold values from -0.15625 to 0.15625
- w_cross_out: bfloat16 [2, 1536, 1536], P(None, 'tensor', 'dp'), may hold values from -0.3125 to 0.3125
- w_up: bfloat16 [2, 1536, 6144], P(None, 'dp', 'tensor'), may hold values from -0.15625 to 0.15625
- w_down: bfloat16 [2, 6144, 1536], P(None, 'tensor', 'dp'), may hold values from -0.109375 to 0.109375
- cotangent: bfloat16 [8, 1024, 1536], P('dp', 'tensor'), may hold values from -8 to 8
Outputs:
- result: bfloat16 [8, 1024, 1536], P('dp', 'tensor')
- grad_frames: float32 [8, 1024, 1536], P('dp', 'tensor')
- grad_text: float32 [8, 64, 1536], P('dp')
- grad_ln_gain: float32 [2, 3, 1536], P(None, None, 'dp')
- grad_ln_bias: float32 [2, 3, 1536], P(None, None, 'dp')
- grad_w_self: float32 [2, 1536, 3, 1536], P(None, 'dp', None, 'tensor')
- grad_w_self_out: float32 [2, 1536, 1536], P(None, 'tensor', 'dp')
- grad_w_cross_q: float32 [2, 1536, 1536], P(None, 'dp', 'tensor')
- grad_w_cross_kv: float32 [2, 1536, 2, 1536], P(None, 'dp', None, 'tensor')
- grad_w_cross_out: float32 [2, 1536, 1536], P(None, 'tensor', 'dp')
- grad_w_up: float32 [2, 1536, 6144], P(None, 'dp', 'tensor')
- grad_w_down: float32 [2, 6144, 1536], P(None, 'tensor', 'dp')
All inputs are finite; a program needn't handle non-finite values.
Results may differ from a plain program's by a relative error of at most 0.03.
Values may be sent and summed in bfloat16 or wider, within the bound.
A program may use at most 320 MiB of HBM per device.

v0:
```python
import jax
import jax.numpy as jnp
from jax import lax
from jax.sharding import PartitionSpec as P

HEAD_DIM = 64
ATT_BLOCK = 512


norm_eps = 1e-05
masked_score = -1e30


def shortened(shard):
    return jax.tree.map(lambda a: a.astype(jnp.bfloat16) if a.dtype == jnp.float32 else a, shard)


def layer_norm(stream, gain, shift):
    centre = jnp.mean(stream, axis=-1, keepdims=True)
    centred = stream - centre
    spread = jnp.mean(centred * centred, axis=-1, keepdims=True)
    return centred * lax.rsqrt(spread + norm_eps) * gain + shift


def exact_gelu(value):
    return jax.nn.gelu(value, approximate=False)


def causal_mask(scores, offset):
    rows = offset + lax.broadcasted_iota(jnp.int32, scores.shape[-2:], 0)
    cols = lax.broadcasted_iota(jnp.int32, scores.shape[-2:], 1)
    return jnp.where(rows >= cols, scores, masked_score)


def gather_normed(normed):
    return jax.tree.map(
        lambda part, own: part.astype(own.dtype),
        lax.all_gather(shortened(normed), "tensor", axis=1, tiled=True),
        normed,
    )


def sum_branch(partial_rows):
    return jax.tree.map(
        lambda part: part.astype(jnp.float32),
        lax.psum_scatter(shortened(partial_rows), "tensor", scatter_dimension=1, tiled=True),
    )


def spread_rows(grad_rows):
    return jax.tree.map(
        lambda part, own: part.astype(own.dtype),
        lax.all_gather(shortened(grad_rows), "tensor", axis=1, tiled=True),
        grad_rows,
    )


def fold_rows(partial_rows):
    return jax.tree.map(
        lambda part: part.astype(jnp.float32),
        lax.psum_scatter(shortened(partial_rows), "tensor", scatter_dimension=1, tiled=True),
    )


def attend_forward(query, keys, values, offset, causal, scale):
    scores = jnp.einsum("cqhd,ckhd->chqk", query, keys, preferred_element_type=jnp.float32) * scale
    if causal:
        scores = causal_mask(scores, offset)
    top = jnp.max(scores, axis=-1, keepdims=True)
    expo = jnp.exp(scores - top)
    total = jnp.sum(expo, axis=-1, keepdims=True)
    probs = (expo / total).astype(jnp.bfloat16)
    mixed = jnp.einsum("chqk,ckhd->cqhd", probs, values, preferred_element_type=jnp.float32)
    return (mixed, top + jnp.log(total))


def attend_backward(query, keys, values, grad_mixed, logsum, offset, causal, scale):
    scores = jnp.einsum("cqhd,ckhd->chqk", query, keys, preferred_element_type=jnp.float32) * scale
    if causal:
        scores = causal_mask(scores, offset)
    probs = jnp.exp(scores - logsum)
    grad_probs = jnp.einsum(
        "cqhd,ckhd->chqk", grad_mixed, values, preferred_element_type=jnp.float32
    )
    grad_values = jnp.einsum(
        "chqk,cqhd->ckhd",
        probs.astype(jnp.bfloat16),
        grad_mixed,
        preferred_element_type=jnp.float32,
    )
    inner = jnp.sum(probs * grad_probs, axis=-1, keepdims=True)
    grad_scores = (probs * (grad_probs - inner)).astype(jnp.bfloat16)
    grad_query = (
        jnp.einsum("chqk,ckhd->cqhd", grad_scores, keys, preferred_element_type=jnp.float32) * scale
    )
    grad_keys = (
        jnp.einsum("chqk,cqhd->ckhd", grad_scores, query, preferred_element_type=jnp.float32)
        * scale
    )
    return (grad_query, grad_keys, grad_values)


def attend_rows(query, keys, values, causal, scale):
    clips, frames, heads = (query.shape[0], query.shape[1], query.shape[2])
    mixed_rows = []
    logsums = []
    for block_index in range(frames // ATT_BLOCK):
        start = block_index * ATT_BLOCK
        stop = start + ATT_BLOCK
        reach = stop if causal else keys.shape[1]
        mixed, logsum = attend_forward(
            query[:, start:stop], keys[:, :reach], values[:, :reach], start, causal, scale
        )
        mixed_rows.append(mixed)
        logsums.append(logsum)
    joined = (
        jnp.concatenate(mixed_rows, axis=1)
        .reshape(clips, frames, heads * HEAD_DIM)
        .astype(jnp.bfloat16)
    )
    return (joined, logsums)


def attend_rows_back(query, keys, values, grad_joined, logsums, causal, scale):
    clips, frames, heads = (query.shape[0], query.shape[1], query.shape[2])
    length = keys.shape[1]
    grad_mixed = grad_joined.reshape(clips, frames, heads, HEAD_DIM)
    query_parts = []
    grad_keys = jnp.zeros(keys.shape, jnp.float32)
    grad_values = jnp.zeros(values.shape, jnp.float32)
    for block_index in range(frames // ATT_BLOCK):
        start = block_index * ATT_BLOCK
        stop = start + ATT_BLOCK
        reach = stop if causal else length
        part_query, part_keys, part_values = attend_backward(
            query[:, start:stop],
            keys[:, :reach],
            values[:, :reach],
            grad_mixed[:, start:stop],
            logsums[block_index],
            start,
            causal,
            scale,
        )
        query_parts.append(part_query)
        padding = ((0, 0), (0, length - reach), (0, 0), (0, 0))
        grad_keys = grad_keys + jnp.pad(part_keys, padding)
        grad_values = grad_values + jnp.pad(part_values, padding)
    return (jnp.concatenate(query_parts, axis=1), grad_keys, grad_values)


def norm_backward(stream, gain, shift, grad_normed, grad_stream):
    pullback = jax.vjp(layer_norm, stream, gain, shift)[1]
    grad_input, grad_gain, grad_shift = pullback(grad_normed)
    return (grad_stream + grad_input, grad_gain, grad_shift)


def forward_layer(stream, text_states, weights, scale):
    gains = weights[0].astype(jnp.float32)
    shifts = weights[1].astype(jnp.float32)
    clips = stream.shape[0]
    saved = {"stream_one": stream}
    first = gather_normed(layer_norm(stream, gains[0], shifts[0]).astype(jnp.bfloat16))
    frames = first.shape[1]
    proj = jnp.einsum(
        "cfd,dke->cfke", first, weights[2], preferred_element_type=jnp.float32
    ).astype(jnp.bfloat16)
    heads = proj.shape[3] // HEAD_DIM
    self_split = proj.reshape(clips, frames, 3, heads, HEAD_DIM)
    joined_self, logsum_self = attend_rows(
        self_split[:, :, 0], self_split[:, :, 1], self_split[:, :, 2], True, scale
    )
    stream = stream + sum_branch(
        jnp.einsum("cfe,ed->cfd", joined_self, weights[3], preferred_element_type=jnp.float32)
    )
    saved.update(
        first=first,
        self_split=self_split,
        joined_self=joined_self,
        logsum_self=logsum_self,
        stream_two=stream,
    )
    second = gather_normed(layer_norm(stream, gains[1], shifts[1]).astype(jnp.bfloat16))
    cross_query = jnp.einsum(
        "cfd,de->cfe", second, weights[4], preferred_element_type=jnp.float32
    ).astype(jnp.bfloat16)
    cross_query = cross_query.reshape(clips, frames, heads, HEAD_DIM)
    cross_pairs = jnp.einsum(
        "ctd,dke->ctke", text_states, weights[5], preferred_element_type=jnp.float32
    ).astype(jnp.bfloat16)
    cross_pairs = cross_pairs.reshape(clips, text_states.shape[1], 2, heads, HEAD_DIM)
    joined_cross, logsum_cross = attend_rows(
        cross_query, cross_pairs[:, :, 0], cross_pairs[:, :, 1], False, scale
    )
    stream = stream + sum_branch(
        jnp.einsum("cfe,ed->cfd", joined_cross, weights[6], preferred_element_type=jnp.float32)
    )
    saved.update(
        second=second,
        cross_query=cross_query,
        cross_pairs=cross_pairs,
        joined_cross=joined_cross,
        logsum_cross=logsum_cross,
        stream_three=stream,
    )
    third = gather_normed(layer_norm(stream, gains[2], shifts[2]).astype(jnp.bfloat16))
    upper = jnp.einsum("cfd,du->cfu", third, weights[7], preferred_element_type=jnp.float32)
    active = exact_gelu(upper).astype(jnp.bfloat16)
    stream = stream + sum_branch(
        jnp.einsum("cfu,ud->cfd", active, weights[8], preferred_element_type=jnp.float32)
    )
    saved.update(third=third, upper=upper, active=active)
    return (stream, saved)


def backward_layer(grad_stream, saved, weights, text_states, scale):
    gains = weights[0].astype(jnp.float32)
    shifts = weights[1].astype(jnp.float32)
    grad_full = spread_rows(grad_stream.astype(jnp.bfloat16))
    grad_down = jnp.einsum(
        "cfu,cfd->ud", saved["active"], grad_full, preferred_element_type=jnp.float32
    )
    grad_active = jnp.einsum(
        "cfd,ud->cfu", grad_full, weights[8], preferred_element_type=jnp.float32
    )
    grad_upper = jax.vjp(exact_gelu, saved["upper"])[1](grad_active)[0].astype(jnp.bfloat16)
    grad_up = jnp.einsum(
        "cfd,cfu->du", saved["third"], grad_upper, preferred_element_type=jnp.float32
    )
    grad_third = fold_rows(
        jnp.einsum("cfu,du->cfd", grad_upper, weights[7], preferred_element_type=jnp.float32)
    )
    grad_stream, gain_three, shift_three = norm_backward(
        saved["stream_three"], gains[2], shifts[2], grad_third, grad_stream
    )
    grad_full = spread_rows(grad_stream.astype(jnp.bfloat16))
    grad_cross_out = jnp.einsum(
        "cfe,cfd->ed", saved["joined_cross"], grad_full, preferred_element_type=jnp.float32
    )
    grad_joined = jnp.einsum(
        "cfd,ed->cfe", grad_full, weights[6], preferred_element_type=jnp.float32
    ).astype(jnp.bfloat16)
    pairs = saved["cross_pairs"]
    grad_query, grad_keys, grad_values = attend_rows_back(
        saved["cross_query"],
        pairs[:, :, 0],
        pairs[:, :, 1],
        grad_joined,
        saved["logsum_cross"],
        False,
        scale,
    )
    clips, frames = (grad_query.shape[0], grad_query.shape[1])
    grad_query = grad_query.reshape(clips, frames, -1).astype(jnp.bfloat16)
    grad_pairs = (
        jnp.stack([grad_keys, grad_values], axis=2)
        .reshape(clips, pairs.shape[1], 2, -1)
        .astype(jnp.bfloat16)
    )
    grad_cross_q = jnp.einsum(
        "cfd,cfe->de", saved["second"], grad_query, preferred_element_type=jnp.float32
    )
    grad_cross_kv = jnp.einsum(
        "ctd,ctke->dke", text_states, grad_pairs, preferred_element_type=jnp.float32
    )
    text_part = jnp.einsum(
        "ctke,dke->ctd", grad_pairs, weights[5], preferred_element_type=jnp.float32
    )
    grad_second = fold_rows(
        jnp.einsum("cfe,de->cfd", grad_query, weights[4], preferred_element_type=jnp.float32)
    )
    grad_stream, gain_two, shift_two = norm_backward(
        saved["stream_two"], gains[1], shifts[1], grad_second, grad_stream
    )
    grad_full = spread_rows(grad_stream.astype(jnp.bfloat16))
    grad_self_out = jnp.einsum(
        "cfe,cfd->ed", saved["joined_self"], grad_full, preferred_element_type=jnp.float32
    )
    grad_joined = jnp.einsum(
        "cfd,ed->cfe", grad_full, weights[3], preferred_element_type=jnp.float32
    ).astype(jnp.bfloat16)
    self_split = saved["self_split"]
    grad_query, grad_keys, grad_values = attend_rows_back(
        self_split[:, :, 0],
        self_split[:, :, 1],
        self_split[:, :, 2],
        grad_joined,
        saved["logsum_self"],
        True,
        scale,
    )
    grad_proj = (
        jnp.stack([grad_query, grad_keys, grad_values], axis=2)
        .reshape(clips, frames, 3, -1)
        .astype(jnp.bfloat16)
    )
    grad_self = jnp.einsum(
        "cfd,cfke->dke", saved["first"], grad_proj, preferred_element_type=jnp.float32
    )
    grad_first = fold_rows(
        jnp.einsum("cfke,dke->cfd", grad_proj, weights[2], preferred_element_type=jnp.float32)
    )
    grad_stream, gain_one, shift_one = norm_backward(
        saved["stream_one"], gains[0], shifts[0], grad_first, grad_stream
    )
    grads = (
        jnp.stack([gain_one, gain_two, gain_three]),
        jnp.stack([shift_one, shift_two, shift_three]),
        grad_self,
        grad_self_out,
        grad_cross_q,
        grad_cross_kv,
        grad_cross_out,
        grad_up,
        grad_down,
    )
    return (grad_stream, text_part, grads)


def body(
    frames_in,
    text_states,
    ln_gain,
    ln_bias,
    w_self,
    w_self_out,
    w_cross_q,
    w_cross_kv,
    w_cross_out,
    w_up,
    w_down,
    cotangent,
):
    scale = float(HEAD_DIM) ** (-0.5)
    layer_count = w_self.shape[0]
    stream = frames_in.astype(jnp.float32)
    records = []
    copies = []
    for layer_index in range(layer_count):
        weights = (
            lax.all_gather(ln_gain[layer_index], "dp", axis=1, tiled=True),
            lax.all_gather(ln_bias[layer_index], "dp", axis=1, tiled=True),
            lax.all_gather(w_self[layer_index], "dp", axis=0, tiled=True),
            lax.all_gather(w_self_out[layer_index], "dp", axis=1, tiled=True),
            lax.all_gather(w_cross_q[layer_index], "dp", axis=0, tiled=True),
            lax.all_gather(w_cross_kv[layer_index], "dp", axis=0, tiled=True),
            lax.all_gather(w_cross_out[layer_index], "dp", axis=1, tiled=True),
            lax.all_gather(w_up[layer_index], "dp", axis=0, tiled=True),
            lax.all_gather(w_down[layer_index], "dp", axis=1, tiled=True),
        )
        copies.append(weights)
        stream, saved = forward_layer(stream, text_states, weights, scale)
        records.append(saved)
    result = stream.astype(jnp.bfloat16)
    grad_stream = cotangent.astype(jnp.float32)
    grad_text = jnp.zeros(text_states.shape, jnp.float32)
    layer_grads = [None] * layer_count
    for layer_index in reversed(range(layer_count)):
        weights = copies[layer_index]
        grad_stream, text_part, grads = backward_layer(
            grad_stream, records[layer_index], weights, text_states, scale
        )
        text_part, norm_part = (
            lax.psum(text_part.astype(jnp.bfloat16), "tensor").astype(jnp.float32),
            lax.psum(jnp.stack([grads[0], grads[1]]).astype(jnp.bfloat16), "tensor").astype(
                jnp.float32
            ),
        )
        grad_text = grad_text + text_part
        grads = (norm_part[0], norm_part[1]) + grads[2:]
        grads = (
            lax.psum_scatter(
                grads[0].astype(jnp.bfloat16), "dp", scatter_dimension=1, tiled=True
            ).astype(jnp.float32),
            lax.psum_scatter(
                grads[1].astype(jnp.bfloat16), "dp", scatter_dimension=1, tiled=True
            ).astype(jnp.float32),
            lax.psum_scatter(
                grads[2].astype(jnp.bfloat16), "dp", scatter_dimension=0, tiled=True
            ).astype(jnp.float32),
            lax.psum_scatter(
                grads[3].astype(jnp.bfloat16), "dp", scatter_dimension=1, tiled=True
            ).astype(jnp.float32),
            lax.psum_scatter(
                grads[4].astype(jnp.bfloat16), "dp", scatter_dimension=0, tiled=True
            ).astype(jnp.float32),
            lax.psum_scatter(
                grads[5].astype(jnp.bfloat16), "dp", scatter_dimension=0, tiled=True
            ).astype(jnp.float32),
            lax.psum_scatter(
                grads[6].astype(jnp.bfloat16), "dp", scatter_dimension=1, tiled=True
            ).astype(jnp.float32),
            lax.psum_scatter(
                grads[7].astype(jnp.bfloat16), "dp", scatter_dimension=0, tiled=True
            ).astype(jnp.float32),
            lax.psum_scatter(
                grads[8].astype(jnp.bfloat16), "dp", scatter_dimension=1, tiled=True
            ).astype(jnp.float32),
        )
        layer_grads[layer_index] = grads
    stacked = [
        jnp.stack([entry[member_index] for entry in layer_grads]) for member_index in range(9)
    ]
    return (
        result,
        grad_stream,
        grad_text,
        stacked[0],
        stacked[1],
        stacked[2],
        stacked[3],
        stacked[4],
        stacked[5],
        stacked[6],
        stacked[7],
        stacked[8],
    )


def solution(mesh):
    return jax.shard_map(
        body,
        mesh=mesh,
        in_specs=(
            P("dp", "tensor", None),
            P("dp", None, None),
            P(None, None, "dp"),
            P(None, None, "dp"),
            P(None, "dp", None, "tensor"),
            P(None, "tensor", "dp"),
            P(None, "dp", "tensor"),
            P(None, "dp", None, "tensor"),
            P(None, "tensor", "dp"),
            P(None, "dp", "tensor"),
            P(None, "tensor", "dp"),
            P("dp", "tensor", None),
        ),
        out_specs=(
            P("dp", "tensor", None),
            P("dp", "tensor", None),
            P("dp", None, None),
            P(None, None, "dp"),
            P(None, None, "dp"),
            P(None, "dp", None, "tensor"),
            P(None, "tensor", "dp"),
            P(None, "dp", "tensor"),
            P(None, "dp", None, "tensor"),
            P(None, "tensor", "dp"),
            P(None, "dp", "tensor"),
            P(None, "tensor", "dp"),
        ),
        check_vma=False,
    )
```

profile of v0, /device:TPU:0, one launch (start us, length us, event | category | flops | bytes accessed | tf_op | source)
XLA Modules:
  0.0 3136.3 jit_solution(16375872641403165832)
XLA Ops:
  24.7 45.0 %slice_reduce_fusion.7 = (f32[1536]{0:T(1024)S(1)}, f32[1536]{0:T(1024)S(1)}, f32[1536]{0:T(1024)S(1)}) fusion(f32[1,3,1536]{1,0,2:T(1,128)S(1)} %convert_element_type.642), kind=kLoop, calls=%fused_computation.360 | loop fusion | bytes 36864 | tf_op jit(solution)/shard_map/slice | solution.py:206
  81.3 45.2 %slice_reduce_fusion.6 = (f32[1536]{0:T(1024)S(1)}, f32[1536]{0:T(1024)S(1)}, f32[1536]{0:T(1024)S(1)}) fusion(f32[1,3,1536]{1,0,2:T(1,128)S(1)} %convert_element_type.643), kind=kLoop, calls=%fused_computation.359 | loop fusion | bytes 36864 | tf_op jit(solution)/shard_map/slice | solution.py:206
  130.3 61.5 %all-gather.45.cloned.1.call-done = bf16[1,1024,1536]{2,1,0:T(8,128)(2,1)} async-done(((bf16[1,256,1536]{2,1,0:T(8,128)(2,1)}), bf16[1,1024,1536]{2,1,0:T(8,128)(2,1)}) %all-gather.45.cloned.1.call-update) | async-done | bytes 3145744 | tf_op jit(solution)/shard_map/all_gather | solution.py:38
  262.1 56.6 %reduce-scatter.37.cloned.1.call-done = bf16[1,256,1536]{2,1,0:T(8,128)(2,1)} async-done(((bf16[1,1024,1536]{2,1,0:T(8,128)(2,1)}), bf16[1,256,1536]{2,1,0:T(8,128)(2,1)}) %reduce-scatter.37.cloned.1.call-update) | async-done | bytes 786448 | tf_op jit(solution)/shard_map/reduce_scatter | solution.py:46
  376.5 65.7 %all-gather.47.cloned.1.call-done = bf16[1,1024,1536]{2,1,0:T(8,128)(2,1)} async-done(((bf16[1,256,1536]{2,1,0:T(8,128)(2,1)}), bf16[1,1024,1536]{2,1,0:T(8,128)(2,1)}) %all-gather.47.cloned.1.call-update) | async-done | bytes 3145744 | tf_op jit(solution)/shard_map/all_gather | solution.py:38
  474.7 58.0 %reduce-scatter.39.cloned.1.call-done = bf16[1,256,1536]{2,1,0:T(8,128)(2,1)} async-done(((bf16[1,1024,1536]{2,1,0:T(8,128)(2,1)}), bf16[1,256,1536]{2,1,0:T(8,128)(2,1)}) %reduce-scatter.39.cloned.1.call-update) | async-done | bytes 786448 | tf_op jit(solution)/shard_map/reduce_scatter | solution.py:46
  574.0 65.7 %all-gather.49.cloned.1.call-done = bf16[1,1024,1536]{2,1,0:T(8,128)(2,1)} async-done(((bf16[1,256,1536]{2,1,0:T(8,128)(2,1)}), bf16[1,1024,1536]{2,1,0:T(8,128)(2,1)}) %all-gather.49.cloned.1.call-update) | async-done | bytes 3145744 | tf_op jit(solution)/shard_map/all_gather | solution.py:38
  711.6 45.0 %slice_reduce_fusion.1 = (f32[1536]{0:T(1024)S(1)}, f32[1536]{0:T(1024)S(1)}, f32[1536]{0:T(1024)S(1)}) fusion(f32[1,3,1536]{1,0,2:T(1,128)S(1)} %convert_element_type.644), kind=kLoop, calls=%fused_computation.353 | loop fusion | bytes 36864 | tf_op jit(solution)/shard_map/slice | solution.py:206
  756.6 45.6 %slice_reduce_fusion = (f32[1536]{0:T(1024)S(1)}, f32[1536]{0:T(1024)S(1)}, f32[1536]{0:T(1024)S(1)}) fusion(f32[1,3,1536]{1,0,2:T(1,128)S(1)} %convert_element_type.645), kind=kLoop, calls=%fused_computation.352 | loop fusion | bytes 36864 | tf_op jit(solution)/shard_map/slice | solution.py:206
  806.7 63.0 %all-gather.51.cloned.1.call-done = bf16[1,1024,1536]{2,1,0:T(8,128)(2,1)} async-done(((bf16[1,256,1536]{2,1,0:T(8,128)(2,1)}), bf16[1,1024,1536]{2,1,0:T(8,128)(2,1)}) %all-gather.51.cloned.1.call-update) | async-done | bytes 3145744 | tf_op jit(solution)/shard_map/all_gather | solution.py:38
  901.5 57.9 %reduce-scatter.43.cloned.1.call-done = bf16[1,256,1536]{2,1,0:T(8,128)(2,1)} async-done(((bf16[1,1024,1536]{2,1,0:T(8,128)(2,1)}), bf16[1,256,1536]{2,1,0:T(8,128)(2,1)}) %reduce-scatter.43.cloned.1.call-update) | async-done | bytes 786448 | tf_op jit(solution)/shard_map/reduce_scatter | solution.py:46
  1016.8 65.5 %all-gather.53.cloned.1.call-done = bf16[1,1024,1536]{2,1,0:T(8,128)(2,1)} async-done(((bf16[1,256,1536]{2,1,0:T(8,128)(2,1)}), bf16[1,1024,1536]{2,1,0:T(8,128)(2,1)}) %all-gather.53.cloned.1.call-update) | async-done | bytes 3145744 | tf_op jit(solution)/shard_map/all_gather | solution.py:38
  1112.6 59.6 %reduce-scatter.45.cloned.1.call-done = bf16[1,256,1536]{2,1,0:T(8,128)(2,1)} async-done(((bf16[1,1024,1536]{2,1,0:T(8,128)(2,1)}), bf16[1,256,1536]{2,1,0:T(8,128)(2,1)}) %reduce-scatter.45.cloned.1.call-update) | async-done | bytes 786448 | tf_op jit(solution)/shard_map/reduce_scatter | solution.py:46
  1213.7 65.5 %all-gather.55.cloned.1.call-done = bf16[1,1024,1536]{2,1,0:T(8,128)(2,1)} async-done(((bf16[1,256,1536]{2,1,0:T(8,128)(2,1)}), bf16[1,1024,1536]{2,1,0:T(8,128)(2,1)}) %all-gather.55.cloned.1.call-update) | async-done | bytes 3145744 | tf_op jit(solution)/shard_map/all_gather | solution.py:38
  1303.0 40.0 %all-gather.57.cloned.1.call-done = bf16[1,1024,1536]{2,1,0:T(8,128)(2,1)} async-done(((bf16[1,256,1536]{2,1,0:T(8,128)(2,1)}), bf16[1,1024,1536]{2,1,0:T(8,128)(2,1)}) %all-gather.57.cloned.1.call-update) | async-done | bytes 3145744 | tf_op jit(solution)/shard_map/all_gather | solution.py:53
  1343.0 39.9 %all-gather.95.cloned.1.call-done = bf16[1,1536,1536]{1,2,0:T(8,128)(2,1)} async-done(((bf16[1,1536,192]{1,2,0:T(8,128)(2,1)}), bf16[1,1536,1536]{1,2,0:T(8,128)(2,1)}) %all-gather.95.cloned.1.call-update) | async-done | bytes 4718608 | tf_op jit(solution)/shard_map/all_gather | solution.py:349
  1412.8 51.0 %reduce-scatter.49.cloned.1.call-done = bf16[1,256,1536]{2,1,0:T(8,128)(2,1)} async-done(((bf16[1,1024,1536]{2,1,0:T(8,128)(2,1)}), bf16[1,256,1536]{2,1,0:T(8,128)(2,1)}) %reduce-scatter.49.cloned.1.call-update) | async-done | bytes 786448 | tf_op jit(solution)/shard_map/reduce_scatter | solution.py:61
  1466.8 59.7 %reduce-scatter.47.cloned.1.call-done = bf16[1,256,1536]{2,1,0:T(8,128)(2,1)} async-done(((bf16[1,1024,1536]{2,1,0:T(8,128)(2,1)}), bf16[1,256,1536]{2,1,0:T(8,128)(2,1)}) %reduce-scatter.47.cloned.1.call-update) | async-done | bytes 786448 | tf_op jit(solution)/shard_map/reduce_scatter | solution.py:46
  1532.2 63.2 %all-gather.59.cloned.1.call-done = bf16[1,1024,1536]{2,1,0:T(8,128)(2,1)} async-done(((bf16[1,256,1536]{2,1,0:T(8,128)(2,1)}), bf16[1,1024,1536]{2,1,0:T(8,128)(2,1)}) %all-gather.59.cloned.1.call-update) | async-done | bytes 3145744 | tf_op jit(solution)/shard_map/all_gather | solution.py:53
  1605.2 59.0 %reduce-scatter.51.cloned.1.call-done = bf16[1,256,1536]{2,1,0:T(8,128)(2,1)} async-done(((bf16[1,1024,1536]{2,1,0:T(8,128)(2,1)}), bf16[1,256,1536]{2,1,0:T(8,128)(2,1)}) %reduce-scatter.51.cloned.1.call-update) | async-done | bytes 786448 | tf_op jit(solution)/shard_map/reduce_scatter | solution.py:61
  1670.7 63.6 %all-gather.61.cloned.1.call-done = bf16[1,1024,1536]{2,1,0:T(8,128)(2,1)} async-done(((bf16[1,256,1536]{2,1,0:T(8,128)(2,1)}), bf16[1,1024,1536]{2,1,0:T(8,128)(2,1)}) %all-gather.61.cloned.1.call-update) | async-done | bytes 3145744 | tf_op jit(solution)/shard_map/all_gather | solution.py:53
  1794.3 59.0 %reduce-scatter.53.cloned.1.call-done = bf16[1,256,1536]{2,1,0:T(8,128)(2,1)} async-done(((bf16[1,1024,1536]{2,1,0:T(8,128)(2,1)}), bf16[1,256,1536]{2,1,0:T(8,128)(2,1)}) %reduce-scatter.53.cloned.1.call-update) | async-done | bytes 786448 | tf_op jit(solution)/shard_map/reduce_scatter | solution.py:61
  1860.0 63.6 %all-gather.63.cloned.1.call-done = bf16[1,1024,1536]{2,1,0:T(8,128)(2,1)} async-done(((bf16[1,256,1536]{2,1,0:T(8,128)(2,1)}), bf16[1,1024,1536]{2,1,0:T(8,128)(2,1)}) %all-gather.63.cloned.1.call-update) | async-done | bytes 3145744 | tf_op jit(solution)/shard_map/all_gather | solution.py:53
  1944.5 59.0 %reduce-scatter.55.cloned.1.call-done = bf16[1,256,1536]{2,1,0:T(8,128)(2,1)} async-done(((bf16[1,1024,1536]{2,1,0:T(8,128)(2,1)}), bf16[1,256,1536]{2,1,0:T(8,128)(2,1)}) %reduce-scatter.55.cloned.1.call-update) | async-done | bytes 786448 | tf_op jit(solution)/shard_map/reduce_scatter | solution.py:61
  2010.0 63.5 %all-gather.65.cloned.1.call-done = bf16[1,1024,1536]{2,1,0:T(8,128)(2,1)} async-done(((bf16[1,256,1536]{2,1,0:T(8,128)(2,1)}), bf16[1,1024,1536]{2,1,0:T(8,128)(2,1)}) %all-gather.65.cloned.1.call-update) | async-done | bytes 3145744 | tf_op jit(solution)/shard_map/all_gather | solution.py:53
  2085.4 58.6 %reduce-scatter.57.cloned.1.call-done = bf16[1,256,1536]{2,1,0:T(8,128)(2,1)} async-done(((bf16[1,1024,1536]{2,1,0:T(8,128)(2,1)}), bf16[1,256,1536]{2,1,0:T(8,128)(2,1)}) %reduce-scatter.57.cloned.1.call-update) | async-done | bytes 786448 | tf_op jit(solution)/shard_map/reduce_scatter | solution.py:61
  2384.8 57.8 %reduce-scatter.77.cloned.1.call-done = bf16[192,1536]{1,0:T(8,128)(2,1)} async-done(((bf16[1536,1536]{1,0:T(8,128)(2,1)}), bf16[192,1536]{1,0:T(8,128)(2,1)}) %reduce-scatter.77.cloned.1.call-update) | async-done | bytes 589840 | tf_op jit(solution)/shard_map/reduce_scatter | solution.py:393
  2522.3 40.0 %reduce-scatter.73.cloned.1.call-done = bf16[384,192]{0,1:T(8,128)(2,1)} async-done(((bf16[384,1536]{0,1:T(8,128)(2,1)}), bf16[384,192]{0,1:T(8,128)(2,1)}) %reduce-scatter.73.cloned.1.call-update) | async-done | bytes 147472 | tf_op jit(solution)/shard_map/reduce_scatter | solution.py:390
  2644.9 88.7 %all-reduce.12.cloned.1.call-done = (bf16[1536,2,384]{2,1,0:T(2,128)(2,1)}, bf16[1536,2,384]{2,1,0:T(2,128)(2,1)}) async-done(((bf16[1536,2,384]{2,1,0:T(2,128)(2,1)}, bf16[1536,2,384]{2,1,0:T(2,128)(2,1)}), (bf16[1536,2,384]{2,1,0:T(2,128)(2,1)}, bf16[1536,2,384]{2,1,0:T(2,128)(2,1)})) %all-reduce.12.cloned.1.call-update) | async-done | bytes 4718608
  2774.2 40.2 %reduce-scatter.65.cloned.1.call-done = bf16[384,192]{0,1:T(8,128)(2,1)} async-done(((bf16[384,1536]{0,1:T(8,128)(2,1)}), bf16[384,192]{0,1:T(8,128)(2,1)}) %reduce-scatter.65.cloned.1.call-update) | async-done | bytes 147472 | tf_op jit(solution)/shard_map/reduce_scatter | solution.py:381
  2816.3 60.8 %reduce-scatter.59.cloned.1.call-done = bf16[1,256,1536]{2,1,0:T(8,128)(2,1)} async-done(((bf16[1,1024,1536]{2,1,0:T(8,128)(2,1)}), bf16[1,256,1536]{2,1,0:T(8,128)(2,1)}) %reduce-scatter.59.cloned.1.call-update) | async-done | bytes 786448 | tf_op jit(solution)/shard_map/reduce_scatter | solution.py:61
  2928.5 51.6 %reduce-scatter.61.cloned.1.call-done = bf16[192,3,384]{2,0,1:T(8,128)(2,1)} async-done(((bf16[1536,3,384]{2,0,1:T(8,128)(2,1)}), bf16[192,3,384]{2,0,1:T(8,128)(2,1)}) %reduce-scatter.61.cloned.1.call-update) | async-done | bytes 442384 | tf_op jit(solution)/shard_map/reduce_scatter | solution.py:378
  (829 shorter events, 1298.2 us)
Async XLA Ops:
  7.2 184.6 %all-gather.45.cloned.1.call-start = ((), (), s32[]{:S(2)}) async-start(), calls=%async_computation.28 | async-start | bytes 3932160 | tf_op jit(solution)/shard_map/all_gather | solution.py:38
  129.7 189.0 %reduce-scatter.37.cloned.1.call-start = ((), (), s32[]{:S(2)}) async-start(), calls=%async_computation.29 | async-start | bytes 3932160 | tf_op jit(solution)/shard_map/reduce_scatter | solution.py:46
  262.1 180.1 %all-gather.47.cloned.1.call-start = ((), (), s32[]{:S(2)}) async-start(), calls=%async_computation.30 | async-start | bytes 3932160 | tf_op jit(solution)/shard_map/all_gather | solution.py:38
  323.9 208.8 %reduce-scatter.39.cloned.1.call-start = ((), (), s32[]{:S(2)}) async-start(), calls=%async_computation.31 | async-start | bytes 3932160 | tf_op jit(solution)/shard_map/reduce_scatter | solution.py:46
  474.6 165.0 %all-gather.49.cloned.1.call-start = ((), (), s32[]{:S(2)}) async-start(), calls=%async_computation.32 | async-start | bytes 3932160 | tf_op jit(solution)/shard_map/all_gather | solution.py:38
  538.2 264.0 %reduce-scatter.41.cloned.1.call-start = ((), (), s32[]{:S(2)}) async-start(), calls=%async_computation.33 | async-start | bytes 3932160 | tf_op jit(solution)/shard_map/reduce_scatter | solution.py:46
  689.6 180.2 %all-gather.51.cloned.1.call-start = ((), (), s32[]{:S(2)}) async-start(), calls=%async_computation.34 | async-start | bytes 3932160 | tf_op jit(solution)/shard_map/all_gather | solution.py:38
  901.4 180.9 %all-gather.53.cloned.1.call-start = ((), (), s32[]{:S(2)}) async-start(), calls=%async_computation.36 | async-start | bytes 3932160 | tf_op jit(solution)/shard_map/all_gather | solution.py:38
  963.1 209.2 %reduce-scatter.45.cloned.1.call-start = ((), (), s32[]{:S(2)}) async-start(), calls=%async_computation.37 | async-start | bytes 3932160 | tf_op jit(solution)/shard_map/reduce_scatter | solution.py:46
  1112.6 166.6 %all-gather.55.cloned.1.call-start = ((), (), s32[]{:S(2)}) async-start(), calls=%async_computation.38 | async-start | bytes 3932160 | tf_op jit(solution)/shard_map/all_gather | solution.py:38
  1176.3 166.7 %all-gather.57.cloned.1.call-start = ((), (), s32[]{:S(2)}) async-start(), calls=%async_computation.40 | async-start | bytes 3932160 | tf_op jit(solution)/shard_map/all_gather | solution.py:53
  1177.1 205.8 %all-gather.95.cloned.1.call-start = ((), (), s32[]{:S(2)}) async-start(), calls=%async_computation.77 | async-start | bytes 5308416 | tf_op jit(solution)/shard_map/all_gather | solution.py:349
  1177.6 286.2 %reduce-scatter.49.cloned.1.call-start = ((), (), s32[]{:S(2)}) async-start(), calls=%async_computation.41 | async-start | bytes 3932160 | tf_op jit(solution)/shard_map/reduce_scatter | solution.py:61
  1412.8 182.6 %all-gather.59.cloned.1.call-start = ((), (), s32[]{:S(2)}) async-start(), calls=%async_computation.42 | async-start | bytes 3932160 | tf_op jit(solution)/shard_map/all_gather | solution.py:53
  1670.5 182.8 %reduce-scatter.53.cloned.1.call-start = ((), (), s32[]{:S(2)}) async-start(), calls=%async_computation.45 | async-start | bytes 3932160 | tf_op jit(solution)/shard_map/reduce_scatter | solution.py:61
  2150.1 201.0 %reduce-scatter.83.cloned.1.call-start = ((), (), s32[]{:S(2)}) async-start(), calls=%async_computation.63 | async-start | bytes 5308416 | tf_op jit(solution)/shard_map/reduce_scatter | solution.py:396
  2159.3 191.9 %reduce-scatter.81.cloned.1.call-start = ((), (), s32[]{:S(2)}) async-start(), calls=%async_computation.62 | async-start | bytes 5308416 | tf_op jit(solution)/shard_map/reduce_scatter | solution.py:396
  2168.6 216.3 %reduce-scatter.79.cloned.1.call-start = ((), (), s32[]{:S(2)}) async-start(), calls=%async_computation.61 | async-start | bytes 5308416 | tf_op jit(solution)/shard_map/reduce_scatter | solution.py:393
  2177.8 264.8 %reduce-scatter.77.cloned.1.call-start = ((), (), s32[]{:S(2)}) async-start(), calls=%async_computation.60 | async-start | bytes 5308416 | tf_op jit(solution)/shard_map/reduce_scatter | solution.py:393
  2187.3 295.4 %all-reduce.14.cloned.1.call-start = ((), (), s32[]{:S(2)}) async-start(), calls=%async_computation.83 | async-start | bytes 786432 | tf_op jit(solution)/shard_map/psum | solution.py:364
  2204.4 318.0 %reduce-scatter.75.cloned.1.call-start = ((), (), s32[]{:S(2)}) async-start(), calls=%async_computation.59 | async-start | bytes 1327104 | tf_op jit(solution)/shard_map/reduce_scatter | solution.py:390
  2209.4 353.0 %reduce-scatter.73.cloned.1.call-start = ((), (), s32[]{:S(2)}) async-start(), calls=%async_computation.58 | async-start | bytes 1327104 | tf_op jit(solution)/shard_map/reduce_scatter | solution.py:390
  2214.3 388.9 %reduce-scatter.71.cloned.1.call-start = ((), (), s32[]{:S(2)}) async-start(), calls=%async_computation.57 | async-start | bytes 1327104 | tf_op jit(solution)/shard_map/reduce_scatter | solution.py:384
  2219.3 423.8 %reduce-scatter.69.cloned.1.call-start = ((), (), s32[]{:S(2)}) async-start(), calls=%async_computation.56 | async-start | bytes 1327104 | tf_op jit(solution)/shard_map/reduce_scatter | solution.py:384
  2224.9 508.8 %all-reduce.12.cloned.1.call-start = ((), (), s32[]{:S(2)}) async-start(), calls=%async_computation.82 | async-start | bytes 9437184
  2243.1 531.1 %reduce-scatter.67.cloned.1.call-start = ((), (), s32[]{:S(2)}) async-start(), calls=%async_computation.55 | async-start | bytes 1327104 | tf_op jit(solution)/shard_map/reduce_scatter | solution.py:381
  2249.1 565.3 %reduce-scatter.65.cloned.1.call-start = ((), (), s32[]{:S(2)}) async-start(), calls=%async_computation.54 | async-start | bytes 1327104 | tf_op jit(solution)/shard_map/reduce_scatter | solution.py:381
  2292.6 584.5 %reduce-scatter.59.cloned.1.call-start = ((), (), s32[]{:S(2)}) async-start(), calls=%async_computation.51 | async-start | bytes 3932160 | tf_op jit(solution)/shard_map/reduce_scatter | solution.py:61
  2326.6 601.9 %reduce-scatter.63.cloned.1.call-start = ((), (), s32[]{:S(2)}) async-start(), calls=%async_computation.53 | async-start | bytes 3981312 | tf_op jit(solution)/shard_map/reduce_scatter | solution.py:378
  2336.1 644.0 %reduce-scatter.61.cloned.1.call-start = ((), (), s32[]{:S(2)}) async-start(), calls=%async_computation.52 | async-start | bytes 3981312 | tf_op jit(solution)/shard_map/reduce_scatter | solution.py:378
  2346.3 670.6 %reduce-scatter.89.cloned.1.call-start = ((), (), s32[]{:S(2)}) async-start(), calls=%async_computation.80 | async-start | bytes 442368
  2902.4 188.3 %reduce-scatter.85.cloned.1.call-start = ((), (), s32[]{:S(2)}) async-start(), calls=%async_computation.78 | async-start | bytes 442368
  (229 other events, 10055.9 us)
Sparse Core Ops, SparseCore 0:
  127.9 63.7 all-gather.44
  258.4 60.2 reduce-scatter.36
  378.6 63.4 all-gather.46
  472.4 60.2 reduce-scatter.38
  576.1 63.4 all-gather.48
  689.1 60.2 reduce-scatter.40
  806.1 63.5 all-gather.50
  899.1 60.2 reduce-scatter.42
  1018.8 63.4 all-gather.52
  1112.0 60.2 reduce-scatter.44
  1174.7 38.9 all-gather.92
  1215.7 63.4 all-gather.54
  1280.8 62.1 all-gather.56
  1403.6 60.2 reduce-scatter.48
  1466.2 60.2 reduce-scatter.46
  1531.8 63.5 all-gather.58
  1605.2 58.8 reduce-scatter.50
  1670.7 63.5 all-gather.60
  1794.4 58.8 reduce-scatter.52
  1860.1 63.5 all-gather.62
  1944.6 58.8 reduce-scatter.54
  2010.0 63.5 all-gather.64
  2085.1 58.8 reduce-scatter.56
  2150.3 63.5 all-gather.66
  2217.3 52.5 reduce-scatter.82
  2273.5 53.9 reduce-scatter.80
  2331.0 53.8 reduce-scatter.78
  2388.7 53.8 reduce-scatter.76
  2646.6 86.9 all-reduce.11
  2816.7 60.2 reduce-scatter.58
  2880.4 48.1 reduce-scatter.62
  2932.0 48.0 reduce-scatter.60
  (24 shorter events, 770.1 us)
where the time goes:
time: 3150 us; the launch traced here: 3140 us
  waiting for transfers between devices  2300 us (73%)
  matrix products  383 us (12%)
  local copies, waits for them, and re-layouts  249 us (8%)
  other arithmetic  124 us (4%)
  blocking collectives  60.7 us (2%)
    all_gather x6, waiting for transfers between devices, gather_normed(): lax.all_gather(shortened(normed), 'tensor', axis=1, tiled=True)  387 us
    reduce_scatter x6, waiting for transfers between devices, fold_rows(): lax.psum_scatter(shortened(partial_rows), 'tensor', scatter_dimension=1,...  347 us
    all_gather x6, waiting for transfers between devices, spread_rows(): lax.all_gather(shortened(grad_rows), 'tensor', axis=1, tiled=True)  294 us
    reduce_scatter x6, waiting for transfers between devices, sum_branch(): lax.psum_scatter(shortened(partial_rows), 'tensor', scatter_dimension=1,...  292 us
    unnamed x61, waiting for transfers between devices  230 us
    slice x2, local copies, waits for them, and re-layouts, forward_layer(): shifts[2]  90.7 us
    slice x2, local copies, waits for them, and re-layouts, forward_layer(): gains[2]  90 us
    reduce_scatter x2, waiting for transfers between devices, body(): lax.psum_scatter(grads[7].astype(jnp.bfloat16), 'dp', scatter_dimension=0...  88.5 us
  transfers between devices with their start and end apart: 56, of which 51 were waited for; matrix products, arithmetic and copies ran while one was open for 15% of the time, Pallas kernels for 0%

commit v1 on v0

v1 whole, which is shorter than its diff:
```python
import functools
import jax
import jax.numpy as jnp
from jax import lax
from jax.sharding import Mesh, PartitionSpec as P

HEAD_DIM = 64
ATT_BLOCK = 512
NORM_EPS = 1e-05
MASKED = -1e30
F32 = jnp.float32
BF16 = jnp.bfloat16


def nn(a, b):
    return lax.dot_general(a, b, (((1,), (0,)), ((), ())), preferred_element_type=F32)


def nt(a, b):
    return lax.dot_general(a, b, (((1,), (1,)), ((), ())), preferred_element_type=F32)


def tn(a, b):
    return lax.dot_general(a, b, (((0,), (0,)), ((), ())), preferred_element_type=F32)


def flip(value, axis):
    return lax.ppermute(value, axis, [(0, 1), (1, 0)])


RING = [(0, 1), (1, 3), (3, 2), (2, 0)]
RING_BACK = [(b, a) for a, b in RING]
SWAP = [(1, 2), (2, 1)]


def diagonal():
    return lax.axis_index("c") == lax.axis_index("zh")


def swap(value):
    return jnp.where(diagonal(), value, lax.ppermute(value, ("c", "zh"), SWAP))


def spread_pair(shard):
    near = jnp.where(diagonal(), shard, lax.ppermute(shard, ("c", "zh"), SWAP))
    far = lax.ppermute(shard, ("c", "zh"), RING)
    return [near, far]


def fold_pair(near, far):
    kept = jnp.where(diagonal(), near, lax.ppermute(near, ("c", "zh"), SWAP))
    return kept.astype(F32) + lax.ppermute(far, ("c", "zh"), RING_BACK).astype(F32)


def spread_bits(parts, order, bits):
    held = {(): parts}
    table = {}
    blocks = {0: parts[0], 1: parts[1]}
    for name in order:
        weight = 2 << (len(bits) - 1 - bits.index(name))
        keys = sorted(blocks)
        packed = jnp.concatenate([blocks[k] for k in keys], axis=0)
        came = flip(packed, name)
        rows = blocks[keys[0]].shape[0]
        for place, k in enumerate(keys):
            blocks[k + weight] = came[place * rows : (place + 1) * rows]
    return jnp.concatenate([blocks[k] for k in sorted(blocks)], axis=0)


def fold_bits(grad, order, bits):
    count = 2 << len(bits)
    rows = grad.shape[0] // count
    blocks = {k: grad[k * rows : (k + 1) * rows] for k in range(count)}
    for name in order:
        weight = 2 << (len(bits) - 1 - bits.index(name))
        keys = sorted(k for k in blocks if not k & weight)
        send = jnp.concatenate([blocks[k + weight] for k in keys], axis=0)
        came = flip(send, name)
        blocks = {
            k: (
                blocks[k].astype(F32) + came[place * rows : (place + 1) * rows].astype(F32)
            ).astype(BF16)
            for place, k in enumerate(keys)
        }
    return blocks[0], blocks[1]


def gather_rows(own):
    over = flip(own, "zl")
    beside = flip(own, "c")
    return [own, beside, over, flip(over, "c")]


def scatter_rows(partial):
    across = partial[2] + flip(partial[3].astype(BF16), "c").astype(F32)
    here = partial[0] + flip(partial[1].astype(BF16), "c").astype(F32)
    return here + flip(across.astype(BF16), "zl").astype(F32)


def normalise(stream, gain, shift):
    centre = jnp.mean(stream, axis=-1, keepdims=True)
    centred = stream - centre
    spread = jnp.mean(centred * centred, axis=-1, keepdims=True)
    return (centred * lax.rsqrt(spread + NORM_EPS) * gain + shift).astype(BF16)


def normalise_back(stream, gain, grad_normed, grad_stream):
    centre = jnp.mean(stream, axis=-1, keepdims=True)
    centred = stream - centre
    spread = jnp.mean(centred * centred, axis=-1, keepdims=True)
    inverse = lax.rsqrt(spread + NORM_EPS)
    unit = centred * inverse
    grad_gain = jnp.sum(grad_normed * unit, axis=0)
    grad_shift = jnp.sum(grad_normed, axis=0)
    scaled = grad_normed * gain
    grad_input = inverse * (
        scaled
        - jnp.mean(scaled, axis=-1, keepdims=True)
        - unit * jnp.mean(scaled * unit, axis=-1, keepdims=True)
    )
    return grad_stream + grad_input, grad_gain, grad_shift


def gelu_pair(upper):
    cdf = 0.5 * (1.0 + lax.erf(upper * (0.5**0.5)))
    density = jnp.exp(-0.5 * upper * upper) * (0.5 / jnp.pi) ** 0.5
    return (upper * cdf).astype(BF16), (cdf + upper * density).astype(BF16)


def causal_mask(scores, offset):
    rows = offset + lax.broadcasted_iota(jnp.int32, scores.shape[-2:], 0)
    cols = lax.broadcasted_iota(jnp.int32, scores.shape[-2:], 1)
    return jnp.where(rows >= cols, scores, MASKED)


def attend_rows(query, keys, values, causal, scale):
    frames = query.shape[0]
    mixed_rows, logsums = [], []
    block = min(ATT_BLOCK, frames)
    for start in range(0, frames, block):
        stop = start + block
        reach = stop if causal else keys.shape[0]
        scores = (
            jnp.einsum(
                "qhd,khd->hqk", query[start:stop], keys[:reach], preferred_element_type=F32
            )
            * scale
        )
        if causal:
            scores = causal_mask(scores, start)
        top = jnp.max(scores, axis=-1, keepdims=True)
        expo = jnp.exp(scores - top)
        total = jnp.sum(expo, axis=-1, keepdims=True)
        probs = (expo / total).astype(BF16)
        mixed_rows.append(
            jnp.einsum("hqk,khd->qhd", probs, values[:reach], preferred_element_type=F32)
        )
        logsums.append(top + jnp.log(total))
    joined = jnp.concatenate(mixed_rows, axis=0).reshape(frames, -1).astype(BF16)
    return joined, logsums


def attend_rows_back(query, keys, values, grad_joined, logsums, causal, scale):
    frames, heads = query.shape[0], query.shape[1]
    length = keys.shape[0]
    grad_mixed = grad_joined.reshape(frames, heads, HEAD_DIM)
    query_parts = []
    grad_keys = jnp.zeros(keys.shape, F32)
    grad_values = jnp.zeros(values.shape, F32)
    block = min(ATT_BLOCK, frames)
    for index, start in enumerate(range(0, frames, block)):
        stop = start + block
        reach = stop if causal else length
        q, k, v, g = query[start:stop], keys[:reach], values[:reach], grad_mixed[start:stop]
        scores = jnp.einsum("qhd,khd->hqk", q, k, preferred_element_type=F32) * scale
        if causal:
            scores = causal_mask(scores, start)
        probs = jnp.exp(scores - logsums[index])
        grad_probs = jnp.einsum("qhd,khd->hqk", g, v, preferred_element_type=F32)
        part_values = jnp.einsum(
            "hqk,qhd->khd", probs.astype(BF16), g, preferred_element_type=F32
        )
        inner = jnp.sum(probs * grad_probs, axis=-1, keepdims=True)
        grad_scores = (probs * (grad_probs - inner)).astype(BF16)
        query_parts.append(
            jnp.einsum("hqk,khd->qhd", grad_scores, k, preferred_element_type=F32) * scale
        )
        part_keys = jnp.einsum("hqk,qhd->khd", grad_scores, q, preferred_element_type=F32) * scale
        padding = ((0, length - reach), (0, 0), (0, 0))
        grad_keys = grad_keys + jnp.pad(part_keys, padding)
        grad_values = grad_values + jnp.pad(part_values, padding)
    return jnp.concatenate(query_parts, axis=0), grad_keys, grad_values


def to_time(parts):
    own, beside, over, both = parts
    c_one = lax.axis_index("c") == 1
    z_one = lax.axis_index("zl") == 1
    first = [jnp.where(z_one, over, own), jnp.where(z_one, own, over)]
    second = [jnp.where(z_one, both, beside), jnp.where(z_one, beside, both)]
    low = [jnp.where(c_one, s, f) for f, s in zip(first, second)]
    high = [jnp.where(c_one, f, s) for f, s in zip(first, second)]
    return jnp.concatenate(low + high, axis=0)


def from_time(rows):
    size = rows.shape[0] // 4
    q = [rows[i * size : (i + 1) * size] for i in range(4)]
    c_one = lax.axis_index("c") == 1
    z_one = lax.axis_index("zl") == 1
    mine = [jnp.where(c_one, q[2 + i], q[i]) for i in range(2)]
    core = [jnp.where(c_one, q[i], q[2 + i]) for i in range(2)]
    own = jnp.where(z_one, mine[1], mine[0])
    over = jnp.where(z_one, mine[0], mine[1])
    beside = jnp.where(z_one, core[1], core[0])
    both = jnp.where(z_one, core[0], core[1])
    return [own, beside, over, both]


def body(bits, frames_in, text_states, ln_gain, ln_bias, w_self, w_self_out, w_cross_q,
         w_cross_kv, w_cross_out, w_up, w_down, cotangent):
    scale = float(HEAD_DIM) ** (-0.5)
    layers = w_self.shape[0]
    width = frames_in.shape[2]
    part = w_self.shape[1]
    blocks = width // part
    cols = w_self.shape[3]
    me = lax.axis_index("zh")
    for place, name in enumerate(reversed(bits)):
        me = me + (lax.axis_index(name) << (place + 1))

    row = lax.broadcasted_iota(jnp.int32, (width, width), 0)
    col = lax.broadcasted_iota(jnp.int32, (width, width), 1)
    permute = ((row // part == ((col // part) ^ me)) & (row % part == col % part)).astype(BF16)

    def reorder(value):
        return nn(value, permute)

    frames_own = swap(frames_in[0])
    text_own = jnp.where(diagonal(), text_states[0], flip(text_states[0], "c"))
    text_own = reorder(text_own).astype(BF16)
    stream = reorder(frames_own)

    norms = jnp.concatenate(
        [ln_gain.reshape(-1, part), ln_bias.reshape(-1, part)], axis=0
    )
    norms = lax.all_gather(norms, (*bits, "c"), axis=0)
    norms = jnp.transpose(norms, (1, 0, 2)).reshape(norms.shape[1], width)
    norms = reorder(norms)
    gains = norms[: 3 * layers].reshape(layers, 3, 1, width)
    shifts = norms[3 * layers :].reshape(layers, 3, 1, width)

    straight = list(bits)
    crossed = list(reversed(bits))
    kinds = {"self": straight, "self_out": crossed, "q": straight, "kv": crossed,
             "out": crossed, "up": straight, "down": crossed}

    weights = []
    for l in range(layers):
        shards = {
            "self": w_self[l].reshape(part, 3 * cols),
            "self_out": w_self_out[l].T,
            "q": w_cross_q[l],
            "kv": w_cross_kv[l].reshape(part, 2 * cols),
            "out": w_cross_out[l].T,
            "up": w_up[l],
            "down": w_down[l].T,
        }
        full = {}
        for name, shard in shards.items():
            full[name] = spread_bits(spread_pair(shard), kinds[name], bits)
        weights.append(full)

    def self_split(proj_rows):
        split = proj_rows.reshape(proj_rows.shape[0], 3, cols // HEAD_DIM, HEAD_DIM)
        return split[:, 0], split[:, 1], split[:, 2]

    records = []
    for l in range(layers):
        w = weights[l]
        saved = {"one": stream}
        first = gather_rows(normalise(stream, gains[l, 0], shifts[l, 0]))
        proj = to_time([nn(r, w["self"]).astype(BF16) for r in first])
        query, keys, values = self_split(proj)
        joined, logsum = attend_rows(query, keys, values, True, scale)
        joined = from_time(joined)
        stream = stream + scatter_rows([nt(r, w["self_out"]) for r in joined])
        saved.update(first=first, proj=proj, joined_self=joined, logsum_self=logsum, two=stream)

        second = gather_rows(normalise(stream, gains[l, 1], shifts[l, 1]))
        cross_query = [nn(r, w["q"]).astype(BF16) for r in second]
        cross_query = jnp.concatenate(cross_query, axis=0).reshape(-1, cols // HEAD_DIM, HEAD_DIM)
        pairs = nn(text_own, w["kv"]).astype(BF16).reshape(-1, 2, cols // HEAD_DIM, HEAD_DIM)
        joined, logsum = attend_rows(cross_query, pairs[:, 0], pairs[:, 1], False, scale)
        size = joined.shape[0] // 4
        joined_parts = [joined[i * size : (i + 1) * size] for i in range(4)]
        stream = stream + scatter_rows([nt(r, w["out"]) for r in joined_parts])
        saved.update(second=second, cross_query=cross_query, pairs=pairs, joined_cross=joined,
                     logsum_cross=logsum, three=stream)

        third = gather_rows(normalise(stream, gains[l, 2], shifts[l, 2]))
        both = [gelu_pair(nn(r, w["up"])) for r in third]
        stream = stream + scatter_rows([nt(a, w["down"]) for a, _ in both])
        saved.update(third=third, active=[a for a, _ in both], slope=[d for _, d in both])
        records.append(saved)
    result = swap(reorder(stream.astype(BF16)).astype(BF16))

    grad = reorder(swap(cotangent[0]))
    grad_text = jnp.zeros((text_own.shape[0], width), F32)
    weight_grads = [None] * layers
    norm_grads = [None] * layers
    cat = lambda parts: jnp.concatenate(parts, axis=0)

    def settle(name, value):
        near, far = fold_bits(value.astype(BF16), list(reversed(kinds[name])), bits)
        return fold_pair(near, far)

    for l in reversed(range(layers)):
        w, saved = weights[l], records[l]
        out = {}
        full = gather_rows(grad.astype(BF16))
        grad_upper = [
            (nn(g, w["down"]) * d.astype(F32)).astype(BF16) for g, d in zip(full, saved["slope"])
        ]
        grad_third = scatter_rows([nt(u, w["up"]) for u in grad_upper])
        out["down"] = settle("down", tn(cat(full), cat(saved["active"])))
        out["up"] = settle("up", tn(cat(saved["third"]), cat(grad_upper)))
        grad, gain_three, shift_three = normalise_back(
            saved["three"], gains[l, 2], grad_third, grad
        )

        full = gather_rows(grad.astype(BF16))
        rows = cat(full)
        out["out"] = settle("out", tn(rows, saved["joined_cross"]))
        grad_joined = nn(rows, w["out"]).astype(BF16)
        pairs = saved["pairs"]
        grad_query, grad_keys, grad_values = attend_rows_back(
            saved["cross_query"], pairs[:, 0], pairs[:, 1], grad_joined, saved["logsum_cross"],
            False, scale,
        )
        grad_query = grad_query.reshape(grad_query.shape[0], cols).astype(BF16)
        grad_pairs = jnp.stack([grad_keys, grad_values], axis=1)
        grad_pairs = grad_pairs.reshape(grad_pairs.shape[0], 2 * cols).astype(BF16)
        size = grad_query.shape[0] // 4
        grad_second = scatter_rows(
            [nt(grad_query[i * size : (i + 1) * size], w["q"]) for i in range(4)]
        )
        out["q"] = settle("q", tn(cat(saved["second"]), grad_query))
        out["kv"] = settle("kv", tn(text_own, grad_pairs))
        grad_text = grad_text + nt(grad_pairs, w["kv"])
        grad, gain_two, shift_two = normalise_back(saved["two"], gains[l, 1], grad_second, grad)

        full = gather_rows(grad.astype(BF16))
        out["self_out"] = settle("self_out", tn(cat(full), cat(saved["joined_self"])))
        grad_joined = to_time([nn(g, w["self_out"]).astype(BF16) for g in full])
        query, keys, values = self_split(saved["proj"])
        grad_parts = attend_rows_back(
            query, keys, values, grad_joined, saved["logsum_self"], True, scale
        )
        grad_proj = jnp.stack(grad_parts, axis=1).reshape(query.shape[0], 3 * cols).astype(BF16)
        grad_proj = from_time(grad_proj)
        grad_first = scatter_rows([nt(p, w["self"]) for p in grad_proj])
        out["self"] = settle("self", tn(cat(saved["first"]), cat(grad_proj)))
        grad, gain_one, shift_one = normalise_back(saved["one"], gains[l, 0], grad_first, grad)
        weight_grads[l] = out
        norm_grads[l] = (gain_one, gain_two, gain_three, shift_one, shift_two, shift_three)

    grad_frames = swap(reorder(grad.astype(BF16)).astype(BF16)).astype(F32)
    text_sum = lax.psum(grad_text.astype(BF16), ("zl", "c"))
    text_sum = swap(reorder(text_sum).astype(BF16)).astype(F32)

    small = jnp.stack([g[:3] for g in norm_grads] and [jnp.stack(g) for g in norm_grads])
    small = small.reshape(layers * 6, blocks, part)
    steps = len(bits) + 1
    small = small.reshape((layers * 6,) + (2,) * steps + (part,))
    for place in range(steps):
        name = bits[place] if place < len(bits) else "zh"
        small = jnp.where(lax.axis_index(name) == 1, jnp.flip(small, axis=1 + place), small)
    small = small.reshape(layers * 6, blocks, part)
    small = lax.psum(small, (*bits, "c", "zh", "zl"))
    mine = lax.axis_index("c")
    for place, name in enumerate(reversed(bits)):
        mine = mine + (lax.axis_index(name) << (place + 1))
    small = lax.dynamic_index_in_dim(small, mine, axis=1, keepdims=False)
    small = small.reshape(layers, 6, part)

    def stacked(name, shape=None, turned=False):
        members = [weight_grads[l][name] for l in range(layers)]
        if turned:
            members = [m.T for m in members]
        if shape is not None:
            members = [m.reshape(shape) for m in members]
        return jnp.stack(members)

    return (
        result[None],
        grad_frames[None],
        text_sum[None],
        small[:, :3],
        small[:, 3:],
        stacked("self", (part, 3, cols)),
        stacked("self_out", turned=True),
        stacked("q"),
        stacked("kv", (part, 2, cols)),
        stacked("out", turned=True),
        stacked("up"),
        stacked("down", turned=True),
    )


def solution(mesh):
    count = mesh.shape["dp"]
    bits = tuple(f"b{i}" for i in range(count.bit_length() - 2))
    dp = (*bits, "c")
    tensor = ("zh", "zl")
    inner = Mesh(mesh.devices.reshape((2,) * (len(bits) + 3)), (*dp, *tensor))
    return jax.shard_map(
        functools.partial(body, bits),
        mesh=inner,
        in_specs=(
            P(dp, tensor, None),
            P(dp, None, None),
            P(None, None, dp),
            P(None, None, dp),
            P(None, dp, None, tensor),
            P(None, tensor, dp),
            P(None, dp, tensor),
            P(None, dp, None, tensor),
            P(None, tensor, dp),
            P(None, dp, tensor),
            P(None, tensor, dp),
            P(dp, tensor, None),
        ),
        out_specs=(
            P(dp, tensor, None),
            P(dp, tensor, None),
            P(dp, None, None),
            P(None, None, dp),
            P(None, None, dp),
            P(None, dp, None, tensor),
            P(None, tensor, dp),
            P(None, dp, tensor),
            P(None, dp, None, tensor),
            P(None, tensor, dp),
            P(None, dp, tensor),
            P(None, tensor, dp),
        ),
        check_vma=False,
    )
```

time: 3150 us -> 1790 us (0.57)
  waiting for transfers between devices: 2300 us -> 700 us
  starting transfers between devices: 4.09 us -> 401 us
  local copies, waits for them, and re-layouts: 249 us -> 102 us
  blocking collectives: 60.7 us -> 12.6 us
    reduce_scatter x24 -> x0, waiting for transfers between devices: 1040 us -> none  [the longest x6 347 us: fold_rows(): lax.psum_scatter(shortened(partial_rows), 'tensor', scatter_dimension=1,...]
    all_gather x26 -> x0, waiting for transfers between devices: 990 us -> none  [the longest x6 387 us: gather_normed(): lax.all_gather(shortened(normed), 'tensor', axis=1, tiled=True)]
    ppermute x0 -> x190, waiting for transfers between devices: none -> 562 us  [the longest x129 471 us: flip(): return lax.ppermute(value, axis, [(0, 1), (1, 0)])]
    ppermute x0 -> x190, starting transfers between devices: none -> 401 us  [the longest x129 203 us: flip(): return lax.ppermute(value, axis, [(0, 1), (1, 0)])]
    unnamed x61 -> x2, waiting for transfers between devices: 230 us -> 0.03 us
    slice x15 -> x34, local copies, waits for them, and re-layouts: 190 us -> 16.3 us  [the longest x14 5.7 us: fold_bits(): blocks = {k: grad[k * rows:(k + 1) * rows] for k in range(count)}]
    psum x1 -> x2, waiting for transfers between devices: 37.2 us -> 138 us  [the longest x1 126 us: body(): small = lax.psum(small, (*bits, 'c', 'zh', 'zl'))]
    concatenate x8 -> x60, other arithmetic: 1.98 us -> 45.9 us  [the longest x26 28.5 us: spread_bits(): packed = jnp.concatenate([blocks[k] for k in keys], axis=0)]
  transfers between devices with their start and end apart: 56 -> 192, of which waited for: 51 -> 58; matrix products, arithmetic and copies ran while one was open for 15% -> 31% of each run, Pallas kernels for 0% -> 0%
where the time goes in v1:
time: 1790 us; the launch traced here: 1770 us
  waiting for transfers between devices  700 us (39%)
  starting transfers between devices  401 us (22%)
  matrix products  377 us (21%)
  other arithmetic  152 us (8%)
  local copies, waits for them, and re-layouts  102 us (6%)
  between operations  22.1 us (1%)
    ppermute x129, waiting for transfers between devices, flip(): return lax.ppermute(value, axis, [(0, 1), (1, 0)])  471 us
    ppermute x129, starting transfers between devices, flip(): return lax.ppermute(value, axis, [(0, 1), (1, 0)])  203 us
    ppermute x14, starting transfers between devices, spread_pair(): far = lax.ppermute(shard, ('c', 'zh'), RING)  146 us
    psum x1, waiting for transfers between devices, body(): small = lax.psum(small, (*bits, 'c', 'zh', 'zl'))  126 us
    dot_general x51, matrix products, nn(): lax.dot_general(a, b, (((1,), (0,)), ((), ())), preferred_element_type=F32)  123 us
    dot_general x49, matrix products, nt(): lax.dot_general(a, b, (((1,), (1,)), ((), ())), preferred_element_type=F32)  108 us
    ppermute x14, waiting for transfers between devices, fold_pair(): lax.ppermute(far, ('c', 'zh'), RING_BACK).astype(F32)  79.7 us
    dot_general x14, matrix products, tn(): lax.dot_general(a, b, (((0,), (0,)), ((), ())), preferred_element_type=F32)  59.5 us
  transfers between devices with their start and end apart: 192, of which 58 were waited for; matrix products, arithmetic and copies ran while one was open for 31% of the time, Pallas kernels for 0%

profile of v1, /device:TPU:0, one launch (start us, length us, event | category | flops | bytes accessed | tf_op | source)
XLA Modules:
  0.0 1767.5 jit_solution(12676260903497548770)
XLA Ops:
  23.1 12.6 all-gather.1
  99.4 14.8 collective-permute-start.63
  121.3 33.7 %collective-permute-start.4 = (bf16[192,1152]{1,0:T(8,128)(2,1)S(1)}, bf16[192,1152]{1,0:T(8,128)(2,1)S(1)}, u32[]{:S(2)}, u32[]{:S(2)}) collective-permute-start(bf16[192,1152]{1,0:T(8,128)(2,1)S(1)} %bitcast.652), channel_id=1, source_target_pairs={{0,2},{2,6},{6,4},{4,0},{1,3},{3,7},{7,5},{5,1},{8,10},{10,14},{14... | collective-permute-start | bytes 1327112 | tf_op jit(solution)/shard_map/ppermute | solution.py:46
  191.3 28.7 %collective-permute-start.35 = (bf16[192,1536]{1,0:T(8,128)(2,1)S(1)}, bf16[192,1536]{1,0:T(8,128)(2,1)S(1)}, u32[]{:S(2)}, u32[]{:S(2)}) collective-permute-start(bf16[192,1536]{1,0:T(8,128)(2,1)S(1)} %copy-done.186), channel_id=1, source_target_pairs={{0,2},{2,6},{6,4},{4,0},{1,3},{3,7},{7,5},{5,1},{8,10},{10,14},{14... | collective-permute-start | bytes 1769480 | tf_op jit(solution)/shard_map/ppermute | solution.py:46
  220.1 16.6 collective-permute-start.85
  238.0 17.6 collective-permute-start.39
  273.6 13.4 collective-permute-done.5
  292.5 19.3 %collective-permute-start.1 = (bf16[256,1536]{1,0:T(8,128)(2,1)S(1)}, bf16[256,1536]{1,0:T(8,128)(2,1)S(1)}, u32[]{:S(2)}, u32[]{:S(2)}) collective-permute-start(bf16[256,1536]{1,0:T(8,128)(2,1)S(1)} %add_convert_fusion.6), channel_id=1, source_target_pairs={{0,1},{1,0},{2,3},{3,2},{4,5},{5,4},{6,7},{7,6},{8,9},{9,8},{10,11... | collective-permute-start | bytes 2359304 | tf_op jit(solution)/shard_map/ppermute | solution.py:28
  324.7 31.2 %collective-permute-start.7 = (bf16[256,1536]{1,0:T(8,128)(2,1)S(1)}, bf16[256,1536]{1,0:T(8,128)(2,1)S(1)}, u32[]{:S(2)}, u32[]{:S(2)}) collective-permute-start(bf16[256,1536]{1,0:T(8,128)(2,1)S(1)} %add_convert_fusion.6), channel_id=1, source_target_pairs={{0,4},{4,0},{1,5},{5,1},{2,6},{6,2},{3,7},{7,3},{8,12},{12,8},{9,1... | collective-permute-start | bytes 2359304 | tf_op jit(solution)/shard_map/ppermute | solution.py:28
  392.3 12.4 collective-permute-start.14
  438.6 27.2 %collective-permute-done.19 = bf16[768,768]{1,0:T(8,128)(2,1)S(1)} collective-permute-done((bf16[768,768]{1,0:T(8,128)(2,1)S(1)}, bf16[768,768]{1,0:T(8,128)(2,1)S(1)}, u32[]{:S(2)}, u32[]{:S(2)}) %collective-permute-start.19) | collective-permute-done | bytes 1179680 | tf_op jit(solution)/shard_map/ppermute | solution.py:28
  500.8 12.5 collective-permute-start.33
  550.7 14.2 collective-permute-done.44
  572.3 11.9 collective-permute-done.41
  597.7 24.9 %collective-permute-done.53 = bf16[768,1152]{1,0:T(8,128)(2,1)S(1)} collective-permute-done((bf16[768,1152]{1,0:T(8,128)(2,1)S(1)}, bf16[768,1152]{1,0:T(8,128)(2,1)S(1)}, u32[]{:S(2)}, u32[]{:S(2)}) %collective-permute-start.53) | collective-permute-done | bytes 1769504 | tf_op jit(solution)/shard_map/ppermute | solution.py:28
  626.1 13.0 collective-permute-done.47
  646.2 13.0 collective-permute-done.48
  691.6 25.8 %collective-permute-done.83 = bf16[768,1536]{1,0:T(8,128)(2,1)} collective-permute-done((bf16[768,1536]{1,0:T(8,128)(2,1)}, bf16[768,1536]{1,0:T(8,128)(2,1)}, u32[]{:S(2)}, u32[]{:S(2)}) %collective-permute-start.83) | collective-permute-done | bytes 2359328 | tf_op jit(solution)/shard_map/ppermute | solution.py:28
  725.0 17.5 collective-permute-done.61
  748.9 15.6 collective-permute-done.76
  785.7 16.9 collective-permute-done.79
  980.4 22.1 %collective-permute-done.155 = bf16[384,384]{1,0:T(8,128)(2,1)S(1)} collective-permute-done((bf16[384,384]{1,0:T(8,128)(2,1)S(1)}, bf16[384,384]{1,0:T(8,128)(2,1)S(1)}, u32[]{:S(2)}, u32[]{:S(2)}) %collective-permute-start.155) | collective-permute-done | bytes 294944 | tf_op jit(solution)/shard_map/ppermute | solution.py:28
  1024.1 12.0 collective-permute-start.173
  1169.1 16.0 collective-permute-done.138
  1277.4 20.6 %collective-permute-done.174 = bf16[768,1536]{1,0:T(8,128)(2,1)S(1)} collective-permute-done((bf16[768,1536]{1,0:T(8,128)(2,1)S(1)}, bf16[768,1536]{1,0:T(8,128)(2,1)S(1)}, u32[]{:S(2)}, u32[]{:S(2)}) %collective-permute-start.174) | collective-permute-done | bytes 2359328 | tf_op jit(solution)/shard_map/ppermute | solution.py:28
  1300.2 12.0 collective-permute-done.182
  1344.7 12.1 all-reduce.7.cloned.1.call-done
  1389.0 16.8 collective-permute-done.177
  1463.8 15.6 collective-permute-done.126
  1577.6 22.1 %collective-permute-done.134 = bf16[768,1152]{1,0:T(8,128)(2,1)} collective-permute-done((bf16[768,1152]{1,0:T(8,128)(2,1)}, bf16[768,1152]{1,0:T(8,128)(2,1)}, u32[]{:S(2)}, u32[]{:S(2)}) %collective-permute-start.134) | collective-permute-done | bytes 1769504 | tf_op jit(solution)/shard_map/ppermute | solution.py:28
  1609.4 125.7 %all-reduce.9.cloned.1.call-done = f32[12,8,192]{2,0,1:T(8,128)} async-done(((f32[12,8,192]{2,0,1:T(8,128)}), f32[12,8,192]{2,0,1:T(8,128)}) %all-reduce.9.cloned.1.call-update) | async-done | bytes 73744 | tf_op jit(solution)/shard_map/psum | solution.py:380
  1741.9 15.6 collective-permute-done.137
  (1595 shorter events, 1062.2 us)
Async XLA Ops:
  8.0 1348.8 %all-reduce.7.cloned.1.call-start = ((), (), s32[]{:S(2)}) async-start(), calls=%async_computation | async-start | bytes 393216 | tf_op jit(solution)/shard_map/psum | solution.py:369
  9.9 83.7 %collective-permute-start.56 = (bf16[192,384]{1,0:T(8,128)(2,1)}, bf16[192,384]{1,0:T(8,128)(2,1)}, u32[]{:S(2)}, u32[]{:S(2)}) collective-permute-start(bf16[192,384]{1,0:T(8,128)(2,1)} %get-tuple-element.236), channel_id=1, source_target_pairs={{0,2},{2,6},{6,4},{4,0},{1,3},{3,7},{7,5},{5,1},{8,10},{10,14},{14... | collective-permute-start | bytes 442376 | tf_op jit(solution)/shard_map/ppermute | solution.py:46
  14.0 54.0 %collective-permute-start.55 = (bf16[192,384]{1,0:T(8,128)(2,1)}, bf16[192,384]{1,0:T(8,128)(2,1)}, u32[]{:S(2)}, u32[]{:S(2)}) collective-permute-start(bf16[192,384]{1,0:T(8,128)(2,1)} %get-tuple-element.236), channel_id=1, source_target_pairs={{2,4},{4,2},{3,5},{5,3},{10,12},{12,10},{11,13},{13,11},{18,20},{2... | collective-permute-start | bytes 442376 | tf_op jit(solution)/shard_map/ppermute | solution.py:45
  15.3 79.4 %collective-permute-start.9 = (bf16[192,384]{1,0:T(8,128)(2,1)}, bf16[192,384]{1,0:T(8,128)(2,1)}, u32[]{:S(2)}, u32[]{:S(2)}) collective-permute-start(bf16[192,384]{1,0:T(8,128)(2,1)} %get-tuple-element.237), channel_id=1, source_target_pairs={{0,2},{2,6},{6,4},{4,0},{1,3},{3,7},{7,5},{5,1},{8,10},{10,14},{14... | collective-permute-start | bytes 442376 | tf_op jit(solution)/shard_map/ppermute | solution.py:46
  94.7 60.4 %collective-permute-start.17 = (bf16[192,768]{1,0:T(8,128)(2,1)}, bf16[192,768]{1,0:T(8,128)(2,1)S(1)}, u32[]{:S(2)}, u32[]{:S(2)}) collective-permute-start(bf16[192,768]{1,0:T(8,128)(2,1)} %bitcast.654), channel_id=1, source_target_pairs={{0,2},{2,6},{6,4},{4,0},{1,3},{3,7},{7,5},{5,1},{8,10},{10,14},{14... | collective-permute-start | bytes 884744 | tf_op jit(solution)/shard_map/ppermute | solution.py:46
  155.1 110.4 %collective-permute-start.81 = (bf16[192,1536]{1,0:T(8,128)(2,1)S(1)}, bf16[192,1536]{1,0:T(8,128)(2,1)S(1)}, u32[]{:S(2)}, u32[]{:S(2)}) collective-permute-start(bf16[192,1536]{1,0:T(8,128)(2,1)S(1)} %copy-done.187), channel_id=1, source_target_pairs={{0,2},{2,6},{6,4},{4,0},{1,3},{3,7},{7,5},{5,1},{8,10},{10,14},{14... | collective-permute-start | bytes 1769480 | tf_op jit(solution)/shard_map/ppermute | solution.py:46
  177.2 60.8 %collective-permute-start.84 = (bf16[192,1536]{1,0:T(8,128)(2,1)S(1)}, bf16[192,1536]{1,0:T(8,128)(2,1)S(1)}, u32[]{:S(2)}, u32[]{:S(2)}) collective-permute-start(bf16[192,1536]{1,0:T(8,128)(2,1)S(1)} %copy-done.189), channel_id=1, source_target_pairs={{2,4},{4,2},{3,5},{5,3},{10,12},{12,10},{11,13},{13,11},{18,20},{2... | collective-permute-start | bytes 1769480 | tf_op jit(solution)/shard_map/ppermute | solution.py:45
  189.7 65.9 %collective-permute-start.38 = (bf16[192,1536]{1,0:T(8,128)(2,1)S(1)}, bf16[192,1536]{1,0:T(8,128)(2,1)S(1)}, u32[]{:S(2)}, u32[]{:S(2)}) collective-permute-start(bf16[192,1536]{1,0:T(8,128)(2,1)S(1)} %copy-done.188), channel_id=1, source_target_pairs={{2,4},{4,2},{3,5},{5,3},{10,12},{12,10},{11,13},{13,11},{18,20},{2... | collective-permute-start | bytes 1769480 | tf_op jit(solution)/shard_map/ppermute | solution.py:45
  191.3 76.1 %collective-permute-start.35 = (bf16[192,1536]{1,0:T(8,128)(2,1)S(1)}, bf16[192,1536]{1,0:T(8,128)(2,1)S(1)}, u32[]{:S(2)}, u32[]{:S(2)}) collective-permute-start(bf16[192,1536]{1,0:T(8,128)(2,1)S(1)} %copy-done.186), channel_id=1, source_target_pairs={{0,2},{2,6},{6,4},{4,0},{1,3},{3,7},{7,5},{5,1},{8,10},{10,14},{14... | collective-permute-start | bytes 1769480 | tf_op jit(solution)/shard_map/ppermute | solution.py:46
  267.4 115.6 %collective-permute-start.11 = (bf16[768,384]{1,0:T(8,128)(2,1)}, bf16[768,384]{1,0:T(8,128)(2,1)}, u32[]{:S(2)}, u32[]{:S(2)}) collective-permute-start(bf16[768,384]{1,0:T(8,128)(2,1)} %pad_maximum_fusion.46), channel_id=1, source_target_pairs={{0,16},{16,0},{1,17},{17,1},{2,18},{18,2},{3,19},{19,3},{4,20},{20... | collective-permute-start | bytes 1769480 | tf_op jit(solution)/shard_map/ppermute | solution.py:28
  287.2 68.8 %collective-permute-start.6 = (bf16[768,1152]{1,0:T(8,128)(2,1)S(1)}, bf16[768,1152]{1,0:T(8,128)(2,1)S(1)}, u32[]{:S(2)}, u32[]{:S(2)}) collective-permute-start(bf16[768,1152]{1,0:T(8,128)(2,1)S(1)} %pad_maximum_fusion.19), channel_id=1, source_target_pairs={{0,8},{8,0},{1,9},{9,1},{2,10},{10,2},{3,11},{11,3},{4,12},{12,4},... | collective-permute-start | bytes 5308424 | tf_op jit(solution)/shard_map/ppermute | solution.py:28
  312.9 72.7 %collective-permute-start.69 = (bf16[768,384]{1,0:T(8,128)(2,1)}, bf16[768,384]{1,0:T(8,128)(2,1)}, u32[]{:S(2)}, u32[]{:S(2)}) collective-permute-start(bf16[768,384]{1,0:T(8,128)(2,1)} %get-tuple-element.321), channel_id=1, source_target_pairs={{0,8},{8,0},{1,9},{9,1},{2,10},{10,2},{3,11},{11,3},{4,12},{12,4},... | collective-permute-start | bytes 1769480 | tf_op jit(solution)/shard_map/ppermute | solution.py:28
  323.2 69.1 %collective-permute-start.52 = (bf16[384,1152]{1,0:T(8,128)(2,1)}, bf16[384,1152]{1,0:T(8,128)(2,1)}, u32[]{:S(2)}, u32[]{:S(2)}) collective-permute-start(bf16[384,1152]{1,0:T(8,128)(2,1)} %pad_maximum_fusion.39), channel_id=1, source_target_pairs={{0,16},{16,0},{1,17},{17,1},{2,18},{18,2},{3,19},{19,3},{4,20},{20... | collective-permute-start | bytes 2654216 | tf_op jit(solution)/shard_map/ppermute | solution.py:28
  407.2 82.8 %collective-permute-start.28 = (bf16[768,384]{1,0:T(8,128)(2,1)}, bf16[768,384]{1,0:T(8,128)(2,1)}, u32[]{:S(2)}, u32[]{:S(2)}) collective-permute-start(bf16[768,384]{1,0:T(8,128)(2,1)} %pad_maximum_fusion.49), channel_id=1, source_target_pairs={{0,16},{16,0},{1,17},{17,1},{2,18},{18,2},{3,19},{19,3},{4,20},{20... | collective-permute-start | bytes 1769480 | tf_op jit(solution)/shard_map/ppermute | solution.py:28
  411.9 364.6 %collective-permute-start.74 = (bf16[768,384]{1,0:T(8,128)(2,1)}, bf16[768,384]{1,0:T(8,128)(2,1)}, u32[]{:S(2)}, u32[]{:S(2)}) collective-permute-start(bf16[768,384]{1,0:T(8,128)(2,1)} %pad_maximum_fusion.53), channel_id=1, source_target_pairs={{0,16},{16,0},{1,17},{17,1},{2,18},{18,2},{3,19},{19,3},{4,20},{20... | collective-permute-start | bytes 1769480 | tf_op jit(solution)/shard_map/ppermute | solution.py:28
  415.3 85.5 %collective-permute-start.40 = (bf16[384,1536]{1,0:T(8,128)(2,1)}, bf16[384,1536]{1,0:T(8,128)(2,1)}, u32[]{:S(2)}, u32[]{:S(2)}) collective-permute-start(bf16[384,1536]{1,0:T(8,128)(2,1)} %pad_maximum_fusion.27), channel_id=1, source_target_pairs={{0,8},{8,0},{1,9},{9,1},{2,10},{10,2},{3,11},{11,3},{4,12},{12,4},... | collective-permute-start | bytes 3538952 | tf_op jit(solution)/shard_map/ppermute | solution.py:28
  481.7 55.4 %collective-permute-start.37 = (bf16[768,1536]{1,0:T(8,128)(2,1)}, bf16[768,1536]{1,0:T(8,128)(2,1)}, u32[]{:S(2)}, u32[]{:S(2)}) collective-permute-start(bf16[768,1536]{1,0:T(8,128)(2,1)} %get-tuple-element.324), channel_id=1, source_target_pairs={{0,8},{8,0},{1,9},{9,1},{2,10},{10,2},{3,11},{11,3},{4,12},{12,4},... | collective-permute-start | bytes 7077896 | tf_op jit(solution)/shard_map/ppermute | solution.py:28
  516.1 172.6 %collective-permute-start.58 = (bf16[768,384]{1,0:T(8,128)(2,1)}, bf16[768,384]{1,0:T(8,128)(2,1)}, u32[]{:S(2)}, u32[]{:S(2)}) collective-permute-start(bf16[768,384]{1,0:T(8,128)(2,1)} %pad_maximum_fusion.50), channel_id=1, source_target_pairs={{0,16},{16,0},{1,17},{17,1},{2,18},{18,2},{3,19},{19,3},{4,20},{20... | collective-permute-start | bytes 1769480 | tf_op jit(solution)/shard_map/ppermute | solution.py:28
  524.5 137.1 %collective-permute-start.98 = (bf16[256,1536]{1,0:T(8,128)(2,1)}, bf16[256,1536]{1,0:T(8,128)(2,1)}, u32[]{:S(2)}, u32[]{:S(2)}) collective-permute-start(bf16[256,1536]{1,0:T(8,128)(2,1)} %get-tuple-element.290), channel_id=1, source_target_pairs={{0,1},{1,0},{2,3},{3,2},{4,5},{5,4},{6,7},{7,6},{8,9},{9,8},{10,11... | collective-permute-start | bytes 2359304 | tf_op jit(solution)/shard_map/ppermute | solution.py:28
  661.6 165.5 %collective-permute-start.96 = (bf16[256,1536]{1,0:T(8,128)(2,1)}, bf16[256,1536]{1,0:T(8,128)(2,1)}, u32[]{:S(2)}, u32[]{:S(2)}) collective-permute-start(bf16[256,1536]{1,0:T(8,128)(2,1)} %get-tuple-element.290), channel_id=1, source_target_pairs={{0,4},{4,0},{1,5},{5,1},{2,6},{6,2},{3,7},{7,3},{8,12},{12,8},{9,1... | collective-permute-start | bytes 2359304 | tf_op jit(solution)/shard_map/ppermute | solution.py:28
  662.2 179.3 %collective-permute-start.99 = (bf16[256,1536]{1,0:T(8,128)(2,1)}, bf16[256,1536]{1,0:T(8,128)(2,1)}, u32[]{:S(2)}, u32[]{:S(2)}) collective-permute-start(bf16[256,1536]{1,0:T(8,128)(2,1)} %collective-permute-done.98), channel_id=1, source_target_pairs={{0,4},{4,0},{1,5},{5,1},{2,6},{6,2},{3,7},{7,3},{8,12},{12,8},{9,1... | collective-permute-start | bytes 2359304 | tf_op jit(solution)/shard_map/ppermute | solution.py:28
  663.5 54.0 %collective-permute-start.83 = (bf16[768,1536]{1,0:T(8,128)(2,1)}, bf16[768,1536]{1,0:T(8,128)(2,1)}, u32[]{:S(2)}, u32[]{:S(2)}) collective-permute-start(bf16[768,1536]{1,0:T(8,128)(2,1)} %get-tuple-element.325), channel_id=1, source_target_pairs={{0,8},{8,0},{1,9},{9,1},{2,10},{10,2},{3,11},{11,3},{4,12},{12,4},... | collective-permute-start | bytes 7077896 | tf_op jit(solution)/shard_map/ppermute | solution.py:28
  827.0 73.3 %collective-permute-start.89 = (bf16[256,1536]{1,0:T(8,128)(2,1)}, bf16[256,1536]{1,0:T(8,128)(2,1)}, u32[]{:S(2)}, u32[]{:S(2)}) collective-permute-start(bf16[256,1536]{1,0:T(8,128)(2,1)} %convolution_convert_fusion.41), channel_id=1, source_target_pairs={{0,4},{4,0},{1,5},{5,1},{2,6},{6,2},{3,7},{7,3},{8,12},{12,8},{9,1... | collective-permute-start | bytes 2359304 | tf_op jit(solution)/shard_map/ppermute | solution.py:28
  877.5 55.7 %collective-permute-start.186 = (bf16[768,1536]{1,0:T(8,128)(2,1)}, bf16[768,1536]{1,0:T(8,128)(2,1)}, u32[]{:S(2)}, u32[]{:S(2)}) collective-permute-start(bf16[768,1536]{1,0:T(8,128)(2,1)} %slice.1660), channel_id=1, source_target_pairs={{0,16},{16,0},{1,17},{17,1},{2,18},{18,2},{3,19},{19,3},{4,20},{20... | collective-permute-start | bytes 7077896 | tf_op jit(solution)/shard_map/ppermute | solution.py:28
  958.7 65.3 %collective-permute-start.162 = (bf16[768,768]{1,0:T(8,128)(2,1)S(1)}, bf16[768,768]{1,0:T(8,128)(2,1)S(1)}, u32[]{:S(2)}, u32[]{:S(2)}) collective-permute-start(bf16[768,768]{1,0:T(8,128)(2,1)S(1)} %slice.1592), channel_id=1, source_target_pairs={{0,16},{16,0},{1,17},{17,1},{2,18},{18,2},{3,19},{19,3},{4,20},{20... | collective-permute-start | bytes 3538952 | tf_op jit(solution)/shard_map/ppermute | solution.py:28
  1192.5 66.1 %collective-permute-start.115 = (bf16[256,1536]{1,0:T(8,128)(2,1)}, bf16[256,1536]{1,0:T(8,128)(2,1)}, u32[]{:S(2)}, u32[]{:S(2)}) collective-permute-start(bf16[256,1536]{1,0:T(8,128)(2,1)} %convolution_convert_fusion.35), channel_id=1, source_target_pairs={{0,4},{4,0},{1,5},{5,1},{2,6},{6,2},{3,7},{7,3},{8,12},{12,8},{9,1... | collective-permute-start | bytes 2359304 | tf_op jit(solution)/shard_map/ppermute | solution.py:28
  1258.0 54.2 %collective-permute-start.182 = (bf16[768,1536]{1,0:T(8,128)(2,1)S(1)}, bf16[768,1536]{1,0:T(8,128)(2,1)S(1)}, u32[]{:S(2)}, u32[]{:S(2)}) collective-permute-start(bf16[768,1536]{1,0:T(8,128)(2,1)S(1)} %slice.1649), channel_id=1, source_target_pairs={{0,16},{16,0},{1,17},{17,1},{2,18},{18,2},{3,19},{19,3},{4,20},{20... | collective-permute-start | bytes 7077896 | tf_op jit(solution)/shard_map/ppermute | solution.py:28
  1299.9 59.5 %collective-permute-start.175 = (bf16[384,1536]{1,0:T(8,128)(2,1)}, bf16[384,1536]{1,0:T(8,128)(2,1)}, u32[]{:S(2)}, u32[]{:S(2)}) collective-permute-start(bf16[384,1536]{1,0:T(8,128)(2,1)} %pad_maximum_fusion.34), channel_id=1, source_target_pairs={{0,16},{16,0},{1,17},{17,1},{2,18},{18,2},{3,19},{19,3},{4,20},{20... | collective-permute-start | bytes 3538952 | tf_op jit(solution)/shard_map/ppermute | solution.py:28
  1327.7 407.3 %all-reduce.9.cloned.1.call-start = ((), (), s32[]{:S(2)}) async-start(), calls=%async_computation.1 | async-start | bytes 262144 | tf_op jit(solution)/shard_map/psum | solution.py:380
  1342.1 95.8 %collective-permute-start.123 = (bf16[256,1536]{1,0:T(8,128)(2,1)}, bf16[256,1536]{1,0:T(8,128)(2,1)}, u32[]{:S(2)}, u32[]{:S(2)}) collective-permute-start(bf16[256,1536]{1,0:T(8,128)(2,1)} %convolution_convert_fusion.20), channel_id=1, source_target_pairs={{0,4},{4,0},{1,5},{5,1},{2,6},{6,2},{3,7},{7,3},{8,12},{12,8},{9,1... | collective-permute-start | bytes 2359304 | tf_op jit(solution)/shard_map/ppermute | solution.py:28
  1602.3 134.7 %collective-permute-start.135 = (bf16[384,1152]{1,0:T(8,128)(2,1)}, bf16[384,1152]{1,0:T(8,128)(2,1)S(1)}, u32[]{:S(2)}, u32[]{:S(2)}) collective-permute-start(bf16[384,1152]{1,0:T(8,128)(2,1)} %pad_maximum_fusion.40), channel_id=1, source_target_pairs={{0,16},{16,0},{1,17},{17,1},{2,18},{18,2},{3,19},{19,3},{4,20},{20... | collective-permute-start | bytes 2654216 | tf_op jit(solution)/shard_map/ppermute | solution.py:28
  1608.7 130.8 %collective-permute-start.132 = (bf16[256,1536]{1,0:T(8,128)(2,1)}, bf16[256,1536]{1,0:T(8,128)(2,1)S(1)}, u32[]{:S(2)}, u32[]{:S(2)}) collective-permute-start(bf16[256,1536]{1,0:T(8,128)(2,1)} %convolution_convert_fusion.18), channel_id=1, source_target_pairs={{2,4},{4,2},{3,5},{5,3},{10,12},{12,10},{11,13},{13,11},{18,20},{2... | collective-permute-start | bytes 2359304 | tf_op jit(solution)/shard_map/ppermute | solution.py:41
  (534 other events, 10502.0 us)
Sparse Core Ops, SparseCore 0:
  1327.9 28.9 all-reduce.6
Sparse Core Ops, SparseCore 1:
  1603.7 131.3 all-reduce.8

commit v2 on v1

v2 whole, which is shorter than its diff:
```python
import functools
import jax
import jax.numpy as jnp
from jax import lax
from jax.experimental import pallas as pl
from jax.experimental.pallas import tpu as pltpu
from jax.sharding import Mesh, PartitionSpec as P

HEAD_DIM = 64
ATT_BLOCK = 512
NORM_EPS = 1e-05
MASKED = -1e30
TILE = 384
F32 = jnp.float32
BF16 = jnp.bfloat16
MESH = pl.DeviceIdType.MESH
ANY = pl.BlockSpec(memory_space=pl.ANY)


def nn(a, b):
    return lax.dot_general(a, b, (((1,), (0,)), ((), ())), preferred_element_type=F32)


def nt(a, b):
    return lax.dot_general(a, b, (((1,), (1,)), ((), ())), preferred_element_type=F32)


def tn(a, b):
    return lax.dot_general(a, b, (((0,), (0,)), ((), ())), preferred_element_type=F32)


def flip(value, axis):
    return lax.ppermute(value, axis, [(0, 1), (1, 0)])


def diagonal():
    return lax.axis_index("c") == lax.axis_index("zh")


def off_diagonal():
    return lax.rem(lax.axis_index("c") + lax.axis_index("zh"), 2)


def target(kind):
    c, zh = lax.axis_index("c"), lax.axis_index("zh")
    off = off_diagonal()
    if kind == "ring":
        return {"c": lax.rem(c + off, 2), "zh": lax.rem(zh + 1 + off, 2)}
    if kind == "back":
        return {"c": lax.rem(c + 1 + off, 2), "zh": lax.rem(zh + off, 2)}
    if kind == "swap":
        return {"c": 1 - c, "zh": 1 - zh}
    return {kind: 1 - lax.axis_index(kind)}


def greeted(kinds):
    names = []
    for kind in kinds:
        pairs = {"ring": [("c",), ("zh",)], "back": [("c",), ("zh",)],
                 "swap": [("c", "zh")], "stay": []}.get(kind, [(kind,)])
        names += [p for p in pairs if p not in names]
    return names


def greet(kinds):
    barrier = pltpu.get_barrier_semaphore()
    names = greeted(kinds)
    for group in names:
        pl.semaphore_signal(
            barrier, inc=1, device_id={n: 1 - lax.axis_index(n) for n in group},
            device_id_type=MESH,
        )
    pl.semaphore_wait(barrier, len(names))


class Copy:
    def __init__(self, kind, src, dst, send, recv):
        self.kind = kind
        if kind == "stay":
            self.copy = pltpu.make_async_copy(src, dst, send)
        else:
            self.copy = pltpu.make_async_remote_copy(
                src_ref=src, dst_ref=dst, send_sem=send, recv_sem=recv,
                device_id=target(kind), device_id_type=MESH,
            )

    def guarded(self, act):
        if self.kind == "swap":
            pl.when(off_diagonal() == 1)(act)
        elif self.kind == "stay":
            pl.when(off_diagonal() == 0)(act)
        else:
            act()

    def start(self):
        self.guarded(lambda: self.copy.start())

    def wait(self):
        self.guarded(lambda: self.copy.wait())


class Ride:
    def __init__(self, ins, outs, stages, kinds, count, alias=()):
        self.ins, self.outs, self.stages = list(ins), list(outs), stages
        self.kinds, self.count, self.alias = list(kinds), count, dict(alias)


def runs(keys):
    keys, out = sorted(keys), []
    for k in keys:
        if out and out[-1][0] + out[-1][1] == k:
            out[-1][1] += 1
        else:
            out.append([k, 1])
    return out


def pair_ride(shard, blocks):
    rows, cols = shard.shape
    out = jax.ShapeDtypeStruct((rows * blocks, cols), shard.dtype)

    def stages(ins, outs):
        near, far = outs[0].at[pl.ds(0, rows)], outs[0].at[pl.ds(rows, rows)]
        return [[("ring", ins[0], far), ("swap", ins[0], near), ("stay", ins[0], near)]]

    return Ride([shard], [out], stages, ["ring", "swap"], 3)


def spread_ride(buffer, pieces, levels, blocks):
    rows = buffer.shape[0] // blocks
    plan = []
    for level in levels:
        stage = []
        for first, cols, order in pieces:
            held = [0, 1]
            for name, weight in order[:level]:
                held = held + [k + weight for k in held]
            name, weight = order[level]
            for k, n in runs(held):
                stage.append((name, k, k + weight, n, first, cols))
        plan.append(stage)

    def stages(ins, outs):
        ref = outs[0]
        return [
            [
                (name, ref.at[pl.ds(a * rows, n * rows), pl.ds(first, cols)],
                 ref.at[pl.ds(b * rows, n * rows), pl.ds(first, cols)])
                for name, a, b, n, first, cols in stage
            ]
            for stage in plan
        ]

    kinds = [item[0] for stage in plan for item in stage]
    out = jax.ShapeDtypeStruct(buffer.shape, buffer.dtype)
    return Ride([buffer], [out], stages, kinds, sum(len(s) for s in plan), {0: 0})


def send_ride(value, kind):
    out = jax.ShapeDtypeStruct(value.shape, value.dtype)
    return Ride([value], [out], lambda ins, outs: [[(kind, ins[0], outs[0])]], [kind], 1)


def launch(name, number, main, ins, outs, scratch, kinds, rides, limit=48):
    in_arrays = list(ins)
    out_shapes = list(outs)
    aliases = {}
    spans = []
    for ride in rides:
        for a, b in ride.alias.items():
            aliases[len(in_arrays) + a] = len(out_shapes) + b
        spans.append((len(in_arrays), len(in_arrays) + len(ride.ins),
                      len(out_shapes), len(out_shapes) + len(ride.outs)))
        in_arrays += ride.ins
        out_shapes += ride.outs
    total = sum(r.count for r in rides)
    all_kinds = list(kinds) + [k for r in rides for k in r.kinds]
    ride_sems = [pltpu.SemaphoreType.DMA((max(total, 1),)) for _ in range(2)]

    def kernel(*refs):
        in_refs = refs[: len(in_arrays)]
        out_refs = refs[len(in_arrays) : len(in_arrays) + len(out_shapes)]
        rest = refs[len(in_arrays) + len(out_shapes) :]
        send, recv = rest[:2]
        early = main(in_refs[: len(ins)], out_refs[: len(outs)], rest[2:], True) if main else None
        greet(all_kinds)
        chains, place = [], 0
        for ride, (a, b, c, d) in zip(rides, spans):
            chain = []
            for stage in ride.stages(in_refs[a:b], out_refs[c:d]):
                chain.append([])
                for kind, src, dst in stage:
                    chain[-1].append(Copy(kind, src, dst, send.at[place], recv.at[place]))
                    place += 1
            chains.append(chain)
        for chain in chains:
            for copy in chain[0]:
                copy.start()
        if main:
            main(in_refs[: len(ins)], out_refs[: len(outs)], rest[2:], early)
        for level in range(max([len(c) for c in chains], default=0)):
            for chain in chains:
                if level < len(chain):
                    for copy in chain[level]:
                        copy.wait()
                    if level + 1 < len(chain):
                        for copy in chain[level + 1]:
                            copy.start()

    results = pl.pallas_call(
        kernel,
        out_shape=tuple(out_shapes),
        in_specs=[ANY] * len(in_arrays),
        out_specs=tuple([ANY] * len(out_shapes)),
        scratch_shapes=ride_sems + list(scratch),
        input_output_aliases=aliases,
        name=name,
        compiler_params=pltpu.CompilerParams(
            collective_id=number, has_side_effects=True, vmem_limit_bytes=limit << 20
        ),
    )(*in_arrays)
    main_outs = results[: len(outs)]
    return main_outs, [results[c:d] for _, _, c, d in spans]


def normalise_value(rows, gain, shift):
    centre = jnp.mean(rows, axis=-1, keepdims=True)
    centred = rows - centre
    spread = jnp.mean(centred * centred, axis=-1, keepdims=True)
    return (centred * lax.rsqrt(spread + NORM_EPS) * gain + shift).astype(BF16)


def gelu_pair(upper):
    cdf = 0.5 * (1.0 + lax.erf(upper * (0.5**0.5)))
    density = jnp.exp(-0.5 * upper * upper) * (0.5 / jnp.pi) ** 0.5
    return (upper * cdf).astype(BF16), (cdf + upper * density).astype(BF16)


def gather_multiply(number, rows_in, norm, weight, ending, slope, rides):
    size, width = rows_in.shape
    n = weight.shape[1]
    tile = min(TILE, n)
    ins = [rows_in, weight]
    if norm is not None:
        ins.append(jnp.concatenate([norm[0], norm[1]], axis=0))
    if slope is not None:
        ins.append(slope)
    double = ending == "gelu"
    outs = [jax.ShapeDtypeStruct((4, size, width), BF16)]
    outs += [jax.ShapeDtypeStruct((4, size, n), BF16)] * (2 if double else 1)
    half = size // 2
    scratch = [
        pltpu.VMEM((size, width), F32),
        pltpu.VMEM((width, n), BF16),
        pltpu.VMEM((2, width), F32),
        pltpu.VMEM((4, size, width), BF16),
        pltpu.VMEM((4, size, n), BF16),
        pltpu.VMEM((4, size, n) if (double or slope is not None) else (8, 128), BF16),
        pltpu.SemaphoreType.DMA((4,)),
        pltpu.SemaphoreType.DMA((6,)),
        pltpu.SemaphoreType.DMA((6,)),
        pltpu.SemaphoreType.DMA((3, 4)),
    ]

    def main(in_refs, out_refs, refs, stage):
        rows, w, norms, x, y, second, load, send, recv, store = refs
        if stage is True:
            loads = [
                pltpu.make_async_copy(in_refs[0], rows, load.at[0]),
                pltpu.make_async_copy(in_refs[1], w, load.at[1]),
            ]
            if norm is not None:
                loads.append(pltpu.make_async_copy(in_refs[2], norms, load.at[2]))
            if slope is not None:
                loads.append(pltpu.make_async_copy(in_refs[-1], second, load.at[3]))
            for copy in loads:
                copy.start()
            return loads
        loads = stage
        loads[0].wait()
        if norm is not None:
            loads[2].wait()
        over, beside, relay, stores = [], [], [], []
        for h in range(2):
            part = pl.ds(h * half, half)
            value = rows[part, :]
            if norm is not None:
                value = normalise_value(value, norms[0:1, :], norms[1:2, :])
            x[0, part, :] = value.astype(BF16)
            over.append(Copy("zl", x.at[0, part], x.at[2, part], send.at[h], recv.at[h]))
            over[-1].start()
        beside = Copy("c", x.at[0], x.at[1], send.at[2], recv.at[2])
        beside.start()
        loads[1].wait()
        if slope is not None:
            loads[-1].wait()

        def multiply(b):
            def step(j, carry):
                cols = pl.ds(pl.multiple_of(j * tile, tile), tile)
                value = nn(x[b], w[:, cols])
                if double:
                    y[b, :, cols], second[b, :, cols] = gelu_pair(value)
                elif slope is not None:
                    y[b, :, cols] = (value * second[b, :, cols].astype(F32)).astype(BF16)
                else:
                    y[b, :, cols] = value.astype(BF16)
                return carry

            lax.fori_loop(0, n // tile, step, 0)
            done = [pltpu.make_async_copy(x.at[b], out_refs[0].at[b], store.at[0, b]),
                    pltpu.make_async_copy(y.at[b], out_refs[1].at[b], store.at[1, b])]
            if double:
                done.append(pltpu.make_async_copy(second.at[b], out_refs[2].at[b], store.at[2, b]))
            for copy in done:
                copy.start()
            stores.extend(done)

        multiply(0)
        beside.wait()
        multiply(1)
        for h in range(2):
            part = pl.ds(h * half, half)
            over[h].wait()
            relay.append(Copy("c", x.at[2, part], x.at[3, part], send.at[3 + h], recv.at[3 + h]))
            relay[-1].start()
        multiply(2)
        for copy in relay:
            copy.wait()
        multiply(3)
        for copy in stores:
            copy.wait()

    return launch(f"gather_{number}", number, main, ins, outs, scratch, ["c", "zl"], rides)


def multiply_scatter(number, parts, weight, base, rides):
    _, size, n = parts.shape
    width = weight.shape[0]
    half = size // 2
    ins = [parts, weight] + ([base] if base is not None else [])
    outs = [jax.ShapeDtypeStruct((size, width), F32)]
    scratch = [
        pltpu.VMEM((4, size, n), BF16),
        pltpu.VMEM((width, n), BF16),
        pltpu.VMEM((size, width), F32),
        pltpu.VMEM((size, width), F32),
        pltpu.VMEM((2, size, width), BF16),
        pltpu.VMEM((2, size, width), BF16),
        pltpu.VMEM((size, width), BF16),
        pltpu.VMEM((size, width), BF16),
        pltpu.SemaphoreType.DMA((7,)),
        pltpu.SemaphoreType.DMA((6,)),
        pltpu.SemaphoreType.DMA((6,)),
    ]

    def main(in_refs, out_refs, refs, stage):
        y, w, total, far, give, came, across, over, load, send, recv = refs
        if stage is True:
            loads = [pltpu.make_async_copy(in_refs[1], w, load.at[0])]
            loads += [
                pltpu.make_async_copy(in_refs[0].at[b], y.at[b], load.at[1 + b])
                for b in range(4)
            ]
            if base is not None:
                loads.append(pltpu.make_async_copy(in_refs[2], total, load.at[5]))
            for place in (0, 4, 3, 2, 1, 5)[: len(loads)]:
                loads[place].start()
            return loads
        loads = stage

        def multiply(b, part, put):
            def step(j, carry):
                cols = pl.ds(pl.multiple_of(j * TILE, TILE), TILE)
                put(cols, nt(y[b, part, :], w[cols, :]))
                return carry

            lax.fori_loop(0, width // TILE, step, 0)

        whole = pl.ds(0, size)
        for place in (0, 4, 3):
            loads[place].wait()
        sent = []
        for h in range(2):
            part = pl.ds(h * half, half)

            def put_give(cols, value, part=part):
                give[0, part, cols] = value.astype(BF16)

            def put_far(cols, value, part=part):
                far[part, cols] = value

            multiply(3, part, put_give)
            copy = Copy("c", give.at[0, part], came.at[0, part], send.at[h], recv.at[h])
            copy.start()
            multiply(2, part, put_far)
            copy.wait()
            across[part, :] = (far[part, :] + came[0, part, :].astype(F32)).astype(BF16)
            copy = Copy("zl", across.at[part], over.at[part], send.at[2 + h], recv.at[2 + h])
            copy.start()
            sent.append(copy)
        loads[2].wait()

        def put_near(cols, value):
            give[1, :, cols] = value.astype(BF16)

        multiply(1, whole, put_near)
        near = Copy("c", give.at[1], came.at[1], send.at[4], recv.at[4])
        near.start()
        loads[1].wait()
        if base is not None:
            loads[5].wait()

        def put_total(cols, value):
            total[:, cols] = value + (total[:, cols] if base is not None else 0.0)

        multiply(0, whole, put_total)
        near.wait()
        total[...] += came[1].astype(F32)
        done = []
        for h in range(2):
            part = pl.ds(h * half, half)
            sent[h].wait()
            total[part, :] += over[part, :].astype(F32)
            copy = pltpu.make_async_copy(total.at[part], out_refs[0].at[part], load.at[5 + h])
            copy.start()
            done.append(copy)
        for copy in done:
            copy.wait()

    (out,), extra = launch(
        f"scatter_{number}", number, main, ins, outs, scratch, ["c", "zl"], rides
    )
    return out, extra


def normalise_back(stream, gain, grad_normed, grad_stream):
    centre = jnp.mean(stream, axis=-1, keepdims=True)
    centred = stream - centre
    spread = jnp.mean(centred * centred, axis=-1, keepdims=True)
    inverse = lax.rsqrt(spread + NORM_EPS)
    unit = centred * inverse
    grad_gain = jnp.sum(grad_normed * unit, axis=0)
    grad_shift = jnp.sum(grad_normed, axis=0)
    scaled = grad_normed * gain
    grad_input = inverse * (
        scaled
        - jnp.mean(scaled, axis=-1, keepdims=True)
        - unit * jnp.mean(scaled * unit, axis=-1, keepdims=True)
    )
    return grad_stream + grad_input, grad_gain, grad_shift


def causal_mask(scores, offset):
    rows = offset + lax.broadcasted_iota(jnp.int32, scores.shape[-2:], 0)
    cols = lax.broadcasted_iota(jnp.int32, scores.shape[-2:], 1)
    return jnp.where(rows >= cols, scores, MASKED)


def attend_rows(query, keys, values, causal, scale):
    frames = query.shape[0]
    mixed_rows, logsums = [], []
    block = min(ATT_BLOCK, frames)
    for start in range(0, frames, block):
        stop = start + block
        reach = stop if causal else keys.shape[0]
        scores = (
            jnp.einsum(
                "qhd,khd->hqk", query[start:stop], keys[:reach], preferred_element_type=F32
            )
            * scale
        )
        if causal:
            scores = causal_mask(scores, start)
        top = jnp.max(scores, axis=-1, keepdims=True)
        expo = jnp.exp(scores - top)
        total = jnp.sum(expo, axis=-1, keepdims=True)
        probs = (expo / total).astype(BF16)
        mixed_rows.append(
            jnp.einsum("hqk,khd->qhd", probs, values[:reach], preferred_element_type=F32)
        )
        logsums.append(top + jnp.log(total))
    joined = jnp.concatenate(mixed_rows, axis=0).reshape(frames, -1).astype(BF16)
    return joined, logsums


def attend_rows_back(query, keys, values, grad_joined, logsums, causal, scale):
    frames, heads = query.shape[0], query.shape[1]
    length = keys.shape[0]
    grad_mixed = grad_joined.reshape(frames, heads, HEAD_DIM)
    query_parts = []
    grad_keys = jnp.zeros(keys.shape, F32)
    grad_values = jnp.zeros(values.shape, F32)
    block = min(ATT_BLOCK, frames)
    for index, start in enumerate(range(0, frames, block)):
        stop = start + block
        reach = stop if causal else length
        q, k, v, g = query[start:stop], keys[:reach], values[:reach], grad_mixed[start:stop]
        scores = jnp.einsum("qhd,khd->hqk", q, k, preferred_element_type=F32) * scale
        if causal:
            scores = causal_mask(scores, start)
        probs = jnp.exp(scores - logsums[index])
        grad_probs = jnp.einsum("qhd,khd->hqk", g, v, preferred_element_type=F32)
        part_values = jnp.einsum(
            "hqk,qhd->khd", probs.astype(BF16), g, preferred_element_type=F32
        )
        inner = jnp.sum(probs * grad_probs, axis=-1, keepdims=True)
        grad_scores = (probs * (grad_probs - inner)).astype(BF16)
        query_parts.append(
            jnp.einsum("hqk,khd->qhd", grad_scores, k, preferred_element_type=F32) * scale
        )
        part_keys = jnp.einsum("hqk,qhd->khd", grad_scores, q, preferred_element_type=F32) * scale
        padding = ((0, length - reach), (0, 0), (0, 0))
        grad_keys = grad_keys + jnp.pad(part_keys, padding)
        grad_values = grad_values + jnp.pad(part_values, padding)
    return jnp.concatenate(query_parts, axis=0), grad_keys, grad_values


def to_time(parts):
    own, beside, over, both = [parts[i] for i in range(4)]
    c_one = lax.axis_index("c") == 1
    z_one = lax.axis_index("zl") == 1
    first = [jnp.where(z_one, over, own), jnp.where(z_one, own, over)]
    second = [jnp.where(z_one, both, beside), jnp.where(z_one, beside, both)]
    low = [jnp.where(c_one, s, f) for f, s in zip(first, second)]
    high = [jnp.where(c_one, f, s) for f, s in zip(first, second)]
    return jnp.concatenate(low + high, axis=0)


def from_time(rows):
    size = rows.shape[0] // 4
    q = [rows[i * size : (i + 1) * size] for i in range(4)]
    c_one = lax.axis_index("c") == 1
    z_one = lax.axis_index("zl") == 1
    mine = [jnp.where(c_one, q[2 + i], q[i]) for i in range(2)]
    core = [jnp.where(c_one, q[i], q[2 + i]) for i in range(2)]
    own = jnp.where(z_one, mine[1], mine[0])
    over = jnp.where(z_one, mine[0], mine[1])
    beside = jnp.where(z_one, core[1], core[0])
    both = jnp.where(z_one, core[0], core[1])
    return jnp.stack([own, beside, over, both])


def flat(parts):
    return parts.reshape(-1, parts.shape[-1])


def body(bits, frames_in, text_states, ln_gain, ln_bias, w_self, w_self_out, w_cross_q,
         w_cross_kv, w_cross_out, w_up, w_down, cotangent):
    scale = float(HEAD_DIM) ** (-0.5)
    layers = w_self.shape[0]
    width = frames_in.shape[2]
    part = w_self.shape[1]
    blocks = width // part
    cols = w_self.shape[3]
    hidden = w_up.shape[2]
    heads = cols // HEAD_DIM
    me = lax.axis_index("zh")
    for place, name in enumerate(reversed(bits)):
        me = me + (lax.axis_index(name) << (place + 1))

    row = lax.broadcasted_iota(jnp.int32, (width, width), 0)
    col = lax.broadcasted_iota(jnp.int32, (width, width), 1)
    permute = ((row // part == ((col // part) ^ me)) & (row % part == col % part)).astype(BF16)

    def reorder(value):
        return nn(value, permute)

    up = [(name, 2 << (len(bits) - 1 - place)) for place, name in enumerate(bits)]
    low_first = list(reversed(up))
    levels = len(bits)
    early, late = list(range(levels // 2)), list(range(levels // 2, levels))
    sizes = {"self": 3 * cols, "self_out": cols, "q": cols, "kv": 2 * cols, "out": cols,
             "up": hidden, "down": hidden, "norm": 128}

    def halves(name):
        n = sizes[name]
        if name == "self":
            return [(0, 2 * cols, low_first), (2 * cols, cols, up)]
        if name in ("up", "down"):
            return [(0, n // 2, low_first), (n // 2, n // 2, up)]
        return [(0, n, low_first if name == "kv" else up)]

    packs = {"a": ["self", "self_out"], "b": ["q", "kv", "out"], "c": ["up"], "d": ["down"]}
    shards = {}
    for l in range(layers):
        shards[l, "self"] = w_self[l].reshape(part, 3 * cols)
        shards[l, "self_out"] = w_self_out[l].T
        shards[l, "q"] = w_cross_q[l]
        shards[l, "kv"] = w_cross_kv[l].reshape(part, 2 * cols)
        shards[l, "out"] = w_cross_out[l].T
        shards[l, "up"] = w_up[l]
        shards[l, "down"] = w_down[l].T
    held = {}
    counter = [0]

    def number():
        counter[0] += 1
        return counter[0] - 1

    def weight_rides(todo):
        rides, keys = [], []
        for l, pack, stage in todo:
            for name in packs[pack]:
                key = (l, name)
                if stage == 1:
                    rides.append(pair_ride(shards[key], blocks))
                else:
                    rides.append(spread_ride(
                        held[key], halves(name), early if stage == 2 else late, blocks))
                keys.append(key)
        return rides, keys

    def keep(keys, extra):
        for key, value in zip(keys, extra):
            held[key] = value[0]

    forward = {
        0: [(0, "b", 2), (0, "c", 1)],
        1: [(0, "b", 3), (0, "c", 2)],
        2: [(0, "c", 3), (0, "d", 1)],
        3: [(0, "d", 2), (1, "a", 1)],
        4: [(0, "d", 3), (1, "a", 2)],
        5: [(1, "a", 3), (1, "b", 1)],
        6: [(1, "b", 2), (1, "c", 1)],
        7: [(1, "b", 3), (1, "c", 2)],
        8: [(1, "c", 3), (1, "d", 1)],
        9: [(1, "d", 2)],
        10: [(1, "d", 3)],
    }
    step = [0]

    def next_rides(more=()):
        todo = [t for t in forward.get(step[0], []) if t[0] < layers]
        step[0] += 1
        rides, keys = weight_rides(todo)
        return rides, keys

    def simple_launch(rides):
        return launch(f"move_{counter[0]}", number(), None, [], [], [], [], rides)[1]

    rides, keys = weight_rides([(0, "a", 1)])
    rides.append(send_ride(frames_in[0], "swap"))
    second, keys_b = weight_rides([(0, "b", 1)])
    extra = simple_launch(rides + second)
    keep(keys, extra[: len(keys)])
    keep(keys_b, extra[len(keys) + 1 :])
    frames_own = jnp.where(diagonal(), frames_in[0], extra[len(keys)][0])
    rides, keys = weight_rides([(0, "a", 2)])
    extra = simple_launch(rides)
    keep(keys, extra)
    rides, keys = weight_rides([(0, "a", 3)])
    extra = simple_launch(rides)
    keep(keys, extra)

    text_own = jnp.where(diagonal(), text_states[0], flip(text_states[0], "c"))
    text_own = reorder(text_own).astype(BF16)
    stream = reorder(frames_own)

    norms = jnp.concatenate([ln_gain.reshape(-1, part), ln_bias.reshape(-1, part)], axis=0)
    norms = lax.all_gather(norms, (*bits, "c"), axis=0)
    norms = jnp.transpose(norms, (1, 0, 2)).reshape(norms.shape[1], width)
    norms = reorder(norms)
    gains = norms[: 3 * layers].reshape(layers, 3, 1, width)
    shifts = norms[3 * layers :].reshape(layers, 3, 1, width)

    def self_split(proj_rows):
        split = proj_rows.reshape(proj_rows.shape[0], 3, heads, HEAD_DIM)
        return split[:, 0], split[:, 1], split[:, 2]

    def gathered(rows, norm, key, ending=None, slope=None, more=()):
        rides, keys = next_rides()
        outs, extra = gather_multiply(
            number(), rows, norm, held[key], ending, slope, rides + list(more))
        keep(keys, extra)
        return outs, [e[0] for e in extra[len(keys):]]

    def scattered(parts, key, base, more=()):
        rides, keys = next_rides()
        out, extra = multiply_scatter(number(), parts, held[key], base, rides + list(more))
        keep(keys, extra)
        return out, [e[0] for e in extra[len(keys):]]

    records = []
    for l in range(layers):
        saved = {"one": stream}
        more = [send_ride(cotangent[0], "swap")] if l == layers - 1 else []
        (first, proj), extra = gathered(stream, (gains[l, 0], shifts[l, 0]), (l, "self"),
                                        more=more)
        if more:
            cot_own = jnp.where(diagonal(), cotangent[0], extra[0])
        proj = to_time(proj)
        query, keys_, values = self_split(proj)
        joined, logsum = attend_rows(query, keys_, values, True, scale)
        joined = from_time(joined)
        stream, _ = scattered(joined, (l, "self_out"), stream)
        saved.update(first=first, proj=proj, joined_self=joined, logsum_self=logsum, two=stream)

        (normed, cross), _ = gathered(stream, (gains[l, 1], shifts[l, 1]), (l, "q"))
        cross_query = flat(cross).reshape(-1, heads, HEAD_DIM)
        pairs = nn(text_own, held[l, "kv"]).astype(BF16).reshape(-1, 2, heads, HEAD_DIM)
        joined, logsum = attend_rows(cross_query, pairs[:, 0], pairs[:, 1], False, scale)
        joined = joined.reshape(4, -1, cols)
        stream, _ = scattered(joined, (l, "out"), stream)
        saved.update(second=normed, cross_query=cross_query, pairs=pairs, joined_cross=joined,
                     logsum_cross=logsum, three=stream)

        (third, active, slope), _ = gathered(
            stream, (gains[l, 2], shifts[l, 2]), (l, "up"), "gelu")
        stream, _ = scattered(active, (l, "down"), stream)
        saved.update(third=third, active=active, slope=slope)
        records.append(saved)
    result_own = reorder(stream.astype(BF16)).astype(BF16)
    grad = reorder(cot_own)

    folding = []
    finished = {}
    grad_text = jnp.zeros((text_own.shape[0], width), F32)
    norm_grads = [None] * layers

    def fold_later(l, name, value):
        value = value.astype(BF16)
        for first, n, order in halves(name):
            chunk = value[:, first : first + n] if n != value.shape[1] else value
            table = {k: chunk[k * part : (k + 1) * part] for k in range(blocks)}
            folding.append({"key": (l, name, first), "table": table,
                            "order": list(reversed(order)), "level": 0})

    def fold_start(limit):
        rides, items, spent = [], [], 0
        for item in list(folding):
            if spent >= limit:
                break
            if item["level"] < len(item["order"]):
                name, weight = item["order"][item["level"]]
                away = sorted(k for k in item["table"] if k & weight)
                value = jnp.concatenate([item["table"][k] for k in away], axis=0)
                rides.append(send_ride(value, name))
                spent += value.size * 2
            else:
                near, far = item["table"][0], item["table"][1]
                ride = Ride(
                    [near, far],
                    [jax.ShapeDtypeStruct(near.shape, BF16)] * 2,
                    lambda ins, outs: [[("swap", ins[0], outs[0]), ("back", ins[1], outs[1])]],
                    ["swap", "back"], 2,
                )
                rides.append(ride)
                spent += near.size * 4
            items.append(item)
        return rides, items

    def fold_end(items, extra):
        for item, came in zip(items, extra):
            if item["level"] < len(item["order"]):
                name, weight = item["order"][item["level"]]
                stay = sorted(k for k in item["table"] if not k & weight)
                item["table"] = {
                    k: (
                        item["table"][k].astype(F32)
                        + came[0][i * part : (i + 1) * part].astype(F32)
                    ).astype(BF16)
                    for i, k in enumerate(stay)
                }
                item["level"] += 1
            else:
                near = jnp.where(diagonal(), item["table"][0], came[0])
                finished[item["key"]] = near.astype(F32) + came[1].astype(F32)
                folding.remove(item)

    budget = 5 << 20

    def back_gathered(rows, key, slope=None, more=()):
        rides, items = fold_start(budget)
        outs, extra = gather_multiply(
            number(), rows, None, held[key], None, slope, rides + list(more))
        fold_end(items, extra)
        return outs, [e[0] for e in extra[len(items):]]

    def back_scattered(parts, key):
        rides, items = fold_start(budget)
        out, extra = multiply_scatter(number(), parts, held[key], None, rides)
        fold_end(items, extra)
        return out

    for l in reversed(range(layers)):
        saved = records[l]
        more = [send_ride(result_own, "swap")] if l == layers - 1 else []
        (full, grad_upper), extra = back_gathered(grad, (l, "down"), saved["slope"], more)
        if more:
            result = jnp.where(diagonal(), result_own, extra[0])
        fold_later(l, "down", tn(flat(full), flat(saved["active"])))
        grad_third = back_scattered(grad_upper, (l, "up"))
        fold_later(l, "up", tn(flat(saved["third"]), flat(grad_upper)))
        grad, gain_three, shift_three = normalise_back(
            saved["three"], gains[l, 2], grad_third, grad)

        (full, grad_joined), _ = back_gathered(grad, (l, "out"))
        fold_later(l, "out", tn(flat(full), flat(saved["joined_cross"])))
        pairs = saved["pairs"]
        grad_query, grad_keys, grad_values = attend_rows_back(
            saved["cross_query"], pairs[:, 0], pairs[:, 1], flat(grad_joined),
            saved["logsum_cross"], False, scale)
        grad_query = grad_query.reshape(4, -1, cols).astype(BF16)
        grad_pairs = jnp.stack([grad_keys, grad_values], axis=1)
        grad_pairs = grad_pairs.reshape(grad_pairs.shape[0], 2 * cols).astype(BF16)
        grad_second = back_scattered(grad_query, (l, "q"))
        fold_later(l, "q", tn(flat(saved["second"]), flat(grad_query)))
        fold_later(l, "kv", tn(text_own, grad_pairs))
        grad_text = grad_text + nt(grad_pairs, held[l, "kv"])
        grad, gain_two, shift_two = normalise_back(saved["two"], gains[l, 1], grad_second, grad)

        (full, grad_joined), _ = back_gathered(grad, (l, "self_out"))
        fold_later(l, "self_out", tn(flat(full), flat(saved["joined_self"])))
        query, keys_, values = self_split(saved["proj"])
        grad_parts = attend_rows_back(
            query, keys_, values, to_time(grad_joined), saved["logsum_self"], True, scale)
        grad_proj = jnp.stack(grad_parts, axis=1).reshape(query.shape[0], 3 * cols).astype(BF16)
        grad_proj = from_time(grad_proj)
        grad_first = back_scattered(grad_proj, (l, "self"))
        fold_later(l, "self", tn(flat(saved["first"]), flat(grad_proj)))
        grad, gain_one, shift_one = normalise_back(saved["one"], gains[l, 0], grad_first, grad)
        norm_grads[l] = [gain_one, gain_two, gain_three, shift_one, shift_two, shift_three]

    small = jnp.stack([row for rows in norm_grads for row in rows], axis=1)
    small = jnp.pad(small, ((0, 0), (0, sizes["norm"] - small.shape[1])))
    fold_later(0, "norm", small)
    frames_back = reorder(grad.astype(BF16)).astype(BF16)
    text_back = grad_text.astype(BF16)
    extras = [send_ride(frames_back, "swap"), send_ride(text_back, "c")]
    round_ = 0
    while folding:
        rides, items = fold_start(1 << 40)
        extra = simple_launch(rides + extras)
        fold_end(items, extra)
        tail = [e[0] for e in extra[len(items):]]
        if round_ == 0:
            grad_frames = jnp.where(diagonal(), frames_back, tail[0]).astype(F32)
            text_sum = (text_back.astype(F32) + tail[1].astype(F32)).astype(BF16)
            extras = [send_ride(text_sum, "zl")]
        elif round_ == 1:
            text_sum = reorder((text_sum.astype(F32) + tail[0].astype(F32)).astype(BF16))
            text_sum = text_sum.astype(BF16)
            extras = [send_ride(text_sum, "swap")]
        elif round_ == 2:
            text_sum = jnp.where(diagonal(), text_sum, tail[0]).astype(F32)
            extras = []
        round_ += 1

    small = finished[0, "norm", 0][:, : 6 * layers]
    for name in ("zl", "zh"):
        small = small + flip(small, name)
    small = small.T.reshape(layers, 6, part)

    def gradient(l, name):
        pieces = [finished[l, name, first] for first, _, _ in halves(name)]
        return jnp.concatenate(pieces, axis=1) if len(pieces) > 1 else pieces[0]

    def stacked(name, shape=None, turned=False):
        members = [gradient(l, name) for l in range(layers)]
        if turned:
            members = [m.T for m in members]
        if shape is not None:
            members = [m.reshape(shape) for m in members]
        return jnp.stack(members)

    return (
        result[None],
        grad_frames[None],
        text_sum[None],
        small[:, :3],
        small[:, 3:],
        stacked("self", (part, 3, cols)),
        stacked("self_out", turned=True),
        stacked("q"),
        stacked("kv", (part, 2, cols)),
        stacked("out", turned=True),
        stacked("up"),
        stacked("down", turned=True),
    )


def solution(mesh):
    count = mesh.shape["dp"]
    bits = tuple(f"b{i}" for i in range(count.bit_length() - 2))
    dp = (*bits, "c")
    tensor = ("zh", "zl")
    inner = Mesh(mesh.devices.reshape((2,) * (len(bits) + 3)), (*dp, *tensor))
    return jax.shard_map(
        functools.partial(body, bits),
        mesh=inner,
        in_specs=(
            P(dp, tensor, None),
            P(dp, None, None),
            P(None, None, dp),
            P(None, None, dp),
            P(None, dp, None, tensor),
            P(None, tensor, dp),
            P(None, dp, tensor),
            P(None, dp, None, tensor),
            P(None, tensor, dp),
            P(None, dp, tensor),
            P(None, tensor, dp),
            P(dp, tensor, None),
        ),
        out_specs=(
            P(dp, tensor, None),
            P(dp, tensor, None),
            P(dp, None, None),
            P(None, None, dp),
            P(None, None, dp),
            P(None, dp, None, tensor),
            P(None, tensor, dp),
            P(None, dp, tensor),
            P(None, dp, None, tensor),
            P(None, tensor, dp),
            P(None, dp, tensor),
            P(None, tensor, dp),
        ),
        check_vma=False,
    )
```

time: 1790 us -> 1610 us (0.90); the launches traced: 1770 us -> 1610 us
  Pallas kernels: 0 us -> 1050 us
  waiting for transfers between devices: 700 us -> 3.09 us
  starting transfers between devices: 401 us -> 3.97 us
  matrix products: 377 us -> 190 us
  local copies, waits for them, and re-layouts: 102 us -> 196 us
    pallas_call x0 -> x30, Pallas kernels: none -> 1050 us  [launch(): pl.pallas_call(kernel, out_shape=tuple(out_shapes), in_specs=[ANY] * len(...]
    ppermute x129 -> x3, waiting for transfers between devices: 471 us -> 3.09 us  [flip(): return lax.ppermute(value, axis, [(0, 1), (1, 0)])]
    ppermute x129 -> x3, starting transfers between devices: 203 us -> 3.97 us  [flip(): return lax.ppermute(value, axis, [(0, 1), (1, 0)])]
    ppermute x61 -> x0, starting transfers between devices: 197 us -> none  [the longest x14 146 us: spread_pair(): far = lax.ppermute(shard, ('c', 'zh'), RING)]
    psum x2 -> x0, waiting for transfers between devices: 138 us -> none  [the longest x1 126 us: body(): small = lax.psum(small, (*bits, 'c', 'zh', 'zl'))]
    dot_general x51 -> x9, matrix products: 123 us -> 17 us  [nn(): lax.dot_general(a, b, (((1,), (0,)), ((), ())), preferred_element_type=F32)]
    dot_general x49 -> x2, matrix products: 108 us -> 4.38 us  [nt(): lax.dot_general(a, b, (((1,), (1,)), ((), ())), preferred_element_type=F32)]
    ppermute x61 -> x0, waiting for transfers between devices: 91 us -> none  [the longest x14 79.7 us: fold_pair(): lax.ppermute(far, ('c', 'zh'), RING_BACK).astype(F32)]
  transfers between devices with their start and end apart: 192 -> 3, of which waited for: 58 -> 1; matrix products, arithmetic and copies ran while one was open for 31% -> 4% of each run, Pallas kernels for 0% -> 14%
where the time goes in v2:
time: 1610 us
  Pallas kernels  1050 us (65%)
  local copies, waits for them, and re-layouts  196 us (12%)
  matrix products  190 us (12%)
  other arithmetic  145 us (9%)
    pallas_call x30, Pallas kernels, launch(): pl.pallas_call(kernel, out_shape=tuple(out_shapes), in_specs=[ANY] * len(...  1050 us
    unnamed x751, local copies, waits for them, and re-layouts  84.7 us
    dot_general x14, matrix products, tn(): lax.dot_general(a, b, (((0,), (0,)), ((), ())), preferred_element_type=F32)  59.8 us
    dot_general x8, matrix products, attend_rows_back(): grad_probs = jnp.einsum('qhd,khd->hqk', g, v, preferred_element_type=F32)  40 us
  transfers between devices with their start and end apart: 3, of which 1 were waited for; matrix products, arithmetic and copies ran while one was open for 4% of the time, Pallas kernels for 14%

profile of v2, /device:TPU:0, one launch (start us, length us, event | category | flops | bytes accessed | tf_op | source)
XLA Modules:
  0.0 1605.5 jit_solution(13348662817888993417)
XLA Ops:
  3.4 10.3 all-gather.1
  28.1 29.3 %move_0.1 = (bf16[1536,1152]{1,0:T(8,128)(2,1)}, bf16[1536,384]{1,0:T(8,128)(2,1)S(1)}, bf16[256,1536]{1,0:T(8,128)(2,1)S(1)}, bf16[1536,384]{1,0:T(8,128)(2,1)S...) custom-call(bf16[192,1152]{1,0:T(8,128)(2,1)S(1)} %bitcast.506, ...), custom_call_target="tpu_custom_call" | custom-call | tf_op jit(solution)/shard_map/move_0/pallas_call | solution.py:210
  69.3 16.4 %move_2.1 = (bf16[1536,1152]{1,0:T(8,128)(2,1)S(1)}, bf16[1536,384]{1,0:T(8,128)(2,1)S(1)}) custom-call(bf16[1536,1152]{1,0:T(8,128)(2,1)S(1)} %get-tuple-element.185.refs_0_, bf16[1536,384]{1,0:T(8,128)(2,1)S(1)} %get-tuple-element.186.refs_1_), custom_call_target="tpu_custom_call", output_to_operand_aliasing={{0}: (0, {}), {1}: (1, {})} | custom-call | tf_op jit(solution)/shard_map/move_2/pallas_call | solution.py:210
  87.5 85.9 %gather_3.1 = (bf16[4,256,1536]{2,1,0:T(8,128)(2,1)}, bf16[4,256,1152]{2,1,0:T(8,128)(2,1)}, bf16[1536,384]{1,0:T(8,128)(2,1)S(1)}, bf16[1536,768]{1,0:T(8,128)(...) custom-call(f32[256,1536]{1,0:T(8,128)S(1)} %get-tuple-element.639.r, ...), custom_call_target="tpu_custom_call", output_to_operand_aliasing={{2}: (3, {}), {3}: (4, {}), {4}: (5, {})} | custom-call | tf_op jit(solution)/shard_map/gather_3/pallas_call | solution.py:210
  209.4 44.2 %scatter_4.1 = (f32[256,1536]{1,0:T(8,128)S(1)}, bf16[1536,384]{1,0:T(8,128)(2,1)S(1)}, bf16[1536,768]{1,0:T(8,128)(2,1)}, bf16[1536,384]{1,0:T(8,128)(2,1)S(1)}, bf16[1536,1536]{1,0:T(8,128)(2,1)}) custom-call(bf16[4,256,384]{2,1,0:T(8,128)(2,1)S(1)} %pad_maximum_fusion.20.refs_0_, ...), custom_call_target="tpu_custom_call", output_to_operand_aliasing={{1}: (3, {}), {2}: (4, {}), {3}: (5, {}), {4}: (6, {})} | custom-call | tf_op jit(solution)/shard_map/scatter_4/pallas_call | solution.py:210
  257.1 36.5 %gather_5.1 = (bf16[4,256,1536]{2,1,0:T(8,128)(2,1)}, bf16[4,256,384]{2,1,0:T(8,128)(2,1)S(1)}, bf16[1536,1536]{1,0:T(8,128)(2,1)}, bf16[1536,1536]{1,0:T(8,128)(2,1)}) custom-call(f32[256,1536]{1,0:T(8,128)S(1)} %get-tuple-element.198.refs_0_.refs_2_, bf16[1536,384]{1,0:T(8,128)(2,1)S(1)} %copy-done.32, ...), custom_call_target="tpu_custom_call", output_to_operand_aliasing={{2}: (3, {})} | custom-call | tf_op jit(solution)/shard_map/gather_5/pallas_call | solution.py:210
  312.4 38.1 %scatter_6.1 = (f32[256,1536]{1,0:T(8,128)S(1)}, bf16[1536,1536]{1,0:T(8,128)(2,1)}, bf16[1536,1152]{1,0:T(8,128)(2,1)}, bf16[1536,384]{1,0:T(8,128)(2,1)S(1)}) custom-call(bf16[4,256,384]{2,1,0:T(8,128)(2,1)S(1)} %copy-done.38, bf16[1536,384]{1,0:T(8,128)(2,1)S(1)} %copy-done.18, f32[256,1536]{1,0:T(8,128)} %copy-done.4, ...), custom_call_target="tpu_custom_call", output_to_operand_aliasing={{1}: (3, {})} | custom-call | tf_op jit(solution)/shard_map/scatter_6/pallas_call | solution.py:210
  351.4 41.2 %gather_7.1 = (bf16[4,256,1536]{2,1,0:T(8,128)(2,1)S(1)}, bf16[4,256,1536]{2,1,0:T(8,128)(2,1)}, bf16[4,256,1536]{2,1,0:T(8,128)(2,1)}, bf16[1536,1536]{1,0:T(8,...) custom-call(f32[256,1536]{1,0:T(8,128)S(1)} %get-tuple-element.204.r, ...), custom_call_target="tpu_custom_call", output_to_operand_aliasing={{3}: (3, {}), {4}: (4, {}), {5}: (5, {})} | custom-call | tf_op jit(solution)/shard_map/gather_7/pallas_call | solution.py:210
  396.5 37.7 %scatter_8.1 = (f32[256,1536]{1,0:T(8,128)S(1)}, bf16[1536,1152]{1,0:T(8,128)(2,1)}, bf16[1536,384]{1,0:T(8,128)(2,1)S(1)}, bf16[1536,384]{1,0:T(8,128)(2,1)S(1)...) custom-call(bf16[4,256,1536]{2,1,0:T(8,128)(2,1)} %get-tuple-element.209, ...), custom_call_target="tpu_custom_call", output_to_operand_aliasing={{1}: (3, {}), {2}: (4, {})} | custom-call | tf_op jit(solution)/shard_map/scatter_8/pallas_call | solution.py:210
  440.1 43.5 %gather_9.1 = (bf16[4,256,1536]{2,1,0:T(8,128)(2,1)}, bf16[4,256,1152]{2,1,0:T(8,128)(2,1)}, bf16[1536,384]{1,0:T(8,128)(2,1)S(1)}, bf16[1536,768]{1,0:T(8,128)(...) custom-call(f32[256,1536]{1,0:T(8,128)S(1)} %get-tuple-element.213.r, ...), custom_call_target="tpu_custom_call", output_to_operand_aliasing={{2}: (3, {}), {3}: (4, {}), {4}: (5, {})} | custom-call | tf_op jit(solution)/shard_map/gather_9/pallas_call | solution.py:210
  510.3 45.0 %scatter_10.1 = (f32[256,1536]{1,0:T(8,128)S(1)}, bf16[1536,384]{1,0:T(8,128)(2,1)S(1)}, bf16[1536,768]{1,0:T(8,128)(2,1)}, bf16[1536,384]{1,0:T(8,128)(2,1)S(1)}, bf16[1536,1536]{1,0:T(8,128)(2,1)}) custom-call(bf16[4,256,384]{2,1,0:T(8,128)(2,1)S(1)} %pad_maximum_fusion.22.refs_0_, ...), custom_call_target="tpu_custom_call", output_to_operand_aliasing={{1}: (3, {}), {2}: (4, {}), {3}: (5, {}), {4}: (6, {})} | custom-call | tf_op jit(solution)/shard_map/scatter_10/pallas_call | solution.py:210
  564.2 36.7 %gather_11.1 = (bf16[4,256,1536]{2,1,0:T(8,128)(2,1)}, bf16[4,256,384]{2,1,0:T(8,128)(2,1)S(1)}, bf16[1536,1536]{1,0:T(8,128)(2,1)}, bf16[1536,1536]{1,0:T(8,128)(2,1)}) custom-call(f32[256,1536]{1,0:T(8,128)S(1)} %get-tuple-element.225.refs_0_.refs_2_, bf16[1536,384]{1,0:T(8,128)(2,1)S(1)} %copy-done.22, ...), custom_call_target="tpu_custom_call", output_to_operand_aliasing={{2}: (3, {})} | custom-call | tf_op jit(solution)/shard_map/gather_11/pallas_call | solution.py:210
  615.2 24.2 %scatter_12.1 = (f32[256,1536]{1,0:T(8,128)S(1)}, bf16[1536,1536]{1,0:T(8,128)(2,1)}) custom-call(bf16[4,256,384]{2,1,0:T(8,128)(2,1)S(1)} %copy-done.39, bf16[1536,384]{1,0:T(8,128)(2,1)S(1)} %copy-done.28, f32[256,1536]{1,0:T(8,128)S(1)} %get-tuple-element.225.refs_0_.refs_2_, ...), custom_call_target="tpu_custom_call", output_to_operand_aliasing={{1}: (3, {})} | custom-call | tf_op jit(solution)/shard_map/scatter_12/pallas_call | solution.py:210
  639.5 28.5 %gather_13.1 = (bf16[4,256,1536]{2,1,0:T(8,128)(2,1)S(1)}, bf16[4,256,1536]{2,1,0:T(8,128)(2,1)}, bf16[4,256,1536]{2,1,0:T(8,128)(2,1)}, bf16[1536,1536]{1,0:T(8,128)(2,1)}) custom-call(f32[256,1536]{1,0:T(8,128)S(1)} %get-tuple-element.231.refs_0_.refs_2_, bf16[1536,1536]{1,0:T(8,128)(2,1)} %get-tuple-element.232.refs_1_, ...), custom_call_target="tpu_custom_call", output_to_operand_aliasing={{3}: (3, {})} | custom-call | tf_op jit(solution)/shard_map/gather_13/pallas_call | solution.py:210
  668.0 25.8 %scatter_14.1 = f32[256,1536]{1,0:T(8,128)S(1)} custom-call(bf16[4,256,1536]{2,1,0:T(8,128)(2,1)} %get-tuple-element.234.refs_0_, bf16[1536,1536]{1,0:T(8,128)(2,1)} %get-tuple-element.235.refs_1_, f32[256,1536]{1,0:T(8,128)S(1)} %get-tuple-element.231.refs_0_.refs_2_), custom_call_target="tpu_custom_call" | custom-call | tf_op jit(solution)/shard_map/scatter_14/pallas_call | solution.py:210
  695.3 34.8 %gather_15.1 = (bf16[4,256,1536]{2,1,0:T(8,128)(2,1)}, bf16[4,256,1536]{2,1,0:T(8,128)(2,1)}, bf16[256,1536]{1,0:T(8,128)(2,1)S(1)}) custom-call(f32[256,1536]{1,0:T(8,128)S(1)} %copy-done.35, bf16[1536,1536]{1,0:T(8,128)(2,1)} %get-tuple-element.235.refs_1_, bf16[4,256,1536]{2,1,0:T(8,128)(2,1)} %get-tuple-element.237.refs_2_, ...), custom_call_target="tpu_custom_call" | custom-call | tf_op jit(solution)/shard_map/gather_15/pallas_call | solution.py:210
  749.7 28.3 %scatter_16.1 = (f32[256,1536]{1,0:T(8,128)}, bf16[768,768]{1,0:T(8,128)(2,1)S(1)}, bf16[768,768]{1,0:T(8,128)(2,1)S(1)}) custom-call(bf16[4,256,1536]{2,1,0:T(8,128)(2,1)} %get-tuple-element.239.refs_0_, bf16[1536,1536]{1,0:T(8,128)(2,1)} %get-tuple-element.232.refs_1_, bf16[768,768]{1,0:T(8,128)(2,1)S(1)} %slice.1696.refs_2_, ...), custom_call_target="tpu_custom_call" | custom-call | tf_op jit(solution)/shard_map/scatter_16/pallas_call | solution.py:210
  786.0 40.6 %gather_17.1 = (bf16[4,256,1536]{2,1,0:T(8,128)(2,1)}, bf16[4,256,384]{2,1,0:T(8,128)(2,1)S(1)}, bf16[384,768]{1,0:T(8,128)(2,1)S(1)}, bf16[384,768]{1,0:T(8,128...) custom-call(f32[256,1536]{1,0:T(8,128)} %multiply_add_fusion.4.refs_0_, ...), custom_call_target="tpu_custom_call" | custom-call | tf_op jit(solution)/shard_map/gather_17/pallas_call | solution.py:210
  870.3 36.2 %scatter_18.1 = (f32[256,1536]{1,0:T(8,128)}, bf16[192,768]{1,0:T(8,128)(2,1)S(1)}, bf16[192,768]{1,0:T(8,128)(2,1)S(1)}, bf16[192,768]{1,0:T(8,128)(2,1)S(1)}, ...) custom-call(bf16[4,256,384]{2,1,0:T(8,128)(2,1)} %copy.286.refs_0_, ...), custom_call_target="tpu_custom_call" | custom-call | tf_op jit(solution)/shard_map/scatter_18/pallas_call | solution.py:210
  914.9 36.0 %gather_19.1 = (bf16[4,256,1536]{2,1,0:T(8,128)(2,1)}, bf16[4,256,384]{2,1,0:T(8,128)(2,1)S(1)}, bf16[192,768]{1,0:T(8,128)(2,1)S(1)}, bf16[192,768]{1,0:T(8,128...) custom-call(f32[256,1536]{1,0:T(8,128)} %multiply_add_fusion.3.refs_, ...), custom_call_target="tpu_custom_call" | custom-call | tf_op jit(solution)/shard_map/gather_19/pallas_call | solution.py:210
  975.8 10.7 multiply_reduce_fusion.1
  1028.9 28.6 %scatter_20.1 = (f32[256,1536]{1,0:T(8,128)S(1)}, bf16[192,384]{1,0:T(8,128)(2,1)S(1)}, bf16[192,384]{1,0:T(8,128)(2,1)S(1)}, bf16[384,384]{1,0:T(8,128)(2,1)S(1...) custom-call(bf16[4,256,1152]{2,1,0:T(8,128)(2,1)} %pad_maximum_fusion.1.refs_0_, ...), custom_call_target="tpu_custom_call" | custom-call | tf_op jit(solution)/shard_map/scatter_20/pallas_call | solution.py:210
  1062.1 36.0 %gather_21.1 = (bf16[4,256,1536]{2,1,0:T(8,128)(2,1)}, bf16[4,256,1536]{2,1,0:T(8,128)(2,1)}, bf16[192,384]{1,0:T(8,128)(2,1)S(1)}, bf16[192,384]{1,0:T(8,128)(2...) custom-call(f32[256,1536]{1,0:T(8,128)} %multiply_add_fusion.2.refs_, ...), custom_call_target="tpu_custom_call" | custom-call | tf_op jit(solution)/shard_map/gather_21/pallas_call | solution.py:210
  1121.6 41.6 %scatter_22.1 = (f32[256,1536]{1,0:T(8,128)}, bf16[192,384]{1,0:T(8,128)(2,1)S(1)}, bf16[192,384]{1,0:T(8,128)(2,1)S(1)}, bf16[384,768]{1,0:T(8,128)(2,1)S(1)}, ...) custom-call(bf16[4,256,1536]{2,1,0:T(8,128)(2,1)} %get-tuple-element.267.refs_0_, ...), custom_call_target="tpu_custom_call" | custom-call | tf_op jit(solution)/shard_map/scatter_22/pallas_call | solution.py:210
  1172.4 41.9 %gather_23.1 = (bf16[4,256,1536]{2,1,0:T(8,128)(2,1)}, bf16[4,256,384]{2,1,0:T(8,128)(2,1)S(1)}, bf16[192,768]{1,0:T(8,128)(2,1)S(1)}, bf16[192,768]{1,0:T(8,128...) custom-call(f32[256,1536]{1,0:T(8,128)} %multiply_add_fusion.1.refs_, ...), custom_call_target="tpu_custom_call" | custom-call | tf_op jit(solution)/shard_map/gather_23/pallas_call | solution.py:210
  1249.3 36.3 %scatter_24.1 = (f32[256,1536]{1,0:T(8,128)}, bf16[192,768]{1,0:T(8,128)(2,1)S(1)}, bf16[192,768]{1,0:T(8,128)(2,1)S(1)}, bf16[192,768]{1,0:T(8,128)(2,1)S(1)}, ...) custom-call(bf16[4,256,384]{2,1,0:T(8,128)(2,1)} %copy.310.refs_0_, ...), custom_call_target="tpu_custom_call" | custom-call | tf_op jit(solution)/shard_map/scatter_24/pallas_call | solution.py:210
  1295.8 35.8 %gather_25.1 = (bf16[4,256,1536]{2,1,0:T(8,128)(2,1)}, bf16[4,256,384]{2,1,0:T(8,128)(2,1)S(1)}, bf16[192,768]{1,0:T(8,128)(2,1)S(1)}, bf16[192,768]{1,0:T(8,128...) custom-call(f32[256,1536]{1,0:T(8,128)} %multiply_add_fusion.refs_0_, ...), custom_call_target="tpu_custom_call" | custom-call | tf_op jit(solution)/shard_map/gather_25/pallas_call | solution.py:210
  1361.8 10.7 multiply_reduce_fusion
  1433.8 28.8 %scatter_26.1 = (f32[256,1536]{1,0:T(8,128)S(1)}, bf16[192,384]{1,0:T(8,128)(2,1)S(1)}, bf16[192,384]{1,0:T(8,128)(2,1)S(1)}, bf16[384,384]{1,0:T(8,128)(2,1)S(1...) custom-call(bf16[4,256,1152]{2,1,0:T(8,128)(2,1)} %pad_maximum_fusion.3.refs_0_, ...), custom_call_target="tpu_custom_call" | custom-call | tf_op jit(solution)/shard_map/scatter_26/pallas_call | solution.py:210
  1480.0 35.6 %move_27.1 = (bf16[192,384]{1,0:T(8,128)(2,1)S(1)}, bf16[192,384]{1,0:T(8,128)(2,1)S(1)}, bf16[192,768]{1,0:T(8,128)(2,1)S(1)}, bf16[192,768]{1,0:T(8,128)(2,1)S...) custom-call(bf16[192,384]{1,0:T(8,128)(2,1)S(1)} %get-tuple-element., ...), custom_call_target="tpu_custom_call" | custom-call | tf_op jit(solution)/shard_map/move_27/pallas_call | solution.py:210
  1524.1 19.8 %move_28.1 = (bf16[192,384]{1,0:T(8,128)(2,1)S(1)}, bf16[192,384]{1,0:T(8,128)(2,1)S(1)}, bf16[384,768]{1,0:T(8,128)(2,1)S(1)}, bf16[384,384]{1,0:T(8,128)(2,1)S...) custom-call(bf16[192,384]{1,0:T(8,128)(2,1)S(1)} %get-tuple-element.507.refs_0_, ...), custom_call_target="tpu_custom_call" | custom-call | tf_op jit(solution)/shard_map/move_28/pallas_call | solution.py:210
  1548.0 27.8 %move_29.1 = (bf16[192,768]{1,0:T(8,128)(2,1)S(1)}, bf16[192,768]{1,0:T(8,128)(2,1)S(1)}, bf16[192,384]{1,0:T(8,128)(2,1)S(1)}, bf16[192,384]{1,0:T(8,128)(2,1)S...) custom-call(bf16[192,768]{1,0:T(8,128)(2,1)S(1)} %get-tuple-element.439.refs_0_, ...), custom_call_target="tpu_custom_call" | custom-call | tf_op jit(solution)/shard_map/move_29/pallas_call | solution.py:210
  (1170 shorter events, 526.8 us)
Async XLA Ops:
  0.7 300.1 %collective-permute-start = (bf16[64,1536]{1,0:T(8,128)(2,1)}, bf16[64,1536]{1,0:T(8,128)(2,1)}, u32[]{:S(2)}, u32[]{:S(2)}) collective-permute-start(bf16[64,1536]{1,0:T(8,128)(2,1)} %bitcast.625), channel_id=1, source_target_pairs={{0,4},{4,0},{1,5},{5,1},{2,6},{6,2},{3,7},{7,3},{8,12},{12,8},{9,1... | collective-permute-start | bytes 589832 | tf_op jit(solution)/shard_map/ppermute | solution.py:33
  27.3 30.1 %copy-start.181 = (pred[1536,1536]{1,0:T(32,128)(4,1)S(1)}, pred[1536,1536]{1,0:T(32,128)(4,1)}, u32[]{:S(2)}) copy-start(pred[1536,1536]{1,0:T(32,128)(4,1)} %copy-done.180) | copy-start | bytes 7077892
  58.9 145.6 %copy-start.8 = (f32[256,1536]{1,0:T(8,128)}, f32[256,1536]{1,0:T(8,128)S(1)}, u32[]{:S(2)}) copy-start(f32[256,1536]{1,0:T(8,128)S(1)} %get-tuple-element.639.refs_0_.refs_2_) | copy-start | bytes 4718596
  87.5 85.9 %copy-start.33 = (bf16[1536,384]{1,0:T(8,128)(2,1)}, bf16[1536,384]{1,0:T(8,128)(2,1)S(1)}, u32[]{:S(2)}) copy-start(bf16[1536,384]{1,0:T(8,128)(2,1)S(1)} %get-tuple-element.192.refs_1_) | copy-start | bytes 3538948
  254.9 38.8 %copy-start.349 = (f32[256]{0:T(256)}, f32[256]{0:T(256)S(1)}, u32[]{:S(2)}) copy-start(f32[256]{0:T(256)S(1)} %broadcast_multiply_fusion.5) | copy-start | bytes 3076
  350.5 42.1 %copy-start.6 = (f32[256,1536]{1,0:T(8,128)}, f32[256,1536]{1,0:T(8,128)S(1)}, u32[]{:S(2)}) copy-start(f32[256,1536]{1,0:T(8,128)S(1)} %get-tuple-element.204.refs_0_.refs_2_) | copy-start | bytes 4718596
  351.4 43.8 %copy-start.72 = (bf16[24,8,2,384]{3,1,2,0:T(8,128)(2,1)S(1)}, bf16[24,8,2,384]{3,1,2,0:T(8,128)(2,1)}, u32[]{:S(2)}) copy-start(bf16[24,8,2,384]{3,1,2,0:T(8,128)(2,1)} %copy.364) | copy-start | bytes 884740
  351.4 43.8 %copy-start.78 = (bf16[192,384]{1,0:T(8,128)(2,1)S(1)}, bf16[192,384]{1,0:T(8,128)(2,1)}, u32[]{:S(2)}) copy-start(bf16[192,384]{1,0:T(8,128)(2,1)} %get-tuple-element.582.refs_5_) | copy-start | bytes 442372
  436.3 47.4 %copy-start = (f32[256,1536]{1,0:T(8,128)}, f32[256,1536]{1,0:T(8,128)S(1)}, u32[]{:S(2)}) copy-start(f32[256,1536]{1,0:T(8,128)S(1)} %get-tuple-element.213.refs_0_.refs_2_) | copy-start | bytes 4718596
  506.6 48.8 %copy-start.299 = (bf16[1,256,384]{2,1,0:T(8,128)(2,1)}, bf16[1,256,384]{2,1,0:T(8,128)(2,1)S(1)}, u32[]{:S(2)}) copy-start(bf16[1,256,384]{2,1,0:T(8,128)(2,1)S(1)} %copy.269) | copy-start | bytes 589828
  506.7 48.6 %copy-start.301 = (bf16[1,256,384]{2,1,0:T(8,128)(2,1)}, bf16[1,256,384]{2,1,0:T(8,128)(2,1)S(1)}, u32[]{:S(2)}) copy-start(bf16[1,256,384]{2,1,0:T(8,128)(2,1)S(1)} %copy.270) | copy-start | bytes 589828
  506.9 48.4 %copy-start.303 = (bf16[1,256,384]{2,1,0:T(8,128)(2,1)}, bf16[1,256,384]{2,1,0:T(8,128)(2,1)S(1)}, u32[]{:S(2)}) copy-start(bf16[1,256,384]{2,1,0:T(8,128)(2,1)S(1)} %copy.271) | copy-start | bytes 589828
  668.0 25.8 %copy-start.184 = (pred[1536,1536]{1,0:T(32,128)(4,1)S(1)}, pred[1536,1536]{1,0:T(32,128)(4,1)}, u32[]{:S(2)}) copy-start(pred[1536,1536]{1,0:T(32,128)(4,1)} %copy-done.180) | copy-start | bytes 7077892
  695.3 34.8 %copy-start.36 = (bf16[256,1536]{1,0:T(8,128)(2,1)}, bf16[256,1536]{1,0:T(8,128)(2,1)S(1)}, u32[]{:S(2)}) copy-start(bf16[256,1536]{1,0:T(8,128)(2,1)S(1)} %convolution_convert_fusion.5.refs_3_) | copy-start | bytes 2359300
  748.0 30.0 %copy-start.223 = (bf16[1536,1536]{1,0:T(8,128)(2,1)}, bf16[1536,1536]{1,0:T(8,128)(2,1)S(1)}, u32[]{:S(2)}) copy-start(bf16[1536,1536]{1,0:T(8,128)(2,1)S(1)} %bitcast_convert_fusion.2) | copy-start | bytes 14155780
  749.7 28.3 %copy-start.338 = (f32[1536]{0:T(1024)S(1)}, f32[1536]{0:T(1024)}, u32[]{:S(2)}) copy-start(f32[1536]{0:T(1024)} %get-tuple-element.405) | copy-start | bytes 18436
  863.8 45.8 %copy-start.280 = (bf16[1536,384]{1,0:T(8,128)(2,1)}, bf16[1536,384]{1,0:T(8,128)(2,1)S(1)}, u32[]{:S(2)}) copy-start(bf16[1536,384]{1,0:T(8,128)(2,1)S(1)} %convolution_convert_fusion.3) | copy-start | bytes 3538948
  870.3 36.2 %copy-start.337 = (f32[1536]{0:T(1024)S(1)}, f32[1536]{0:T(1024)}, u32[]{:S(2)}) copy-start(f32[1536]{0:T(1024)} %get-tuple-element.404) | copy-start | bytes 18436
  1028.5 31.6 %copy-start.282 = (bf16[1536,384]{1,0:T(8,128)(2,1)}, bf16[1536,384]{1,0:T(8,128)(2,1)S(1)}, u32[]{:S(2)}) copy-start(bf16[1536,384]{1,0:T(8,128)(2,1)S(1)} %fusion.28) | copy-start | bytes 3538948
  1062.1 36.1 %copy-start.241 = (bf16[4,256,1536]{2,1,0:T(8,128)(2,1)S(1)}, bf16[4,256,1536]{2,1,0:T(8,128)(2,1)}, u32[]{:S(2)}) copy-start(bf16[4,256,1536]{2,1,0:T(8,128)(2,1)} %get-tuple-element.209.refs_0_) | copy-start | bytes 9437188
  1243.0 46.0 %copy-start.279 = (bf16[1536,384]{1,0:T(8,128)(2,1)}, bf16[1536,384]{1,0:T(8,128)(2,1)S(1)}, u32[]{:S(2)}) copy-start(bf16[1536,384]{1,0:T(8,128)(2,1)S(1)} %convolution_convert_fusion.2) | copy-start | bytes 3538948
  1249.2 36.5 %copy-start.5 = (f32[256,1536]{1,0:T(8,128)S(1)}, f32[256,1536]{1,0:T(8,128)}, u32[]{:S(2)}) copy-start(f32[256,1536]{1,0:T(8,128)} %copy-done.4) | copy-start | bytes 4718596
  1249.3 36.4 %copy-start.334 = (f32[1536]{0:T(1024)S(1)}, f32[1536]{0:T(1024)}, u32[]{:S(2)}) copy-start(f32[1536]{0:T(1024)} %get-tuple-element.401) | copy-start | bytes 18436
  1249.3 36.4 %copy-start.350 = (f32[256]{0:T(256)S(1)}, f32[256]{0:T(256)}, u32[]{:S(2)}) copy-start(f32[256]{0:T(256)} %copy-done.349) | copy-start | bytes 3076
  1249.3 36.4 %copy-start.353 = (f32[256]{0:T(256)S(1)}, f32[256]{0:T(256)}, u32[]{:S(2)}) copy-start(f32[256]{0:T(256)} %add_rsqrt_fusion.1) | copy-start | bytes 3076
  1335.2 98.2 %copy-start.70 = (bf16[768,768]{1,0:T(8,128)(2,1)}, bf16[768,768]{1,0:T(8,128)(2,1)S(1)}, u32[]{:S(2)}) copy-start(bf16[768,768]{1,0:T(8,128)(2,1)S(1)} %get-tuple-element.292) | copy-start | bytes 3538948
  1433.3 34.7 %copy-start.281 = (bf16[1536,384]{1,0:T(8,128)(2,1)}, bf16[1536,384]{1,0:T(8,128)(2,1)S(1)}, u32[]{:S(2)}) copy-start(bf16[1536,384]{1,0:T(8,128)(2,1)S(1)} %fusion.30) | copy-start | bytes 3538948
  1433.7 28.9 %copy-start.71 = (bf16[768,768]{1,0:T(8,128)(2,1)S(1)}, bf16[768,768]{1,0:T(8,128)(2,1)}, u32[]{:S(2)}) copy-start(bf16[768,768]{1,0:T(8,128)(2,1)} %copy-done.70) | copy-start | bytes 3538948
  1480.0 35.7 %copy-start.89 = (bf16[768,384]{1,0:T(8,128)(2,1)S(1)}, bf16[768,384]{1,0:T(8,128)(2,1)}, u32[]{:S(2)}) copy-start(bf16[768,384]{1,0:T(8,128)(2,1)} %copy-done.88) | copy-start | bytes 1769476
  1524.1 21.2 %copy-start.283 = (bf16[768,768]{1,0:T(8,128)(2,1)S(1)}, bf16[768,768]{1,0:T(8,128)(2,1)}, u32[]{:S(2)}) copy-start(bf16[768,768]{1,0:T(8,128)(2,1)} %get-tuple-element.302) | copy-start | bytes 3538948
  1576.6 17.4 %collective-permute-start.1 = (f32[192,12]{1,0:T(8,128)S(1)}, f32[192,12]{1,0:T(8,128)}, u32[]{:S(2)}, u32[]{:S(2)}) collective-permute-start(f32[192,12]{1,0:T(8,128)S(1)} %convert_add_fusion.14), channel_id=1, source_target_pairs={{0,1},{1,0},{2,3},{3,2},{4,5},{5,4},{6,7},{7,6},{8,9},{9,8},{10,11... | collective-permute-start | bytes 27656 | tf_op jit(solution)/shard_map/ppermute | solution.py:33
  1595.0 8.6 collective-permute-start.2
  (341 other events, 1158.9 us)

commit v3 on v2

--- a/solution.py
+++ b/solution.py
@@ -7,10 +7,10 @@
 from jax.sharding import Mesh, PartitionSpec as P
 
 HEAD_DIM = 64
-ATT_BLOCK = 512
 NORM_EPS = 1e-05
 MASKED = -1e30
 TILE = 384
+LINK_BYTES = 1400000
 F32 = jnp.float32
 BF16 = jnp.bfloat16
 MESH = pl.DeviceIdType.MESH
@@ -156,12 +156,22 @@
     return Ride([buffer], [out], stages, kinds, sum(len(s) for s in plan), {0: 0})
 
 
+def chain_ride(shard, pieces, blocks):
+    first = pair_ride(shard, blocks)
+    rest = spread_ride(first.outs[0], pieces, range(len(pieces[0][2])), blocks)
+
+    def stages(ins, outs):
+        return first.stages(ins, outs) + rest.stages(ins, outs)
+
+    return Ride([shard], first.outs, stages, first.kinds + rest.kinds, first.count + rest.count)
+
+
 def send_ride(value, kind):
     out = jax.ShapeDtypeStruct(value.shape, value.dtype)
     return Ride([value], [out], lambda ins, outs: [[(kind, ins[0], outs[0])]], [kind], 1)
 
 
-def launch(name, number, main, ins, outs, scratch, kinds, rides, limit=48):
+def launch(name, number, main, ins, outs, scratch, kinds, rides, limit=56):
     in_arrays = list(ins)
     out_shapes = list(outs)
     aliases = {}
@@ -183,7 +193,8 @@
         rest = refs[len(in_arrays) + len(out_shapes) :]
         send, recv = rest[:2]
         early = main(in_refs[: len(ins)], out_refs[: len(outs)], rest[2:], True) if main else None
-        greet(all_kinds)
+        if all_kinds:
+            greet(all_kinds)
         chains, place = [], 0
         for ride, (a, b, c, d) in zip(rides, spans):
             chain = []
@@ -216,7 +227,9 @@
         input_output_aliases=aliases,
         name=name,
         compiler_params=pltpu.CompilerParams(
-            collective_id=number, has_side_effects=True, vmem_limit_bytes=limit << 20
+            collective_id=number if all_kinds else None,
+            has_side_effects=bool(all_kinds),
+            vmem_limit_bytes=limit << 20,
         ),
     )(*in_arrays)
     main_outs = results[: len(outs)]
@@ -334,14 +347,27 @@
     return launch(f"gather_{number}", number, main, ins, outs, scratch, ["c", "zl"], rides)
 
 
-def multiply_scatter(number, parts, weight, base, rides):
+def multiply_scatter(number, parts, weight, base, norm, fills, rides):
     _, size, n = parts.shape
     width = weight.shape[0]
     half = size // 2
-    ins = [parts, weight] + ([base] if base is not None else [])
+    rows = 4 * size
+    ins = [parts.reshape(rows, n), weight] + ([base] if base is not None else [])
+    if norm is not None:
+        ins += list(norm)
+    fill_at = len(ins)
+    fill_cols = []
+    for a, b in fills:
+        ins.append(a)
+        if b is not None:
+            ins.append(b)
+        fill_cols.append(n if b is None else b.shape[1])
     outs = [jax.ShapeDtypeStruct((size, width), F32)]
+    if norm is not None:
+        outs.append(jax.ShapeDtypeStruct((2, width), F32))
+    outs += [jax.ShapeDtypeStruct((width, k), BF16) for k in fill_cols]
     scratch = [
-        pltpu.VMEM((4, size, n), BF16),
+        pltpu.VMEM((rows, n), BF16),
         pltpu.VMEM((width, n), BF16),
         pltpu.VMEM((size, width), F32),
         pltpu.VMEM((size, width), F32),
@@ -349,35 +375,68 @@
         pltpu.VMEM((2, size, width), BF16),
         pltpu.VMEM((size, width), BF16),
         pltpu.VMEM((size, width), BF16),
-        pltpu.SemaphoreType.DMA((7,)),
+        pltpu.SemaphoreType.DMA((8,)),
         pltpu.SemaphoreType.DMA((6,)),
         pltpu.SemaphoreType.DMA((6,)),
     ]
+    if norm is not None:
+        scratch += [
+            pltpu.VMEM((size, width), F32),
+            pltpu.VMEM((1, width), F32),
+            pltpu.VMEM((size, width), F32),
+            pltpu.VMEM((2, width), F32),
+            pltpu.SemaphoreType.DMA((4,)),
+        ]
+    for (a, b), k in zip(fills, fill_cols):
+        scratch.append(pltpu.VMEM((rows, width), BF16))
+        if b is not None:
+            scratch.append(pltpu.VMEM((rows, k), BF16))
+        scratch += [pltpu.VMEM((width, k), BF16), pltpu.SemaphoreType.DMA((3,))]
 
     def main(in_refs, out_refs, refs, stage):
-        y, w, total, far, give, came, across, over, load, send, recv = refs
+        y, w, total, far, give, came, across, over, load, send, recv = refs[:11]
+        refs = list(refs[11:])
+        if norm is not None:
+            stream, gain, back, sums, norm_sem = refs[:5]
+            refs = refs[5:]
         if stage is True:
             loads = [pltpu.make_async_copy(in_refs[1], w, load.at[0])]
             loads += [
-                pltpu.make_async_copy(in_refs[0].at[b], y.at[b], load.at[1 + b])
+                pltpu.make_async_copy(
+                    in_refs[0].at[pl.ds(b * size, size)], y.at[pl.ds(b * size, size)],
+                    load.at[1 + b])
                 for b in range(4)
             ]
             if base is not None:
                 loads.append(pltpu.make_async_copy(in_refs[2], total, load.at[5]))
             for place in (0, 4, 3, 2, 1, 5)[: len(loads)]:
                 loads[place].start()
-            return loads
-        loads = stage
-
-        def multiply(b, part, put):
+            others = []
+            if norm is not None:
+                at = 3 if base is not None else 2
+                for i, ref in enumerate((stream, gain, back)):
+                    others.append(pltpu.make_async_copy(in_refs[at + i], ref, norm_sem.at[i]))
+            at = fill_at
+            for a, b in fills:
+                others.append(pltpu.make_async_copy(in_refs[at], refs[0], refs[2 if b is None else 3].at[0]))
+                at += 1
+                if b is not None:
+                    others.append(pltpu.make_async_copy(in_refs[at], refs[1], refs[3].at[1]))
+                    at += 1
+                refs = refs[3 if b is None else 4 :]
+            for copy in others:
+                copy.start()
+            return loads, others
+        loads, others = stage
+
+        def multiply(b, part, count, put):
             def step(j, carry):
                 cols = pl.ds(pl.multiple_of(j * TILE, TILE), TILE)
-                put(cols, nt(y[b, part, :], w[cols, :]))
+                put(cols, nt(y[pl.ds(b * size + part, count), :], w[cols, :]))
                 return carry
 
             lax.fori_loop(0, width // TILE, step, 0)
 
-        whole = pl.ds(0, size)
         for place in (0, 4, 3):
             loads[place].wait()
         sent = []
@@ -390,10 +449,10 @@
             def put_far(cols, value, part=part):
                 far[part, cols] = value
 
-            multiply(3, part, put_give)
+            multiply(3, h * half, half, put_give)
             copy = Copy("c", give.at[0, part], came.at[0, part], send.at[h], recv.at[h])
             copy.start()
-            multiply(2, part, put_far)
+            multiply(2, h * half, half, put_far)
             copy.wait()
             across[part, :] = (far[part, :] + came[0, part, :].astype(F32)).astype(BF16)
             copy = Copy("zl", across.at[part], over.at[part], send.at[2 + h], recv.at[2 + h])
@@ -404,7 +463,7 @@
         def put_near(cols, value):
             give[1, :, cols] = value.astype(BF16)
 
-        multiply(1, whole, put_near)
+        multiply(1, 0, size, put_near)
         near = Copy("c", give.at[1], came.at[1], send.at[4], recv.at[4])
         near.start()
         loads[1].wait()
@@ -414,131 +473,338 @@
         def put_total(cols, value):
             total[:, cols] = value + (total[:, cols] if base is not None else 0.0)
 
-        multiply(0, whole, put_total)
+        multiply(0, 0, size, put_total)
+        for copy in others:
+            copy.wait()
+        stores = []
+        fill_refs = refs
+        for k, (a, b) in enumerate(fills):
+            if b is None:
+                left, result, sem = fill_refs[:3]
+                right, fill_refs = y, fill_refs[3:]
+            else:
+                left, right, result, sem = fill_refs[:4]
+                fill_refs = fill_refs[4:]
+            count = fill_cols[k]
+            wide = min(768, count)
+            if count % wide:
+                wide = count
+
+            def step(j, carry, left=left, right=right, result=result, wide=wide, count=count):
+                rows_ = pl.ds(pl.multiple_of(j * 256, 256), 256)
+                turned = left[:, rows_].T
+                for q in range(count // wide):
+                    cols = slice(q * wide, (q + 1) * wide)
+                    result[rows_, cols] = nn(turned, right[:, cols]).astype(BF16)
+                return carry
+
+            lax.fori_loop(0, width // 256, step, 0)
+            where = len(outs) - len(fills) + k
+            stores.append(pltpu.make_async_copy(result, out_refs[where], sem.at[2]))
+            stores[-1].start()
         near.wait()
         total[...] += came[1].astype(F32)
-        done = []
         for h in range(2):
             part = pl.ds(h * half, half)
             sent[h].wait()
             total[part, :] += over[part, :].astype(F32)
-            copy = pltpu.make_async_copy(total.at[part], out_refs[0].at[part], load.at[5 + h])
+            if norm is not None:
+                value = total[part, :]
+                rows_in = stream[part, :]
+                centred = rows_in - jnp.mean(rows_in, axis=-1, keepdims=True)
+                inverse = lax.rsqrt(jnp.mean(centred * centred, axis=-1, keepdims=True) + NORM_EPS)
+                unit = centred * inverse
+                gain_sum = jnp.sum(value * unit, axis=0, keepdims=True)
+                shift_sum = jnp.sum(value, axis=0, keepdims=True)
+                sums[0:1, :] = gain_sum if h == 0 else sums[0:1, :] + gain_sum
+                sums[1:2, :] = shift_sum if h == 0 else sums[1:2, :] + shift_sum
+                scaled = value * gain[...]
+                total[part, :] = back[part, :] + inverse * (
+                    scaled
+                    - jnp.mean(scaled, axis=-1, keepdims=True)
+                    - unit * jnp.mean(scaled * unit, axis=-1, keepdims=True)
+                )
+            copy = pltpu.make_async_copy(total.at[part], out_refs[0].at[part], load.at[6 + h])
             copy.start()
-            done.append(copy)
-        for copy in done:
+            stores.append(copy)
+        if norm is not None:
+            copy = pltpu.make_async_copy(sums, out_refs[1], norm_sem.at[3])
+            copy.start()
+            stores.append(copy)
+        for copy in stores:
             copy.wait()
 
-    (out,), extra = launch(
-        f"scatter_{number}", number, main, ins, outs, scratch, ["c", "zl"], rides
-    )
-    return out, extra
-
-
-def normalise_back(stream, gain, grad_normed, grad_stream):
-    centre = jnp.mean(stream, axis=-1, keepdims=True)
-    centred = stream - centre
-    spread = jnp.mean(centred * centred, axis=-1, keepdims=True)
-    inverse = lax.rsqrt(spread + NORM_EPS)
-    unit = centred * inverse
-    grad_gain = jnp.sum(grad_normed * unit, axis=0)
-    grad_shift = jnp.sum(grad_normed, axis=0)
-    scaled = grad_normed * gain
-    grad_input = inverse * (
-        scaled
-        - jnp.mean(scaled, axis=-1, keepdims=True)
-        - unit * jnp.mean(scaled * unit, axis=-1, keepdims=True)
-    )
-    return grad_stream + grad_input, grad_gain, grad_shift
-
-
-def causal_mask(scores, offset):
-    rows = offset + lax.broadcasted_iota(jnp.int32, scores.shape[-2:], 0)
-    cols = lax.broadcasted_iota(jnp.int32, scores.shape[-2:], 1)
-    return jnp.where(rows >= cols, scores, MASKED)
-
-
-def attend_rows(query, keys, values, causal, scale):
-    frames = query.shape[0]
-    mixed_rows, logsums = [], []
-    block = min(ATT_BLOCK, frames)
-    for start in range(0, frames, block):
-        stop = start + block
-        reach = stop if causal else keys.shape[0]
-        scores = (
-            jnp.einsum(
-                "qhd,khd->hqk", query[start:stop], keys[:reach], preferred_element_type=F32
-            )
-            * scale
-        )
-        if causal:
-            scores = causal_mask(scores, start)
-        top = jnp.max(scores, axis=-1, keepdims=True)
+    return launch(f"scatter_{number}", number, main, ins, outs, scratch, ["c", "zl"], rides)
+
+
+def place_of(i):
+    c, zl = lax.axis_index("c"), lax.axis_index("zl")
+    dc, dz = i // 2, i % 2
+    return (c + dc) % 2 + 2 * ((zl + dz) % 2)
+
+
+def head_only(value, u):
+    lane = lax.broadcasted_iota(jnp.int32, value.shape, 1)
+    keep = (lane < HEAD_DIM) if u == 0 else (lane >= HEAD_DIM)
+    return jnp.where(keep, value, jnp.zeros_like(value))
+
+
+def masked(scores):
+    key = lax.broadcasted_iota(jnp.int32, scores.shape, 0)
+    query = lax.broadcasted_iota(jnp.int32, scores.shape, 1)
+    return jnp.where(key <= query, scores, MASKED)
+
+
+def softmax_parts(parts, value_rows):
+    top = parts[0].max(axis=0, keepdims=True)
+    for scores in parts[1:]:
+        top = jnp.maximum(top, scores.max(axis=0, keepdims=True))
+    total, mixed = 0.0, 0.0
+    for scores, values in zip(parts, value_rows):
         expo = jnp.exp(scores - top)
-        total = jnp.sum(expo, axis=-1, keepdims=True)
-        probs = (expo / total).astype(BF16)
-        mixed_rows.append(
-            jnp.einsum("hqk,khd->qhd", probs, values[:reach], preferred_element_type=F32)
-        )
-        logsums.append(top + jnp.log(total))
-    joined = jnp.concatenate(mixed_rows, axis=0).reshape(frames, -1).astype(BF16)
-    return joined, logsums
-
-
-def attend_rows_back(query, keys, values, grad_joined, logsums, causal, scale):
-    frames, heads = query.shape[0], query.shape[1]
-    length = keys.shape[0]
-    grad_mixed = grad_joined.reshape(frames, heads, HEAD_DIM)
-    query_parts = []
-    grad_keys = jnp.zeros(keys.shape, F32)
-    grad_values = jnp.zeros(values.shape, F32)
-    block = min(ATT_BLOCK, frames)
-    for index, start in enumerate(range(0, frames, block)):
-        stop = start + block
-        reach = stop if causal else length
-        q, k, v, g = query[start:stop], keys[:reach], values[:reach], grad_mixed[start:stop]
-        scores = jnp.einsum("qhd,khd->hqk", q, k, preferred_element_type=F32) * scale
-        if causal:
-            scores = causal_mask(scores, start)
-        probs = jnp.exp(scores - logsums[index])
-        grad_probs = jnp.einsum("qhd,khd->hqk", g, v, preferred_element_type=F32)
-        part_values = jnp.einsum(
-            "hqk,qhd->khd", probs.astype(BF16), g, preferred_element_type=F32
-        )
-        inner = jnp.sum(probs * grad_probs, axis=-1, keepdims=True)
-        grad_scores = (probs * (grad_probs - inner)).astype(BF16)
-        query_parts.append(
-            jnp.einsum("hqk,khd->qhd", grad_scores, k, preferred_element_type=F32) * scale
-        )
-        part_keys = jnp.einsum("hqk,qhd->khd", grad_scores, q, preferred_element_type=F32) * scale
-        padding = ((0, length - reach), (0, 0), (0, 0))
-        grad_keys = grad_keys + jnp.pad(part_keys, padding)
-        grad_values = grad_values + jnp.pad(part_values, padding)
-    return jnp.concatenate(query_parts, axis=0), grad_keys, grad_values
-
-
-def to_time(parts):
-    own, beside, over, both = [parts[i] for i in range(4)]
-    c_one = lax.axis_index("c") == 1
-    z_one = lax.axis_index("zl") == 1
-    first = [jnp.where(z_one, over, own), jnp.where(z_one, own, over)]
-    second = [jnp.where(z_one, both, beside), jnp.where(z_one, beside, both)]
-    low = [jnp.where(c_one, s, f) for f, s in zip(first, second)]
-    high = [jnp.where(c_one, f, s) for f, s in zip(first, second)]
-    return jnp.concatenate(low + high, axis=0)
-
-
-def from_time(rows):
-    size = rows.shape[0] // 4
-    q = [rows[i * size : (i + 1) * size] for i in range(4)]
-    c_one = lax.axis_index("c") == 1
-    z_one = lax.axis_index("zl") == 1
-    mine = [jnp.where(c_one, q[2 + i], q[i]) for i in range(2)]
-    core = [jnp.where(c_one, q[i], q[2 + i]) for i in range(2)]
-    own = jnp.where(z_one, mine[1], mine[0])
-    over = jnp.where(z_one, mine[0], mine[1])
-    beside = jnp.where(z_one, core[1], core[0])
-    both = jnp.where(z_one, core[0], core[1])
-    return jnp.stack([own, beside, over, both])
+        total = total + expo.sum(axis=0, keepdims=True)
+        mixed = mixed + nn(values, expo.astype(BF16))
+    return mixed / total, top + jnp.log(total)
+
+
+def softmax_back(scores, slopes, logsum):
+    probs = [jnp.exp(s - logsum) for s in scores]
+    inner = 0.0
+    for p, d in zip(probs, slopes):
+        inner = inner + (p * d).sum(axis=0, keepdims=True)
+    return [p.astype(BF16) for p in probs], [
+        (p * (d - inner)).astype(BF16) for p, d in zip(probs, slopes)
+    ]
+
+
+def attend_self(number, proj, scale, rides):
+    _, size, wide = proj.shape
+    cols = wide // 3
+    frames, heads = 4 * size, cols // HEAD_DIM
+    outs = [jax.ShapeDtypeStruct((4, size, cols), BF16), jax.ShapeDtypeStruct((heads, frames), F32)]
+    scratch = [
+        pltpu.VMEM((4, size, wide), BF16),
+        pltpu.VMEM((frames, 128), BF16),
+        pltpu.VMEM((128, frames), BF16),
+        pltpu.VMEM((4, size, cols), BF16),
+        pltpu.VMEM((heads, frames), F32),
+        pltpu.SemaphoreType.DMA((3,)),
+    ]
+
+    def main(in_refs, out_refs, refs, stage):
+        x, keys, values, out, logs, sem = refs
+        if stage is True:
+            copy = pltpu.make_async_copy(in_refs[0], x, sem.at[0])
+            copy.start()
+            return copy
+        stage.wait()
+        for g in range(cols // 128):
+            lanes = [pl.ds(part * cols + g * 128, 128) for part in range(3)]
+            for i in range(4):
+                rows = pl.ds(i * size, size)
+                keys[rows, :] = x[place_of(i), :, lanes[1]]
+                values[:, rows] = x[place_of(i), :, lanes[2]].T
+            for i in range(4):
+                query = x[place_of(i), :, lanes[0]]
+                before = i * size
+                done = []
+                for u in range(2):
+                    q = head_only(query, u)
+                    mine = pl.ds(u * HEAD_DIM, HEAD_DIM)
+                    parts = [masked(nt(keys[pl.ds(before, size), :], q) * scale)]
+                    rows = [values[mine, pl.ds(before, size)]]
+                    if i:
+                        parts.append(nt(keys[pl.ds(0, before), :], q) * scale)
+                        rows.append(values[mine, pl.ds(0, before)])
+                    mixed, logsum = softmax_parts(parts, rows)
+                    done.append(mixed)
+                    logs[pl.ds(2 * g + u, 1), pl.ds(before, size)] = logsum
+                joined = jnp.concatenate(done, axis=0).T
+                out[place_of(i), :, pl.ds(g * 128, 128)] = joined.astype(BF16)
+        copies = [pltpu.make_async_copy(out, out_refs[0], sem.at[1]),
+                  pltpu.make_async_copy(logs, out_refs[1], sem.at[2])]
+        for copy in copies:
+            copy.start()
+        for copy in copies:
+            copy.wait()
+
+    return launch(f"attend_{number}", number, main, [proj], outs, scratch, [], rides)
+
+
+def attend_self_back(number, proj, grad_joined, logsum, scale, rides):
+    _, size, wide = proj.shape
+    cols = wide // 3
+    frames, heads = 4 * size, cols // HEAD_DIM
+    outs = [jax.ShapeDtypeStruct((4, size, wide), BF16)]
+    scratch = [
+        pltpu.VMEM((4, size, wide), BF16),
+        pltpu.VMEM((4, size, cols), BF16),
+        pltpu.VMEM((heads, frames), F32),
+        pltpu.VMEM((frames, 128), BF16),
+        pltpu.VMEM((128, frames), BF16),
+        pltpu.VMEM((frames, 128), BF16),
+        pltpu.VMEM((frames, 128), F32),
+        pltpu.VMEM((frames, 128), F32),
+        pltpu.VMEM((4, size, wide), BF16),
+        pltpu.SemaphoreType.DMA((4,)),
+    ]
+
+    def main(in_refs, out_refs, refs, stage):
+        x, grads, logs, keys, keys_t, values, grad_k, grad_v, out, sem = refs
+        if stage is True:
+            copies = [
+                pltpu.make_async_copy(in_refs[i], ref, sem.at[i])
+                for i, ref in enumerate((x, grads, logs))
+            ]
+            for copy in copies:
+                copy.start()
+            return copies
+        for copy in stage:
+            copy.wait()
+        for g in range(cols // 128):
+            lanes = [pl.ds(part * cols + g * 128, 128) for part in range(3)]
+            for i in range(4):
+                rows = pl.ds(i * size, size)
+                keys[rows, :] = x[place_of(i), :, lanes[1]]
+                keys_t[:, rows] = x[place_of(i), :, lanes[1]].T
+                values[rows, :] = x[place_of(i), :, lanes[2]]
+            grad_k[...] = jnp.zeros_like(grad_k)
+            grad_v[...] = jnp.zeros_like(grad_v)
+            for i in range(4):
+                query = x[place_of(i), :, lanes[0]]
+                grad = grads[place_of(i), :, lanes[0]]
+                before = i * size
+                spans = [pl.ds(before, size)] + ([pl.ds(0, before)] if i else [])
+                done = []
+                for u in range(2):
+                    q, go = head_only(query, u), head_only(grad, u)
+                    mine = pl.ds(u * HEAD_DIM, HEAD_DIM)
+                    scores = [nt(keys[span, :], q) * scale for span in spans]
+                    scores[0] = masked(scores[0])
+                    slopes = [nt(values[span, :], go) for span in spans]
+                    probs, grad_scores = softmax_back(
+                        scores, slopes, logs[pl.ds(2 * g + u, 1), pl.ds(before, size)])
+                    grad_q = 0.0
+                    for span, p, d in zip(spans, probs, grad_scores):
+                        grad_v[span, :] += nn(p, go)
+                        grad_k[span, :] += nn(d, q)
+                        grad_q = grad_q + nn(keys_t[mine, span], d)
+                    done.append(grad_q)
+                grad_q = jnp.concatenate(done, axis=0).T * scale
+                out[place_of(i), :, lanes[0]] = grad_q.astype(BF16)
+            for i in range(4):
+                rows = pl.ds(i * size, size)
+                out[place_of(i), :, lanes[1]] = (grad_k[rows, :] * scale).astype(BF16)
+                out[place_of(i), :, lanes[2]] = grad_v[rows, :].astype(BF16)
+        copy = pltpu.make_async_copy(out, out_refs[0], sem.at[3])
+        copy.start()
+        copy.wait()
+
+    return launch(f"attend_back_{number}", number, main, [proj, grad_joined, logsum], outs, scratch,
+                  [], rides)
+
+
+def attend_cross(number, query, pairs, scale, rides):
+    _, size, cols = query.shape
+    frames, heads, text = 4 * size, cols // HEAD_DIM, pairs.shape[0]
+    outs = [jax.ShapeDtypeStruct((4, size, cols), BF16), jax.ShapeDtypeStruct((heads, frames), F32)]
+    scratch = [
+        pltpu.VMEM((4, size, cols), BF16),
+        pltpu.VMEM((text, 2 * cols), BF16),
+        pltpu.VMEM((4, size, cols), BF16),
+        pltpu.VMEM((heads, frames), F32),
+        pltpu.SemaphoreType.DMA((4,)),
+    ]
+
+    def main(in_refs, out_refs, refs, stage):
+        x, kv, out, logs, sem = refs
+        if stage is True:
+            copies = [pltpu.make_async_copy(in_refs[0], x, sem.at[0]),
+                      pltpu.make_async_copy(in_refs[1], kv, sem.at[1])]
+            for copy in copies:
+                copy.start()
+            return copies
+        for copy in stage:
+            copy.wait()
+        for g in range(cols // 128):
+            lanes = pl.ds(g * 128, 128)
+            keys = kv[:, lanes]
+            values = kv[:, pl.ds(cols + g * 128, 128)].T
+            for i in range(4):
+                rows = x[i, :, lanes]
+                done = []
+                for u in range(2):
+                    scores = nt(keys, head_only(rows, u)) * scale
+                    mixed, logsum = softmax_parts(
+                        [scores], [values[u * HEAD_DIM : (u + 1) * HEAD_DIM, :]])
+                    done.append(mixed)
+                    logs[pl.ds(2 * g + u, 1), pl.ds(i * size, size)] = logsum
+                out[i, :, lanes] = jnp.concatenate(done, axis=0).T.astype(BF16)
+        copies = [pltpu.make_async_copy(out, out_refs[0], sem.at[2]),
+                  pltpu.make_async_copy(logs, out_refs[1], sem.at[3])]
+        for copy in copies:
+            copy.start()
+        for copy in copies:
+            copy.wait()
+
+    return launch(f"cross_{number}", number, main, [query, pairs], outs, scratch, [], rides)
+
+
+def attend_cross_back(number, query, pairs, grad_joined, logsum, scale, rides):
+    _, size, cols = query.shape
+    frames, heads, text = 4 * size, cols // HEAD_DIM, pairs.shape[0]
+    outs = [jax.ShapeDtypeStruct((4, size, cols), BF16),
+            jax.ShapeDtypeStruct((text, 2 * cols), BF16)]
+    scratch = [
+        pltpu.VMEM((4, size, cols), BF16),
+        pltpu.VMEM((text, 2 * cols), BF16),
+        pltpu.VMEM((4, size, cols), BF16),
+        pltpu.VMEM((heads, frames), F32),
+        pltpu.VMEM((4, size, cols), BF16),
+        pltpu.VMEM((text, 2 * cols), BF16),
+        pltpu.SemaphoreType.DMA((6,)),
+    ]
+
+    def main(in_refs, out_refs, refs, stage):
+        x, kv, grads, logs, out, out_kv, sem = refs
+        if stage is True:
+            copies = [
+                pltpu.make_async_copy(in_refs[i], ref, sem.at[i])
+                for i, ref in enumerate((x, kv, grads, logs))
+            ]
+            for copy in copies:
+                copy.start()
+            return copies
+        for copy in stage:
+            copy.wait()
+        for g in range(cols // 128):
+            lanes, lanes_v = pl.ds(g * 128, 128), pl.ds(cols + g * 128, 128)
+            keys, values = kv[:, lanes], kv[:, lanes_v]
+            keys_t = keys.T
+            grad_k, grad_v = 0.0, 0.0
+            for i in range(4):
+                done = []
+                for u in range(2):
+                    q, go = head_only(x[i, :, lanes], u), head_only(grads[i, :, lanes], u)
+                    scores = nt(keys, q) * scale
+                    probs, grad_scores = softmax_back(
+                        [scores], [nt(values, go)],
+                        logs[pl.ds(2 * g + u, 1), pl.ds(i * size, size)])
+                    grad_v = grad_v + nn(probs[0], go)
+                    grad_k = grad_k + nn(grad_scores[0], q)
+                    done.append(nn(keys_t[u * HEAD_DIM : (u + 1) * HEAD_DIM, :], grad_scores[0]))
+                out[i, :, lanes] = (jnp.concatenate(done, axis=0).T * scale).astype(BF16)
+            out_kv[:, lanes] = (grad_k * scale).astype(BF16)
+            out_kv[:, lanes_v] = grad_v.astype(BF16)
+        copies = [pltpu.make_async_copy(out, out_refs[0], sem.at[4]),
+                  pltpu.make_async_copy(out_kv, out_refs[1], sem.at[5])]
+        for copy in copies:
+            copy.start()
+        for copy in copies:
+            copy.wait()
+
+    return launch(f"cross_back_{number}", number, main, [query, pairs, grad_joined, logsum], outs,
+                  scratch, [], rides)
 
 
 def flat(parts):
@@ -554,7 +820,6 @@
     blocks = width // part
     cols = w_self.shape[3]
     hidden = w_up.shape[2]
-    heads = cols // HEAD_DIM
     me = lax.axis_index("zh")
     for place, name in enumerate(reversed(bits)):
         me = me + (lax.axis_index(name) << (place + 1))
@@ -575,14 +840,15 @@
 
     def halves(name):
         n = sizes[name]
-        if name == "self":
-            return [(0, 2 * cols, low_first), (2 * cols, cols, up)]
-        if name in ("up", "down"):
-            return [(0, n // 2, low_first), (n // 2, n // 2, up)]
-        return [(0, n, low_first if name == "kv" else up)]
-
-    packs = {"a": ["self", "self_out"], "b": ["q", "kv", "out"], "c": ["up"], "d": ["down"]}
-    shards = {}
+        if name in ("self", "up", "down"):
+            first = (n // 2 + 127) // 128 * 128
+            return [(0, first, low_first), (first, n - first, up)]
+        return [(0, n, low_first if name in ("kv", "norm") else up)]
+
+    packs = {"a": ["self"], "o": ["self_out"], "b": ["q", "kv", "out"], "c": ["up"], "d": ["down"]}
+    norm_rows = jnp.concatenate([ln_gain.reshape(-1, part), ln_bias.reshape(-1, part)], axis=0).T
+    norm_rows = jnp.pad(norm_rows, ((0, 0), (0, sizes["norm"] - norm_rows.shape[1])))
+    shards = {(0, "norm"): norm_rows}
     for l in range(layers):
         shards[l, "self"] = w_self[l].reshape(part, 3 * cols)
         shards[l, "self_out"] = w_self_out[l].T
@@ -606,8 +872,8 @@
                 if stage == 1:
                     rides.append(pair_ride(shards[key], blocks))
                 else:
-                    rides.append(spread_ride(
-                        held[key], halves(name), early if stage == 2 else late, blocks))
+                    which = {2: early, 3: late, 4: early + late}[stage]
+                    rides.append(spread_ride(held[key], halves(name), which, blocks))
                 keys.append(key)
         return rides, keys
 
@@ -616,98 +882,76 @@
             held[key] = value[0]
 
     forward = {
-        0: [(0, "b", 2), (0, "c", 1)],
-        1: [(0, "b", 3), (0, "c", 2)],
-        2: [(0, "c", 3), (0, "d", 1)],
-        3: [(0, "d", 2), (1, "a", 1)],
-        4: [(0, "d", 3), (1, "a", 2)],
-        5: [(1, "a", 3), (1, "b", 1)],
-        6: [(1, "b", 2), (1, "c", 1)],
-        7: [(1, "b", 3), (1, "c", 2)],
-        8: [(1, "c", 3), (1, "d", 1)],
-        9: [(1, "d", 2)],
-        10: [(1, "d", 3)],
+        0: [(0, "o", 4), (0, "b", 1)],
+        1: [(0, "b", 2)],
+        2: [(0, "b", 3), (0, "c", 1)],
+        3: [(0, "c", 2), (0, "d", 1)],
+        5: [(0, "c", 3), (0, "d", 2), (1, "a", 1)],
+        6: [(0, "d", 3), (1, "a", 2), (1, "o", 1)],
+        7: [(1, "a", 3), (1, "o", 2), (1, "b", 1)],
+        8: [(1, "o", 3), (1, "b", 2), (1, "c", 1)],
+        9: [(1, "b", 3)],
+        10: [(1, "c", 2), (1, "d", 1)],
+        11: [(1, "c", 3)],
+        13: [(1, "d", 2)],
+        14: [(1, "d", 3)],
     }
     step = [0]
 
-    def next_rides(more=()):
+    def next_rides():
         todo = [t for t in forward.get(step[0], []) if t[0] < layers]
         step[0] += 1
-        rides, keys = weight_rides(todo)
-        return rides, keys
-
-    def simple_launch(rides):
+        return weight_rides(todo)
+
+    def move(rides):
         return launch(f"move_{counter[0]}", number(), None, [], [], [], [], rides)[1]
 
-    rides, keys = weight_rides([(0, "a", 1)])
-    rides.append(send_ride(frames_in[0], "swap"))
-    second, keys_b = weight_rides([(0, "b", 1)])
-    extra = simple_launch(rides + second)
-    keep(keys, extra[: len(keys)])
-    keep(keys_b, extra[len(keys) + 1 :])
-    frames_own = jnp.where(diagonal(), frames_in[0], extra[len(keys)][0])
-    rides, keys = weight_rides([(0, "a", 2)])
-    extra = simple_launch(rides)
-    keep(keys, extra)
-    rides, keys = weight_rides([(0, "a", 3)])
-    extra = simple_launch(rides)
-    keep(keys, extra)
-
-    text_own = jnp.where(diagonal(), text_states[0], flip(text_states[0], "c"))
-    text_own = reorder(text_own).astype(BF16)
-    stream = reorder(frames_own)
-
-    norms = jnp.concatenate([ln_gain.reshape(-1, part), ln_bias.reshape(-1, part)], axis=0)
-    norms = lax.all_gather(norms, (*bits, "c"), axis=0)
-    norms = jnp.transpose(norms, (1, 0, 2)).reshape(norms.shape[1], width)
-    norms = reorder(norms)
+    extra = move([
+        chain_ride(shards[0, "self"], halves("self"), blocks),
+        chain_ride(shards[0, "norm"], halves("norm"), blocks),
+        send_ride(frames_in[0], "swap"),
+        send_ride(text_states[0], "c"),
+        pair_ride(shards[0, "self_out"], blocks),
+    ])
+    held[0, "self"], norms, frames_far, text_far, held[0, "self_out"] = [e[0] for e in extra]
+    stream = reorder(jnp.where(diagonal(), frames_in[0], frames_far))
+    text_own = reorder(jnp.where(diagonal(), text_states[0], text_far)).astype(BF16)
+    norms = norms.astype(F32).T
     gains = norms[: 3 * layers].reshape(layers, 3, 1, width)
-    shifts = norms[3 * layers :].reshape(layers, 3, 1, width)
-
-    def self_split(proj_rows):
-        split = proj_rows.reshape(proj_rows.shape[0], 3, heads, HEAD_DIM)
-        return split[:, 0], split[:, 1], split[:, 2]
-
-    def gathered(rows, norm, key, ending=None, slope=None, more=()):
+    shifts = norms[3 * layers : 6 * layers].reshape(layers, 3, 1, width)
+
+    def riding(call, more=()):
         rides, keys = next_rides()
-        outs, extra = gather_multiply(
-            number(), rows, norm, held[key], ending, slope, rides + list(more))
+        outs, extra = call(rides + list(more))
         keep(keys, extra)
         return outs, [e[0] for e in extra[len(keys):]]
-
-    def scattered(parts, key, base, more=()):
-        rides, keys = next_rides()
-        out, extra = multiply_scatter(number(), parts, held[key], base, rides + list(more))
-        keep(keys, extra)
-        return out, [e[0] for e in extra[len(keys):]]
 
     records = []
     for l in range(layers):
         saved = {"one": stream}
         more = [send_ride(cotangent[0], "swap")] if l == layers - 1 else []
-        (first, proj), extra = gathered(stream, (gains[l, 0], shifts[l, 0]), (l, "self"),
-                                        more=more)
+        (first, proj), extra = riding(lambda r: gather_multiply(
+            number(), stream, (gains[l, 0], shifts[l, 0]), held[l, "self"], None, None, r), more)
         if more:
             cot_own = jnp.where(diagonal(), cotangent[0], extra[0])
-        proj = to_time(proj)
-        query, keys_, values = self_split(proj)
-        joined, logsum = attend_rows(query, keys_, values, True, scale)
-        joined = from_time(joined)
-        stream, _ = scattered(joined, (l, "self_out"), stream)
+        (joined, logsum), _ = riding(lambda r: attend_self(number(), proj, scale, r))
+        (stream,), _ = riding(lambda r: multiply_scatter(
+            number(), joined, held[l, "self_out"], stream, None, [], r))
         saved.update(first=first, proj=proj, joined_self=joined, logsum_self=logsum, two=stream)
 
-        (normed, cross), _ = gathered(stream, (gains[l, 1], shifts[l, 1]), (l, "q"))
-        cross_query = flat(cross).reshape(-1, heads, HEAD_DIM)
-        pairs = nn(text_own, held[l, "kv"]).astype(BF16).reshape(-1, 2, heads, HEAD_DIM)
-        joined, logsum = attend_rows(cross_query, pairs[:, 0], pairs[:, 1], False, scale)
-        joined = joined.reshape(4, -1, cols)
-        stream, _ = scattered(joined, (l, "out"), stream)
-        saved.update(second=normed, cross_query=cross_query, pairs=pairs, joined_cross=joined,
+        (second, query), _ = riding(lambda r: gather_multiply(
+            number(), stream, (gains[l, 1], shifts[l, 1]), held[l, "q"], None, None, r))
+        pairs = nn(text_own, held[l, "kv"]).astype(BF16)
+        (joined, logsum), _ = riding(lambda r: attend_cross(number(), query, pairs, scale, r))
+        (stream,), _ = riding(lambda r: multiply_scatter(
+            number(), joined, held[l, "out"], stream, None, [], r))
+        saved.update(second=second, query=query, pairs=pairs, joined_cross=joined,
                      logsum_cross=logsum, three=stream)
 
-        (third, active, slope), _ = gathered(
-            stream, (gains[l, 2], shifts[l, 2]), (l, "up"), "gelu")
-        stream, _ = scattered(active, (l, "down"), stream)
+        (third, active, slope), _ = riding(lambda r: gather_multiply(
+            number(), stream, (gains[l, 2], shifts[l, 2]), held[l, "up"], "gelu", None, r))
+        (stream,), _ = riding(lambda r: multiply_scatter(
+            number(), active, held[l, "down"], stream, None, [], r))
         saved.update(third=third, active=active, slope=slope)
         records.append(saved)
     result_own = reorder(stream.astype(BF16)).astype(BF16)
@@ -716,7 +960,7 @@
     folding = []
     finished = {}
     grad_text = jnp.zeros((text_own.shape[0], width), F32)
-    norm_grads = [None] * layers
+    norm_grads = {}
 
     def fold_later(l, name, value):
         value = value.astype(BF16)
@@ -727,26 +971,29 @@
                             "order": list(reversed(order)), "level": 0})
 
     def fold_start(limit):
-        rides, items, spent = [], [], 0
-        for item in list(folding):
-            if spent >= limit:
-                break
+        rides, items, spent = [], [], {}
+        for item in folding:
             if item["level"] < len(item["order"]):
                 name, weight = item["order"][item["level"]]
                 away = sorted(k for k in item["table"] if k & weight)
+                bytes_ = sum(item["table"][k].size for k in away) * 2
+                if spent.get(name, 0) and spent[name] + bytes_ > limit:
+                    continue
                 value = jnp.concatenate([item["table"][k] for k in away], axis=0)
                 rides.append(send_ride(value, name))
-                spent += value.size * 2
             else:
+                name = "pair"
                 near, far = item["table"][0], item["table"][1]
-                ride = Ride(
+                bytes_ = near.size * 4
+                if spent.get(name, 0) and spent[name] + bytes_ > limit // 2:
+                    continue
+                rides.append(Ride(
                     [near, far],
                     [jax.ShapeDtypeStruct(near.shape, BF16)] * 2,
                     lambda ins, outs: [[("swap", ins[0], outs[0]), ("back", ins[1], outs[1])]],
                     ["swap", "back"], 2,
-                )
-                rides.append(ride)
-                spent += near.size * 4
+                ))
+            spent[name] = spent.get(name, 0) + bytes_
             items.append(item)
         return rides, items
 
@@ -768,84 +1015,72 @@
                 finished[item["key"]] = near.astype(F32) + came[1].astype(F32)
                 folding.remove(item)
 
-    budget = 5 << 20
-
-    def back_gathered(rows, key, slope=None, more=()):
-        rides, items = fold_start(budget)
-        outs, extra = gather_multiply(
-            number(), rows, None, held[key], None, slope, rides + list(more))
+    def folds(call, more=(), limit=LINK_BYTES):
+        rides, items = fold_start(limit)
+        outs, extra = call(rides + list(more))
         fold_end(items, extra)
         return outs, [e[0] for e in extra[len(items):]]
 
-    def back_scattered(parts, key):
-        rides, items = fold_start(budget)
-        out, extra = multiply_scatter(number(), parts, held[key], None, rides)
-        fold_end(items, extra)
-        return out
-
+    text_parts = []
     for l in reversed(range(layers)):
         saved = records[l]
         more = [send_ride(result_own, "swap")] if l == layers - 1 else []
-        (full, grad_upper), extra = back_gathered(grad, (l, "down"), saved["slope"], more)
+        (full, grad_upper), extra = folds(lambda r: gather_multiply(
+            number(), grad, None, held[l, "down"], None, saved["slope"], r), more)
         if more:
             result = jnp.where(diagonal(), result_own, extra[0])
-        fold_later(l, "down", tn(flat(full), flat(saved["active"])))
-        grad_third = back_scattered(grad_upper, (l, "up"))
-        fold_later(l, "up", tn(flat(saved["third"]), flat(grad_upper)))
-        grad, gain_three, shift_three = normalise_back(
-            saved["three"], gains[l, 2], grad_third, grad)
-
-        (full, grad_joined), _ = back_gathered(grad, (l, "out"))
-        fold_later(l, "out", tn(flat(full), flat(saved["joined_cross"])))
-        pairs = saved["pairs"]
-        grad_query, grad_keys, grad_values = attend_rows_back(
-            saved["cross_query"], pairs[:, 0], pairs[:, 1], flat(grad_joined),
-            saved["logsum_cross"], False, scale)
-        grad_query = grad_query.reshape(4, -1, cols).astype(BF16)
-        grad_pairs = jnp.stack([grad_keys, grad_values], axis=1)
-        grad_pairs = grad_pairs.reshape(grad_pairs.shape[0], 2 * cols).astype(BF16)
-        grad_second = back_scattered(grad_query, (l, "q"))
-        fold_later(l, "q", tn(flat(saved["second"]), flat(grad_query)))
+        (grad, norm_grads[l, 2], down, up_), _ = folds(lambda r: multiply_scatter(
+            number(), grad_upper, held[l, "up"], None, (saved["three"], gains[l, 2], grad),
+            [(flat(full), flat(saved["active"])), (flat(saved["third"]), None)], r))
+        fold_later(l, "down", down)
+        fold_later(l, "up", up_)
+
+        (full, grad_joined), _ = folds(lambda r: gather_multiply(
+            number(), grad, None, held[l, "out"], None, None, r))
+        (grad_query, grad_pairs), _ = folds(lambda r: attend_cross_back(
+            number(), saved["query"], saved["pairs"], grad_joined, saved["logsum_cross"], scale,
+            r), limit=LINK_BYTES // 4)
+        grad_text = grad_text + nt(grad_pairs, held[l, "kv"])
         fold_later(l, "kv", tn(text_own, grad_pairs))
-        grad_text = grad_text + nt(grad_pairs, held[l, "kv"])
-        grad, gain_two, shift_two = normalise_back(saved["two"], gains[l, 1], grad_second, grad)
-
-        (full, grad_joined), _ = back_gathered(grad, (l, "self_out"))
-        fold_later(l, "self_out", tn(flat(full), flat(saved["joined_self"])))
-        query, keys_, values = self_split(saved["proj"])
-        grad_parts = attend_rows_back(
-            query, keys_, values, to_time(grad_joined), saved["logsum_self"], True, scale)
-        grad_proj = jnp.stack(grad_parts, axis=1).reshape(query.shape[0], 3 * cols).astype(BF16)
-        grad_proj = from_time(grad_proj)
-        grad_first = back_scattered(grad_proj, (l, "self"))
-        fold_later(l, "self", tn(flat(saved["first"]), flat(grad_proj)))
-        grad, gain_one, shift_one = normalise_back(saved["one"], gains[l, 0], grad_first, grad)
-        norm_grads[l] = [gain_one, gain_two, gain_three, shift_one, shift_two, shift_three]
-
-    small = jnp.stack([row for rows in norm_grads for row in rows], axis=1)
+        (grad, norm_grads[l, 1], out_, q_), _ = folds(lambda r: multiply_scatter(
+            number(), grad_query, held[l, "q"], None, (saved["two"], gains[l, 1], grad),
+            [(flat(full), flat(saved["joined_cross"])), (flat(saved["second"]), None)], r))
+        fold_later(l, "out", out_)
+        fold_later(l, "q", q_)
+
+        more = [send_ride(grad_text.astype(BF16), "c")] if l == 0 else []
+        (full, grad_joined), extra = folds(lambda r: gather_multiply(
+            number(), grad, None, held[l, "self_out"], None, None, r), more)
+        if more:
+            grad_text = grad_text.astype(BF16).astype(F32) + extra[0].astype(F32)
+        (grad_proj,), _ = folds(lambda r: attend_self_back(
+            number(), saved["proj"], grad_joined, saved["logsum_self"], scale, r))
+        more = [send_ride(grad_text.astype(BF16), "zl")] if l == 0 else []
+        (grad, norm_grads[l, 0], out_, self_), extra = folds(lambda r: multiply_scatter(
+            number(), grad_proj, held[l, "self"], None, (saved["one"], gains[l, 0], grad),
+            [(flat(full), flat(saved["joined_self"])), (flat(saved["first"]), None)], r), more)
+        if more:
+            grad_text = grad_text.astype(BF16).astype(F32) + extra[0].astype(F32)
+        fold_later(l, "self_out", out_)
+        fold_later(l, "self", self_)
+
+    small = [norm_grads[l, j][k] for l in range(layers) for k in range(2) for j in range(3)]
+    small = jnp.stack(small, axis=1)
     small = jnp.pad(small, ((0, 0), (0, sizes["norm"] - small.shape[1])))
     fold_later(0, "norm", small)
     frames_back = reorder(grad.astype(BF16)).astype(BF16)
-    text_back = grad_text.astype(BF16)
-    extras = [send_ride(frames_back, "swap"), send_ride(text_back, "c")]
-    round_ = 0
+    text_back = reorder(grad_text.astype(BF16)).astype(BF16)
+    extras = [send_ride(frames_back, "swap"), send_ride(text_back, "swap")]
     while folding:
         rides, items = fold_start(1 << 40)
-        extra = simple_launch(rides + extras)
+        extra = move(rides + extras)
         fold_end(items, extra)
-        tail = [e[0] for e in extra[len(items):]]
-        if round_ == 0:
-            grad_frames = jnp.where(diagonal(), frames_back, tail[0]).astype(F32)
-            text_sum = (text_back.astype(F32) + tail[1].astype(F32)).astype(BF16)
-            extras = [send_ride(text_sum, "zl")]
-        elif round_ == 1:
-            text_sum = reorder((text_sum.astype(F32) + tail[0].astype(F32)).astype(BF16))
-            text_sum = text_sum.astype(BF16)
-            extras = [send_ride(text_sum, "swap")]
-        elif round_ == 2:
-            text_sum = jnp.where(diagonal(), text_sum, tail[0]).astype(F32)
+        if extras:
+            grad_frames, text_sum = [
+                jnp.where(diagonal(), mine, came[0]).astype(F32)
+                for mine, came in zip((frames_back, text_back), extra[len(items):])
+            ]
             extras = []
-        round_ += 1
 
     small = finished[0, "norm", 0][:, : 6 * layers]
     for name in ("zl", "zh"):

time: 1610 us -> 1320 us (0.82)
  matrix products: 190 us -> 26.4 us
  local copies, waits for them, and re-layouts: 196 us -> 56.6 us
  Pallas kernels: 1050 us -> 1130 us
  other arithmetic: 145 us -> 92.5 us
    dot_general x48 -> x0, matrix products: 109 us -> none  [the longest x8 40 us: attend_rows_back(): grad_probs = jnp.einsum('qhd,khd->hqk', g, v, preferred_element_type=F32)]
    pallas_call x30 -> x36, Pallas kernels: 1050 us -> 1130 us  [launch(): pl.pallas_call(kernel, out_shape=tuple(out_shapes), in_specs=[ANY] * len(...]
    unnamed x751 -> x317, local copies, waits for them, and re-layouts: 84.7 us -> 16.4 us
    dot_general x14 -> x2, matrix products: 59.8 us -> 2.65 us  [tn(): lax.dot_general(a, b, (((0,), (0,)), ((), ())), preferred_element_type=F32)]
    another operation x30 -> x8, local copies, waits for them, and re-layouts: 30.1 us -> 0.46 us  [body(): small = jnp.stack(small, axis=1)]
    reduce_sum x25 -> x0, other arithmetic: 24.7 us -> none  [the longest x6 12.9 us: normalise_back(): grad_gain = jnp.sum(grad_normed * unit, axis=0)]
    slice x23 -> x1, local copies, waits for them, and re-layouts: 24.7 us -> 0.26 us  [body(): shifts = norms[3 * layers:6 * layers].reshape(layers, 3, 1, width)]
    concatenate x34 -> x33, other arithmetic: 4.71 us -> 28.3 us  [fold_start(): value = jnp.concatenate([item['table'][k] for k in away], axis=0)]
  transfers between devices with their start and end apart: 3 -> 2, of which waited for: 1 -> 1; matrix products, arithmetic and copies ran while one was open for 4% -> 1% of each run, Pallas kernels for 14% -> 0%
where the time goes in v3:
time: 1320 us; the launch traced here: 1310 us
  Pallas kernels  1130 us (86%)
  other arithmetic  92.5 us (7%)
  local copies, waits for them, and re-layouts  56.6 us (4%)
  matrix products  26.4 us (2%)
    pallas_call x36, Pallas kernels, launch(): pl.pallas_call(kernel, out_shape=tuple(out_shapes), in_specs=[ANY] * len(...  1130 us
    convert_element_type x34, other arithmetic, fold_end(): item['table'] = {k: (item['table'][k].astype(F32) + came[0][i * part:(i +...  40.6 us
    concatenate x33, other arithmetic, fold_start(): value = jnp.concatenate([item['table'][k] for k in away], axis=0)  28.3 us
  transfers between devices with their start and end apart: 2, of which 1 were waited for; matrix products, arithmetic and copies ran while one was open for 1% of the time, Pallas kernels for 0%

profile of v3, /device:TPU:0, one launch (start us, length us, event | category | flops | bytes accessed | tf_op | source)
XLA Modules:
  0.0 1311.7 jit_solution(15441343578761886999)
XLA Ops:
  14.9 45.1 %move_0.1 = (bf16[1536,1152]{1,0:T(8,128)(2,1)}, bf16[1536,128]{1,0:T(8,128)(2,1)}, bf16[256,1536]{1,0:T(8,128)(2,1)}, bf16[64,1536]{1,0:T(8,128)(2,1)}, bf16[1536,384]{1,0:T(8,128)(2,1)}) custom-call(bf16[192,1152]{1,0:T(8,128)(2,1)} %bitcast.224, bf16[192,128]{1,0:T(8,128)(2,1)} %pad.9.refs_1_, bf16[256,1536]{1,0:T(8,128)(2,1)} %bitcast.234, ...), custom_call_target="tpu_custom_call" | custom-call | tf_op jit(solution)/shard_map/move_0/pallas_call | solution.py:221
  72.0 83.2 %gather_1.1 = (bf16[4,256,1536]{2,1,0:T(8,128)(2,1)}, bf16[4,256,1152]{2,1,0:T(8,128)(2,1)}, bf16[1536,384]{1,0:T(8,128)(2,1)}, bf16[1536,384]{1,0:T(8,128)(2,1)...) custom-call(f32[256,1536]{1,0:T(8,128)} %fusion.6.refs_0_.refs_2_, ...), custom_call_target="tpu_custom_call", output_to_operand_aliasing={{2}: (3, {})} | custom-call | tf_op jit(solution)/shard_map/gather_1/pallas_call | solution.py:221
  155.3 15.1 %attend_2.1 = (bf16[4,256,384]{2,1,0:T(8,128)(2,1)}, f32[6,1024]{1,0:T(8,128)}, bf16[1536,384]{1,0:T(8,128)(2,1)}, bf16[1536,768]{1,0:T(8,128)(2,1)}, bf16[1536,384]{1,0:T(8,128)(2,1)}) custom-call(bf16[4,256,1152]{2,1,0:T(8,128)(2,1)} %get-tuple-element.217.refs_0_, ...), custom_call_target="tpu_custom_call", output_to_operand_aliasing={{2}: (1, {}), {3}: (2, {}), {4}: (3, {})} | custom-call | tf_op jit(solution)/shard_map/attend_2/pallas_call | solution.py:221
  170.4 38.5 %scatter_3.1 = (f32[256,1536]{1,0:T(8,128)}, bf16[1536,384]{1,0:T(8,128)(2,1)}, bf16[1536,768]{1,0:T(8,128)(2,1)}, bf16[1536,384]{1,0:T(8,128)(2,1)}, bf16[1536,1536]{1,0:T(8,128)(2,1)}) custom-call(bf16[1024,384]{1,0:T(8,128)(2,1)} %bitcast.216, ...), custom_call_target="tpu_custom_call", output_to_operand_aliasing={{1}: (3, {}), {2}: (4, {}), {3}: (5, {})} | custom-call | tf_op jit(solution)/shard_map/scatter_3/pallas_call | solution.py:221
  211.7 35.6 %gather_4.1 = (bf16[4,256,1536]{2,1,0:T(8,128)(2,1)}, bf16[4,256,384]{2,1,0:T(8,128)(2,1)}, bf16[1536,1536]{1,0:T(8,128)(2,1)}, bf16[1536,1536]{1,0:T(8,128)(2,1)}) custom-call(f32[256,1536]{1,0:T(8,128)} %get-tuple-element.226.refs_0_.refs_2_, bf16[1536,384]{1,0:T(8,128)(2,1)} %get-tuple-element.227.refs_1_, ...), custom_call_target="tpu_custom_call", output_to_operand_aliasing={{2}: (3, {})} | custom-call | tf_op jit(solution)/shard_map/gather_4/pallas_call | solution.py:221
  254.8 41.5 %scatter_6.1 = (f32[256,1536]{1,0:T(8,128)}, bf16[1536,1536]{1,0:T(8,128)(2,1)}, bf16[1536,1536]{1,0:T(8,128)(2,1)}, bf16[1536,1152]{1,0:T(8,128)(2,1)}) custom-call(bf16[1024,384]{1,0:T(8,128)(2,1)} %bitcast.198, bf16[1536,384]{1,0:T(8,128)(2,1)} %get-tuple-element.233.refs_1_, ...), custom_call_target="tpu_custom_call", output_to_operand_aliasing={{1}: (3, {}), {2}: (4, {})} | custom-call | tf_op jit(solution)/shard_map/scatter_6/pallas_call | solution.py:221
  296.4 40.7 %gather_7.1 = (bf16[4,256,1536]{2,1,0:T(8,128)(2,1)}, bf16[4,256,1536]{2,1,0:T(8,128)(2,1)}, bf16[4,256,1536]{2,1,0:T(8,128)(2,1)}, bf16[1536,1536]{1,0:T(8,128)...) custom-call(f32[256,1536]{1,0:T(8,128)} %get-tuple-element.236.refs_0_, ...), custom_call_target="tpu_custom_call", output_to_operand_aliasing={{3}: (3, {}), {4}: (4, {})} | custom-call | tf_op jit(solution)/shard_map/gather_7/pallas_call | solution.py:221
  337.1 39.0 %scatter_8.1 = (f32[256,1536]{1,0:T(8,128)}, bf16[1536,1152]{1,0:T(8,128)(2,1)}, bf16[1536,384]{1,0:T(8,128)(2,1)}, bf16[1536,384]{1,0:T(8,128)(2,1)}, bf16[1536...) custom-call(bf16[1024,1536]{1,0:T(8,128)(2,1)} %bitcast.194, ...), custom_call_target="tpu_custom_call", output_to_operand_aliasing={{1}: (3, {}), {2}: (4, {})} | custom-call | tf_op jit(solution)/shard_map/scatter_8/pallas_call | solution.py:221
  376.1 43.5 %gather_9.1 = (bf16[4,256,1536]{2,1,0:T(8,128)(2,1)}, bf16[4,256,1152]{2,1,0:T(8,128)(2,1)}, bf16[1536,384]{1,0:T(8,128)(2,1)}, bf16[1536,384]{1,0:T(8,128)(2,1)...) custom-call(f32[256,1536]{1,0:T(8,128)} %get-tuple-element.244.refs_, ...), custom_call_target="tpu_custom_call", output_to_operand_aliasing={{2}: (3, {}), {3}: (4, {}), {4}: (5, {}), {5}: (6, {})} | custom-call | tf_op jit(solution)/shard_map/gather_9/pallas_call | solution.py:221
  419.6 27.7 %attend_10.1 = (bf16[4,256,384]{2,1,0:T(8,128)(2,1)}, f32[6,1024]{1,0:T(8,128)}, bf16[1536,384]{1,0:T(8,128)(2,1)}, bf16[1536,768]{1,0:T(8,128)(2,1)}, bf16[1536,384]{1,0:T(8,128)(2,1)}) custom-call(bf16[4,256,1152]{2,1,0:T(8,128)(2,1)} %get-tuple-element.250.refs_0_, ...), custom_call_target="tpu_custom_call", output_to_operand_aliasing={{2}: (1, {}), {3}: (2, {}), {4}: (3, {})} | custom-call | tf_op jit(solution)/shard_map/attend_10/pallas_call | solution.py:221
  453.5 37.5 %scatter_11.1 = (f32[256,1536]{1,0:T(8,128)}, bf16[1536,1536]{1,0:T(8,128)(2,1)}, bf16[1536,1536]{1,0:T(8,128)(2,1)}) custom-call(bf16[1024,384]{1,0:T(8,128)(2,1)} %bitcast.218, bf16[1536,384]{1,0:T(8,128)(2,1)} %get-tuple-element.255.refs_1_, f32[256,1536]{1,0:T(8,128)} %get-tuple-element.244.refs_0_.refs_2_, ...), custom_call_target="tpu_custom_call", output_to_operand_aliasing={{1}: (3, {})} | custom-call | tf_op jit(solution)/shard_map/scatter_11/pallas_call | solution.py:221
  491.0 28.4 %gather_12.1 = (bf16[4,256,1536]{2,1,0:T(8,128)(2,1)}, bf16[4,256,384]{2,1,0:T(8,128)(2,1)}, bf16[1536,1536]{1,0:T(8,128)(2,1)}) custom-call(f32[256,1536]{1,0:T(8,128)} %get-tuple-element.257.refs_0_.refs_2_, bf16[1536,384]{1,0:T(8,128)(2,1)} %get-tuple-element.258.refs_1_, f32[2,1536]{1,0:T(2,128)} %get-tuple-element.614.refs_2_, ...), custom_call_target="tpu_custom_call", output_to_operand_aliasing={{2}: (3, {})} | custom-call | tf_op jit(solution)/shard_map/gather_12/pallas_call | solution.py:221
  526.2 23.7 %scatter_14.1 = (f32[256,1536]{1,0:T(8,128)}, bf16[1536,1536]{1,0:T(8,128)(2,1)}) custom-call(bf16[1024,384]{1,0:T(8,128)(2,1)} %bitcast.203, bf16[1536,384]{1,0:T(8,128)(2,1)} %get-tuple-element.263.refs_1_, f32[256,1536]{1,0:T(8,128)} %get-tuple-element.257.refs_0_.refs_2_, ...), custom_call_target="tpu_custom_call", output_to_operand_aliasing={{1}: (3, {})} | custom-call | tf_op jit(solution)/shard_map/scatter_14/pallas_call | solution.py:221
  549.9 28.7 %gather_15.1 = (bf16[4,256,1536]{2,1,0:T(8,128)(2,1)}, bf16[4,256,1536]{2,1,0:T(8,128)(2,1)}, bf16[4,256,1536]{2,1,0:T(8,128)(2,1)}, bf16[1536,1536]{1,0:T(8,128)(2,1)}) custom-call(f32[256,1536]{1,0:T(8,128)} %get-tuple-element.265.refs_0_.refs_2_, bf16[1536,1536]{1,0:T(8,128)(2,1)} %get-tuple-element.266.refs_1_, ...), custom_call_target="tpu_custom_call", output_to_operand_aliasing={{3}: (3, {})} | custom-call | tf_op jit(solution)/shard_map/gather_15/pallas_call | solution.py:221
  578.6 26.5 %scatter_16.1 = f32[256,1536]{1,0:T(8,128)} custom-call(bf16[1024,1536]{1,0:T(8,128)(2,1)} %bitcast.196, bf16[1536,1536]{1,0:T(8,128)(2,1)} %get-tuple-element.269.refs_1_, f32[256,1536]{1,0:T(8,128)} %get-tuple-element.265.refs_0_.refs_2_), custom_call_target="tpu_custom_call" | custom-call | tf_op jit(solution)/shard_map/scatter_16/pallas_call | solution.py:221
  608.9 34.4 %gather_17.1 = (bf16[4,256,1536]{2,1,0:T(8,128)(2,1)}, bf16[4,256,1536]{2,1,0:T(8,128)(2,1)}, bf16[256,1536]{1,0:T(8,128)(2,1)}) custom-call(f32[256,1536]{1,0:T(8,128)} %fusion.3.refs_0_.refs_4_, bf16[1536,1536]{1,0:T(8,128)(2,1)} %get-tuple-element.269.refs_1_, bf16[4,256,1536]{2,1,0:T(8,128)(2,1)} %get-tuple-element.271.refs_2_, ...), custom_call_target="tpu_custom_call" | custom-call | tf_op jit(solution)/shard_map/gather_17/pallas_call | solution.py:221
  643.4 31.3 %scatter_18.1 = (f32[256,1536]{1,0:T(8,128)}, f32[2,1536]{1,0:T(2,128)}, bf16[1536,1536]{1,0:T(8,128)(2,1)}, bf16[1536,1536]{1,0:T(8,128)(2,1)}) custom-call(bf16[1024,1536]{1,0:T(8,128)(2,1)} %bitcast.215, bf16[1536,1536]{1,0:T(8,128)(2,1)} %get-tuple-element.266.refs_1_, f32[256,1536]{1,0:T(8,128)} %get-tuple-element.265.refs_0_.refs_2_, ...), custom_call_target="tpu_custom_call" | custom-call | tf_op jit(solution)/shard_map/scatter_18/pallas_call | solution.py:221
  680.8 28.5 %gather_19.1 = (bf16[4,256,1536]{2,1,0:T(8,128)(2,1)}, bf16[4,256,384]{2,1,0:T(8,128)(2,1)}, bf16[768,768]{1,0:T(8,128)(2,1)}, bf16[768,768]{1,0:T(8,128)(2,1)}) custom-call(f32[256,1536]{1,0:T(8,128)} %get-tuple-element.276.refs_0_.refs_4_, bf16[1536,384]{1,0:T(8,128)(2,1)} %get-tuple-element.263.refs_1_, bf16[768,768]{1,0:T(8,128)(2,1)} %slice.1096.refs_2_, ...), custom_call_target="tpu_custom_call" | custom-call | tf_op jit(solution)/shard_map/gather_19/pallas_call | solution.py:221
  735.0 30.4 %scatter_21.1 = (f32[256,1536]{1,0:T(8,128)}, f32[2,1536]{1,0:T(2,128)}, bf16[1536,384]{1,0:T(8,128)(2,1)}, bf16[1536,384]{1,0:T(8,128)(2,1)}, bf16[192,768]{1,0...) custom-call(bf16[1024,384]{1,0:T(8,128)(2,1)} %bitcast.231, ...), custom_call_target="tpu_custom_call" | custom-call | tf_op jit(solution)/shard_map/scatter_21/pallas_call | solution.py:221
  773.1 29.8 %gather_22.1 = (bf16[4,256,1536]{2,1,0:T(8,128)(2,1)}, bf16[4,256,384]{2,1,0:T(8,128)(2,1)}, bf16[192,768]{1,0:T(8,128)(2,1)}, bf16[192,768]{1,0:T(8,128)(2,1)},...) custom-call(f32[256,1536]{1,0:T(8,128)} %get-tuple-element.287.refs_0_.refs_4_, ...), custom_call_target="tpu_custom_call" | custom-call | tf_op jit(solution)/shard_map/gather_22/pallas_call | solution.py:221
  805.9 28.9 %attend_back_23.1 = (bf16[4,256,1152]{2,1,0:T(8,128)(2,1)}, bf16[192,768]{1,0:T(8,128)(2,1)}, bf16[192,768]{1,0:T(8,128)(2,1)}, bf16[768,768]{1,0:T(8,128)(2,1)}, bf16[768,384]{1,0:T(8,128)(2,1)}) custom-call(bf16[4,256,1152]{2,1,0:T(8,128)(2,1)} %get-tuple-element.250.refs_0_, bf16[4,256,384]{2,1,0:T(8,128)(2,1)} %get-tuple-element.292.refs_1_, ...), custom_call_target="tpu_custom_call" | custom-call | tf_op jit(solution)/shard_map/attend_back_23/pallas_call | solution.py:221
  838.8 32.1 %scatter_24.1 = (f32[256,1536]{1,0:T(8,128)}, f32[2,1536]{1,0:T(2,128)}, bf16[1536,384]{1,0:T(8,128)(2,1)}, bf16[1536,1152]{1,0:T(8,128)(2,1)}, bf16[192,768]{1,...) custom-call(bf16[1024,1152]{1,0:T(8,128)(2,1)} %bitcast.223, ...), custom_call_target="tpu_custom_call" | custom-call | tf_op jit(solution)/shard_map/scatter_24/pallas_call | solution.py:221
  880.2 32.6 %gather_25.1 = (bf16[4,256,1536]{2,1,0:T(8,128)(2,1)}, bf16[4,256,1536]{2,1,0:T(8,128)(2,1)}, bf16[192,768]{1,0:T(8,128)(2,1)}, bf16[192,768]{1,0:T(8,128)(2,1)}...) custom-call(f32[256,1536]{1,0:T(8,128)} %get-tuple-element.304.refs_0_.refs_4_, ...), custom_call_target="tpu_custom_call" | custom-call | tf_op jit(solution)/shard_map/gather_25/pallas_call | solution.py:221
  917.7 33.6 %scatter_26.1 = (f32[256,1536]{1,0:T(8,128)}, f32[2,1536]{1,0:T(2,128)}, bf16[1536,1536]{1,0:T(8,128)(2,1)}, bf16[1536,1536]{1,0:T(8,128)(2,1)}, bf16[192,384]{1...) custom-call(bf16[1024,1536]{1,0:T(8,128)(2,1)} %bitcast.202, ...), custom_call_target="tpu_custom_call" | custom-call | tf_op jit(solution)/shard_map/scatter_26/pallas_call | solution.py:221
  962.5 30.1 %gather_27.1 = (bf16[4,256,1536]{2,1,0:T(8,128)(2,1)}, bf16[4,256,384]{2,1,0:T(8,128)(2,1)}, bf16[192,384]{1,0:T(8,128)(2,1)}, bf16[192,384]{1,0:T(8,128)(2,1)},...) custom-call(f32[256,1536]{1,0:T(8,128)} %get-tuple-element.317.refs_0, ...), custom_call_target="tpu_custom_call" | custom-call | tf_op jit(solution)/shard_map/gather_27/pallas_call | solution.py:221
  996.2 16.1 %cross_back_28.1 = (bf16[4,256,384]{2,1,0:T(8,128)(2,1)}, bf16[64,768]{1,0:T(8,128)(2,1)}, bf16[192,640]{1,0:T(8,128)(2,1)}, bf16[192,640]{1,0:T(8,128)(2,1)}, b...) custom-call(bf16[4,256,384]{2,1,0:T(8,128)(2,1)} %get-tuple-element.229.refs_0_, ...), custom_call_target="tpu_custom_call" | custom-call | tf_op jit(solution)/shard_map/cross_back_28/pallas_call | solution.py:221
  1020.4 30.5 %scatter_29.1 = (f32[256,1536]{1,0:T(8,128)}, f32[2,1536]{1,0:T(2,128)}, bf16[1536,384]{1,0:T(8,128)(2,1)}, bf16[1536,384]{1,0:T(8,128)(2,1)}, bf16[192,768]{1,0...) custom-call(bf16[1024,384]{1,0:T(8,128)(2,1)} %bitcast.230, ...), custom_call_target="tpu_custom_call" | custom-call | tf_op jit(solution)/shard_map/scatter_29/pallas_call | solution.py:221
  1057.6 30.1 %gather_30.1 = (bf16[4,256,1536]{2,1,0:T(8,128)(2,1)}, bf16[4,256,384]{2,1,0:T(8,128)(2,1)}, bf16[192,768]{1,0:T(8,128)(2,1)}, bf16[192,768]{1,0:T(8,128)(2,1)},...) custom-call(f32[256,1536]{1,0:T(8,128)} %get-tuple-element.331.refs_0, ...), custom_call_target="tpu_custom_call" | custom-call | tf_op jit(solution)/shard_map/gather_30/pallas_call | solution.py:221
  1093.1 29.0 %attend_back_31.1 = (bf16[4,256,1152]{2,1,0:T(8,128)(2,1)}, bf16[192,768]{1,0:T(8,128)(2,1)}, bf16[192,768]{1,0:T(8,128)(2,1)}, bf16[768,768]{1,0:T(8,128)(2,1)}, bf16[768,384]{1,0:T(8,128)(2,1)}) custom-call(bf16[4,256,1152]{2,1,0:T(8,128)(2,1)} %get-tuple-element.217.refs_0_, bf16[4,256,384]{2,1,0:T(8,128)(2,1)} %get-tuple-element.337.refs_1_, ...), custom_call_target="tpu_custom_call" | custom-call | tf_op jit(solution)/shard_map/attend_back_31/pallas_call | solution.py:221
  1126.0 32.9 %scatter_32.1 = (f32[256,1536]{1,0:T(8,128)}, f32[2,1536]{1,0:T(2,128)}, bf16[1536,384]{1,0:T(8,128)(2,1)}, bf16[1536,1152]{1,0:T(8,128)(2,1)}, bf16[192,768]{1,...) custom-call(bf16[1024,1152]{1,0:T(8,128)(2,1)} %bitcast.222, ...), custom_call_target="tpu_custom_call" | custom-call | tf_op jit(solution)/shard_map/scatter_32/pallas_call | solution.py:221
  1173.0 40.9 %move_33.1 = (bf16[192,768]{1,0:T(8,128)(2,1)}, bf16[192,768]{1,0:T(8,128)(2,1)}, bf16[192,384]{1,0:T(8,128)(2,1)}, bf16[192,384]{1,0:T(8,128)(2,1)}, bf16[192,3...) custom-call(bf16[192,768]{1,0:T(8,128)(2,1)} %get-tuple-element.511., ...), custom_call_target="tpu_custom_call" | custom-call | tf_op jit(solution)/shard_map/move_33/pallas_call | solution.py:221
  1236.0 41.1 %move_35.1 = (bf16[192,384]{1,0:T(8,128)(2,1)}, bf16[192,384]{1,0:T(8,128)(2,1)}, bf16[192,640]{1,0:T(8,128)(2,1)}, bf16[192,640]{1,0:T(8,128)(2,1)}, bf16[192,5...) custom-call(bf16[192,384]{1,0:T(8,128)(2,1)} %get-tuple-element.523.refs_0_, ...), custom_call_target="tpu_custom_call" | custom-call | tf_op jit(solution)/shard_map/move_35/pallas_call | solution.py:221
  (515 shorter events, 221.6 us)
Async XLA Ops:
  0.6 7.0 copy-start.72
  5.8 3.7 copy-start.59
  60.0 4.4 copy-start.62
  60.0 4.4 copy-start.123
  71.0 84.3 %copy-start.139 = (f32[1,1536]{1,0:T(1,128)}, f32[1,1536]{1,0:T(1,128)S(1)}, u32[]{:S(2)}) copy-start(f32[1,1536]{1,0:T(1,128)S(1)} %get-tuple-element.582.refs_3_) | copy-start | bytes 18436
  71.0 84.3 %copy-start.142 = (f32[1,1536]{1,0:T(1,128)}, f32[1,1536]{1,0:T(1,128)S(1)}, u32[]{:S(2)}) copy-start(f32[1,1536]{1,0:T(1,128)S(1)} %get-tuple-element.583.refs_3_) | copy-start | bytes 18436
  71.0 183.2 %copy-start.140 = (f32[1,1536]{1,0:T(1,128)}, f32[1,1536]{1,0:T(1,128)S(1)}, u32[]{:S(2)}) copy-start(f32[1,1536]{1,0:T(1,128)S(1)} %get-tuple-element.581.refs_3_) | copy-start | bytes 18436
  71.0 183.2 %copy-start.143 = (f32[1,1536]{1,0:T(1,128)}, f32[1,1536]{1,0:T(1,128)S(1)}, u32[]{:S(2)}) copy-start(f32[1,1536]{1,0:T(1,128)S(1)} %get-tuple-element.580.refs_3_) | copy-start | bytes 18436
  71.0 381.8 %copy-start.141 = (f32[1,1536]{1,0:T(1,128)}, f32[1,1536]{1,0:T(1,128)S(1)}, u32[]{:S(2)}) copy-start(f32[1,1536]{1,0:T(1,128)S(1)} %get-tuple-element.579.refs_3_) | copy-start | bytes 18436
  71.0 381.8 %copy-start.144 = (f32[1,1536]{1,0:T(1,128)}, f32[1,1536]{1,0:T(1,128)S(1)}, u32[]{:S(2)}) copy-start(f32[1,1536]{1,0:T(1,128)S(1)} %get-tuple-element.578.refs_3_) | copy-start | bytes 18436
  674.7 3.8 copy-start.3
  712.9 14.8 %copy-start = (bf16[1536,768]{1,0:T(8,128)(2,1)S(1)}, bf16[1536,768]{1,0:T(8,128)(2,1)}, u32[]{:S(2)}) copy-start(bf16[1536,768]{1,0:T(8,128)(2,1)} %get-tuple-element.261) | copy-start | bytes 7077892
  805.9 30.2 %copy-start.49 = (bf16[1536,384]{1,0:T(8,128)(2,1)S(1)}, bf16[1536,384]{1,0:T(8,128)(2,1)}, u32[]{:S(2)}) copy-start(bf16[1536,384]{1,0:T(8,128)(2,1)} %get-tuple-element.291) | copy-start | bytes 3538948
  805.9 30.2 %copy-start.76 = (bf16[768,384]{1,0:T(8,128)(2,1)S(1)}, bf16[768,384]{1,0:T(8,128)(2,1)}, u32[]{:S(2)}) copy-start(bf16[768,384]{1,0:T(8,128)(2,1)} %get-tuple-element.302) | copy-start | bytes 1769476
  872.2 4.2 copy-start.111
  880.2 33.9 %copy-start.6 = (bf16[1536,1152]{1,0:T(8,128)(2,1)S(1)}, bf16[1536,1152]{1,0:T(8,128)(2,1)}, u32[]{:S(2)}) copy-start(bf16[1536,1152]{1,0:T(8,128)(2,1)} %get-tuple-element.308) | copy-start | bytes 10616836
  951.3 3.8 copy-start.2
  1057.6 30.2 %copy-start.28 = (bf16[64,1536]{1,0:T(8,128)(2,1)S(1)}, bf16[64,1536]{1,0:T(8,128)(2,1)}, u32[]{:S(2)}) copy-start(bf16[64,1536]{1,0:T(8,128)(2,1)} %fusion.1.refs_7_) | copy-start | bytes 589828
  1093.0 29.0 %copy-start.48 = (bf16[1536,384]{1,0:T(8,128)(2,1)S(1)}, bf16[1536,384]{1,0:T(8,128)(2,1)}, u32[]{:S(2)}) copy-start(bf16[1536,384]{1,0:T(8,128)(2,1)} %get-tuple-element.340) | copy-start | bytes 3538948
  1093.0 30.2 %copy-start.46 = (bf16[1536,384]{1,0:T(8,128)(2,1)S(1)}, bf16[1536,384]{1,0:T(8,128)(2,1)}, u32[]{:S(2)}) copy-start(bf16[1536,384]{1,0:T(8,128)(2,1)} %get-tuple-element.335) | copy-start | bytes 3538948
  1093.0 30.2 %copy-start.73 = (bf16[768,384]{1,0:T(8,128)(2,1)S(1)}, bf16[768,384]{1,0:T(8,128)(2,1)}, u32[]{:S(2)}) copy-start(bf16[768,384]{1,0:T(8,128)(2,1)} %get-tuple-element.346) | copy-start | bytes 1769476
  1158.9 3.6 copy-start.147
  1159.0 3.7 copy-start.148
  1159.0 3.7 copy-start.149
  1159.0 3.7 copy-start.24
  1159.0 3.7 copy-start.120
  1173.0 42.9 %copy-start.5 = (bf16[1536,1152]{1,0:T(8,128)(2,1)S(1)}, bf16[1536,1152]{1,0:T(8,128)(2,1)}, u32[]{:S(2)}) copy-start(bf16[1536,1152]{1,0:T(8,128)(2,1)} %get-tuple-element.354) | copy-start | bytes 10616836
  1218.5 12.9 copy-start.65
  1234.5 44.3 %copy-start.7 = (bf16[256,1536]{1,0:T(8,128)(2,1)S(1)}, bf16[256,1536]{1,0:T(8,128)(2,1)}, u32[]{:S(2)}) copy-start(bf16[256,1536]{1,0:T(8,128)(2,1)} %convolution_convert_fusion.3.refs_3_) | copy-start | bytes 2359300
  1234.5 44.3 %copy-start.61 = (bf16[256,1536]{1,0:T(8,128)(2,1)S(1)}, bf16[256,1536]{1,0:T(8,128)(2,1)}, u32[]{:S(2)}) copy-start(bf16[256,1536]{1,0:T(8,128)(2,1)} %get-tuple-element.272) | copy-start | bytes 2359300
  1278.7 22.2 %collective-permute-start = (f32[192,12]{1,0:T(8,128)}, f32[192,12]{1,0:T(8,128)}, u32[]{:S(2)}, u32[]{:S(2)}) collective-permute-start(f32[192,12]{1,0:T(8,128)} %convert_add_fusion.14), channel_id=1, source_target_pairs={{0,1},{1,0},{2,3},{3,2},{4,5},{5,4},{6,7},{7,6},{8,9},{9,8},{10,11... | collective-permute-start | bytes 27656 | tf_op jit(solution)/shard_map/ppermute | solution.py:33
  1301.8 8.3 collective-permute-start.1
  (124 other events, 221.8 us)

commit v4 on v3

v4 whole, which is shorter than its diff:
```python
import functools
import jax
import jax.numpy as jnp
from jax import lax
from jax.experimental import pallas as pl
from jax.experimental.pallas import tpu as pltpu
from jax.sharding import Mesh, PartitionSpec as P

HEAD_DIM = 64
NORM_EPS = 1e-05
MASKED = -1e30
TILE = 384
F32 = jnp.float32
BF16 = jnp.bfloat16
MESH = pl.DeviceIdType.MESH
ANY = pl.BlockSpec(memory_space=pl.ANY)


def nn(a, b):
    return lax.dot_general(a, b, (((1,), (0,)), ((), ())), preferred_element_type=F32)


def nt(a, b):
    return lax.dot_general(a, b, (((1,), (1,)), ((), ())), preferred_element_type=F32)


def tn(a, b):
    return lax.dot_general(a, b, (((0,), (0,)), ((), ())), preferred_element_type=F32)


def flip(value, axis):
    return lax.ppermute(value, axis, [(0, 1), (1, 0)])


def diagonal():
    return lax.axis_index("c") == lax.axis_index("zh")


def off_diagonal():
    return lax.rem(lax.axis_index("c") + lax.axis_index("zh"), 2)


def target(kind):
    c, zh = lax.axis_index("c"), lax.axis_index("zh")
    off = off_diagonal()
    if kind == "ring":
        return {"c": lax.rem(c + off, 2), "zh": lax.rem(zh + 1 + off, 2)}
    if kind == "back":
        return {"c": lax.rem(c + 1 + off, 2), "zh": lax.rem(zh + off, 2)}
    if kind == "swap":
        return {"c": 1 - c, "zh": 1 - zh}
    return {kind: 1 - lax.axis_index(kind)}


def greeted(kinds):
    names = []
    for kind in kinds:
        pairs = {"ring": [("c",), ("zh",)], "back": [("c",), ("zh",)],
                 "swap": [("c", "zh")], "stay": []}.get(kind, [(kind,)])
        names += [p for p in pairs if p not in names]
    return names


def greet(kinds):
    barrier = pltpu.get_barrier_semaphore()
    names = greeted(kinds)
    for group in names:
        pl.semaphore_signal(
            barrier, inc=1, device_id={n: 1 - lax.axis_index(n) for n in group},
            device_id_type=MESH,
        )
    pl.semaphore_wait(barrier, len(names))


class Copy:
    def __init__(self, kind, src, dst, send, recv):
        self.kind = kind
        if kind == "stay":
            self.copy = pltpu.make_async_copy(src, dst, send)
        else:
            self.copy = pltpu.make_async_remote_copy(
                src_ref=src, dst_ref=dst, send_sem=send, recv_sem=recv,
                device_id=target(kind), device_id_type=MESH,
            )

    def guarded(self, act):
        if self.kind == "swap":
            pl.when(off_diagonal() == 1)(act)
        elif self.kind == "stay":
            pl.when(off_diagonal() == 0)(act)
        else:
            act()

    def start(self):
        self.guarded(lambda: self.copy.start())

    def wait(self):
        self.guarded(lambda: self.copy.wait())


class Ride:
    def __init__(self, ins, outs, stages, kinds, count, alias=()):
        self.ins, self.outs, self.stages = list(ins), list(outs), stages
        self.kinds, self.alias = list(kinds), dict(alias)
        self.scratch = [pltpu.SemaphoreType.DMA((count,)), pltpu.SemaphoreType.DMA((count,))]

    def chain(self, ins, outs, refs):
        return Chain(self.stages(ins, outs), *refs)


class Chain:
    def __init__(self, stages, send, recv):
        self.copies, place = [], 0
        for stage in stages:
            self.copies.append([])
            for kind, src, dst in stage:
                self.copies[-1].append(Copy(kind, src, dst, send.at[place], recv.at[place]))
                place += 1
        self.level, self.levels = 0, len(self.copies)

    def start(self):
        for copy in self.copies[0]:
            copy.start()

    def step(self):
        for copy in self.copies[self.level]:
            copy.wait()
        self.level += 1
        if self.level < self.levels:
            for copy in self.copies[self.level]:
                copy.start()


class Fold(Ride):
    def __init__(self, grad, first, cols, order, blocks, came=None, sums=()):
        self.rows, self.first, self.cols = grad.shape[0] // blocks, first, cols
        self.order, self.came, self.sums = order, came, list(sums)
        rows, half = self.rows, grad.shape[0] // 2
        keys = list(range(blocks))
        self.away0 = [k for k in keys if k & order[0][1]]
        self.held = [k for k in keys if not k & order[0][1]]
        self.ins = [grad] + ([came] if came is not None else [])
        self.outs = [jax.ShapeDtypeStruct((rows, cols), F32)]
        self.alias = {}
        self.kinds = [name for name, _ in order[0 if came is None else 1 :]]
        self.kinds += ["swap", "back"] + self.sums
        self.scratch = [pltpu.VMEM((half, cols), BF16), pltpu.VMEM((half, cols), BF16)]
        for level in range(1, len(order)):
            self.scratch.append(pltpu.VMEM((half >> level, cols), BF16))
        self.scratch += [
            pltpu.VMEM((2 * rows, cols), BF16),
            pltpu.VMEM((1 + len(self.sums), rows, cols), F32),
            pltpu.SemaphoreType.DMA((blocks + 2,)),
            pltpu.SemaphoreType.DMA((blocks * 2 + 4,)),
            pltpu.SemaphoreType.DMA((blocks * 2 + 4,)),
        ]
        self.levels = len(order) + 2 + len(self.sums)

    def chain(self, ins, outs, refs):
        self.in_refs, self.out = ins, outs[0]
        self.own, self.got = refs[0], list(refs[1 : 1 + len(self.order)])
        self.pair, self.total, self.load, self.send, self.recv = refs[1 + len(self.order) :]
        self.level, self.place, self.live = 0, 0, None
        return self

    def remote(self, kind, src, dst):
        copy = Copy(kind, src, dst, self.send.at[self.place], self.recv.at[self.place])
        self.place += 1
        copy.start()
        return copy

    def block(self, at, count=1):
        return pl.ds(at * self.rows, count * self.rows)

    def start(self):
        cols = pl.ds(self.first, self.cols)
        grad = self.in_refs[0]
        self.live, at = [], 0
        for i, (k, n) in enumerate(runs(self.held)):
            copy = pltpu.make_async_copy(
                grad.at[self.block(k, n), cols], self.own.at[self.block(at, n)], self.load.at[i])
            copy.start()
            self.live.append(copy)
            at += n
        if self.came is not None:
            copy = pltpu.make_async_copy(self.in_refs[1], self.got[0], self.load.at[len(self.live)])
            copy.start()
            self.live.append(copy)
        else:
            at = 0
            for k, n in runs(self.away0):
                self.live.append(self.remote(
                    self.order[0][0], grad.at[self.block(k, n), cols],
                    self.got[0].at[self.block(at, n)]))
                at += n

    def add(self, got, places):
        def one(i, p):
            value = self.own[self.block(p), :].astype(F32) + got[self.block(i), :].astype(F32)
            self.own[self.block(i), :] = value.astype(BF16)

        for i, p in enumerate(places):
            one(i, p)

    def step(self):
        for copy in self.live:
            copy.wait()
        bits = len(self.order)
        level = self.level
        self.level += 1
        if level < bits:
            if level == 0:
                self.add(self.got[0], range(len(self.held)))
            else:
                self.add(self.got[level], self.stay)
                self.held = [self.held[p] for p in self.stay]
            if level + 1 < bits:
                name, weight = self.order[level + 1]
                self.stay = [p for p, k in enumerate(self.held) if not k & weight]
                away = [p for p, k in enumerate(self.held) if k & weight]
                self.live, at = [], 0
                for p, n in runs(away):
                    self.live.append(self.remote(
                        name, self.own.at[self.block(p, n)],
                        self.got[level + 1].at[self.block(at, n)]))
                    at += n
            else:
                self.live = [
                    self.remote("swap", self.own.at[self.block(0)], self.pair.at[self.block(0)]),
                    self.remote("back", self.own.at[self.block(1)], self.pair.at[self.block(1)]),
                ]
            return
        if level == bits:
            def diagonal_sum():
                self.total[0] = (self.own[self.block(0), :].astype(F32)
                                 + self.pair[self.block(1), :].astype(F32))

            def other_sum():
                self.total[0] = (self.pair[self.block(0), :].astype(F32)
                                 + self.pair[self.block(1), :].astype(F32))

            pl.when(off_diagonal() == 0)(diagonal_sum)
            pl.when(off_diagonal() == 1)(other_sum)
        elif level <= bits + len(self.sums):
            self.total[0] = self.total[0] + self.total[level - bits]
        else:
            return
        nth = level - bits
        if nth < len(self.sums):
            self.live = [self.remote(self.sums[nth], self.total.at[0], self.total.at[nth + 1])]
        else:
            copy = pltpu.make_async_copy(self.total.at[0], self.out, self.load.at[0])
            copy.start()
            self.live = [copy]


def runs(keys):
    keys, out = sorted(keys), []
    for k in keys:
        if out and out[-1][0] + out[-1][1] == k:
            out[-1][1] += 1
        else:
            out.append([k, 1])
    return out


def pair_ride(shard, blocks):
    rows, cols = shard.shape
    out = jax.ShapeDtypeStruct((rows * blocks, cols), shard.dtype)

    def stages(ins, outs):
        near, far = outs[0].at[pl.ds(0, rows)], outs[0].at[pl.ds(rows, rows)]
        return [[("ring", ins[0], far), ("swap", ins[0], near), ("stay", ins[0], near)]]

    return Ride([shard], [out], stages, ["ring", "swap"], 3)


def spread_ride(buffer, pieces, levels, blocks):
    rows = buffer.shape[0] // blocks
    plan = []
    for level in levels:
        stage = []
        for first, cols, order in pieces:
            held = [0, 1]
            for name, weight in order[:level]:
                held = held + [k + weight for k in held]
            name, weight = order[level]
            for k, n in runs(held):
                stage.append((name, k, k + weight, n, first, cols))
        plan.append(stage)

    def stages(ins, outs):
        ref = outs[0]
        return [
            [
                (name, ref.at[pl.ds(a * rows, n * rows), pl.ds(first, cols)],
                 ref.at[pl.ds(b * rows, n * rows), pl.ds(first, cols)])
                for name, a, b, n, first, cols in stage
            ]
            for stage in plan
        ]

    kinds = [item[0] for stage in plan for item in stage]
    out = jax.ShapeDtypeStruct(buffer.shape, buffer.dtype)
    return Ride([buffer], [out], stages, kinds, sum(len(s) for s in plan), {0: 0})


def chain_ride(shard, pieces, levels, blocks):
    first = pair_ride(shard, blocks)
    rest = spread_ride(first.outs[0], pieces, levels, blocks)

    def stages(ins, outs):
        return first.stages(ins, outs) + rest.stages(ins, outs)

    count = len(first.kinds) + 1 + len(rest.kinds)
    return Ride([shard], first.outs, stages, first.kinds + rest.kinds, count)


def send_ride(value, kind, after=0):
    out = jax.ShapeDtypeStruct(value.shape, value.dtype)
    return Ride([value], [out], lambda ins, outs: [[]] * after + [[(kind, ins[0], outs[0])]],
                [kind], 1)


class Part:
    ins, outs, scratch, kinds = (), (), (), ()

    def early(self, in_refs, out_refs, refs):
        pass

    def begin(self):
        pass

    def run(self, rides):
        pass

    def settle(self):
        pass


class Rides:
    def __init__(self, chains, outs):
        self.chains, self.outs = chains, outs
        for chain in chains:
            chain.start()

    def advance(self, kind=object):
        for chain in self.chains:
            if chain.levels - chain.level > 1 and isinstance(chain, kind):
                chain.step()

    def finish(self, i):
        while self.chains[i].level < self.chains[i].levels:
            self.chains[i].step()

    def end(self):
        for level in range(max([c.levels for c in self.chains], default=0)):
            for chain in self.chains:
                if chain.level == level and level < chain.levels:
                    chain.step()


def launch(name, number, parts, rides, limit=62):
    ins = [x for p in parts for x in p.ins]
    outs = [x for p in parts for x in p.outs]
    in_arrays, out_shapes = list(ins), list(outs)
    aliases, spans = {}, []
    for ride in rides:
        for a, b in ride.alias.items():
            aliases[len(in_arrays) + a] = len(out_shapes) + b
        spans.append((len(in_arrays), len(in_arrays) + len(ride.ins),
                      len(out_shapes), len(out_shapes) + len(ride.outs)))
        in_arrays += ride.ins
        out_shapes += ride.outs
    kinds = [k for p in parts for k in p.kinds] + [k for r in rides for k in r.kinds]
    scratch = [x for p in parts for x in p.scratch]
    parts_scratch = len(scratch)
    scratch += [x for r in rides for x in r.scratch]

    def kernel(*refs):
        in_refs = refs[: len(in_arrays)]
        out_refs = refs[len(in_arrays) : len(in_arrays) + len(out_shapes)]
        rest = refs[len(in_arrays) + len(out_shapes) :]
        i, o, c = 0, 0, 0
        for p in parts:
            p.early(in_refs[i : i + len(p.ins)], out_refs[o : o + len(p.outs)],
                    rest[c : c + len(p.scratch)])
            i, o, c = i + len(p.ins), o + len(p.outs), c + len(p.scratch)
        if kinds:
            greet(kinds)
        chains, at = [], parts_scratch
        for ride, (a, b, c, d) in zip(rides, spans):
            more = len(ride.scratch)
            chains.append(ride.chain(in_refs[a:b], out_refs[c:d], rest[at : at + more]))
            at += more
        under_way = Rides(chains, [out_refs[c] for _, _, c, _ in spans])
        for p in parts:
            p.begin()
        for p in parts:
            p.run(under_way)
        for p in parts:
            p.settle()
        under_way.end()

    results = pl.pallas_call(
        kernel,
        out_shape=tuple(out_shapes),
        in_specs=[ANY] * len(in_arrays),
        out_specs=tuple([ANY] * len(out_shapes)),
        scratch_shapes=scratch,
        input_output_aliases=aliases,
        name=name,
        compiler_params=pltpu.CompilerParams(
            collective_id=number if kinds else None,
            has_side_effects=bool(kinds),
            vmem_limit_bytes=limit << 20,
        ),
    )(*in_arrays)
    main_outs, at = [], 0
    for p in parts:
        main_outs.append(results[at : at + len(p.outs)])
        at += len(p.outs)
    return main_outs, [results[c:d] for _, _, c, d in spans]


def normalise_value(rows, gain, shift):
    centre = jnp.mean(rows, axis=-1, keepdims=True)
    centred = rows - centre
    spread = jnp.mean(centred * centred, axis=-1, keepdims=True)
    return (centred * lax.rsqrt(spread + NORM_EPS) * gain + shift).astype(BF16)


def gelu_pair(upper):
    cdf = 0.5 * (1.0 + lax.erf(upper * (0.5**0.5)))
    density = jnp.exp(-0.5 * upper * upper) * (0.5 / jnp.pi) ** 0.5
    return (upper * cdf).astype(BF16), (cdf + upper * density).astype(BF16)


class Gather(Part):
    def __init__(self, rows, size, norm, weight, width, n, ending=None, slope=None):
        self.size, self.width, self.n = size, width, n
        self.has_rows, self.has_norm, self.has_slope = rows is not None, norm is not None, slope is not None
        self.double = ending == "gelu"
        self.filler = lambda: None
        self.ride = weight if isinstance(weight, int) else None
        self.kinds = ["c", "zl"]
        self.ins = []
        if self.has_rows:
            self.ins.append(rows)
        if self.ride is None:
            self.ins.append(weight)
        if self.has_norm:
            self.ins.append(jnp.concatenate([norm[0], norm[1]], axis=0))
        if self.has_slope:
            self.ins.append(slope)
        self.outs = [jax.ShapeDtypeStruct((4, size, width), BF16)]
        self.outs += [jax.ShapeDtypeStruct((4, size, n), BF16)] * (2 if self.double else 1)
        tall = self.double or self.has_slope
        self.scratch = [
            pltpu.VMEM((size, width) if self.has_rows else (8, 128), F32),
            pltpu.VMEM((width, n), BF16),
            pltpu.VMEM((2, width), F32),
            pltpu.VMEM((4, size, width), BF16),
            pltpu.VMEM((4, size, n), BF16),
            pltpu.VMEM((4, size, n) if tall else (1, 16, 128), BF16),
            pltpu.SemaphoreType.DMA((4,)),
            pltpu.SemaphoreType.DMA((6,)),
            pltpu.SemaphoreType.DMA((6,)),
            pltpu.SemaphoreType.DMA((3, 4)),
        ]

    def early(self, in_refs, out_refs, refs):
        self.rows, self.w, self.norms, self.x, self.y, self.second = refs[:6]
        self.load, self.send, self.recv, self.store = refs[6:]
        self.out_refs, self.over = out_refs, []
        todo, self.loads = list(in_refs), {}
        if self.has_rows:
            self.loads["rows"] = pltpu.make_async_copy(todo.pop(0), self.rows, self.load.at[0])
        if self.ride is None:
            self.loads["w"] = pltpu.make_async_copy(todo.pop(0), self.w, self.load.at[1])
        if self.has_norm:
            self.loads["norm"] = pltpu.make_async_copy(todo.pop(0), self.norms, self.load.at[2])
        if self.has_slope:
            self.loads["slope"] = pltpu.make_async_copy(todo.pop(0), self.second, self.load.at[3])
        for copy in self.loads.values():
            copy.start()

    def send_half(self, h, source):
        half = self.size // 2
        part = pl.ds(h * half, half)
        if h == 0 and self.has_norm:
            self.loads["norm"].wait()
        value = source[part, :]
        if self.has_norm:
            value = normalise_value(value, self.norms[0:1, :], self.norms[1:2, :])
        x = self.x
        x[0, part, :] = value.astype(BF16)
        self.over.append(
            Copy("zl", x.at[0, part], x.at[2, part], self.send.at[h], self.recv.at[h]))
        self.over[-1].start()
        if h == 1:
            self.beside = Copy("c", x.at[0], x.at[1], self.send.at[2], self.recv.at[2])
            self.beside.start()

    def begin(self):
        if self.has_rows:
            self.loads["rows"].wait()
            for h in range(2):
                self.send_half(h, self.rows)

    def run(self, rides):
        x, y, w, second, n = self.x, self.y, self.w, self.second, self.n
        tile, half = min(TILE, n), self.size // 2
        if self.ride is not None:
            rides.finish(self.ride)
            copy = pltpu.make_async_copy(rides.outs[self.ride], w, self.load.at[1])
            copy.start()
            copy.wait()
        else:
            self.loads["w"].wait()
        if self.has_slope:
            self.loads["slope"].wait()
        stores = []

        def multiply(b):
            def step(j, carry):
                cols = pl.ds(pl.multiple_of(j * tile, tile), tile)
                value = nn(x[b], w[:, cols])
                if self.double:
                    y[b, :, cols], second[b, :, cols] = gelu_pair(value)
                elif self.has_slope:
                    y[b, :, cols] = (value * second[b, :, cols].astype(F32)).astype(BF16)
                else:
                    y[b, :, cols] = value.astype(BF16)
                return carry

            lax.fori_loop(0, n // tile, step, 0)
            for k, ref in enumerate([x, y] + ([second] if self.double else [])):
                stores.append(pltpu.make_async_copy(
                    ref.at[b], self.out_refs[k].at[b], self.store.at[k, b]))
                stores[-1].start()

        multiply(0)
        self.beside.wait()
        multiply(1)
        self.filler()
        relay = []
        for h in range(2):
            part = pl.ds(h * half, half)
            self.over[h].wait()
            relay.append(Copy("c", x.at[2, part], x.at[3, part],
                              self.send.at[3 + h], self.recv.at[3 + h]))
            relay[-1].start()
        multiply(2)
        for copy in relay:
            copy.wait()
        multiply(3)
        for copy in stores:
            copy.wait()


class Scatter(Part):
    def __init__(self, parts, weight, base, norm, fills, hand=None):
        _, size, n = parts.shape
        width = weight.shape[0]
        half = size // 2
        rows = 4 * size
        ins = [parts.reshape(rows, n), weight] + ([base] if base is not None else [])
        if norm is not None:
            ins += list(norm)
        fill_at = len(ins)
        fill_cols = []
        for a, b, _ in fills:
            ins.append(a)
            if b is not None:
                ins.append(b)
            fill_cols.append(n if b is None else b.shape[1])
        outs = [jax.ShapeDtypeStruct((size, width), F32)]
        if norm is not None:
            outs.append(jax.ShapeDtypeStruct((2, width), F32))
        outs += [jax.ShapeDtypeStruct((width, k), BF16) for k in fill_cols]
        sends_at, copies = len(outs), 0
        for _, _, sends in fills:
            for _, rows_away, _, k in sends:
                outs.append(jax.ShapeDtypeStruct((sum(n for _, n in rows_away), k), BF16))
                copies += len(rows_away)
        scratch = [
            pltpu.VMEM((rows, n), BF16),
            pltpu.VMEM((width, n), BF16),
            pltpu.VMEM((size, width), F32),
            pltpu.VMEM((size, width), F32),
            pltpu.VMEM((2, size, width), BF16),
            pltpu.VMEM((2, size, width), BF16),
            pltpu.VMEM((size, width), BF16),
            pltpu.VMEM((size, width), BF16),
            pltpu.SemaphoreType.DMA((8,)),
            pltpu.SemaphoreType.DMA((6,)),
            pltpu.SemaphoreType.DMA((6,)),
        ]
        if norm is not None:
            scratch += [
                pltpu.VMEM((size, width), F32),
                pltpu.VMEM((1, width), F32),
                pltpu.VMEM((size, width), F32),
                pltpu.VMEM((2, width), F32),
                pltpu.SemaphoreType.DMA((4,)),
            ]
        for (a, b, _), k in zip(fills, fill_cols):
            scratch.append(pltpu.VMEM((rows, width), BF16))
            if b is not None:
                scratch.append(pltpu.VMEM((rows, k), BF16))
            scratch += [pltpu.VMEM((width, k), BF16), pltpu.SemaphoreType.DMA((3,))]
        scratch += [pltpu.SemaphoreType.DMA((max(copies, 1),))] * 2
        self.kinds = ["c", "zl"] + [name for _, _, sends in fills for name, _, _, _ in sends]
        self.sends_at = sends_at
        self.ins, self.outs, self.scratch = ins, outs, scratch
        self.facts = (size, n, width, half, base, norm, fills, fill_at, fill_cols, outs)
        self.hand = hand

    def early(self, in_refs, out_refs, refs):
        size, n, width, half, base, norm, fills, fill_at, fill_cols, outs = self.facts
        self.out_refs, self.refs = out_refs, refs
        y, w, total, far, give, came, across, over, load, send, recv = refs[:11]
        refs = list(refs[11:])
        if norm is not None:
            stream, gain, back, sums, norm_sem = refs[:5]
            refs = refs[5:]
        loads = [pltpu.make_async_copy(in_refs[1], w, load.at[0])]
        loads += [
            pltpu.make_async_copy(
                in_refs[0].at[pl.ds(b * size, size)], y.at[pl.ds(b * size, size)],
                load.at[1 + b])
            for b in range(4)
        ]
        if base is not None:
            loads.append(pltpu.make_async_copy(in_refs[2], total, load.at[5]))
        for place in (0, 4, 3, 2, 1, 5)[: len(loads)]:
            loads[place].start()
        others = []
        if norm is not None:
            at = 3 if base is not None else 2
            for i, ref in enumerate((stream, gain, back)):
                others.append(pltpu.make_async_copy(in_refs[at + i], ref, norm_sem.at[i]))
        at = fill_at
        for a, b, _ in fills:
            others.append(pltpu.make_async_copy(in_refs[at], refs[0], refs[2 if b is None else 3].at[0]))
            at += 1
            if b is not None:
                others.append(pltpu.make_async_copy(in_refs[at], refs[1], refs[3].at[1]))
                at += 1
            refs = refs[3 if b is None else 4 :]
        for copy in others:
            copy.start()
        self.loads, self.others = loads, others

    def run(self, rides):
        size, n, width, half, base, norm, fills, fill_at, fill_cols, outs = self.facts
        out_refs, refs = self.out_refs, self.refs
        y, w, total, far, give, came, across, over, load, send, recv = refs[:11]
        refs = list(refs[11:])
        if norm is not None:
            stream, gain, back, sums, norm_sem = refs[:5]
            refs = refs[5:]
        loads, others = self.loads, self.others

        def multiply(b, part, count, put):
            def step(j, carry):
                cols = pl.ds(pl.multiple_of(j * TILE, TILE), TILE)
                put(cols, nt(y[pl.ds(b * size + part, count), :], w[cols, :]))
                return carry

            lax.fori_loop(0, width // TILE, step, 0)

        for place in (0, 4, 3):
            loads[place].wait()
        sent = []
        for h in range(2):
            part = pl.ds(h * half, half)

            def put_give(cols, value, part=part):
                give[0, part, cols] = value.astype(BF16)

            def put_far(cols, value, part=part):
                far[part, cols] = value

            multiply(3, h * half, half, put_give)
            copy = Copy("c", give.at[0, part], came.at[0, part], send.at[h], recv.at[h])
            copy.start()
            multiply(2, h * half, half, put_far)
            copy.wait()
            across[part, :] = (far[part, :] + came[0, part, :].astype(F32)).astype(BF16)
            copy = Copy("zl", across.at[part], over.at[part], send.at[2 + h], recv.at[2 + h])
            copy.start()
            sent.append(copy)
        rides.advance(Fold)
        loads[2].wait()

        def put_near(cols, value):
            give[1, :, cols] = value.astype(BF16)

        multiply(1, 0, size, put_near)
        near = Copy("c", give.at[1], came.at[1], send.at[4], recv.at[4])
        near.start()
        loads[1].wait()
        if base is not None:
            loads[5].wait()

        def put_total(cols, value):
            total[:, cols] = value + (total[:, cols] if base is not None else 0.0)

        multiply(0, 0, size, put_total)
        for copy in others:
            copy.wait()
        stores, fill_refs, refs_all = [], refs, self.refs
        slot = [self.sends_at, 0]

        def fill(k, left, right, result, sem):
            count = fill_cols[k]
            wide = 768 if count % 768 == 0 else count

            def step(j, carry):
                rows_ = pl.ds(pl.multiple_of(j * 256, 256), 256)
                turned = left[:, rows_].T
                for q in range(count // wide):
                    cols = slice(q * wide, (q + 1) * wide)
                    result[rows_, cols] = nn(turned, right[:, cols]).astype(BF16)
                return carry

            lax.fori_loop(0, width // 256, step, 0)
            where = self.sends_at - len(fills) + k
            stores.append(pltpu.make_async_copy(result, out_refs[where], sem.at[2]))
            stores[-1].start()
            for name, rows_away, first, cols in fills[k][2]:
                at = 0
                for row, count in rows_away:
                    copy = Copy(name, result.at[pl.ds(row, count), pl.ds(first, cols)],
                                out_refs[slot[0]].at[pl.ds(at, count)],
                                refs_all[-2].at[slot[1]], refs_all[-1].at[slot[1]])
                    copy.start()
                    stores.append(copy)
                    at += count
                    slot[1] += 1
                slot[0] += 1

        for k, (a, b, _) in enumerate(fills):
            if b is None:
                left, result, sem = fill_refs[:3]
                right, fill_refs = y, fill_refs[3:]
            else:
                left, right, result, sem = fill_refs[:4]
                fill_refs = fill_refs[4:]
            job = functools.partial(fill, k, left, right, result, sem)
            if self.hand is not None and k == len(fills) - 1 and not fills[k][2]:
                self.hand.filler = job
            else:
                job()
        rides.advance()
        near.wait()
        total[...] += came[1].astype(F32)
        for h in range(2):
            part = pl.ds(h * half, half)
            sent[h].wait()
            total[part, :] += over[part, :].astype(F32)
            if norm is not None:
                value = total[part, :]
                rows_in = stream[part, :]
                centred = rows_in - jnp.mean(rows_in, axis=-1, keepdims=True)
                inverse = lax.rsqrt(jnp.mean(centred * centred, axis=-1, keepdims=True) + NORM_EPS)
                unit = centred * inverse
                gain_sum = jnp.sum(value * unit, axis=0, keepdims=True)
                shift_sum = jnp.sum(value, axis=0, keepdims=True)
                sums[0:1, :] = gain_sum if h == 0 else sums[0:1, :] + gain_sum
                sums[1:2, :] = shift_sum if h == 0 else sums[1:2, :] + shift_sum
                scaled = value * gain[...]
                total[part, :] = back[part, :] + inverse * (
                    scaled
                    - jnp.mean(scaled, axis=-1, keepdims=True)
                    - unit * jnp.mean(scaled * unit, axis=-1, keepdims=True)
                )
            if self.hand is not None:
                self.hand.send_half(h, total)
            copy = pltpu.make_async_copy(total.at[part], out_refs[0].at[part], load.at[6 + h])
            copy.start()
            stores.append(copy)
        if norm is not None:
            copy = pltpu.make_async_copy(sums, out_refs[1], norm_sem.at[3])
            copy.start()
            stores.append(copy)
        self.stores = stores

    def settle(self):
        for copy in self.stores:
            copy.wait()


def place_of(i):
    c, zl = lax.axis_index("c"), lax.axis_index("zl")
    dc, dz = i // 2, i % 2
    return (c + dc) % 2 + 2 * ((zl + dz) % 2)


def head_only(value, u):
    lane = lax.broadcasted_iota(jnp.int32, value.shape, 1)
    keep = (lane < HEAD_DIM) if u == 0 else (lane >= HEAD_DIM)
    return jnp.where(keep, value, jnp.zeros_like(value))


def masked(scores):
    key = lax.broadcasted_iota(jnp.int32, scores.shape, 0)
    query = lax.broadcasted_iota(jnp.int32, scores.shape, 1)
    return jnp.where(key <= query, scores, MASKED)


def softmax_parts(parts, value_rows):
    top = parts[0].max(axis=0, keepdims=True)
    for scores in parts[1:]:
        top = jnp.maximum(top, scores.max(axis=0, keepdims=True))
    total, mixed = 0.0, 0.0
    for scores, values in zip(parts, value_rows):
        expo = jnp.exp(scores - top)
        total = total + expo.sum(axis=0, keepdims=True)
        mixed = mixed + nn(values, expo.astype(BF16))
    return mixed / total, top + jnp.log(total)


def softmax_back(scores, slopes, logsum):
    probs = [jnp.exp(s - logsum) for s in scores]
    inner = 0.0
    for p, d in zip(probs, slopes):
        inner = inner + (p * d).sum(axis=0, keepdims=True)
    return [p.astype(BF16) for p in probs], [
        (p * (d - inner)).astype(BF16) for p, d in zip(probs, slopes)
    ]


class Local(Part):
    def __init__(self, ins, outs, scratch, main):
        self.ins, self.outs, self.scratch, self.main = ins, outs, scratch, main

    def early(self, in_refs, out_refs, refs):
        self.refs = (in_refs, out_refs, refs)
        self.stage = self.main(in_refs, out_refs, refs, True)

    def run(self, rides):
        self.main(*self.refs, self.stage, rides)


def attend_self(proj, scale):
    _, size, wide = proj.shape
    cols = wide // 3
    frames, heads = 4 * size, cols // HEAD_DIM
    outs = [jax.ShapeDtypeStruct((4, size, cols), BF16), jax.ShapeDtypeStruct((heads, frames), F32)]
    scratch = [
        pltpu.VMEM((4, size, wide), BF16),
        pltpu.VMEM((frames, 128), BF16),
        pltpu.VMEM((128, frames), BF16),
        pltpu.VMEM((4, size, cols), BF16),
        pltpu.VMEM((heads, frames), F32),
        pltpu.SemaphoreType.DMA((3,)),
    ]

    def main(in_refs, out_refs, refs, stage, rides=None):
        x, keys, values, out, logs, sem = refs
        if stage is True:
            copy = pltpu.make_async_copy(in_refs[0], x, sem.at[0])
            copy.start()
            return copy
        stage.wait()
        for g in range(cols // 128):
            if g:
                rides.advance()
            lanes = [pl.ds(part * cols + g * 128, 128) for part in range(3)]
            for i in range(4):
                rows = pl.ds(i * size, size)
                keys[rows, :] = x[place_of(i), :, lanes[1]]
                values[:, rows] = x[place_of(i), :, lanes[2]].T
            for i in range(4):
                query = x[place_of(i), :, lanes[0]]
                before = i * size
                done = []
                for u in range(2):
                    q = head_only(query, u)
                    mine = pl.ds(u * HEAD_DIM, HEAD_DIM)
                    parts = [masked(nt(keys[pl.ds(before, size), :], q) * scale)]
                    rows = [values[mine, pl.ds(before, size)]]
                    if i:
                        parts.append(nt(keys[pl.ds(0, before), :], q) * scale)
                        rows.append(values[mine, pl.ds(0, before)])
                    mixed, logsum = softmax_parts(parts, rows)
                    done.append(mixed)
                    logs[pl.ds(2 * g + u, 1), pl.ds(before, size)] = logsum
                joined = jnp.concatenate(done, axis=0).T
                out[place_of(i), :, pl.ds(g * 128, 128)] = joined.astype(BF16)
        copies = [pltpu.make_async_copy(out, out_refs[0], sem.at[1]),
                  pltpu.make_async_copy(logs, out_refs[1], sem.at[2])]
        for copy in copies:
            copy.start()
        for copy in copies:
            copy.wait()

    return Local([proj], outs, scratch, main)


def attend_self_back(proj, grad_joined, logsum, scale):
    _, size, wide = proj.shape
    cols = wide // 3
    frames, heads = 4 * size, cols // HEAD_DIM
    outs = [jax.ShapeDtypeStruct((4, size, wide), BF16)]
    scratch = [
        pltpu.VMEM((4, size, wide), BF16),
        pltpu.VMEM((4, size, cols), BF16),
        pltpu.VMEM((heads, frames), F32),
        pltpu.VMEM((frames, 128), BF16),
        pltpu.VMEM((128, frames), BF16),
        pltpu.VMEM((frames, 128), BF16),
        pltpu.VMEM((frames, 128), F32),
        pltpu.VMEM((frames, 128), F32),
        pltpu.VMEM((4, size, wide), BF16),
        pltpu.SemaphoreType.DMA((4,)),
    ]

    def main(in_refs, out_refs, refs, stage, rides=None):
        x, grads, logs, keys, keys_t, values, grad_k, grad_v, out, sem = refs
        if stage is True:
            copies = [
                pltpu.make_async_copy(in_refs[i], ref, sem.at[i])
                for i, ref in enumerate((x, grads, logs))
            ]
            for copy in copies:
                copy.start()
            return copies
        for copy in stage:
            copy.wait()
        for g in range(cols // 128):
            if g < 2:
                rides.advance(Fold)
            lanes = [pl.ds(part * cols + g * 128, 128) for part in range(3)]
            for i in range(4):
                rows = pl.ds(i * size, size)
                keys[rows, :] = x[place_of(i), :, lanes[1]]
                keys_t[:, rows] = x[place_of(i), :, lanes[1]].T
                values[rows, :] = x[place_of(i), :, lanes[2]]
            grad_k[...] = jnp.zeros_like(grad_k)
            grad_v[...] = jnp.zeros_like(grad_v)
            for i in range(4):
                query = x[place_of(i), :, lanes[0]]
                grad = grads[place_of(i), :, lanes[0]]
                before = i * size
                spans = [pl.ds(before, size)] + ([pl.ds(0, before)] if i else [])
                done = []
                for u in range(2):
                    q, go = head_only(query, u), head_only(grad, u)
                    mine = pl.ds(u * HEAD_DIM, HEAD_DIM)
                    scores = [nt(keys[span, :], q) * scale for span in spans]
                    scores[0] = masked(scores[0])
                    slopes = [nt(values[span, :], go) for span in spans]
                    probs, grad_scores = softmax_back(
                        scores, slopes, logs[pl.ds(2 * g + u, 1), pl.ds(before, size)])
                    grad_q = 0.0
                    for span, p, d in zip(spans, probs, grad_scores):
                        grad_v[span, :] += nn(p, go)
                        grad_k[span, :] += nn(d, q)
                        grad_q = grad_q + nn(keys_t[mine, span], d)
                    done.append(grad_q)
                grad_q = jnp.concatenate(done, axis=0).T * scale
                out[place_of(i), :, lanes[0]] = grad_q.astype(BF16)
            for i in range(4):
                rows = pl.ds(i * size, size)
                out[place_of(i), :, lanes[1]] = (grad_k[rows, :] * scale).astype(BF16)
                out[place_of(i), :, lanes[2]] = grad_v[rows, :].astype(BF16)
        copy = pltpu.make_async_copy(out, out_refs[0], sem.at[3])
        copy.start()
        copy.wait()

    return Local([proj, grad_joined, logsum], outs, scratch, main)


def attend_cross(query, text, weight, scale):
    _, size, cols = query.shape
    frames, heads = 4 * size, cols // HEAD_DIM
    states, width = text.shape
    outs = [jax.ShapeDtypeStruct((4, size, cols), BF16), jax.ShapeDtypeStruct((heads, frames), F32),
            jax.ShapeDtypeStruct((states, 2 * cols), BF16)]
    scratch = [
        pltpu.VMEM((4, size, cols), BF16),
        pltpu.VMEM((states, 2 * cols), BF16),
        pltpu.VMEM((4, size, cols), BF16),
        pltpu.VMEM((heads, frames), F32),
        pltpu.VMEM((states, width), BF16),
        pltpu.VMEM((width, 2 * cols), BF16),
        pltpu.SemaphoreType.DMA((6,)),
    ]

    def main(in_refs, out_refs, refs, stage, rides=None):
        x, kv, out, logs, states_in, w, sem = refs
        if stage is True:
            copies = [
                pltpu.make_async_copy(in_refs[i], ref, sem.at[i])
                for i, ref in enumerate((x, states_in, w))
            ]
            for copy in copies:
                copy.start()
            return copies
        for copy in stage:
            copy.wait()
        kv[...] = nn(states_in[...], w[...]).astype(BF16)
        for g in range(cols // 128):
            lanes = pl.ds(g * 128, 128)
            keys = kv[:, lanes]
            values = kv[:, pl.ds(cols + g * 128, 128)].T
            for i in range(4):
                rows = x[i, :, lanes]
                done = []
                for u in range(2):
                    scores = nt(keys, head_only(rows, u)) * scale
                    mixed, logsum = softmax_parts(
                        [scores], [values[u * HEAD_DIM : (u + 1) * HEAD_DIM, :]])
                    done.append(mixed)
                    logs[pl.ds(2 * g + u, 1), pl.ds(i * size, size)] = logsum
                out[i, :, lanes] = jnp.concatenate(done, axis=0).T.astype(BF16)
        copies = [
            pltpu.make_async_copy(ref, out_refs[i], sem.at[3 + i])
            for i, ref in enumerate((out, logs, kv))
        ]
        for copy in copies:
            copy.start()
        for copy in copies:
            copy.wait()

    return Local([query, text, weight], outs, scratch, main)


def attend_cross_back(query, pairs, grad_joined, logsum, text, weight, scale):
    _, size, cols = query.shape
    frames, heads = 4 * size, cols // HEAD_DIM
    states, width = text.shape
    outs = [jax.ShapeDtypeStruct((4, size, cols), BF16),
            jax.ShapeDtypeStruct((width, 2 * cols), BF16),
            jax.ShapeDtypeStruct((states, width), F32)]
    scratch = [
        pltpu.VMEM((4, size, cols), BF16),
        pltpu.VMEM((states, 2 * cols), BF16),
        pltpu.VMEM((4, size, cols), BF16),
        pltpu.VMEM((heads, frames), F32),
        pltpu.VMEM((states, width), BF16),
        pltpu.VMEM((width, 2 * cols), BF16),
        pltpu.VMEM((4, size, cols), BF16),
        pltpu.VMEM((states, 2 * cols), BF16),
        pltpu.VMEM((width, 2 * cols), BF16),
        pltpu.VMEM((states, width), F32),
        pltpu.SemaphoreType.DMA((9,)),
    ]

    def main(in_refs, out_refs, refs, stage, rides=None):
        x, kv, grads, logs, states_in, w, out, out_kv, out_w, out_text, sem = refs
        if stage is True:
            copies = [
                pltpu.make_async_copy(in_refs[i], ref, sem.at[i])
                for i, ref in enumerate((x, kv, grads, logs, states_in, w))
            ]
            for copy in copies:
                copy.start()
            return copies
        for copy in stage:
            copy.wait()
        for g in range(cols // 128):
            if g:
                rides.advance()
            lanes, lanes_v = pl.ds(g * 128, 128), pl.ds(cols + g * 128, 128)
            keys, values = kv[:, lanes], kv[:, lanes_v]
            keys_t = keys.T
            grad_k, grad_v = 0.0, 0.0
            for i in range(4):
                done = []
                for u in range(2):
                    q, go = head_only(x[i, :, lanes], u), head_only(grads[i, :, lanes], u)
                    scores = nt(keys, q) * scale
                    probs, grad_scores = softmax_back(
                        [scores], [nt(values, go)],
                        logs[pl.ds(2 * g + u, 1), pl.ds(i * size, size)])
                    grad_v = grad_v + nn(probs[0], go)
                    grad_k = grad_k + nn(grad_scores[0], q)
                    done.append(nn(keys_t[u * HEAD_DIM : (u + 1) * HEAD_DIM, :], grad_scores[0]))
                out[i, :, lanes] = (jnp.concatenate(done, axis=0).T * scale).astype(BF16)
            out_kv[:, lanes] = (grad_k * scale).astype(BF16)
            out_kv[:, lanes_v] = grad_v.astype(BF16)
        grad_pairs = out_kv[...]
        out_w[...] = nn(states_in[...].T, grad_pairs).astype(BF16)
        out_text[...] = nt(grad_pairs, w[...])
        copies = [
            pltpu.make_async_copy(ref, out_refs[i], sem.at[6 + i])
            for i, ref in enumerate((out, out_w, out_text))
        ]
        for copy in copies:
            copy.start()
        for copy in copies:
            copy.wait()

    return Local([query, pairs, grad_joined, logsum, text, weight], outs, scratch, main)


def flat(parts):
    return parts.reshape(-1, parts.shape[-1])


def body(bits, frames_in, text_states, ln_gain, ln_bias, w_self, w_self_out, w_cross_q,
         w_cross_kv, w_cross_out, w_up, w_down, cotangent):
    scale = float(HEAD_DIM) ** (-0.5)
    layers = w_self.shape[0]
    width = frames_in.shape[2]
    part = w_self.shape[1]
    blocks = width // part
    cols = w_self.shape[3]
    hidden = w_up.shape[2]
    me = lax.axis_index("zh")
    for place, name in enumerate(reversed(bits)):
        me = me + (lax.axis_index(name) << (place + 1))

    row = lax.broadcasted_iota(jnp.int32, (width, width), 0)
    col = lax.broadcasted_iota(jnp.int32, (width, width), 1)
    permute = ((row // part == ((col // part) ^ me)) & (row % part == col % part)).astype(BF16)

    def reorder(value):
        return nn(value, permute)

    up = [(name, 2 << (len(bits) - 1 - place)) for place, name in enumerate(bits)]
    low_first = list(reversed(up))
    levels = len(bits)
    early, late = list(range(levels // 2)), list(range(levels // 2, levels))
    sizes = {"self": 3 * cols, "self_out": cols, "q": cols, "kv": 2 * cols, "out": cols,
             "up": hidden, "down": hidden, "norm": 128}

    def halves(name):
        n = sizes[name]
        if name in ("self", "kv", "up", "down"):
            first = (n // 2 + 127) // 128 * 128
            return [(0, first, low_first), (first, n - first, up)]
        return [(0, n, low_first if name in ("q", "norm") else up)]

    packs = {"a": "self", "o": "self_out", "q": "q", "k": "kv", "u": "out", "c": "up", "d": "down"}
    norm_rows = jnp.concatenate([ln_gain.reshape(-1, part), ln_bias.reshape(-1, part)], axis=0).T
    norm_rows = jnp.pad(norm_rows, ((0, 0), (0, sizes["norm"] - norm_rows.shape[1])))
    shards = {}
    for l in range(layers):
        shards[l, "self"] = w_self[l].reshape(part, 3 * cols)
        shards[l, "self_out"] = w_self_out[l].T
        shards[l, "q"] = w_cross_q[l]
        shards[l, "kv"] = w_cross_kv[l].reshape(part, 2 * cols)
        shards[l, "out"] = w_cross_out[l].T
        shards[l, "up"] = w_up[l]
        shards[l, "down"] = w_down[l].T
    held = {}
    counter = [0]

    def number():
        counter[0] += 1
        return counter[0] - 1

    def forward(parts, todo=(), more=()):
        rides, keys = [], []
        for word in todo:
            l, name, stage = int(word[0]), packs[word[1]], int(word[2])
            if l >= layers:
                continue
            if stage == 1:
                rides.append(pair_ride(shards[l, name], blocks))
            else:
                which = {2: early, 3: late, 4: early + late}[stage]
                rides.append(spread_ride(held[l, name], halves(name), which, blocks))
            keys.append((l, name))
        outs, extra = launch(f"step_{counter[0]}", number(), parts, rides + list(more))
        for key, value in zip(keys, extra):
            held[key] = value[0]
        return outs, [e[0] for e in extra[len(keys):]]

    def move(rides):
        return launch(f"move_{counter[0]}", number(), [], rides)[1]

    extra = move([
        chain_ride(shards[0, "self"], halves("self"), early, blocks),
        chain_ride(norm_rows, halves("norm"), early + late, blocks),
        send_ride(text_states[0], "c"),
        send_ride(frames_in[0], "swap", 1),
    ])
    held[0, "self"], norms, text_far, frames_far = [e[0] for e in extra]
    stream = reorder(jnp.where(diagonal(), frames_in[0], frames_far))
    text_own = reorder(jnp.where(diagonal(), text_states[0], text_far)).astype(BF16)
    norms = norms.astype(F32).T
    gains = norms[: 3 * layers].reshape(layers, 3, 1, width)
    shifts = norms[3 * layers : 6 * layers].reshape(layers, 3, 1, width)
    size = stream.shape[0]

    def norm_of(l, j):
        return gains[l, j], shifts[l, j]

    records = []
    (((first, proj),), _) = forward(
        [Gather(stream, size, norm_of(0, 0), 0, width, 3 * cols)], ["0a3", "0o1", "0q1", "0k1", "0u1"])
    for l in range(layers):
        n = l + 1
        saved = {"one": stream, "first": first, "proj": proj}
        (((joined, logsum),), _) = forward(
            [attend_self(proj, scale)], [f"{l}o4", f"{l}q4", f"{l}c1"])
        saved.update(joined_self=joined, logsum_self=logsum)
        hand = Gather(None, size, norm_of(l, 1), held[l, "q"], width, cols)
        (((stream,), (second, query)), _) = forward(
            [Scatter(joined, held[l, "self_out"], stream, None, [], hand), hand],
            [f"{l}k4", f"{l}u4", f"{l}c2", f"{l}d1"])
        saved.update(two=stream, second=second, query=query)

        (((joined, logsum, pairs),), _) = forward(
            [attend_cross(query, text_own, held[l, "kv"], scale)], [f"{l}d2"])
        saved.update(pairs=pairs, joined_cross=joined, logsum_cross=logsum)
        hand = Gather(None, size, norm_of(l, 2), 0, width, hidden, "gelu")
        more = [send_ride(cotangent[0], "swap")] if n == layers else []
        (((stream,), (third, active, slope)), extra) = forward(
            [Scatter(joined, held[l, "out"], stream, None, [], hand), hand],
            [f"{l}c3", f"{l}d3", f"{n}a1"], more)
        saved.update(three=stream, third=third, active=active, slope=slope)
        records.append(saved)

        if n < layers:
            hand = Gather(None, size, norm_of(n, 0), 0, width, 3 * cols)
            (((stream,), (first, proj)), _) = forward(
                [Scatter(active, held[l, "down"], stream, None, [], hand), hand],
                [f"{n}a4", f"{n}o1", f"{n}q1", f"{n}k1", f"{n}u1"])
        else:
            grad = reorder(jnp.where(diagonal(), cotangent[0], extra[0]))
            gather = Gather(grad, size, None, held[l, "down"], width, hidden, slope=slope)
            (((stream,), (full, grad_upper)), _) = forward(
                [Scatter(active, held[l, "down"], stream, None, []), gather])
    result_own = reorder(stream.astype(BF16)).astype(BF16)

    folding = []
    finished = {}
    grad_text = jnp.zeros((text_own.shape[0], width), F32)
    norm_grads = {}

    def fold_later(l, name, value, came=None):
        for i, (first, n, order) in enumerate(halves(name)):
            folding.append({"key": (l, name, first), "grad": value.astype(BF16), "first": first,
                            "cols": n, "order": list(reversed(order)),
                            "came": came[i] if came else None})

    def first_sends(name):
        sends = []
        for first, n, order in halves(name):
            axis, weight = order[-1]
            away = runs([k for k in range(blocks) if k & weight])
            sends.append((axis, [(k * part, count * part) for k, count in away], first, n))
        return sends

    def fold_ride(item):
        sums = ("zl", "zh") if item["key"][1] == "norm" else ()
        return Fold(item["grad"], item["first"], item["cols"], item["order"], blocks,
                    item["came"], sums)

    def first_ride(item):
        name, weight = item["order"][0]
        away = runs([k for k in range(blocks) if k & weight])
        grad, first, n = item["grad"], item["first"], item["cols"]
        out = jax.ShapeDtypeStruct((grad.shape[0] // 2, n), BF16)

        def stages(ins, outs):
            copies, at = [], 0
            for k, count in away:
                copies.append((name, ins[0].at[pl.ds(k * part, count * part), pl.ds(first, n)],
                               outs[0].at[pl.ds(at * part, count * part)]))
                at += count
            return [copies]

        return Ride([grad], [out], stages, [name] * len(away), len(away))

    def folds(parts, end=(), begin=(), more=()):
        ending = [i for i in folding if i["key"][:2] in end]
        beginning = [i for i in folding if i["key"][:2] in begin]
        rides = [fold_ride(i) for i in ending] + [first_ride(i) for i in beginning]
        outs, extra = launch(f"step_{counter[0]}", number(), parts, rides + list(more))
        for item, came in zip(ending, extra):
            finished[item["key"]] = came[0]
            folding.remove(item)
        for item, came in zip(beginning, extra[len(ending):]):
            item["came"] = came[0]
        return outs, [e[0] for e in extra[len(rides):]]

    for l in reversed(range(layers)):
        saved = records[l]
        more = [send_ride(result_own, "swap")] if l == layers - 1 else []
        hand = Gather(None, size, None, held[l, "out"], width, cols)
        fills = [(flat(full), flat(saved["active"]), first_sends("down")),
                 (flat(saved["third"]), None, [])]
        (((grad, norm_grads[l, 2], down, up_, *came), (full, grad_joined)), extra) = folds(
            [Scatter(grad_upper, held[l, "up"], None, (saved["three"], gains[l, 2], grad), fills,
                     hand), hand], [(l + 1, "self_out"), (l + 1, "self")], (), more)
        if more:
            result = jnp.where(diagonal(), result_own, extra[0])
        fold_later(l, "down", down, came)
        fold_later(l, "up", up_)

        (((grad_query, kv_, text_part),), _) = folds(
            [attend_cross_back(saved["query"], saved["pairs"], grad_joined,
                               saved["logsum_cross"], text_own, held[l, "kv"], scale)],
            (), [(l, "up")])
        grad_text = grad_text + text_part
        fold_later(l, "kv", kv_)
        more = [send_ride(grad_text.astype(BF16), "c")] if l == 0 else []
        hand = Gather(None, size, None, held[l, "self_out"], width, cols)
        fills = [(flat(full), flat(saved["joined_cross"]), first_sends("out")),
                 (flat(saved["second"]), None, first_sends("q"))]
        (((grad, norm_grads[l, 1], out_, q_, *came), (full, grad_joined)), extra) = folds(
            [Scatter(grad_query, held[l, "q"], None, (saved["two"], gains[l, 1], grad), fills,
                     hand), hand], [(l, "down")], [(l, "kv")], more)
        fold_later(l, "out", out_, came[:1])
        fold_later(l, "q", q_, came[1:])
        if more:
            grad_text = grad_text.astype(BF16).astype(F32) + extra[0].astype(F32)
            more = [send_ride(grad_text.astype(BF16), "zl")]

        (((grad_proj,),), extra) = folds(
            [attend_self_back(saved["proj"], grad_joined, saved["logsum_self"], scale)],
            [(l, "up")], (), more)
        if more:
            grad_text = grad_text.astype(BF16).astype(F32) + extra[0].astype(F32)
        fills = [(flat(full), flat(saved["joined_self"]), first_sends("self_out")),
                 (flat(saved["first"]), None, first_sends("self"))]
        chain = (saved["one"], gains[l, 0], grad)
        parts = [Scatter(grad_proj, held[l, "self"], None, chain, fills)]
        if l:
            hand = Gather(None, size, None, held[l - 1, "down"], width, hidden,
                          slope=records[l - 1]["slope"])
            parts = [Scatter(grad_proj, held[l, "self"], None, chain, fills, hand), hand]
        (((grad, norm_grads[l, 0], out_, self_, *came), *after), _) = folds(
            parts, [(l, "out"), (l, "q"), (l, "kv")])
        if l:
            ((full, grad_upper),) = after
        fold_later(l, "self_out", out_, came[:1])
        fold_later(l, "self", self_, came[1:])

    small = [norm_grads[l, j][k] for l in range(layers) for k in range(2) for j in range(3)]
    small = jnp.stack(small, axis=1)
    small = jnp.pad(small, ((0, 0), (0, sizes["norm"] - small.shape[1])))
    fold_later(0, "norm", small)
    frames_back = reorder(grad.astype(BF16)).astype(BF16)
    text_back = reorder(grad_text.astype(BF16)).astype(BF16)
    folds_left = [fold_ride(item) for item in folding]
    extra = move(folds_left + [send_ride(frames_back, "swap"), send_ride(text_back, "swap")])
    for item, came in zip(folding, extra):
        finished[item["key"]] = came[0]
    grad_frames, text_sum = [
        jnp.where(diagonal(), mine, came[0]).astype(F32)
        for mine, came in zip((frames_back, text_back), extra[len(folds_left):])
    ]
    small = finished[0, "norm", 0][:, : 6 * layers]
    small = small.T.reshape(layers, 6, part)

    def gradient(l, name):
        pieces = [finished[l, name, first] for first, _, _ in halves(name)]
        return jnp.concatenate(pieces, axis=1) if len(pieces) > 1 else pieces[0]

    def stacked(name, shape=None, turned=False):
        members = [gradient(l, name) for l in range(layers)]
        if turned:
            members = [m.T for m in members]
        if shape is not None:
            members = [m.reshape(shape) for m in members]
        return jnp.stack(members)

    return (
        result[None],
        grad_frames[None],
        text_sum[None],
        small[:, :3],
        small[:, 3:],
        stacked("self", (part, 3, cols)),
        stacked("self_out", turned=True),
        stacked("q"),
        stacked("kv", (part, 2, cols)),
        stacked("out", turned=True),
        stacked("up"),
        stacked("down", turned=True),
    )


def solution(mesh):
    count = mesh.shape["dp"]
    bits = tuple(f"b{i}" for i in range(count.bit_length() - 2))
    dp = (*bits, "c")
    tensor = ("zh", "zl")
    inner = Mesh(mesh.devices.reshape((2,) * (len(bits) + 3)), (*dp, *tensor))
    return jax.shard_map(
        functools.partial(body, bits),
        mesh=inner,
        in_specs=(
            P(dp, tensor, None),
            P(dp, None, None),
            P(None, None, dp),
            P(None, None, dp),
            P(None, dp, None, tensor),
            P(None, tensor, dp),
            P(None, dp, tensor),
            P(None, dp, None, tensor),
            P(None, tensor, dp),
            P(None, dp, tensor),
            P(None, tensor, dp),
            P(dp, tensor, None),
        ),
        out_specs=(
            P(dp, tensor, None),
            P(dp, tensor, None),
            P(dp, None, None),
            P(None, None, dp),
            P(None, None, dp),
            P(None, dp, None, tensor),
            P(None, tensor, dp),
            P(None, dp, tensor),
            P(None, dp, None, tensor),
            P(None, tensor, dp),
            P(None, dp, tensor),
            P(None, tensor, dp),
        ),
        check_vma=False,
    )
```

time: 1320 us -> 1190 us (0.902)
  other arithmetic: 92.5 us -> 28.6 us
  local copies, waits for them, and re-layouts: 56.6 us -> 23.6 us
  Pallas kernels: 1130 us -> 1100 us
    convert_element_type x35 -> x2, other arithmetic: 42.3 us -> 3.36 us  [the longest x1 1.71 us: body(): more = [send_ride(grad_text.astype(BF16), 'c')] if l == 0 else []]
    concatenate x36 -> x3, other arithmetic: 30.2 us -> 1.87 us  [__init__(): self.ins.append(jnp.concatenate([norm[0], norm[1]], axis=0))]
    pallas_call x36 -> x23, Pallas kernels: 1130 us -> 1100 us  [launch(): pl.pallas_call(kernel, out_shape=tuple(out_shapes), in_specs=[ANY] * len(...]
    slice x21 -> x0, local copies, waits for them, and re-layouts: 23.3 us -> none  [fold_later(): table = {k: chunk[k * part:(k + 1) * part] for k in range(blocks)}]
  transfers between devices with their start and end apart: 2 -> 0, of which waited for: 1 -> 0; matrix products, arithmetic and copies ran while one was open for 1% -> 0% of each run, Pallas kernels for 0% -> 0%
where the time goes in v4:
time: 1190 us; the launch traced here: 1180 us
  Pallas kernels  1100 us (92%)
  other arithmetic  28.6 us (2%)
  local copies, waits for them, and re-layouts  23.6 us (2%)
  matrix products  23.6 us (2%)
    pallas_call x23, Pallas kernels, launch(): pl.pallas_call(kernel, out_shape=tuple(out_shapes), in_specs=[ANY] * len(...  1100 us

profile of v4, /device:TPU:0, one launch (start us, length us, event | category | flops | bytes accessed | tf_op | source)
XLA Modules:
  0.0 1180.4 jit_solution(7037018839553412608)
XLA Ops:
  13.3 5.5 fusion
  18.8 35.8 %move_0.1 = (bf16[1536,1152]{1,0:T(8,128)(2,1)}, bf16[1536,128]{1,0:T(8,128)(2,1)}, bf16[64,1536]{1,0:T(8,128)(2,1)}, bf16[256,1536]{1,0:T(8,128)(2,1)}) custom-call(bf16[192,1152]{1,0:T(8,128)(2,1)} %bitcast.206, bf16[192,128]{1,0:T(8,128)(2,1)} %pad.9.refs_1_, bf16[64,1536]{1,0:T(8,128)(2,1)} %bitcast.214, bf16[256,1536]{1,0:T(8,128)(2,1)} %bitcast.213), custom_call_target="tpu_custom_call" | custom-call | tf_op jit(solution)/shard_map/move_0/pallas_call | solution.py:405
  54.6 3.9 convolution_convert_fusion.3.refs_1_.refs_4_
  58.6 2.6 fusion.5.refs_0_.refs_2_
  64.1 52.5 %step_1.1 = (bf16[4,256,1536]{2,1,0:T(8,128)(2,1)}, bf16[4,256,1152]{2,1,0:T(8,128)(2,1)}, bf16[1536,1152]{1,0:T(8,128)(2,1)}, bf16[1536,384]{1,0:T(8,128)(2,1)}...) custom-call(f32[256,1536]{1,0:T(8,128)} %fusion.5.refs_0_.refs_2_, ...), custom_call_target="tpu_custom_call", output_to_operand_aliasing={{2}: (2, {})} | custom-call | tf_op jit(solution)/shard_map/step_1/pallas_call | solution.py:405
  116.7 25.3 %step_2.1 = (bf16[4,256,384]{2,1,0:T(8,128)(2,1)}, f32[6,1024]{1,0:T(8,128)}, bf16[1536,384]{1,0:T(8,128)(2,1)}, bf16[1536,384]{1,0:T(8,128)(2,1)}, bf16[1536,1536]{1,0:T(8,128)(2,1)}) custom-call(bf16[4,256,1152]{2,1,0:T(8,128)(2,1)} %get-tuple-element.175.refs_0_, ...), custom_call_target="tpu_custom_call", output_to_operand_aliasing={{2}: (1, {}), {3}: (2, {})} | custom-call | tf_op jit(solution)/shard_map/step_2/pallas_call | solution.py:405
  141.9 59.9 %step_3.1 = (f32[256,1536]{1,0:T(8,128)}, bf16[4,256,1536]{2,1,0:T(8,128)(2,1)}, bf16[4,256,384]{2,1,0:T(8,128)(2,1)}, bf16[1536,768]{1,0:T(8,128)(2,1)}, bf16[1...) custom-call(bf16[1024,384]{1,0:T(8,128)(2,1)} %bitcast.188, ...), custom_call_target="tpu_custom_call", output_to_operand_aliasing={{3}: (5, {}), {4}: (6, {}), {5}: (7, {})} | custom-call | tf_op jit(solution)/shard_map/step_3/pallas_call | solution.py:405
  201.8 16.4 %step_4.1 = (bf16[4,256,384]{2,1,0:T(8,128)(2,1)}, f32[6,1024]{1,0:T(8,128)}, bf16[64,768]{1,0:T(8,128)(2,1)}, bf16[1536,1536]{1,0:T(8,128)(2,1)}) custom-call(bf16[4,256,384]{2,1,0:T(8,128)(2,1)} %get-tuple-element.184.refs_0_, bf16[64,1536]{1,0:T(8,128)(2,1)} %convolution_convert_fusion.3.refs_1_.refs_4_, ...), custom_call_target="tpu_custom_call", output_to_operand_aliasing={{3}: (3, {})} | custom-call | tf_op jit(solution)/shard_map/step_4/pallas_call | solution.py:405
  218.3 56.1 %step_5.1 = (f32[256,1536]{1,0:T(8,128)}, bf16[4,256,1536]{2,1,0:T(8,128)(2,1)}, bf16[4,256,1536]{2,1,0:T(8,128)(2,1)}, bf16[4,256,1536]{2,1,0:T(8,128)(2,1)}, b...) custom-call(bf16[1024,384]{1,0:T(8,128)(2,1)} %bitcast.198, ...), custom_call_target="tpu_custom_call", output_to_operand_aliasing={{4}: (4, {}), {5}: (5, {})} | custom-call | tf_op jit(solution)/shard_map/step_5/pallas_call | solution.py:405
  274.4 62.6 %step_6.1 = (f32[256,1536]{1,0:T(8,128)}, bf16[4,256,1536]{2,1,0:T(8,128)(2,1)}, bf16[4,256,1152]{2,1,0:T(8,128)(2,1)}, bf16[1536,1152]{1,0:T(8,128)(2,1)}, bf16...) custom-call(bf16[1024,1536]{1,0:T(8,128)(2,1)} %bitcast.178, ...), custom_call_target="tpu_custom_call", output_to_operand_aliasing={{3}: (4, {})} | custom-call | tf_op jit(solution)/shard_map/step_6/pallas_call | solution.py:405
  337.0 23.5 %step_7.1 = (bf16[4,256,384]{2,1,0:T(8,128)(2,1)}, f32[6,1024]{1,0:T(8,128)}, bf16[1536,384]{1,0:T(8,128)(2,1)}, bf16[1536,384]{1,0:T(8,128)(2,1)}, bf16[1536,1536]{1,0:T(8,128)(2,1)}) custom-call(bf16[4,256,1152]{2,1,0:T(8,128)(2,1)} %get-tuple-element.197.refs_0_, ...), custom_call_target="tpu_custom_call", output_to_operand_aliasing={{2}: (1, {}), {3}: (2, {})} | custom-call | tf_op jit(solution)/shard_map/step_7/pallas_call | solution.py:405
  360.5 61.3 %step_8.1 = (f32[256,1536]{1,0:T(8,128)}, bf16[4,256,1536]{2,1,0:T(8,128)(2,1)}, bf16[4,256,384]{2,1,0:T(8,128)(2,1)}, bf16[1536,768]{1,0:T(8,128)(2,1)}, bf16[1...) custom-call(bf16[1024,384]{1,0:T(8,128)(2,1)} %bitcast.200, ...), custom_call_target="tpu_custom_call", output_to_operand_aliasing={{3}: (5, {}), {4}: (6, {}), {5}: (7, {})} | custom-call | tf_op jit(solution)/shard_map/step_8/pallas_call | solution.py:405
  421.7 16.1 %step_9.1 = (bf16[4,256,384]{2,1,0:T(8,128)(2,1)}, f32[6,1024]{1,0:T(8,128)}, bf16[64,768]{1,0:T(8,128)(2,1)}, bf16[1536,1536]{1,0:T(8,128)(2,1)}) custom-call(bf16[4,256,384]{2,1,0:T(8,128)(2,1)} %get-tuple-element.207.refs_0_, bf16[64,1536]{1,0:T(8,128)(2,1)} %convolution_convert_fusion.3.refs_1_.refs_4_, ...), custom_call_target="tpu_custom_call", output_to_operand_aliasing={{3}: (3, {})} | custom-call | tf_op jit(solution)/shard_map/step_9/pallas_call | solution.py:405
  437.8 54.6 %step_10.1 = (f32[256,1536]{1,0:T(8,128)}, bf16[4,256,1536]{2,1,0:T(8,128)(2,1)}, bf16[4,256,1536]{2,1,0:T(8,128)(2,1)}, bf16[4,256,1536]{2,1,0:T(8,128)(2,1)}, ...) custom-call(bf16[1024,384]{1,0:T(8,128)(2,1)} %bitcast.196, ...), custom_call_target="tpu_custom_call", output_to_operand_aliasing={{4}: (4, {}), {5}: (5, {})} | custom-call | tf_op jit(solution)/shard_map/step_10/pallas_call | solution.py:405
  492.5 4.2 fusion.3.refs_3_.refs_4_
  496.7 50.1 %step_11.1 = (f32[256,1536]{1,0:T(8,128)}, bf16[4,256,1536]{2,1,0:T(8,128)(2,1)}, bf16[4,256,1536]{2,1,0:T(8,128)(2,1)}) custom-call(bf16[1024,1536]{1,0:T(8,128)(2,1)} %bitcast.176, bf16[1536,1536]{1,0:T(8,128)(2,1)} %get-tuple-element.216.refs_1_.refs_4_, f32[256,1536]{1,0:T(8,128)} %get-tuple-element.217.refs_2_, f32[256,1536]{1,0:T(8,128)} %fusion.3.refs_3_.refs_4_, ...), custom_call_target="tpu_custom_call" | custom-call | tf_op jit(solution)/shard_map/step_11/pallas_call | solution.py:405
  546.8 4.4 convolution_convert_fusion.1.refs_9_
  551.2 53.3 %step_12.1 = (f32[256,1536]{1,0:T(8,128)}, f32[2,1536]{1,0:T(2,128)}, bf16[1536,1536]{1,0:T(8,128)(2,1)}, bf16[1536,1536]{1,0:T(8,128)(2,1)}, bf16[768,768]{1,0:...) custom-call(bf16[1024,1536]{1,0:T(8,128)(2,1)} %bitcast.187, ...), custom_call_target="tpu_custom_call" | custom-call | tf_op jit(solution)/shard_map/step_12/pallas_call | solution.py:405
  605.5 28.9 %step_13.1 = (bf16[4,256,384]{2,1,0:T(8,128)(2,1)}, bf16[1536,768]{1,0:T(8,128)(2,1)}, f32[64,1536]{1,0:T(8,128)}, bf16[768,768]{1,0:T(8,128)(2,1)}, bf16[768,768]{1,0:T(8,128)(2,1)}) custom-call(bf16[4,256,384]{2,1,0:T(8,128)(2,1)} %get-tuple-element.207.refs_0_, bf16[64,768]{1,0:T(8,128)(2,1)} %get-tuple-element.227.refs_1_, ...), custom_call_target="tpu_custom_call" | custom-call | tf_op jit(solution)/shard_map/step_13/pallas_call | solution.py:405
  634.5 67.0 %step_14.1 = (f32[256,1536]{1,0:T(8,128)}, f32[2,1536]{1,0:T(2,128)}, bf16[1536,384]{1,0:T(8,128)(2,1)}, bf16[1536,384]{1,0:T(8,128)(2,1)}, bf16[768,384]{1,0:T(...) custom-call(bf16[1024,384]{1,0:T(8,128)(2,1)} %bitcast.216, ...), custom_call_target="tpu_custom_call" | custom-call | tf_op jit(solution)/shard_map/step_14/pallas_call | solution.py:405
  701.5 48.6 %step_15.1 = (bf16[4,256,1152]{2,1,0:T(8,128)(2,1)}, f32[192,768]{1,0:T(8,128)}, f32[192,768]{1,0:T(8,128)}) custom-call(bf16[4,256,1152]{2,1,0:T(8,128)(2,1)} %get-tuple-element.197.refs_0_, bf16[4,256,384]{2,1,0:T(8,128)(2,1)} %get-tuple-element.239.refs_1_, f32[6,1024]{1,0:T(8,128)} %get-tuple-element.240.refs_2_, ...), custom_call_target="tpu_custom_call" | custom-call | tf_op jit(solution)/shard_map/step_15/pallas_call | solution.py:405
  750.1 63.5 %step_16.1 = (f32[256,1536]{1,0:T(8,128)}, f32[2,1536]{1,0:T(2,128)}, bf16[1536,384]{1,0:T(8,128)(2,1)}, bf16[1536,1152]{1,0:T(8,128)(2,1)}, bf16[768,384]{1,0:T...) custom-call(bf16[1024,1152]{1,0:T(8,128)(2,1)} %bitcast.202, ...), custom_call_target="tpu_custom_call" | custom-call | tf_op jit(solution)/shard_map/step_16/pallas_call | solution.py:405
  813.6 64.4 %step_17.1 = (f32[256,1536]{1,0:T(8,128)}, f32[2,1536]{1,0:T(2,128)}, bf16[1536,1536]{1,0:T(8,128)(2,1)}, bf16[1536,1536]{1,0:T(8,128)(2,1)}, bf16[768,768]{1,0:...) custom-call(bf16[1024,1536]{1,0:T(8,128)(2,1)} %bitcast.184, ...), custom_call_target="tpu_custom_call" | custom-call | tf_op jit(solution)/shard_map/step_17/pallas_call | solution.py:405
  883.0 28.8 %step_18.1 = (bf16[4,256,384]{2,1,0:T(8,128)(2,1)}, bf16[1536,768]{1,0:T(8,128)(2,1)}, f32[64,1536]{1,0:T(8,128)}, bf16[768,768]{1,0:T(8,128)(2,1)}, bf16[768,768]{1,0:T(8,128)(2,1)}) custom-call(bf16[4,256,384]{2,1,0:T(8,128)(2,1)} %get-tuple-element.184.refs_0_, bf16[64,768]{1,0:T(8,128)(2,1)} %get-tuple-element.226.refs_1_, ...), custom_call_target="tpu_custom_call" | custom-call | tf_op jit(solution)/shard_map/step_18/pallas_call | solution.py:405
  913.5 64.1 %step_19.1 = (f32[256,1536]{1,0:T(8,128)}, f32[2,1536]{1,0:T(2,128)}, bf16[1536,384]{1,0:T(8,128)(2,1)}, bf16[1536,384]{1,0:T(8,128)(2,1)}, bf16[768,384]{1,0:T(...) custom-call(bf16[1024,384]{1,0:T(8,128)(2,1)} %bitcast.215, ...), custom_call_target="tpu_custom_call" | custom-call | tf_op jit(solution)/shard_map/step_19/pallas_call | solution.py:405
  979.3 49.5 %step_20.1 = (bf16[4,256,1152]{2,1,0:T(8,128)(2,1)}, f32[192,768]{1,0:T(8,128)}, f32[192,768]{1,0:T(8,128)}, bf16[64,1536]{1,0:T(8,128)(2,1)}) custom-call(bf16[4,256,1152]{2,1,0:T(8,128)(2,1)} %get-tuple-element.175.refs_0_, bf16[4,256,384]{2,1,0:T(8,128)(2,1)} %get-tuple-element.278.refs_1_, f32[6,1024]{1,0:T(8,128)} %get-tuple-element.279.refs_2_, ...), custom_call_target="tpu_custom_call" | custom-call | tf_op jit(solution)/shard_map/step_20/pallas_call | solution.py:405
  1028.8 3.9 convolution_convert_fusion.2.refs_8_
  1032.7 56.5 %step_21.1 = (f32[256,1536]{1,0:T(8,128)}, f32[2,1536]{1,0:T(2,128)}, bf16[1536,384]{1,0:T(8,128)(2,1)}, bf16[1536,1152]{1,0:T(8,128)(2,1)}, bf16[768,384]{1,0:T...) custom-call(bf16[1024,1152]{1,0:T(8,128)(2,1)} %bitcast.205, ...), custom_call_target="tpu_custom_call" | custom-call | tf_op jit(solution)/shard_map/step_21/pallas_call | solution.py:405
  1089.3 4.5 convolution_convert_fusion.refs_7_
  1096.9 63.9 %move_22.1 = (f32[192,384]{1,0:T(8,128)}, f32[192,640]{1,0:T(8,128)}, f32[192,512]{1,0:T(8,128)}, f32[192,128]{1,0:T(8,128)}, bf16[256,1536]{1,0:T(8,128)(2,1)}, /*index=5*/bf16[64,1536]{1,0:T(8,128)(2,1)}) custom-call(bf16[1536,384]{1,0:T(8,128)(2,1)} %get-tuple-element.295.refs_0_, bf16[768,384]{1,0:T(8,128)(2,1)} %get-tuple-element.296.refs_1_, ...), custom_call_target="tpu_custom_call" | custom-call | tf_op jit(solution)/shard_map/move_22/pallas_call | solution.py:405
  1167.9 2.2 pad_maximum_fusion.4
  1170.2 2.3 stack_reshape.12
  (177 shorter events, 42.1 us)
Async XLA Ops:
  0.6 6.1 copy-start.15
  0.7 8.0 copy-start.11
  13.3 41.3 %copy-start.14 = (bf16[1,64,1536]{2,1,0:T(8,128)(2,1)S(1)}, bf16[1,64,1536]{2,1,0:T(8,128)(2,1)}, u32[]{:S(2)}) copy-start(bf16[1,64,1536]{2,1,0:T(8,128)(2,1)} %param.13) | copy-start | bytes 589828
  18.8 39.8 %copy-start.13 = (bf16[1,256,1536]{2,1,0:T(8,128)(2,1)S(1)}, bf16[1,256,1536]{2,1,0:T(8,128)(2,1)}, u32[]{:S(2)}) copy-start(bf16[1,256,1536]{2,1,0:T(8,128)(2,1)} %param.12) | copy-start | bytes 2359300
  54.6 3.9 copy-start
  61.8 54.8 %copy-start.39 = (f32[1,1536]{1,0:T(1,128)}, f32[1,1536]{1,0:T(1,128)S(1)}, u32[]{:S(2)}) copy-start(f32[1,1536]{1,0:T(1,128)S(1)} %get-tuple-element.372.refs_3_) | copy-start | bytes 18436
  61.8 54.8 %copy-start.40 = (f32[1,1536]{1,0:T(1,128)}, f32[1,1536]{1,0:T(1,128)S(1)}, u32[]{:S(2)}) copy-start(f32[1,1536]{1,0:T(1,128)S(1)} %get-tuple-element.377.refs_3_) | copy-start | bytes 18436
  61.8 54.8 %copy-start.41 = (f32[1,1536]{1,0:T(1,128)}, f32[1,1536]{1,0:T(1,128)S(1)}, u32[]{:S(2)}) copy-start(f32[1,1536]{1,0:T(1,128)S(1)} %get-tuple-element.375.refs_3_) | copy-start | bytes 18436
  61.8 54.8 %copy-start.42 = (f32[1,1536]{1,0:T(1,128)}, f32[1,1536]{1,0:T(1,128)S(1)}, u32[]{:S(2)}) copy-start(f32[1,1536]{1,0:T(1,128)S(1)} %get-tuple-element.374.refs_3_) | copy-start | bytes 18436
  61.8 54.8 %copy-start.43 = (f32[1,1536]{1,0:T(1,128)}, f32[1,1536]{1,0:T(1,128)S(1)}, u32[]{:S(2)}) copy-start(f32[1,1536]{1,0:T(1,128)S(1)} %get-tuple-element.376.refs_3_) | copy-start | bytes 18436
  61.9 54.8 %copy-start.44 = (f32[1,1536]{1,0:T(1,128)}, f32[1,1536]{1,0:T(1,128)S(1)}, u32[]{:S(2)}) copy-start(f32[1,1536]{1,0:T(1,128)S(1)} %get-tuple-element.373.refs_3_) | copy-start | bytes 18436
  437.8 54.6 %copy-start.12 = (bf16[1,256,1536]{2,1,0:T(8,128)(2,1)S(1)}, bf16[1,256,1536]{2,1,0:T(8,128)(2,1)}, u32[]{:S(2)}) copy-start(bf16[1,256,1536]{2,1,0:T(8,128)(2,1)} %param.23) | copy-start | bytes 2359300
  551.2 53.3 %copy-start.3 = (bf16[256,1536]{1,0:T(8,128)(2,1)S(1)}, bf16[256,1536]{1,0:T(8,128)(2,1)}, u32[]{:S(2)}) copy-start(bf16[256,1536]{1,0:T(8,128)(2,1)} %convolution_convert_fusion.1.refs_9_) | copy-start | bytes 2359300
  813.6 65.3 %copy-start.47 = (f32[2,1536]{1,0:T(2,128)S(1)}, f32[2,1536]{1,0:T(2,128)}, u32[]{:S(2)}) copy-start(f32[2,1536]{1,0:T(2,128)} %get-tuple-element.303) | copy-start | bytes 36868
  813.6 65.3 %copy-start.45 = (f32[2,1536]{1,0:T(2,128)S(1)}, f32[2,1536]{1,0:T(2,128)}, u32[]{:S(2)}) copy-start(f32[2,1536]{1,0:T(2,128)} %get-tuple-element.304) | copy-start | bytes 36868
  813.6 65.4 %copy-start.33 = (f32[192,384]{1,0:T(8,128)S(1)}, f32[192,384]{1,0:T(8,128)}, u32[]{:S(2)}) copy-start(f32[192,384]{1,0:T(8,128)} %get-tuple-element.320) | copy-start | bytes 884740
  813.6 65.4 %copy-start.34 = (f32[192,384]{1,0:T(8,128)S(1)}, f32[192,384]{1,0:T(8,128)}, u32[]{:S(2)}) copy-start(f32[192,384]{1,0:T(8,128)} %get-tuple-element.321) | copy-start | bytes 884740
  883.0 28.8 %copy-start.26 = (f32[64,1536]{1,0:T(8,128)S(1)}, f32[64,1536]{1,0:T(8,128)}, u32[]{:S(2)}) copy-start(f32[64,1536]{1,0:T(8,128)} %get-tuple-element.276) | copy-start | bytes 1179652
  913.5 64.1 %copy-start.6 = (bf16[64,1536]{1,0:T(8,128)(2,1)S(1)}, bf16[64,1536]{1,0:T(8,128)(2,1)}, u32[]{:S(2)}) copy-start(bf16[64,1536]{1,0:T(8,128)(2,1)} %add_convert_fusion.2.refs_15_) | copy-start | bytes 589828
  979.3 49.5 %copy-start.8 = (bf16[64,1536]{1,0:T(8,128)(2,1)S(1)}, bf16[64,1536]{1,0:T(8,128)(2,1)}, u32[]{:S(2)}) copy-start(bf16[64,1536]{1,0:T(8,128)(2,1)} %add_convert_fusion.1.refs_7_) | copy-start | bytes 589828
  1089.2 4.6 copy-start.48
  1089.2 4.6 copy-start.46
  1089.2 4.8 copy-start.30
  1089.3 4.8 copy-start.36
  1089.3 5.6 copy-start.29
  1089.3 5.6 copy-start.35
  1096.8 63.9 %copy-start.4 = (bf16[256,1536]{1,0:T(8,128)(2,1)S(1)}, bf16[256,1536]{1,0:T(8,128)(2,1)}, u32[]{:S(2)}) copy-start(bf16[256,1536]{1,0:T(8,128)(2,1)} %convolution_convert_fusion.refs_7_) | copy-start | bytes 2359300
  1160.8 3.4 copy-start.28
  1160.8 5.2 copy-start.31
  1162.1 3.9 copy-start.32
  1162.1 4.3 copy-start.5
  1167.9 4.5 copy-start.2
  (18 other events, 36.1 us)

commit v5 on v4

--- a/solution.py
+++ b/solution.py
@@ -116,7 +116,7 @@
             for kind, src, dst in stage:
                 self.copies[-1].append(Copy(kind, src, dst, send.at[place], recv.at[place]))
                 place += 1
-        self.level, self.levels = 0, len(self.copies)
+        self.level, self.levels, self.until = 0, len(self.copies), len(self.copies)
 
     def start(self):
         for copy in self.copies[0]:
@@ -132,10 +132,14 @@
 
 
 class Fold(Ride):
-    def __init__(self, grad, first, cols, order, blocks, came=None, sums=()):
-        self.rows, self.first, self.cols = grad.shape[0] // blocks, first, cols
+    def __init__(self, grad, first, cols, order, blocks, came=None, sums=(), phase="all"):
+        self.phase = phase
+        if phase == "pair":
+            order, blocks = [(None, 2)], 4
+        rows = grad.shape[0] // (2 if phase == "pair" else blocks)
+        half = rows * blocks // 2
+        self.rows, self.first, self.cols = rows, first, cols
         self.order, self.came, self.sums = order, came, list(sums)
-        rows, half = self.rows, grad.shape[0] // 2
         keys = list(range(blocks))
         self.away0 = [k for k in keys if k & order[0][1]]
         self.held = [k for k in keys if not k & order[0][1]]
@@ -143,7 +147,12 @@
         self.outs = [jax.ShapeDtypeStruct((rows, cols), F32)]
         self.alias = {}
         self.kinds = [name for name, _ in order[0 if came is None else 1 :]]
-        self.kinds += ["swap", "back"] + self.sums
+        if phase == "exchange":
+            self.outs = [jax.ShapeDtypeStruct((2 * rows, cols), BF16)]
+        elif phase == "pair":
+            self.kinds = ["swap", "back"]
+        else:
+            self.kinds += ["swap", "back"] + self.sums
         self.scratch = [pltpu.VMEM((half, cols), BF16), pltpu.VMEM((half, cols), BF16)]
         for level in range(1, len(order)):
             self.scratch.append(pltpu.VMEM((half >> level, cols), BF16))
@@ -154,7 +163,8 @@
             pltpu.SemaphoreType.DMA((blocks * 2 + 4,)),
             pltpu.SemaphoreType.DMA((blocks * 2 + 4,)),
         ]
-        self.levels = len(order) + 2 + len(self.sums)
+        self.levels = len(order) + (1 if phase == "exchange" else 2 + len(self.sums))
+        self.until = {"all": self.levels, "exchange": 1, "pair": 0}[phase]
 
     def chain(self, ins, outs, refs):
         self.in_refs, self.out = ins, outs[0]
@@ -176,6 +186,15 @@
         cols = pl.ds(self.first, self.cols)
         grad = self.in_refs[0]
         self.live, at = [], 0
+        if self.phase == "pair":
+            self.level = len(self.order)
+            copy = pltpu.make_async_copy(grad, self.own, self.load.at[0])
+            copy.start()
+            self.live = [copy] + [
+                self.remote(kind, grad.at[self.block(k)], self.pair.at[self.block(k)])
+                for k, kind in enumerate(("swap", "back"))
+            ]
+            return
         for i, (k, n) in enumerate(runs(self.held)):
             copy = pltpu.make_async_copy(
                 grad.at[self.block(k, n), cols], self.own.at[self.block(at, n)], self.load.at[i])
@@ -224,11 +243,18 @@
                         name, self.own.at[self.block(p, n)],
                         self.got[level + 1].at[self.block(at, n)]))
                     at += n
+            elif self.phase == "exchange":
+                copy = pltpu.make_async_copy(
+                    self.own.at[self.block(0, 2)], self.out, self.load.at[0])
+                copy.start()
+                self.live = [copy]
             else:
                 self.live = [
                     self.remote("swap", self.own.at[self.block(0)], self.pair.at[self.block(0)]),
                     self.remote("back", self.own.at[self.block(1)], self.pair.at[self.block(1)]),
                 ]
+            return
+        if self.phase == "exchange":
             return
         if level == bits:
             def diagonal_sum():
@@ -346,7 +372,8 @@
 
     def advance(self, kind=object):
         for chain in self.chains:
-            if chain.levels - chain.level > 1 and isinstance(chain, kind):
+            more = chain.levels - chain.level > 1 and chain.level < chain.until
+            if more and isinstance(chain, kind):
                 chain.step()
 
     def finish(self, i):
@@ -360,7 +387,7 @@
                     chain.step()
 
 
-def launch(name, number, parts, rides, limit=62):
+def launch(name, number, parts, rides, quick=(), limit=62):
     ins = [x for p in parts for x in p.ins]
     outs = [x for p in parts for x in p.outs]
     in_arrays, out_shapes = list(ins), list(outs)
@@ -400,6 +427,10 @@
             p.run(under_way)
         for p in parts:
             p.settle()
+        if quick:
+            under_way.advance(Fold)
+        for i in quick:
+            under_way.finish(i)
         under_way.end()
 
     results = pl.pallas_call(
@@ -1173,8 +1204,8 @@
             held[key] = value[0]
         return outs, [e[0] for e in extra[len(keys):]]
 
-    def move(rides):
-        return launch(f"move_{counter[0]}", number(), [], rides)[1]
+    def move(rides, quick=()):
+        return launch(f"move_{counter[0]}", number(), [], rides, quick)[1]
 
     extra = move([
         chain_ride(shards[0, "self"], halves("self"), early, blocks),
@@ -1209,7 +1240,7 @@
         saved.update(two=stream, second=second, query=query)
 
         (((joined, logsum, pairs),), _) = forward(
-            [attend_cross(query, text_own, held[l, "kv"], scale)], [f"{l}d2"])
+            [attend_cross(query, text_own, held[l, "kv"], scale)], [f"{l}d2", f"{n}k1"])
         saved.update(pairs=pairs, joined_cross=joined, logsum_cross=logsum)
         hand = Gather(None, size, norm_of(l, 2), 0, width, hidden, "gelu")
         more = [send_ride(cotangent[0], "swap")] if n == layers else []
@@ -1223,7 +1254,7 @@
             hand = Gather(None, size, norm_of(n, 0), 0, width, 3 * cols)
             (((stream,), (first, proj)), _) = forward(
                 [Scatter(active, held[l, "down"], stream, None, [], hand), hand],
-                [f"{n}a4", f"{n}o1", f"{n}q1", f"{n}k1", f"{n}u1"])
+                [f"{n}a4", f"{n}o1", f"{n}q1", f"{n}u1"])
         else:
             grad = reorder(jnp.where(diagonal(), cotangent[0], extra[0]))
             gather = Gather(grad, size, None, held[l, "down"], width, hidden, slope=slope)
@@ -1240,7 +1271,7 @@
         for i, (first, n, order) in enumerate(halves(name)):
             folding.append({"key": (l, name, first), "grad": value.astype(BF16), "first": first,
                             "cols": n, "order": list(reversed(order)),
-                            "came": came[i] if came else None})
+                            "came": came[i] if came else None, "pair": None})
 
     def first_sends(name):
         sends = []
@@ -1250,10 +1281,12 @@
             sends.append((axis, [(k * part, count * part) for k, count in away], first, n))
         return sends
 
-    def fold_ride(item):
+    def fold_ride(item, phase="all"):
+        if phase == "pair":
+            return Fold(item["pair"], 0, item["cols"], None, 4, phase=phase)
         sums = ("zl", "zh") if item["key"][1] == "norm" else ()
         return Fold(item["grad"], item["first"], item["cols"], item["order"], blocks,
-                    item["came"], sums)
+                    item["came"], sums, phase)
 
     def first_ride(item):
         name, weight = item["order"][0]
@@ -1271,17 +1304,25 @@
 
         return Ride([grad], [out], stages, [name] * len(away), len(away))
 
-    def folds(parts, end=(), begin=(), more=()):
-        ending = [i for i in folding if i["key"][:2] in end]
-        beginning = [i for i in folding if i["key"][:2] in begin]
-        rides = [fold_ride(i) for i in ending] + [first_ride(i) for i in beginning]
+    def folds(parts, begin=(), exchange=(), pair=(), end=(), more=()):
+        def of(names):
+            return [i for i in folding if i["key"][:2] in names]
+
+        begins, exchanges, pairs, ends = of(begin), of(exchange), of(pair), of(end)
+        rides = [first_ride(i) for i in begins]
+        rides += [fold_ride(i, "exchange") for i in exchanges]
+        rides += [fold_ride(i, "pair") for i in pairs]
+        rides += [fold_ride(i) for i in ends]
         outs, extra = launch(f"step_{counter[0]}", number(), parts, rides + list(more))
-        for item, came in zip(ending, extra):
-            finished[item["key"]] = came[0]
+        extra = [e[0] for e in extra]
+        for item in begins:
+            item["came"] = extra.pop(0)
+        for item in exchanges:
+            item["pair"] = extra.pop(0)
+        for item in pairs + ends:
+            finished[item["key"]] = extra.pop(0)
             folding.remove(item)
-        for item, came in zip(beginning, extra[len(ending):]):
-            item["came"] = came[0]
-        return outs, [e[0] for e in extra[len(rides):]]
+        return outs, extra
 
     for l in reversed(range(layers)):
         saved = records[l]
@@ -1291,7 +1332,8 @@
                  (flat(saved["third"]), None, [])]
         (((grad, norm_grads[l, 2], down, up_, *came), (full, grad_joined)), extra) = folds(
             [Scatter(grad_upper, held[l, "up"], None, (saved["three"], gains[l, 2], grad), fills,
-                     hand), hand], [(l + 1, "self_out"), (l + 1, "self")], (), more)
+                     hand), hand], exchange=[(l + 1, "self_out"), (l + 1, "self")],
+            pair=[(l + 1, "out"), (l + 1, "q"), (l + 1, "kv")], more=more)
         if more:
             result = jnp.where(diagonal(), result_own, extra[0])
         fold_later(l, "down", down, came)
@@ -1300,7 +1342,7 @@
         (((grad_query, kv_, text_part),), _) = folds(
             [attend_cross_back(saved["query"], saved["pairs"], grad_joined,
                                saved["logsum_cross"], text_own, held[l, "kv"], scale)],
-            (), [(l, "up")])
+            begin=[(l, "up")], pair=[(l + 1, "self_out"), (l + 1, "self")])
         grad_text = grad_text + text_part
         fold_later(l, "kv", kv_)
         more = [send_ride(grad_text.astype(BF16), "c")] if l == 0 else []
@@ -1309,7 +1351,7 @@
                  (flat(saved["second"]), None, first_sends("q"))]
         (((grad, norm_grads[l, 1], out_, q_, *came), (full, grad_joined)), extra) = folds(
             [Scatter(grad_query, held[l, "q"], None, (saved["two"], gains[l, 1], grad), fills,
-                     hand), hand], [(l, "down")], [(l, "kv")], more)
+                     hand), hand], begin=[(l, "kv")], exchange=[(l, "down")], more=more)
         fold_later(l, "out", out_, came[:1])
         fold_later(l, "q", q_, came[1:])
         if more:
@@ -1318,7 +1360,7 @@
 
         (((grad_proj,),), extra) = folds(
             [attend_self_back(saved["proj"], grad_joined, saved["logsum_self"], scale)],
-            [(l, "up")], (), more)
+            exchange=[(l, "up")], pair=[(l, "down")], more=more)
         if more:
             grad_text = grad_text.astype(BF16).astype(F32) + extra[0].astype(F32)
         fills = [(flat(full), flat(saved["joined_self"]), first_sends("self_out")),
@@ -1330,7 +1372,8 @@
                           slope=records[l - 1]["slope"])
             parts = [Scatter(grad_proj, held[l, "self"], None, chain, fills, hand), hand]
         (((grad, norm_grads[l, 0], out_, self_, *came), *after), _) = folds(
-            parts, [(l, "out"), (l, "q"), (l, "kv")])
+            parts, pair=[(l, "up")],
+            **{"exchange" if l else "end": [(l, "out"), (l, "q"), (l, "kv")]})
         if l:
             ((full, grad_upper),) = after
         fold_later(l, "self_out", out_, came[:1])
@@ -1343,7 +1386,9 @@
     frames_back = reorder(grad.astype(BF16)).astype(BF16)
     text_back = reorder(grad_text.astype(BF16)).astype(BF16)
     folds_left = [fold_ride(item) for item in folding]
-    extra = move(folds_left + [send_ride(frames_back, "swap"), send_ride(text_back, "swap")])
+    quick = [i for i, item in enumerate(folding) if item["key"][1] == "norm"]
+    extra = move(
+        folds_left + [send_ride(frames_back, "swap"), send_ride(text_back, "swap")], quick)
     for item, came in zip(folding, extra):
         finished[item["key"]] = came[0]
     grad_frames, text_sum = [

time: 1190 us -> 1110 us (0.933)
  Pallas kernels: 1100 us -> 1020 us
    pallas_call x23, Pallas kernels: 1100 us -> 1020 us  [launch(): pl.pallas_call(kernel, out_shape=tuple(out_shapes), in_specs=[ANY] * len(...]
where the time goes in v5:
time: 1110 us; the launch traced here: 1100 us
  Pallas kernels  1020 us (92%)
  other arithmetic  30.6 us (3%)
  local copies, waits for them, and re-layouts  23.7 us (2%)
  matrix products  23.6 us (2%)
    pallas_call x23, Pallas kernels, launch(): pl.pallas_call(kernel, out_shape=tuple(out_shapes), in_specs=[ANY] * len(...  1020 us
    dot_general x6, matrix products, nn(): lax.dot_general(a, b, (((1,), (0,)), ((), ())), preferred_element_type=F32)  23.6 us

profile of v5, /device:TPU:0, one launch (start us, length us, event | category | flops | bytes accessed | tf_op | source)
XLA Modules:
  0.0 1104.4 jit_solution(11332471844516261558)
XLA Ops:
  13.3 5.5 fusion
  18.8 35.8 %move_0.1 = (bf16[1536,1152]{1,0:T(8,128)(2,1)}, bf16[1536,128]{1,0:T(8,128)(2,1)}, bf16[64,1536]{1,0:T(8,128)(2,1)}, bf16[256,1536]{1,0:T(8,128)(2,1)}) custom-call(bf16[192,1152]{1,0:T(8,128)(2,1)} %bitcast.206, bf16[192,128]{1,0:T(8,128)(2,1)} %pad.9.refs_1_, bf16[64,1536]{1,0:T(8,128)(2,1)} %bitcast.214, bf16[256,1536]{1,0:T(8,128)(2,1)} %bitcast.213), custom_call_target="tpu_custom_call" | custom-call | tf_op jit(solution)/shard_map/move_0/pallas_call | solution.py:436
  54.7 3.9 convolution_convert_fusion.3.refs_1_.refs_4_
  58.6 2.6 fusion.5.refs_0_.refs_2_
  64.1 52.5 %step_1.1 = (bf16[4,256,1536]{2,1,0:T(8,128)(2,1)}, bf16[4,256,1152]{2,1,0:T(8,128)(2,1)}, bf16[1536,1152]{1,0:T(8,128)(2,1)}, bf16[1536,384]{1,0:T(8,128)(2,1)}...) custom-call(f32[256,1536]{1,0:T(8,128)} %fusion.5.refs_0_.refs_2_, ...), custom_call_target="tpu_custom_call", output_to_operand_aliasing={{2}: (2, {})} | custom-call | tf_op jit(solution)/shard_map/step_1/pallas_call | solution.py:436
  116.7 25.3 %step_2.1 = (bf16[4,256,384]{2,1,0:T(8,128)(2,1)}, f32[6,1024]{1,0:T(8,128)}, bf16[1536,384]{1,0:T(8,128)(2,1)}, bf16[1536,384]{1,0:T(8,128)(2,1)}, bf16[1536,1536]{1,0:T(8,128)(2,1)}) custom-call(bf16[4,256,1152]{2,1,0:T(8,128)(2,1)} %get-tuple-element.190.refs_0_, ...), custom_call_target="tpu_custom_call", output_to_operand_aliasing={{2}: (1, {}), {3}: (2, {})} | custom-call | tf_op jit(solution)/shard_map/step_2/pallas_call | solution.py:436
  141.9 59.9 %step_3.1 = (f32[256,1536]{1,0:T(8,128)}, bf16[4,256,1536]{2,1,0:T(8,128)(2,1)}, bf16[4,256,384]{2,1,0:T(8,128)(2,1)}, bf16[1536,768]{1,0:T(8,128)(2,1)}, bf16[1...) custom-call(bf16[1024,384]{1,0:T(8,128)(2,1)} %bitcast.188, ...), custom_call_target="tpu_custom_call", output_to_operand_aliasing={{3}: (5, {}), {4}: (6, {}), {5}: (7, {})} | custom-call | tf_op jit(solution)/shard_map/step_3/pallas_call | solution.py:436
  201.8 16.5 %step_4.1 = (bf16[4,256,384]{2,1,0:T(8,128)(2,1)}, f32[6,1024]{1,0:T(8,128)}, bf16[64,768]{1,0:T(8,128)(2,1)}, bf16[1536,1536]{1,0:T(8,128)(2,1)}, bf16[1536,768]{1,0:T(8,128)(2,1)}) custom-call(bf16[4,256,384]{2,1,0:T(8,128)(2,1)} %get-tuple-element.199.refs_0_, ...), custom_call_target="tpu_custom_call", output_to_operand_aliasing={{3}: (3, {})} | custom-call | tf_op jit(solution)/shard_map/step_4/pallas_call | solution.py:436
  218.3 56.3 %step_5.1 = (f32[256,1536]{1,0:T(8,128)}, bf16[4,256,1536]{2,1,0:T(8,128)(2,1)}, bf16[4,256,1536]{2,1,0:T(8,128)(2,1)}, bf16[4,256,1536]{2,1,0:T(8,128)(2,1)}, b...) custom-call(bf16[1024,384]{1,0:T(8,128)(2,1)} %bitcast.198, ...), custom_call_target="tpu_custom_call", output_to_operand_aliasing={{4}: (4, {}), {5}: (5, {})} | custom-call | tf_op jit(solution)/shard_map/step_5/pallas_call | solution.py:436
  274.6 56.0 %step_6.1 = (f32[256,1536]{1,0:T(8,128)}, bf16[4,256,1536]{2,1,0:T(8,128)(2,1)}, bf16[4,256,1152]{2,1,0:T(8,128)(2,1)}, bf16[1536,1152]{1,0:T(8,128)(2,1)}, bf16...) custom-call(bf16[1024,1536]{1,0:T(8,128)(2,1)} %bitcast.178, ...), custom_call_target="tpu_custom_call", output_to_operand_aliasing={{3}: (4, {})} | custom-call | tf_op jit(solution)/shard_map/step_6/pallas_call | solution.py:436
  330.6 23.4 %step_7.1 = (bf16[4,256,384]{2,1,0:T(8,128)(2,1)}, f32[6,1024]{1,0:T(8,128)}, bf16[1536,384]{1,0:T(8,128)(2,1)}, bf16[1536,384]{1,0:T(8,128)(2,1)}, bf16[1536,1536]{1,0:T(8,128)(2,1)}) custom-call(bf16[4,256,1152]{2,1,0:T(8,128)(2,1)} %get-tuple-element.212.refs_0_, ...), custom_call_target="tpu_custom_call", output_to_operand_aliasing={{2}: (1, {}), {3}: (2, {})} | custom-call | tf_op jit(solution)/shard_map/step_7/pallas_call | solution.py:436
  354.0 61.6 %step_8.1 = (f32[256,1536]{1,0:T(8,128)}, bf16[4,256,1536]{2,1,0:T(8,128)(2,1)}, bf16[4,256,384]{2,1,0:T(8,128)(2,1)}, bf16[1536,768]{1,0:T(8,128)(2,1)}, bf16[1...) custom-call(bf16[1024,384]{1,0:T(8,128)(2,1)} %bitcast.200, ...), custom_call_target="tpu_custom_call", output_to_operand_aliasing={{3}: (5, {}), {4}: (6, {}), {5}: (7, {})} | custom-call | tf_op jit(solution)/shard_map/step_8/pallas_call | solution.py:436
  415.7 16.1 %step_9.1 = (bf16[4,256,384]{2,1,0:T(8,128)(2,1)}, f32[6,1024]{1,0:T(8,128)}, bf16[64,768]{1,0:T(8,128)(2,1)}, bf16[1536,1536]{1,0:T(8,128)(2,1)}) custom-call(bf16[4,256,384]{2,1,0:T(8,128)(2,1)} %get-tuple-element.222.refs_0_, bf16[64,1536]{1,0:T(8,128)(2,1)} %convolution_convert_fusion.3.refs_1_.refs_4_, ...), custom_call_target="tpu_custom_call", output_to_operand_aliasing={{3}: (3, {})} | custom-call | tf_op jit(solution)/shard_map/step_9/pallas_call | solution.py:436
  431.8 54.6 %step_10.1 = (f32[256,1536]{1,0:T(8,128)}, bf16[4,256,1536]{2,1,0:T(8,128)(2,1)}, bf16[4,256,1536]{2,1,0:T(8,128)(2,1)}, bf16[4,256,1536]{2,1,0:T(8,128)(2,1)}, ...) custom-call(bf16[1024,384]{1,0:T(8,128)(2,1)} %bitcast.196, ...), custom_call_target="tpu_custom_call", output_to_operand_aliasing={{4}: (4, {}), {5}: (5, {})} | custom-call | tf_op jit(solution)/shard_map/step_10/pallas_call | solution.py:436
  486.4 4.2 fusion.3.refs_3_.refs_4_
  490.7 49.5 %step_11.1 = (f32[256,1536]{1,0:T(8,128)}, bf16[4,256,1536]{2,1,0:T(8,128)(2,1)}, bf16[4,256,1536]{2,1,0:T(8,128)(2,1)}) custom-call(bf16[1024,1536]{1,0:T(8,128)(2,1)} %bitcast.176, bf16[1536,1536]{1,0:T(8,128)(2,1)} %get-tuple-element.231.refs_1_.refs_4_, f32[256,1536]{1,0:T(8,128)} %get-tuple-element.232.refs_2_, f32[256,1536]{1,0:T(8,128)} %fusion.3.refs_3_.refs_4_, ...), custom_call_target="tpu_custom_call" | custom-call | tf_op jit(solution)/shard_map/step_11/pallas_call | solution.py:436
  540.2 4.4 convolution_convert_fusion.1.refs_9_
  544.7 54.1 %step_12.1 = (f32[256,1536]{1,0:T(8,128)}, f32[2,1536]{1,0:T(2,128)}, bf16[1536,1536]{1,0:T(8,128)(2,1)}, bf16[1536,1536]{1,0:T(8,128)(2,1)}, bf16[768,768]{1,0:...) custom-call(bf16[1024,1536]{1,0:T(8,128)(2,1)} %bitcast.187, ...), custom_call_target="tpu_custom_call" | custom-call | tf_op jit(solution)/shard_map/step_12/pallas_call | solution.py:436
  599.8 28.9 %step_13.1 = (bf16[4,256,384]{2,1,0:T(8,128)(2,1)}, bf16[1536,768]{1,0:T(8,128)(2,1)}, f32[64,1536]{1,0:T(8,128)}, bf16[768,768]{1,0:T(8,128)(2,1)}, bf16[768,768]{1,0:T(8,128)(2,1)}) custom-call(bf16[4,256,384]{2,1,0:T(8,128)(2,1)} %get-tuple-element.222.refs_0_, bf16[64,768]{1,0:T(8,128)(2,1)} %get-tuple-element.242.refs_1_, ...), custom_call_target="tpu_custom_call" | custom-call | tf_op jit(solution)/shard_map/step_13/pallas_call | solution.py:436
  628.7 44.8 %step_14.1 = (f32[256,1536]{1,0:T(8,128)}, f32[2,1536]{1,0:T(2,128)}, bf16[1536,384]{1,0:T(8,128)(2,1)}, bf16[1536,384]{1,0:T(8,128)(2,1)}, bf16[768,384]{1,0:T(...) custom-call(bf16[1024,384]{1,0:T(8,128)(2,1)} %bitcast.216, ...), custom_call_target="tpu_custom_call" | custom-call | tf_op jit(solution)/shard_map/step_14/pallas_call | solution.py:436
  673.4 32.5 %step_15.1 = (bf16[4,256,1152]{2,1,0:T(8,128)(2,1)}, bf16[384,768]{1,0:T(8,128)(2,1)}, bf16[384,768]{1,0:T(8,128)(2,1)}, f32[192,768]{1,0:T(8,128)}, f32[192,768]{1,0:T(8,128)}) custom-call(bf16[4,256,1152]{2,1,0:T(8,128)(2,1)} %get-tuple-element.212.refs_0_, bf16[4,256,384]{2,1,0:T(8,128)(2,1)} %get-tuple-element.254.refs_1_, ...), custom_call_target="tpu_custom_call" | custom-call | tf_op jit(solution)/shard_map/step_15/pallas_call | solution.py:436
  705.9 62.8 %step_16.1 = (f32[256,1536]{1,0:T(8,128)}, f32[2,1536]{1,0:T(2,128)}, bf16[1536,384]{1,0:T(8,128)(2,1)}, bf16[1536,1152]{1,0:T(8,128)(2,1)}, bf16[768,384]{1,0:T...) custom-call(bf16[1024,1152]{1,0:T(8,128)(2,1)} %bitcast.202, ...), custom_call_target="tpu_custom_call" | custom-call | tf_op jit(solution)/shard_map/step_16/pallas_call | solution.py:436
  768.8 61.2 %step_17.1 = (f32[256,1536]{1,0:T(8,128)}, f32[2,1536]{1,0:T(2,128)}, bf16[1536,1536]{1,0:T(8,128)(2,1)}, bf16[1536,1536]{1,0:T(8,128)(2,1)}, bf16[768,768]{1,0:...) custom-call(bf16[1024,1536]{1,0:T(8,128)(2,1)} %bitcast.184, ...), custom_call_target="tpu_custom_call" | custom-call | tf_op jit(solution)/shard_map/step_17/pallas_call | solution.py:436
  834.5 31.8 %step_18.1 = (bf16[4,256,384]{2,1,0:T(8,128)(2,1)}, bf16[1536,768]{1,0:T(8,128)(2,1)}, f32[64,1536]{1,0:T(8,128)}, bf16[768,768]{1,0:T(8,128)(2,1)}, bf16[768,76...) custom-call(bf16[4,256,384]{2,1,0:T(8,128)(2,1)} %get-tuple-element.199.refs_0_, ...), custom_call_target="tpu_custom_call" | custom-call | tf_op jit(solution)/shard_map/step_18/pallas_call | solution.py:436
  868.1 44.7 %step_19.1 = (f32[256,1536]{1,0:T(8,128)}, f32[2,1536]{1,0:T(2,128)}, bf16[1536,384]{1,0:T(8,128)(2,1)}, bf16[1536,384]{1,0:T(8,128)(2,1)}, bf16[768,384]{1,0:T(...) custom-call(bf16[1024,384]{1,0:T(8,128)(2,1)} %bitcast.215, ...), custom_call_target="tpu_custom_call" | custom-call | tf_op jit(solution)/shard_map/step_19/pallas_call | solution.py:436
  914.5 32.4 %step_20.1 = (bf16[4,256,1152]{2,1,0:T(8,128)(2,1)}, bf16[384,768]{1,0:T(8,128)(2,1)}, bf16[384,768]{1,0:T(8,128)(2,1)}, f32[192,768]{1,0:T(8,128)}, f32[192,768]{1,0:T(8,128)}, /*index=5*/bf16[64,1536]{1,0:T(8,128)(2,1)}) custom-call(bf16[4,256,1152]{2,1,0:T(8,128)(2,1)} %get-tuple-element.190.refs_0_, bf16[4,256,384]{2,1,0:T(8,128)(2,1)} %get-tuple-element.304.refs_1_, ...), custom_call_target="tpu_custom_call" | custom-call | tf_op jit(solution)/shard_map/step_20/pallas_call | solution.py:436
  946.9 3.9 convolution_convert_fusion.2.refs_8_
  950.8 58.5 %step_21.1 = (f32[256,1536]{1,0:T(8,128)}, f32[2,1536]{1,0:T(2,128)}, bf16[1536,384]{1,0:T(8,128)(2,1)}, bf16[1536,1152]{1,0:T(8,128)(2,1)}, bf16[768,384]{1,0:T...) custom-call(bf16[1024,1152]{1,0:T(8,128)(2,1)} %bitcast.203, ...), custom_call_target="tpu_custom_call" | custom-call | tf_op jit(solution)/shard_map/step_21/pallas_call | solution.py:436
  1009.3 4.5 convolution_convert_fusion.refs_7_
  1016.9 65.4 %move_22.1 = (f32[192,384]{1,0:T(8,128)}, f32[192,640]{1,0:T(8,128)}, f32[192,512]{1,0:T(8,128)}, f32[192,128]{1,0:T(8,128)}, bf16[256,1536]{1,0:T(8,128)(2,1)}, /*index=5*/bf16[64,1536]{1,0:T(8,128)(2,1)}) custom-call(bf16[1536,384]{1,0:T(8,128)(2,1)} %get-tuple-element.325.refs_0_, bf16[768,384]{1,0:T(8,128)(2,1)} %get-tuple-element.326.refs_1_, ...), custom_call_target="tpu_custom_call" | custom-call | tf_op jit(solution)/shard_map/move_22/pallas_call | solution.py:436
  1088.5 2.2 pad_maximum_fusion.4
  1094.1 2.3 stack_reshape.13
  (171 shorter events, 44.4 us)
Async XLA Ops:
  0.6 6.1 copy-start.14
  0.7 8.0 copy-start.10
  13.3 41.3 %copy-start.13 = (bf16[1,64,1536]{2,1,0:T(8,128)(2,1)S(1)}, bf16[1,64,1536]{2,1,0:T(8,128)(2,1)}, u32[]{:S(2)}) copy-start(bf16[1,64,1536]{2,1,0:T(8,128)(2,1)} %param.13) | copy-start | bytes 589828
  18.8 39.8 %copy-start.12 = (bf16[1,256,1536]{2,1,0:T(8,128)(2,1)S(1)}, bf16[1,256,1536]{2,1,0:T(8,128)(2,1)}, u32[]{:S(2)}) copy-start(bf16[1,256,1536]{2,1,0:T(8,128)(2,1)} %param.12) | copy-start | bytes 2359300
  54.7 3.9 copy-start
  61.8 54.8 %copy-start.36 = (f32[1,1536]{1,0:T(1,128)}, f32[1,1536]{1,0:T(1,128)S(1)}, u32[]{:S(2)}) copy-start(f32[1,1536]{1,0:T(1,128)S(1)} %get-tuple-element.402.refs_3_) | copy-start | bytes 18436
  61.8 54.8 %copy-start.37 = (f32[1,1536]{1,0:T(1,128)}, f32[1,1536]{1,0:T(1,128)S(1)}, u32[]{:S(2)}) copy-start(f32[1,1536]{1,0:T(1,128)S(1)} %get-tuple-element.407.refs_3_) | copy-start | bytes 18436
  61.9 54.8 %copy-start.38 = (f32[1,1536]{1,0:T(1,128)}, f32[1,1536]{1,0:T(1,128)S(1)}, u32[]{:S(2)}) copy-start(f32[1,1536]{1,0:T(1,128)S(1)} %get-tuple-element.405.refs_3_) | copy-start | bytes 18436
  61.9 54.8 %copy-start.39 = (f32[1,1536]{1,0:T(1,128)}, f32[1,1536]{1,0:T(1,128)S(1)}, u32[]{:S(2)}) copy-start(f32[1,1536]{1,0:T(1,128)S(1)} %get-tuple-element.404.refs_3_) | copy-start | bytes 18436
  61.9 54.8 %copy-start.40 = (f32[1,1536]{1,0:T(1,128)}, f32[1,1536]{1,0:T(1,128)S(1)}, u32[]{:S(2)}) copy-start(f32[1,1536]{1,0:T(1,128)S(1)} %get-tuple-element.406.refs_3_) | copy-start | bytes 18436
  61.9 54.8 %copy-start.41 = (f32[1,1536]{1,0:T(1,128)}, f32[1,1536]{1,0:T(1,128)S(1)}, u32[]{:S(2)}) copy-start(f32[1,1536]{1,0:T(1,128)S(1)} %get-tuple-element.403.refs_3_) | copy-start | bytes 18436
  431.8 54.7 %copy-start.11 = (bf16[1,256,1536]{2,1,0:T(8,128)(2,1)S(1)}, bf16[1,256,1536]{2,1,0:T(8,128)(2,1)}, u32[]{:S(2)}) copy-start(bf16[1,256,1536]{2,1,0:T(8,128)(2,1)} %param.23) | copy-start | bytes 2359300
  544.7 54.1 %copy-start.2 = (bf16[256,1536]{1,0:T(8,128)(2,1)S(1)}, bf16[256,1536]{1,0:T(8,128)(2,1)}, u32[]{:S(2)}) copy-start(bf16[256,1536]{1,0:T(8,128)(2,1)} %convolution_convert_fusion.1.refs_9_) | copy-start | bytes 2359300
  768.8 62.0 %copy-start.44 = (f32[2,1536]{1,0:T(2,128)S(1)}, f32[2,1536]{1,0:T(2,128)}, u32[]{:S(2)}) copy-start(f32[2,1536]{1,0:T(2,128)} %get-tuple-element.333) | copy-start | bytes 36868
  768.8 62.0 %copy-start.42 = (f32[2,1536]{1,0:T(2,128)S(1)}, f32[2,1536]{1,0:T(2,128)}, u32[]{:S(2)}) copy-start(f32[2,1536]{1,0:T(2,128)} %get-tuple-element.334) | copy-start | bytes 36868
  829.9 3.3 copy-start.21
  830.9 3.5 copy-start.19
  830.9 3.5 copy-start.20
  834.5 31.9 %copy-start.24 = (f32[64,1536]{1,0:T(8,128)S(1)}, f32[64,1536]{1,0:T(8,128)}, u32[]{:S(2)}) copy-start(f32[64,1536]{1,0:T(8,128)} %get-tuple-element.302) | copy-start | bytes 1179652
  868.1 44.7 %copy-start.6 = (bf16[64,1536]{1,0:T(8,128)(2,1)S(1)}, bf16[64,1536]{1,0:T(8,128)(2,1)}, u32[]{:S(2)}) copy-start(bf16[64,1536]{1,0:T(8,128)(2,1)} %add_convert_fusion.2.refs_15_) | copy-start | bytes 589828
  914.5 32.4 %copy-start.5 = (bf16[64,1536]{1,0:T(8,128)(2,1)S(1)}, bf16[64,1536]{1,0:T(8,128)(2,1)}, u32[]{:S(2)}) copy-start(bf16[64,1536]{1,0:T(8,128)(2,1)} %add_convert_fusion.1.refs_9_) | copy-start | bytes 589828
  1009.2 4.6 copy-start.45
  1009.3 4.6 copy-start.43
  1009.3 4.8 copy-start.27
  1009.3 4.8 copy-start.32
  1009.3 5.6 copy-start.26
  1009.3 5.6 copy-start.31
  1016.9 65.4 %copy-start.3 = (bf16[256,1536]{1,0:T(8,128)(2,1)S(1)}, bf16[256,1536]{1,0:T(8,128)(2,1)}, u32[]{:S(2)}) copy-start(bf16[256,1536]{1,0:T(8,128)(2,1)} %convolution_convert_fusion.refs_7_) | copy-start | bytes 2359300
  1082.3 3.4 copy-start.28
  1082.3 3.4 copy-start.33
  1083.6 3.3 copy-start.4
  1088.5 3.6 copy-start.23
  (15 other events, 30.9 us)

commit v6 on v5

--- a/solution.py
+++ b/solution.py
@@ -497,7 +497,7 @@
             pltpu.SemaphoreType.DMA((4,)),
             pltpu.SemaphoreType.DMA((6,)),
             pltpu.SemaphoreType.DMA((6,)),
-            pltpu.SemaphoreType.DMA((3, 4)),
+            pltpu.SemaphoreType.DMA((3, 6)),
         ]
 
     def early(self, in_refs, out_refs, refs):
@@ -553,39 +553,38 @@
             self.loads["slope"].wait()
         stores = []
 
-        def multiply(b):
+        def multiply(b, rows, slot):
             def step(j, carry):
                 cols = pl.ds(pl.multiple_of(j * tile, tile), tile)
-                value = nn(x[b], w[:, cols])
+                value = nn(x[b, rows, :], w[:, cols])
                 if self.double:
-                    y[b, :, cols], second[b, :, cols] = gelu_pair(value)
+                    y[b, rows, cols], second[b, rows, cols] = gelu_pair(value)
                 elif self.has_slope:
-                    y[b, :, cols] = (value * second[b, :, cols].astype(F32)).astype(BF16)
+                    y[b, rows, cols] = (value * second[b, rows, cols].astype(F32)).astype(BF16)
                 else:
-                    y[b, :, cols] = value.astype(BF16)
+                    y[b, rows, cols] = value.astype(BF16)
                 return carry
 
             lax.fori_loop(0, n // tile, step, 0)
             for k, ref in enumerate([x, y] + ([second] if self.double else [])):
                 stores.append(pltpu.make_async_copy(
-                    ref.at[b], self.out_refs[k].at[b], self.store.at[k, b]))
+                    ref.at[b, rows], self.out_refs[k].at[b, rows], self.store.at[k, slot]))
                 stores[-1].start()
 
-        multiply(0)
+        whole = pl.ds(0, self.size)
+
+        multiply(0, whole, 0)
         self.beside.wait()
-        multiply(1)
+        multiply(1, whole, 1)
         self.filler()
-        relay = []
         for h in range(2):
             part = pl.ds(h * half, half)
             self.over[h].wait()
-            relay.append(Copy("c", x.at[2, part], x.at[3, part],
-                              self.send.at[3 + h], self.recv.at[3 + h]))
-            relay[-1].start()
-        multiply(2)
-        for copy in relay:
-            copy.wait()
-        multiply(3)
+            relay = Copy("c", x.at[2, part], x.at[3, part], self.send.at[3 + h], self.recv.at[3 + h])
+            relay.start()
+            multiply(2, part, 2 + h)
+            relay.wait()
+            multiply(3, part, 4 + h)
         for copy in stores:
             copy.wait()
 
@@ -1150,6 +1149,7 @@
     row = lax.broadcasted_iota(jnp.int32, (width, width), 0)
     col = lax.broadcasted_iota(jnp.int32, (width, width), 1)
     permute = ((row // part == ((col // part) ^ me)) & (row % part == col % part)).astype(BF16)
+    permute = lax.optimization_barrier(permute)
 
     def reorder(value):
         return nn(value, permute)
@@ -1163,7 +1163,9 @@
 
     def halves(name):
         n = sizes[name]
-        if name in ("self", "kv", "up", "down"):
+        if name == "up":
+            return [(i * n // 4, n // 4, up if i % 2 else low_first) for i in range(4)]
+        if name in ("self", "kv", "down"):
             first = (n // 2 + 127) // 128 * 128
             return [(0, first, low_first), (first, n - first, up)]
         return [(0, n, low_first if name in ("q", "norm") else up)]
@@ -1306,7 +1308,7 @@
 
     def folds(parts, begin=(), exchange=(), pair=(), end=(), more=()):
         def of(names):
-            return [i for i in folding if i["key"][:2] in names]
+            return [i for i in folding if i["key"][:2] in names or i["key"] in names]
 
         begins, exchanges, pairs, ends = of(begin), of(exchange), of(pair), of(end)
         rides = [first_ride(i) for i in begins]
@@ -1342,7 +1344,7 @@
         (((grad_query, kv_, text_part),), _) = folds(
             [attend_cross_back(saved["query"], saved["pairs"], grad_joined,
                                saved["logsum_cross"], text_own, held[l, "kv"], scale)],
-            begin=[(l, "up")], pair=[(l + 1, "self_out"), (l + 1, "self")])
+            begin=[(l, "up", 0), (l, "up", hidden // 4)], pair=[(l + 1, "self", 0)])
         grad_text = grad_text + text_part
         fold_later(l, "kv", kv_)
         more = [send_ride(grad_text.astype(BF16), "c")] if l == 0 else []
@@ -1351,7 +1353,8 @@
                  (flat(saved["second"]), None, first_sends("q"))]
         (((grad, norm_grads[l, 1], out_, q_, *came), (full, grad_joined)), extra) = folds(
             [Scatter(grad_query, held[l, "q"], None, (saved["two"], gains[l, 1], grad), fills,
-                     hand), hand], begin=[(l, "kv")], exchange=[(l, "down")], more=more)
+                     hand), hand], begin=[(l, "up", hidden // 2), (l, "up", hidden // 4 * 3)],
+            exchange=[(l, "down")], pair=[(l + 1, "self"), (l + 1, "self_out")], more=more)
         fold_later(l, "out", out_, came[:1])
         fold_later(l, "q", q_, came[1:])
         if more:
@@ -1360,7 +1363,7 @@
 
         (((grad_proj,),), extra) = folds(
             [attend_self_back(saved["proj"], grad_joined, saved["logsum_self"], scale)],
-            exchange=[(l, "up")], pair=[(l, "down")], more=more)
+            begin=[(l, "kv")], exchange=[(l, "up")], pair=[(l, "down")], more=more)
         if more:
             grad_text = grad_text.astype(BF16).astype(F32) + extra[0].astype(F32)
         fills = [(flat(full), flat(saved["joined_self"]), first_sends("self_out")),

time: 1110 us -> 1080 us (0.973)
  Pallas kernels: 1020 us -> 1000 us
    pallas_call x23, Pallas kernels: 1020 us -> 1000 us  [launch(): pl.pallas_call(kernel, out_shape=tuple(out_shapes), in_specs=[ANY] * len(...]
where the time goes in v6:
time: 1080 us; the launch traced here: 1070 us
  Pallas kernels  1000 us (93%)
  matrix products  23.3 us (2%)
  other arithmetic  22.3 us (2%)
  local copies, waits for them, and re-layouts  21.5 us (2%)
    pallas_call x23, Pallas kernels, launch(): pl.pallas_call(kernel, out_shape=tuple(out_shapes), in_specs=[ANY] * len(...  1000 us
    dot_general x6, matrix products, nn(): lax.dot_general(a, b, (((1,), (0,)), ((), ())), preferred_element_type=F32)  23.3 us

profile of v6, /device:TPU:0, one launch (start us, length us, event | category | flops | bytes accessed | tf_op | source)
XLA Modules:
  0.0 1072.2 jit_solution(16089926923568933404)
XLA Ops:
  3.0 1.7 slice_bitcast_fusion.5
  4.8 1.9 slice_bitcast_fusion.4
  13.3 35.8 %move_0.1 = (bf16[1536,1152]{1,0:T(8,128)(2,1)}, bf16[1536,128]{1,0:T(8,128)(2,1)}, bf16[64,1536]{1,0:T(8,128)(2,1)}, bf16[256,1536]{1,0:T(8,128)(2,1)}) custom-call(bf16[192,1152]{1,0:T(8,128)(2,1)} %bitcast.206, bf16[192,128]{1,0:T(8,128)(2,1)} %pad.9.refs_1_, bf16[64,1536]{1,0:T(8,128)(2,1)} %bitcast.212, bf16[256,1536]{1,0:T(8,128)(2,1)} %bitcast.214), custom_call_target="tpu_custom_call" | custom-call | tf_op jit(solution)/shard_map/move_0/pallas_call | solution.py:436
  53.1 2.6 fusion.1
  58.4 2.5 fusion.6.refs_0_.refs_2_
  60.9 50.1 %step_1.1 = (bf16[4,256,1536]{2,1,0:T(8,128)(2,1)}, bf16[4,256,1152]{2,1,0:T(8,128)(2,1)}, bf16[1536,1152]{1,0:T(8,128)(2,1)}, bf16[1536,384]{1,0:T(8,128)(2,1)}...) custom-call(f32[256,1536]{1,0:T(8,128)} %fusion.6.refs_0_.refs_2_, ...), custom_call_target="tpu_custom_call", output_to_operand_aliasing={{2}: (2, {})} | custom-call | tf_op jit(solution)/shard_map/step_1/pallas_call | solution.py:436
  111.0 26.5 %step_2.1 = (bf16[4,256,384]{2,1,0:T(8,128)(2,1)}, f32[6,1024]{1,0:T(8,128)}, bf16[1536,384]{1,0:T(8,128)(2,1)}, bf16[1536,384]{1,0:T(8,128)(2,1)}, bf16[1536,1536]{1,0:T(8,128)(2,1)}) custom-call(bf16[4,256,1152]{2,1,0:T(8,128)(2,1)} %get-tuple-element.202.refs_0_, ...), custom_call_target="tpu_custom_call", output_to_operand_aliasing={{2}: (1, {}), {3}: (2, {})} | custom-call | tf_op jit(solution)/shard_map/step_2/pallas_call | solution.py:436
  137.5 59.1 %step_3.1 = (f32[256,1536]{1,0:T(8,128)}, bf16[4,256,1536]{2,1,0:T(8,128)(2,1)}, bf16[4,256,384]{2,1,0:T(8,128)(2,1)}, bf16[1536,768]{1,0:T(8,128)(2,1)}, bf16[1...) custom-call(bf16[1024,384]{1,0:T(8,128)(2,1)} %bitcast.190, ...), custom_call_target="tpu_custom_call", output_to_operand_aliasing={{3}: (5, {}), {4}: (6, {}), {5}: (7, {})} | custom-call | tf_op jit(solution)/shard_map/step_3/pallas_call | solution.py:436
  196.6 16.1 %step_4.1 = (bf16[4,256,384]{2,1,0:T(8,128)(2,1)}, f32[6,1024]{1,0:T(8,128)}, bf16[64,768]{1,0:T(8,128)(2,1)}, bf16[1536,1536]{1,0:T(8,128)(2,1)}, bf16[1536,768]{1,0:T(8,128)(2,1)}) custom-call(bf16[4,256,384]{2,1,0:T(8,128)(2,1)} %get-tuple-element.211.refs_0_, ...), custom_call_target="tpu_custom_call", output_to_operand_aliasing={{3}: (3, {})} | custom-call | tf_op jit(solution)/shard_map/step_4/pallas_call | solution.py:436
  212.7 55.7 %step_5.1 = (f32[256,1536]{1,0:T(8,128)}, bf16[4,256,1536]{2,1,0:T(8,128)(2,1)}, bf16[4,256,1536]{2,1,0:T(8,128)(2,1)}, bf16[4,256,1536]{2,1,0:T(8,128)(2,1)}, b...) custom-call(bf16[1024,384]{1,0:T(8,128)(2,1)} %bitcast.198, ...), custom_call_target="tpu_custom_call", output_to_operand_aliasing={{4}: (4, {}), {5}: (5, {})} | custom-call | tf_op jit(solution)/shard_map/step_5/pallas_call | solution.py:436
  268.5 55.1 %step_6.1 = (f32[256,1536]{1,0:T(8,128)}, bf16[4,256,1536]{2,1,0:T(8,128)(2,1)}, bf16[4,256,1152]{2,1,0:T(8,128)(2,1)}, bf16[1536,1152]{1,0:T(8,128)(2,1)}, bf16...) custom-call(bf16[1024,1536]{1,0:T(8,128)(2,1)} %bitcast.178, ...), custom_call_target="tpu_custom_call", output_to_operand_aliasing={{3}: (4, {})} | custom-call | tf_op jit(solution)/shard_map/step_6/pallas_call | solution.py:436
  323.6 24.1 %step_7.1 = (bf16[4,256,384]{2,1,0:T(8,128)(2,1)}, f32[6,1024]{1,0:T(8,128)}, bf16[1536,384]{1,0:T(8,128)(2,1)}, bf16[1536,384]{1,0:T(8,128)(2,1)}, bf16[1536,1536]{1,0:T(8,128)(2,1)}) custom-call(bf16[4,256,1152]{2,1,0:T(8,128)(2,1)} %get-tuple-element.224.refs_0_, ...), custom_call_target="tpu_custom_call", output_to_operand_aliasing={{2}: (1, {}), {3}: (2, {})} | custom-call | tf_op jit(solution)/shard_map/step_7/pallas_call | solution.py:436
  347.7 60.7 %step_8.1 = (f32[256,1536]{1,0:T(8,128)}, bf16[4,256,1536]{2,1,0:T(8,128)(2,1)}, bf16[4,256,384]{2,1,0:T(8,128)(2,1)}, bf16[1536,768]{1,0:T(8,128)(2,1)}, bf16[1...) custom-call(bf16[1024,384]{1,0:T(8,128)(2,1)} %bitcast.200, ...), custom_call_target="tpu_custom_call", output_to_operand_aliasing={{3}: (5, {}), {4}: (6, {}), {5}: (7, {})} | custom-call | tf_op jit(solution)/shard_map/step_8/pallas_call | solution.py:436
  408.3 16.1 %step_9.1 = (bf16[4,256,384]{2,1,0:T(8,128)(2,1)}, f32[6,1024]{1,0:T(8,128)}, bf16[64,768]{1,0:T(8,128)(2,1)}, bf16[1536,1536]{1,0:T(8,128)(2,1)}) custom-call(bf16[4,256,384]{2,1,0:T(8,128)(2,1)} %get-tuple-element.234.refs_0_, bf16[64,1536]{1,0:T(8,128)(2,1)} %convolution_convert_fusion.3.refs_1_.refs_4_, ...), custom_call_target="tpu_custom_call", output_to_operand_aliasing={{3}: (3, {})} | custom-call | tf_op jit(solution)/shard_map/step_9/pallas_call | solution.py:436
  424.4 54.0 %step_10.1 = (f32[256,1536]{1,0:T(8,128)}, bf16[4,256,1536]{2,1,0:T(8,128)(2,1)}, bf16[4,256,1536]{2,1,0:T(8,128)(2,1)}, bf16[4,256,1536]{2,1,0:T(8,128)(2,1)}, ...) custom-call(bf16[1024,384]{1,0:T(8,128)(2,1)} %bitcast.194, ...), custom_call_target="tpu_custom_call", output_to_operand_aliasing={{4}: (4, {}), {5}: (5, {})} | custom-call | tf_op jit(solution)/shard_map/step_10/pallas_call | solution.py:436
  478.4 4.9 fusion.4.refs_3_.refs_4_
  483.3 51.6 %step_11.1 = (f32[256,1536]{1,0:T(8,128)}, bf16[4,256,1536]{2,1,0:T(8,128)(2,1)}, bf16[4,256,1536]{2,1,0:T(8,128)(2,1)}) custom-call(bf16[1024,1536]{1,0:T(8,128)(2,1)} %bitcast.176, bf16[1536,1536]{1,0:T(8,128)(2,1)} %get-tuple-element.243.refs_1_.refs_4_, f32[256,1536]{1,0:T(8,128)} %get-tuple-element.244.refs_2_, f32[256,1536]{1,0:T(8,128)} %fusion.4.refs_3_.refs_4_, ...), custom_call_target="tpu_custom_call" | custom-call | tf_op jit(solution)/shard_map/step_11/pallas_call | solution.py:436
  534.9 5.1 convolution_convert_fusion.1.refs_9_
  540.0 52.5 %step_12.1 = (f32[256,1536]{1,0:T(8,128)}, f32[2,1536]{1,0:T(2,128)}, bf16[1536,1536]{1,0:T(8,128)(2,1)}, bf16[1536,1536]{1,0:T(8,128)(2,1)}, bf16[768,768]{1,0:...) custom-call(bf16[1024,1536]{1,0:T(8,128)(2,1)} %bitcast.189, ...), custom_call_target="tpu_custom_call" | custom-call | tf_op jit(solution)/shard_map/step_12/pallas_call | solution.py:436
  593.5 16.2 %step_13.1 = (bf16[4,256,384]{2,1,0:T(8,128)(2,1)}, bf16[1536,768]{1,0:T(8,128)(2,1)}, f32[64,1536]{1,0:T(8,128)}, bf16[768,384]{1,0:T(8,128)(2,1)}, bf16[768,384]{1,0:T(8,128)(2,1)}) custom-call(bf16[4,256,384]{2,1,0:T(8,128)(2,1)} %get-tuple-element.234.refs_0_, bf16[64,768]{1,0:T(8,128)(2,1)} %get-tuple-element.254.refs_1_, ...), custom_call_target="tpu_custom_call" | custom-call | tf_op jit(solution)/shard_map/step_13/pallas_call | solution.py:436
  609.8 44.5 %step_14.1 = (f32[256,1536]{1,0:T(8,128)}, f32[2,1536]{1,0:T(2,128)}, bf16[1536,384]{1,0:T(8,128)(2,1)}, bf16[1536,384]{1,0:T(8,128)(2,1)}, bf16[768,384]{1,0:T(...) custom-call(bf16[1024,384]{1,0:T(8,128)(2,1)} %bitcast.216, ...), custom_call_target="tpu_custom_call" | custom-call | tf_op jit(solution)/shard_map/step_14/pallas_call | solution.py:436
  654.3 33.6 %step_15.1 = (bf16[4,256,1152]{2,1,0:T(8,128)(2,1)}, bf16[768,384]{1,0:T(8,128)(2,1)}, bf16[768,384]{1,0:T(8,128)(2,1)}, bf16[384,384]{1,0:T(8,128)(2,1)}, bf16[...) custom-call(bf16[4,256,1152]{2,1,0:T(8,128)(2,1)} %get-tuple-element, ...), custom_call_target="tpu_custom_call" | custom-call | tf_op jit(solution)/shard_map/step_15/pallas_call | solution.py:436
  687.9 62.6 %step_16.1 = (f32[256,1536]{1,0:T(8,128)}, f32[2,1536]{1,0:T(2,128)}, bf16[1536,384]{1,0:T(8,128)(2,1)}, bf16[1536,1152]{1,0:T(8,128)(2,1)}, bf16[768,384]{1,0:T...) custom-call(bf16[1024,1152]{1,0:T(8,128)(2,1)} %bitcast.202, ...), custom_call_target="tpu_custom_call" | custom-call | tf_op jit(solution)/shard_map/step_16/pallas_call | solution.py:436
  750.5 60.9 %step_17.1 = (f32[256,1536]{1,0:T(8,128)}, f32[2,1536]{1,0:T(2,128)}, bf16[1536,1536]{1,0:T(8,128)(2,1)}, bf16[1536,1536]{1,0:T(8,128)(2,1)}, bf16[768,768]{1,0:...) custom-call(bf16[1024,1536]{1,0:T(8,128)(2,1)} %bitcast.185, ...), custom_call_target="tpu_custom_call" | custom-call | tf_op jit(solution)/shard_map/step_17/pallas_call | solution.py:436
  812.3 17.3 %step_18.1 = (bf16[4,256,384]{2,1,0:T(8,128)(2,1)}, bf16[1536,768]{1,0:T(8,128)(2,1)}, f32[64,1536]{1,0:T(8,128)}, bf16[768,384]{1,0:T(8,128)(2,1)}, bf16[768,384]{1,0:T(8,128)(2,1)}, /*index=5*/f32[192,640]{1,0:T(8,128)}) custom-call(bf16[4,256,384]{2,1,0:T(8,128)(2,1)} %get-tuple-element.211.refs_0_, bf16[64,768]{1,0:T(8,128)(2,1)} %get-tuple-element.253.refs_1_, ...), custom_call_target="tpu_custom_call" | custom-call | tf_op jit(solution)/shard_map/step_18/pallas_call | solution.py:436
  829.6 1.7 add_convert_fusion.2.refs_17_
  831.3 52.6 %step_19.1 = (f32[256,1536]{1,0:T(8,128)}, f32[2,1536]{1,0:T(2,128)}, bf16[1536,384]{1,0:T(8,128)(2,1)}, bf16[1536,384]{1,0:T(8,128)(2,1)}, bf16[768,384]{1,0:T(...) custom-call(bf16[1024,384]{1,0:T(8,128)(2,1)} %bitcast.215, ...), custom_call_target="tpu_custom_call" | custom-call | tf_op jit(solution)/shard_map/step_19/pallas_call | solution.py:436
  885.6 33.3 %step_20.1 = (bf16[4,256,1152]{2,1,0:T(8,128)(2,1)}, bf16[768,384]{1,0:T(8,128)(2,1)}, bf16[768,384]{1,0:T(8,128)(2,1)}, bf16[384,384]{1,0:T(8,128)(2,1)}, bf16[...) custom-call(bf16[4,256,1152]{2,1,0:T(8,128)(2,1)} %get-tuple-element, ...), custom_call_target="tpu_custom_call" | custom-call | tf_op jit(solution)/shard_map/step_20/pallas_call | solution.py:436
  918.9 4.0 convolution_convert_fusion.2.refs_8_
  923.0 59.4 %step_21.1 = (f32[256,1536]{1,0:T(8,128)}, f32[2,1536]{1,0:T(2,128)}, bf16[1536,384]{1,0:T(8,128)(2,1)}, bf16[1536,1152]{1,0:T(8,128)(2,1)}, bf16[768,384]{1,0:T...) custom-call(bf16[1024,1152]{1,0:T(8,128)(2,1)} %bitcast.203, ...), custom_call_target="tpu_custom_call" | custom-call | tf_op jit(solution)/shard_map/step_21/pallas_call | solution.py:436
  982.4 5.2 convolution_convert_fusion.refs_7_
  990.6 65.4 %move_22.1 = (f32[192,384]{1,0:T(8,128)}, f32[192,640]{1,0:T(8,128)}, f32[192,512]{1,0:T(8,128)}, f32[192,128]{1,0:T(8,128)}, bf16[256,1536]{1,0:T(8,128)(2,1)}, /*index=5*/bf16[64,1536]{1,0:T(8,128)(2,1)}) custom-call(bf16[1536,384]{1,0:T(8,128)(2,1)} %get-tuple-element.345.refs_0_, bf16[768,384]{1,0:T(8,128)(2,1)} %get-tuple-element.346.refs_1_, ...), custom_call_target="tpu_custom_call" | custom-call | tf_op jit(solution)/shard_map/move_22/pallas_call | solution.py:436
  (183 shorter events, 37.4 us)
Async XLA Ops:
  0.6 6.1 copy-start.12
  0.7 8.0 copy-start.8
  8.7 2.4 copy-start.6
  9.9 2.3 copy-start.7
  50.8 4.9 copy-start.41
  50.8 4.9 copy-start.42
  50.8 4.9 copy-start.43
  50.8 4.9 copy-start.44
  50.8 4.9 copy-start.45
  50.9 4.9 copy-start.46
  53.1 2.7 copy-start.9
  53.1 2.7 copy-start.38
  55.8 2.2 copy-start
  55.8 2.5 copy-start.52
  424.4 54.0 %copy-start.10 = (bf16[1,256,1536]{2,1,0:T(8,128)(2,1)S(1)}, bf16[1,256,1536]{2,1,0:T(8,128)(2,1)}, u32[]{:S(2)}) copy-start(bf16[1,256,1536]{2,1,0:T(8,128)(2,1)} %param.23) | copy-start | bytes 2359300
  540.0 52.5 %copy-start.1 = (bf16[256,1536]{1,0:T(8,128)(2,1)S(1)}, bf16[256,1536]{1,0:T(8,128)(2,1)}, u32[]{:S(2)}) copy-start(bf16[256,1536]{1,0:T(8,128)(2,1)} %convolution_convert_fusion.1.refs_9_) | copy-start | bytes 2359300
  750.5 61.7 %copy-start.49 = (f32[2,1536]{1,0:T(2,128)S(1)}, f32[2,1536]{1,0:T(2,128)}, u32[]{:S(2)}) copy-start(f32[2,1536]{1,0:T(2,128)} %get-tuple-element.353) | copy-start | bytes 36868
  750.5 61.7 %copy-start.47 = (f32[2,1536]{1,0:T(2,128)S(1)}, f32[2,1536]{1,0:T(2,128)}, u32[]{:S(2)}) copy-start(f32[2,1536]{1,0:T(2,128)} %get-tuple-element.354) | copy-start | bytes 36868
  812.3 17.3 %copy-start.19 = (f32[64,1536]{1,0:T(8,128)S(1)}, f32[64,1536]{1,0:T(8,128)}, u32[]{:S(2)}) copy-start(f32[64,1536]{1,0:T(8,128)} %get-tuple-element.317) | copy-start | bytes 1179652
  831.3 52.6 %copy-start.3 = (bf16[64,1536]{1,0:T(8,128)(2,1)S(1)}, bf16[64,1536]{1,0:T(8,128)(2,1)}, u32[]{:S(2)}) copy-start(bf16[64,1536]{1,0:T(8,128)(2,1)} %add_convert_fusion.2.refs_17_) | copy-start | bytes 589828
  885.6 33.4 %copy-start.4 = (bf16[64,1536]{1,0:T(8,128)(2,1)S(1)}, bf16[64,1536]{1,0:T(8,128)(2,1)}, u32[]{:S(2)}) copy-start(bf16[64,1536]{1,0:T(8,128)(2,1)} %add_convert_fusion.1.refs_15_) | copy-start | bytes 589828
  982.4 5.2 copy-start.50
  982.4 5.2 copy-start.48
  982.4 5.4 copy-start.31
  982.4 5.4 copy-start.36
  982.4 6.3 copy-start.30
  982.4 6.3 copy-start.35
  990.6 65.5 %copy-start.2 = (bf16[256,1536]{1,0:T(8,128)(2,1)S(1)}, bf16[256,1536]{1,0:T(8,128)(2,1)}, u32[]{:S(2)}) copy-start(bf16[256,1536]{1,0:T(8,128)(2,1)} %convolution_convert_fusion.refs_7_) | copy-start | bytes 2359300
  1056.0 3.4 copy-start.32
  1056.1 3.4 copy-start.37
  1056.1 4.2 copy-start.17
  1056.1 4.2 copy-start.18
  (21 other events, 30.7 us)

commit v7 on v6

--- a/solution.py
+++ b/solution.py
@@ -503,7 +503,7 @@
     def early(self, in_refs, out_refs, refs):
         self.rows, self.w, self.norms, self.x, self.y, self.second = refs[:6]
         self.load, self.send, self.recv, self.store = refs[6:]
-        self.out_refs, self.over = out_refs, []
+        self.out_refs, self.over, self.rest = out_refs, [], None
         todo, self.loads = list(in_refs), {}
         if self.has_rows:
             self.loads["rows"] = pltpu.make_async_copy(todo.pop(0), self.rows, self.load.at[0])
@@ -539,7 +539,7 @@
             for h in range(2):
                 self.send_half(h, self.rows)
 
-    def run(self, rides):
+    def near(self, rides):
         x, y, w, second, n = self.x, self.y, self.w, self.second, self.n
         tile, half = min(TILE, n), self.size // 2
         if self.ride is not None:
@@ -576,6 +576,13 @@
         multiply(0, whole, 0)
         self.beside.wait()
         multiply(1, whole, 1)
+        self.rest = multiply, stores
+
+    def run(self, rides):
+        if self.rest is None:
+            self.near(rides)
+        multiply, stores = self.rest
+        x, half = self.x, self.size // 2
         self.filler()
         for h in range(2):
             part = pl.ds(h * half, half)
@@ -643,6 +650,7 @@
         scratch += [pltpu.SemaphoreType.DMA((max(copies, 1),))] * 2
         self.kinds = ["c", "zl"] + [name for _, _, sends in fills for name, _, _, _ in sends]
         self.sends_at = sends_at
+        self.middle = lambda rides: None
         self.ins, self.outs, self.scratch = ins, outs, scratch
         self.facts = (size, n, width, half, base, norm, fills, fill_at, fill_cols, outs)
         self.hand = hand
@@ -784,6 +792,7 @@
                 self.hand.filler = job
             else:
                 job()
+        self.middle(rides)
         rides.advance()
         near.wait()
         total[...] += came[1].astype(F32)
@@ -1260,8 +1269,9 @@
         else:
             grad = reorder(jnp.where(diagonal(), cotangent[0], extra[0]))
             gather = Gather(grad, size, None, held[l, "down"], width, hidden, slope=slope)
-            (((stream,), (full, grad_upper)), _) = forward(
-                [Scatter(active, held[l, "down"], stream, None, []), gather])
+            scatter = Scatter(active, held[l, "down"], stream, None, [])
+            scatter.middle = gather.near
+            (((stream,), (full, grad_upper)), _) = forward([scatter, gather])
     result_own = reorder(stream.astype(BF16)).astype(BF16)
 
     folding = []

time: 1080 us -> 1070 us (level)
  no operation moved by 1% of the time
where the time goes in v7:
time: 1070 us
  Pallas kernels  999 us (93%)
  matrix products  23.3 us (2%)
  other arithmetic  22.3 us (2%)
  local copies, waits for them, and re-layouts  21.5 us (2%)
    pallas_call x23, Pallas kernels, launch(): pl.pallas_call(kernel, out_shape=tuple(out_shapes), in_specs=[ANY] * len(...  999 us
    dot_general x6, matrix products, nn(): lax.dot_general(a, b, (((1,), (0,)), ((), ())), preferred_element_type=F32)  23.3 us

profile of v7, /device:TPU:0, one launch (start us, length us, event | category | flops | bytes accessed | tf_op | source)
XLA Modules:
  0.0 1067.6 jit_solution(7863083778556817201)
XLA Ops:
  3.0 1.7 slice_bitcast_fusion.5
  4.8 1.9 slice_bitcast_fusion.4
  13.3 35.8 %move_0.1 = (bf16[1536,1152]{1,0:T(8,128)(2,1)}, bf16[1536,128]{1,0:T(8,128)(2,1)}, bf16[64,1536]{1,0:T(8,128)(2,1)}, bf16[256,1536]{1,0:T(8,128)(2,1)}) custom-call(bf16[192,1152]{1,0:T(8,128)(2,1)} %bitcast.206, bf16[192,128]{1,0:T(8,128)(2,1)} %pad.9.refs_1_, bf16[64,1536]{1,0:T(8,128)(2,1)} %bitcast.212, bf16[256,1536]{1,0:T(8,128)(2,1)} %bitcast.214), custom_call_target="tpu_custom_call" | custom-call | tf_op jit(solution)/shard_map/move_0/pallas_call | solution.py:436
  53.1 2.6 fusion.1
  58.4 2.5 fusion.6.refs_0_.refs_2_
  60.9 50.1 %step_1.1 = (bf16[4,256,1536]{2,1,0:T(8,128)(2,1)}, bf16[4,256,1152]{2,1,0:T(8,128)(2,1)}, bf16[1536,1152]{1,0:T(8,128)(2,1)}, bf16[1536,384]{1,0:T(8,128)(2,1)}...) custom-call(f32[256,1536]{1,0:T(8,128)} %fusion.6.refs_0_.refs_2_, ...), custom_call_target="tpu_custom_call", output_to_operand_aliasing={{2}: (2, {})} | custom-call | tf_op jit(solution)/shard_map/step_1/pallas_call | solution.py:436
  111.0 26.5 %step_2.1 = (bf16[4,256,384]{2,1,0:T(8,128)(2,1)}, f32[6,1024]{1,0:T(8,128)}, bf16[1536,384]{1,0:T(8,128)(2,1)}, bf16[1536,384]{1,0:T(8,128)(2,1)}, bf16[1536,1536]{1,0:T(8,128)(2,1)}) custom-call(bf16[4,256,1152]{2,1,0:T(8,128)(2,1)} %get-tuple-element.202.refs_0_, ...), custom_call_target="tpu_custom_call", output_to_operand_aliasing={{2}: (1, {}), {3}: (2, {})} | custom-call | tf_op jit(solution)/shard_map/step_2/pallas_call | solution.py:436
  137.5 59.1 %step_3.1 = (f32[256,1536]{1,0:T(8,128)}, bf16[4,256,1536]{2,1,0:T(8,128)(2,1)}, bf16[4,256,384]{2,1,0:T(8,128)(2,1)}, bf16[1536,768]{1,0:T(8,128)(2,1)}, bf16[1...) custom-call(bf16[1024,384]{1,0:T(8,128)(2,1)} %bitcast.190, ...), custom_call_target="tpu_custom_call", output_to_operand_aliasing={{3}: (5, {}), {4}: (6, {}), {5}: (7, {})} | custom-call | tf_op jit(solution)/shard_map/step_3/pallas_call | solution.py:436
  196.6 16.1 %step_4.1 = (bf16[4,256,384]{2,1,0:T(8,128)(2,1)}, f32[6,1024]{1,0:T(8,128)}, bf16[64,768]{1,0:T(8,128)(2,1)}, bf16[1536,1536]{1,0:T(8,128)(2,1)}, bf16[1536,768]{1,0:T(8,128)(2,1)}) custom-call(bf16[4,256,384]{2,1,0:T(8,128)(2,1)} %get-tuple-element.211.refs_0_, ...), custom_call_target="tpu_custom_call", output_to_operand_aliasing={{3}: (3, {})} | custom-call | tf_op jit(solution)/shard_map/step_4/pallas_call | solution.py:436
  212.7 55.7 %step_5.1 = (f32[256,1536]{1,0:T(8,128)}, bf16[4,256,1536]{2,1,0:T(8,128)(2,1)}, bf16[4,256,1536]{2,1,0:T(8,128)(2,1)}, bf16[4,256,1536]{2,1,0:T(8,128)(2,1)}, b...) custom-call(bf16[1024,384]{1,0:T(8,128)(2,1)} %bitcast.198, ...), custom_call_target="tpu_custom_call", output_to_operand_aliasing={{4}: (4, {}), {5}: (5, {})} | custom-call | tf_op jit(solution)/shard_map/step_5/pallas_call | solution.py:436
  268.5 55.1 %step_6.1 = (f32[256,1536]{1,0:T(8,128)}, bf16[4,256,1536]{2,1,0:T(8,128)(2,1)}, bf16[4,256,1152]{2,1,0:T(8,128)(2,1)}, bf16[1536,1152]{1,0:T(8,128)(2,1)}, bf16...) custom-call(bf16[1024,1536]{1,0:T(8,128)(2,1)} %bitcast.178, ...), custom_call_target="tpu_custom_call", output_to_operand_aliasing={{3}: (4, {})} | custom-call | tf_op jit(solution)/shard_map/step_6/pallas_call | solution.py:436
  323.6 24.1 %step_7.1 = (bf16[4,256,384]{2,1,0:T(8,128)(2,1)}, f32[6,1024]{1,0:T(8,128)}, bf16[1536,384]{1,0:T(8,128)(2,1)}, bf16[1536,384]{1,0:T(8,128)(2,1)}, bf16[1536,1536]{1,0:T(8,128)(2,1)}) custom-call(bf16[4,256,1152]{2,1,0:T(8,128)(2,1)} %get-tuple-element.224.refs_0_, ...), custom_call_target="tpu_custom_call", output_to_operand_aliasing={{2}: (1, {}), {3}: (2, {})} | custom-call | tf_op jit(solution)/shard_map/step_7/pallas_call | solution.py:436
  347.7 60.7 %step_8.1 = (f32[256,1536]{1,0:T(8,128)}, bf16[4,256,1536]{2,1,0:T(8,128)(2,1)}, bf16[4,256,384]{2,1,0:T(8,128)(2,1)}, bf16[1536,768]{1,0:T(8,128)(2,1)}, bf16[1...) custom-call(bf16[1024,384]{1,0:T(8,128)(2,1)} %bitcast.200, ...), custom_call_target="tpu_custom_call", output_to_operand_aliasing={{3}: (5, {}), {4}: (6, {}), {5}: (7, {})} | custom-call | tf_op jit(solution)/shard_map/step_8/pallas_call | solution.py:436
  408.3 16.1 %step_9.1 = (bf16[4,256,384]{2,1,0:T(8,128)(2,1)}, f32[6,1024]{1,0:T(8,128)}, bf16[64,768]{1,0:T(8,128)(2,1)}, bf16[1536,1536]{1,0:T(8,128)(2,1)}) custom-call(bf16[4,256,384]{2,1,0:T(8,128)(2,1)} %get-tuple-element.234.refs_0_, bf16[64,1536]{1,0:T(8,128)(2,1)} %convolution_convert_fusion.3.refs_1_.refs_4_, ...), custom_call_target="tpu_custom_call", output_to_operand_aliasing={{3}: (3, {})} | custom-call | tf_op jit(solution)/shard_map/step_9/pallas_call | solution.py:436
  424.4 54.0 %step_10.1 = (f32[256,1536]{1,0:T(8,128)}, bf16[4,256,1536]{2,1,0:T(8,128)(2,1)}, bf16[4,256,1536]{2,1,0:T(8,128)(2,1)}, bf16[4,256,1536]{2,1,0:T(8,128)(2,1)}, ...) custom-call(bf16[1024,384]{1,0:T(8,128)(2,1)} %bitcast.194, ...), custom_call_target="tpu_custom_call", output_to_operand_aliasing={{4}: (4, {}), {5}: (5, {})} | custom-call | tf_op jit(solution)/shard_map/step_10/pallas_call | solution.py:436
  478.4 4.9 fusion.4.refs_3_.refs_4_
  483.3 46.9 %step_11.1 = (f32[256,1536]{1,0:T(8,128)}, bf16[4,256,1536]{2,1,0:T(8,128)(2,1)}, bf16[4,256,1536]{2,1,0:T(8,128)(2,1)}) custom-call(bf16[1024,1536]{1,0:T(8,128)(2,1)} %bitcast.176, bf16[1536,1536]{1,0:T(8,128)(2,1)} %get-tuple-element.243.refs_1_.refs_4_, f32[256,1536]{1,0:T(8,128)} %get-tuple-element.244.refs_2_, f32[256,1536]{1,0:T(8,128)} %fusion.4.refs_3_.refs_4_, ...), custom_call_target="tpu_custom_call" | custom-call | tf_op jit(solution)/shard_map/step_11/pallas_call | solution.py:436
  530.3 5.1 convolution_convert_fusion.1.refs_9_
  535.3 52.5 %step_12.1 = (f32[256,1536]{1,0:T(8,128)}, f32[2,1536]{1,0:T(2,128)}, bf16[1536,1536]{1,0:T(8,128)(2,1)}, bf16[1536,1536]{1,0:T(8,128)(2,1)}, bf16[768,768]{1,0:...) custom-call(bf16[1024,1536]{1,0:T(8,128)(2,1)} %bitcast.189, ...), custom_call_target="tpu_custom_call" | custom-call | tf_op jit(solution)/shard_map/step_12/pallas_call | solution.py:436
  588.9 16.2 %step_13.1 = (bf16[4,256,384]{2,1,0:T(8,128)(2,1)}, bf16[1536,768]{1,0:T(8,128)(2,1)}, f32[64,1536]{1,0:T(8,128)}, bf16[768,384]{1,0:T(8,128)(2,1)}, bf16[768,384]{1,0:T(8,128)(2,1)}) custom-call(bf16[4,256,384]{2,1,0:T(8,128)(2,1)} %get-tuple-element.234.refs_0_, bf16[64,768]{1,0:T(8,128)(2,1)} %get-tuple-element.254.refs_1_, ...), custom_call_target="tpu_custom_call" | custom-call | tf_op jit(solution)/shard_map/step_13/pallas_call | solution.py:436
  605.1 44.5 %step_14.1 = (f32[256,1536]{1,0:T(8,128)}, f32[2,1536]{1,0:T(2,128)}, bf16[1536,384]{1,0:T(8,128)(2,1)}, bf16[1536,384]{1,0:T(8,128)(2,1)}, bf16[768,384]{1,0:T(...) custom-call(bf16[1024,384]{1,0:T(8,128)(2,1)} %bitcast.216, ...), custom_call_target="tpu_custom_call" | custom-call | tf_op jit(solution)/shard_map/step_14/pallas_call | solution.py:436
  649.7 33.6 %step_15.1 = (bf16[4,256,1152]{2,1,0:T(8,128)(2,1)}, bf16[768,384]{1,0:T(8,128)(2,1)}, bf16[768,384]{1,0:T(8,128)(2,1)}, bf16[384,384]{1,0:T(8,128)(2,1)}, bf16[...) custom-call(bf16[4,256,1152]{2,1,0:T(8,128)(2,1)} %get-tuple-element, ...), custom_call_target="tpu_custom_call" | custom-call | tf_op jit(solution)/shard_map/step_15/pallas_call | solution.py:436
  683.3 62.6 %step_16.1 = (f32[256,1536]{1,0:T(8,128)}, f32[2,1536]{1,0:T(2,128)}, bf16[1536,384]{1,0:T(8,128)(2,1)}, bf16[1536,1152]{1,0:T(8,128)(2,1)}, bf16[768,384]{1,0:T...) custom-call(bf16[1024,1152]{1,0:T(8,128)(2,1)} %bitcast.202, ...), custom_call_target="tpu_custom_call" | custom-call | tf_op jit(solution)/shard_map/step_16/pallas_call | solution.py:436
  745.9 60.9 %step_17.1 = (f32[256,1536]{1,0:T(8,128)}, f32[2,1536]{1,0:T(2,128)}, bf16[1536,1536]{1,0:T(8,128)(2,1)}, bf16[1536,1536]{1,0:T(8,128)(2,1)}, bf16[768,768]{1,0:...) custom-call(bf16[1024,1536]{1,0:T(8,128)(2,1)} %bitcast.185, ...), custom_call_target="tpu_custom_call" | custom-call | tf_op jit(solution)/shard_map/step_17/pallas_call | solution.py:436
  807.7 17.3 %step_18.1 = (bf16[4,256,384]{2,1,0:T(8,128)(2,1)}, bf16[1536,768]{1,0:T(8,128)(2,1)}, f32[64,1536]{1,0:T(8,128)}, bf16[768,384]{1,0:T(8,128)(2,1)}, bf16[768,384]{1,0:T(8,128)(2,1)}, /*index=5*/f32[192,640]{1,0:T(8,128)}) custom-call(bf16[4,256,384]{2,1,0:T(8,128)(2,1)} %get-tuple-element.211.refs_0_, bf16[64,768]{1,0:T(8,128)(2,1)} %get-tuple-element.253.refs_1_, ...), custom_call_target="tpu_custom_call" | custom-call | tf_op jit(solution)/shard_map/step_18/pallas_call | solution.py:436
  825.0 1.7 add_convert_fusion.2.refs_17_
  826.7 52.6 %step_19.1 = (f32[256,1536]{1,0:T(8,128)}, f32[2,1536]{1,0:T(2,128)}, bf16[1536,384]{1,0:T(8,128)(2,1)}, bf16[1536,384]{1,0:T(8,128)(2,1)}, bf16[768,384]{1,0:T(...) custom-call(bf16[1024,384]{1,0:T(8,128)(2,1)} %bitcast.215, ...), custom_call_target="tpu_custom_call" | custom-call | tf_op jit(solution)/shard_map/step_19/pallas_call | solution.py:436
  880.9 33.3 %step_20.1 = (bf16[4,256,1152]{2,1,0:T(8,128)(2,1)}, bf16[768,384]{1,0:T(8,128)(2,1)}, bf16[768,384]{1,0:T(8,128)(2,1)}, bf16[384,384]{1,0:T(8,128)(2,1)}, bf16[...) custom-call(bf16[4,256,1152]{2,1,0:T(8,128)(2,1)} %get-tuple-element, ...), custom_call_target="tpu_custom_call" | custom-call | tf_op jit(solution)/shard_map/step_20/pallas_call | solution.py:436
  914.3 4.0 convolution_convert_fusion.2.refs_8_
  918.3 59.4 %step_21.1 = (f32[256,1536]{1,0:T(8,128)}, f32[2,1536]{1,0:T(2,128)}, bf16[1536,384]{1,0:T(8,128)(2,1)}, bf16[1536,1152]{1,0:T(8,128)(2,1)}, bf16[768,384]{1,0:T...) custom-call(bf16[1024,1152]{1,0:T(8,128)(2,1)} %bitcast.203, ...), custom_call_target="tpu_custom_call" | custom-call | tf_op jit(solution)/shard_map/step_21/pallas_call | solution.py:436
  977.7 5.2 convolution_convert_fusion.refs_7_
  985.9 65.4 %move_22.1 = (f32[192,384]{1,0:T(8,128)}, f32[192,640]{1,0:T(8,128)}, f32[192,512]{1,0:T(8,128)}, f32[192,128]{1,0:T(8,128)}, bf16[256,1536]{1,0:T(8,128)(2,1)}, /*index=5*/bf16[64,1536]{1,0:T(8,128)(2,1)}) custom-call(bf16[1536,384]{1,0:T(8,128)(2,1)} %get-tuple-element.345.refs_0_, bf16[768,384]{1,0:T(8,128)(2,1)} %get-tuple-element.346.refs_1_, ...), custom_call_target="tpu_custom_call" | custom-call | tf_op jit(solution)/shard_map/move_22/pallas_call | solution.py:436
  (183 shorter events, 37.4 us)
Async XLA Ops:
  0.6 6.1 copy-start.12
  0.7 8.0 copy-start.8
  8.7 2.4 copy-start.6
  9.9 2.3 copy-start.7
  50.8 4.9 copy-start.41
  50.8 4.9 copy-start.42
  50.8 4.9 copy-start.43
  50.8 4.9 copy-start.44
  50.8 4.9 copy-start.45
  50.9 4.9 copy-start.46
  53.1 2.7 copy-start.9
  53.1 2.7 copy-start.38
  55.8 2.2 copy-start
  55.8 2.5 copy-start.52
  424.4 54.0 %copy-start.10 = (bf16[1,256,1536]{2,1,0:T(8,128)(2,1)S(1)}, bf16[1,256,1536]{2,1,0:T(8,128)(2,1)}, u32[]{:S(2)}) copy-start(bf16[1,256,1536]{2,1,0:T(8,128)(2,1)} %param.23) | copy-start | bytes 2359300
  535.3 52.5 %copy-start.1 = (bf16[256,1536]{1,0:T(8,128)(2,1)S(1)}, bf16[256,1536]{1,0:T(8,128)(2,1)}, u32[]{:S(2)}) copy-start(bf16[256,1536]{1,0:T(8,128)(2,1)} %convolution_convert_fusion.1.refs_9_) | copy-start | bytes 2359300
  745.9 61.7 %copy-start.49 = (f32[2,1536]{1,0:T(2,128)S(1)}, f32[2,1536]{1,0:T(2,128)}, u32[]{:S(2)}) copy-start(f32[2,1536]{1,0:T(2,128)} %get-tuple-element.353) | copy-start | bytes 36868
  745.9 61.7 %copy-start.47 = (f32[2,1536]{1,0:T(2,128)S(1)}, f32[2,1536]{1,0:T(2,128)}, u32[]{:S(2)}) copy-start(f32[2,1536]{1,0:T(2,128)} %get-tuple-element.354) | copy-start | bytes 36868
  807.7 17.3 %copy-start.19 = (f32[64,1536]{1,0:T(8,128)S(1)}, f32[64,1536]{1,0:T(8,128)}, u32[]{:S(2)}) copy-start(f32[64,1536]{1,0:T(8,128)} %get-tuple-element.317) | copy-start | bytes 1179652
  826.7 52.6 %copy-start.3 = (bf16[64,1536]{1,0:T(8,128)(2,1)S(1)}, bf16[64,1536]{1,0:T(8,128)(2,1)}, u32[]{:S(2)}) copy-start(bf16[64,1536]{1,0:T(8,128)(2,1)} %add_convert_fusion.2.refs_17_) | copy-start | bytes 589828
  880.9 33.3 %copy-start.4 = (bf16[64,1536]{1,0:T(8,128)(2,1)S(1)}, bf16[64,1536]{1,0:T(8,128)(2,1)}, u32[]{:S(2)}) copy-start(bf16[64,1536]{1,0:T(8,128)(2,1)} %add_convert_fusion.1.refs_15_) | copy-start | bytes 589828
  977.7 5.2 copy-start.50
  977.7 5.2 copy-start.48
  977.7 5.4 copy-start.31
  977.7 5.4 copy-start.36
  977.7 6.3 copy-start.30
  977.7 6.3 copy-start.35
  985.9 65.5 %copy-start.2 = (bf16[256,1536]{1,0:T(8,128)(2,1)S(1)}, bf16[256,1536]{1,0:T(8,128)(2,1)}, u32[]{:S(2)}) copy-start(bf16[256,1536]{1,0:T(8,128)(2,1)} %convolution_convert_fusion.refs_7_) | copy-start | bytes 2359300
  1051.4 3.4 copy-start.32
  1051.4 3.4 copy-start.37
  1051.4 4.2 copy-start.17
  1051.4 4.2 copy-start.18
  (21 other events, 30.7 us)
